TPU v7x, 32 devices: a whole 2x2x4 slice. The times are simulated.
32 devices in a mesh: dp: 4 (over z), expert: 2 (over y), tensor: 4 (over x, core).
Axes of the slice: x: 2, y: 2, z: 4, core: 2. Of those that a mesh axis runs over, the one named last changes fastest.
Arguments:
- tokens: bfloat16 [8192, 768], P(('dp', 'expert', 'tensor')), may hold values from -6 to 6
- cotangent: bfloat16 [8192, 768], P(('dp', 'expert', 'tensor')), may hold values from -6 to 6
- timesteps: int32 [32], P(('dp', 'expert')), may hold values from 0 to 999
- ada_weight: bfloat16 [768, 6, 768], P(None, None, 'tensor'), may hold values from -0.4375 to 0.4375
- ada_bias: float32 [6, 768], P(None, 'tensor'), may hold values from -1.5 to 1.5
- qkv_weight: bfloat16 [768, 3, 768], P(None, None, 'tensor'), may hold values from -0.21875 to 0.21875
- out_weight: bfloat16 [768, 768], P('tensor'), may hold values from -0.875 to 0.875
- router_weight: bfloat16 [768, 8], replicated, may hold values from -0.15625 to 0.15625
- shared_up: bfloat16 [768, 3072], P(None, 'tensor'), may hold values from -0.21875 to 0.21875
- shared_down: bfloat16 [3072, 768], P('tensor'), may hold values from -0.109375 to 0.109375
- expert_up: bfloat16 [8, 768, 3072], P('expert', None, 'tensor'), may hold values from -0.21875 to 0.21875
- expert_down: bfloat16 [8, 3072, 768], P('expert', 'tensor'), may hold values from -0.109375 to 0.109375
- routes: int32 [8192, 2], P(('dp', 'expert', 'tensor')), may hold values from 0 to 7, as said below
- places: int32 [8192, 2], P(('dp', 'expert', 'tensor')), may hold values from 0 to 80, as said below
Outputs:
- output: bfloat16 [8192, 768], P(('dp', 'expert', 'tensor'))
- grad_tokens: float32 [8192, 768], P(('dp', 'expert', 'tensor'))
- grad_ada_weight: float32 [768, 6, 768], P(None, None, 'tensor')
- grad_ada_bias: float32 [6, 768], P(None, 'tensor')
- grad_qkv_weight: float32 [768, 3, 768], P(None, None, 'tensor')
- grad_out_weight: float32 [768, 768], P('tensor')
- grad_router_weight: float32 [768, 8], replicated
- grad_shared_up: float32 [768, 3072], P(None, 'tensor')
- grad_shared_down: float32 [3072, 768], P('tensor')
- grad_expert_up: float32 [8, 768, 3072], P('expert', None, 'tensor')
- grad_expert_down: float32 [8, 3072, 768], P('expert', 'tensor')
- expert_counts: int32 [8], replicated
Inputs may be any that keep to these rules, and one draw needn't show every extreme that they name: `routes`: each row names two different experts. places[p, k] is the smaller of 80 and the number of pairs (p', k') that come before (p, k), in the order of patches and then of k, within the same aligned block of 256 rows and name the same expert as routes[p, k]. Pairs with a place of 80 are dropped.
All inputs are finite; a program needn't handle non-finite values.
Results may differ from a plain program's by a relative error of at most 0.0165.
The roundings to bfloat16 on the way count: a program that leaves them out, or rounds other values in their place, can miss the bound.
Values may be sent and summed in bfloat16 or wider, within the bound.
No kernel may reach another device: no remote copies, remote signals or barrier semaphores. Data moves between devices by JAX's collectives and lax.ppermute only.
A program may use at most 192 MiB of HBM per device.

v0:
```python
import math

import jax
import jax.numpy as jnp
from jax import lax
from jax.sharding import PartitionSpec as P

HD = 64
EXPERTS = 8
TOPK = 2
PATCHES = 256
CAP = 80


EPSILON = 1e-06


def tanh_gelu(values):
    return jax.nn.gelu(values, approximate=True)


def normalize(values):
    center = jnp.mean(values, axis=-1, keepdims=True)
    shifted = values - center
    inverse = lax.rsqrt(jnp.mean(shifted * shifted, axis=-1, keepdims=True) + EPSILON)
    return (shifted * inverse, inverse)


def normalize_back(normed, inverse, upstream):
    return inverse * (
        upstream
        - jnp.mean(upstream, axis=-1, keepdims=True)
        - normed * jnp.mean(upstream * normed, axis=-1, keepdims=True)
    )


def embedding(steps, model_width):
    half_width = model_width // 2
    freqs_all = jnp.exp(-math.log(10000.0) * jnp.arange(half_width, dtype=jnp.float32) / half_width)
    angles = steps.astype(jnp.float32)[:, None] * freqs_all[None, :]
    return jnp.concatenate([jnp.cos(angles), jnp.sin(angles)], axis=1)


def feed_both(inputs, cotans, weight_in, weight_out):
    pre_act = jnp.einsum("end,edf->enf", inputs, weight_in, preferred_element_type=jnp.float32)
    active, gelu_back = jax.vjp(tanh_gelu, pre_act)
    act_low = active.astype(jnp.bfloat16)
    result = jnp.einsum("enf,efd->end", act_low, weight_out, preferred_element_type=jnp.float32)
    act_grad = jnp.einsum("end,efd->enf", cotans, weight_out, preferred_element_type=jnp.float32)
    pre_grad = gelu_back(act_grad)[0].astype(jnp.bfloat16)
    back_rows = jnp.einsum("enf,edf->end", pre_grad, weight_in, preferred_element_type=jnp.float32)
    grad_in = jnp.einsum("end,enf->edf", inputs, pre_grad, preferred_element_type=jnp.float32)
    grad_out = jnp.einsum("enf,end->efd", act_low, cotans, preferred_element_type=jnp.float32)
    return (result, back_rows, grad_in, grad_out)


def local(
    tokens,
    cotangent,
    timesteps,
    ada_weight,
    ada_bias,
    qkv_weight,
    out_weight,
    router_weight,
    shared_up,
    shared_down,
    expert_up,
    expert_down,
    routes,
    places,
):
    local_tokens, model_width = tokens.shape
    images_dev = local_tokens // PATCHES
    slot_count = EXPERTS * CAP
    scale_factor = 1.0 / math.sqrt(HD)
    condition = jax.nn.silu(embedding(timesteps, model_width)).astype(jnp.bfloat16)
    mod_cols = (
        jnp.einsum("id,dcf->icf", condition, ada_weight, preferred_element_type=jnp.float32)
        + ada_bias[None]
    )
    modulation = lax.all_to_all(mod_cols, "tensor", split_axis=0, concat_axis=2, tiled=True)
    shift_one, scale_one, gate_one, shift_two, scale_two, gate_two = [
        modulation[:, column, None, :] for column in range(6)
    ]
    stream = tokens.astype(jnp.float32).reshape(images_dev, PATCHES, model_width)
    first_norm, first_inv = normalize(stream)
    attn_in = (
        (first_norm * (1.0 + scale_one) + shift_one)
        .astype(jnp.bfloat16)
        .reshape(local_tokens, model_width)
    )
    attn_rows = lax.all_gather(attn_in, "tensor", axis=0, tiled=True)
    group_rows = attn_rows.shape[0]
    group_images = group_rows // PATCHES
    triple = jnp.einsum(
        "rd,dcf->rcf", attn_rows, qkv_weight, preferred_element_type=jnp.float32
    ).astype(jnp.bfloat16)
    local_width = triple.shape[2]
    local_heads = local_width // HD
    triple = triple.reshape(group_images, PATCHES, 3, local_heads, HD)
    queries = triple[:, :, 0]
    keys_all = triple[:, :, 1]
    values_all = triple[:, :, 2]
    scores = (
        jnp.einsum("iphd,iqhd->ihpq", queries, keys_all, preferred_element_type=jnp.float32)
        * scale_factor
    )
    soft_weights = jax.nn.softmax(scores, axis=-1)
    soft_low = soft_weights.astype(jnp.bfloat16)
    context = (
        jnp.einsum("ihpq,iqhd->iphd", soft_low, values_all, preferred_element_type=jnp.float32)
        .astype(jnp.bfloat16)
        .reshape(group_rows, local_width)
    )
    picked = context
    attn_out = lax.psum_scatter(
        jnp.dot(picked, out_weight, preferred_element_type=jnp.float32),
        "tensor",
        scatter_dimension=0,
        tiled=True,
    ).reshape(images_dev, PATCHES, model_width)
    residual = stream + gate_one * attn_out
    second_norm, second_inv = normalize(residual)
    moe_in = (
        (second_norm * (1.0 + scale_two) + shift_two)
        .astype(jnp.bfloat16)
        .reshape(local_tokens, model_width)
    )
    logits = jnp.dot(moe_in, router_weight, preferred_element_type=jnp.float32)
    pair_hot = (routes[:, :, None] == jnp.arange(EXPERTS, dtype=jnp.int32)[None, None, :]).astype(
        jnp.float32
    )
    chosen = jnp.sum(pair_hot * logits[:, None, :], axis=2)
    pair_gates = jax.nn.softmax(chosen, axis=1)
    kept_pair = (places < CAP).astype(jnp.float32)
    pair_scale = kept_pair * pair_gates
    upstream = cotangent.astype(jnp.float32).reshape(images_dev, PATCHES, model_width)
    moe_grad = (gate_two * upstream).reshape(local_tokens, model_width)
    shared_cot = moe_grad.astype(jnp.bfloat16)
    slot_index = jnp.where(places < CAP, routes * CAP + places, slot_count)
    flat_slots = slot_index.reshape(-1)
    owner_token = jnp.repeat(jnp.arange(local_tokens, dtype=jnp.int32), TOPK)
    slot_token = (
        jnp.zeros((slot_count + 1,), jnp.int32).at[flat_slots].set(owner_token)[:slot_count]
    )
    slot_used = jnp.zeros((slot_count + 1,), jnp.bfloat16).at[flat_slots].set(1.0)[:slot_count]
    slot_scale = (
        jnp.zeros((slot_count + 1,), jnp.float32)
        .at[flat_slots]
        .set(pair_scale.reshape(-1))[:slot_count]
    )
    send_rows = (moe_in[slot_token] * slot_used[:, None]).reshape(EXPERTS, CAP, model_width)
    send_cot = (
        (moe_grad[slot_token] * slot_scale[:, None])
        .astype(jnp.bfloat16)
        .reshape(EXPERTS, CAP, model_width)
    )
    recv_rows, recv_cot = (
        lax.all_to_all(send_rows, "expert", split_axis=0, concat_axis=1, tiled=True),
        lax.all_to_all(send_cot, "expert", split_axis=0, concat_axis=1, tiled=True),
    )
    rows_all, cot_all, routed_all, routed_cot_all = (
        lax.all_gather(moe_in, "tensor", axis=0, tiled=True),
        lax.all_gather(shared_cot, "tensor", axis=0, tiled=True),
        lax.all_gather(recv_rows, "tensor", axis=1, tiled=True),
        lax.all_gather(recv_cot, "tensor", axis=1, tiled=True),
    )
    shared_res, shared_back, shared_up_grad, shared_down_grad = feed_both(
        rows_all[None], cot_all[None], shared_up[None], shared_down[None]
    )
    routed_res, routed_back, expert_up_grad, expert_down_grad = feed_both(
        routed_all, routed_cot_all, expert_up, expert_down
    )
    shared_res, shared_back, routed_res, routed_back = (
        lax.psum_scatter(shared_res[0], "tensor", scatter_dimension=0, tiled=True),
        lax.psum_scatter(shared_back[0], "tensor", scatter_dimension=0, tiled=True),
        lax.psum_scatter(routed_res, "tensor", scatter_dimension=1, tiled=True),
        lax.psum_scatter(routed_back, "tensor", scatter_dimension=1, tiled=True),
    )
    shared_up_grad = shared_up_grad[0]
    shared_down_grad = shared_down_grad[0]
    back_res, back_grad = (
        lax.all_to_all(routed_res, "expert", split_axis=1, concat_axis=0, tiled=True),
        lax.all_to_all(routed_back, "expert", split_axis=1, concat_axis=0, tiled=True),
    )
    safe_index = jnp.minimum(slot_index, slot_count - 1)
    pair_res = back_res.reshape(slot_count, model_width)[safe_index] * kept_pair[:, :, None]
    pair_back = back_grad.reshape(slot_count, model_width)[safe_index] * kept_pair[:, :, None]
    moe_out = shared_res + jnp.sum(pair_gates[:, :, None] * pair_res, axis=1)
    moe_block = moe_out.reshape(images_dev, PATCHES, model_width)
    output = (
        (residual + gate_two * moe_block).astype(jnp.bfloat16).reshape(local_tokens, model_width)
    )
    gate_two_grad = jnp.sum(upstream * moe_block, axis=1)
    gates_grad = jnp.sum(moe_grad[:, None, :] * pair_res, axis=2)
    chosen_grad = pair_gates * (
        gates_grad - jnp.sum(pair_gates * gates_grad, axis=1, keepdims=True)
    )
    logits_grad = jnp.sum(chosen_grad[:, :, None] * pair_hot, axis=1).astype(jnp.bfloat16)
    router_grad = jnp.einsum("td,te->de", moe_in, logits_grad, preferred_element_type=jnp.float32)
    moe_in_grad = (
        shared_back
        + jnp.sum(pair_back, axis=1)
        + jnp.einsum("te,de->td", logits_grad, router_weight, preferred_element_type=jnp.float32)
    )
    moe_in_grad = moe_in_grad.reshape(images_dev, PATCHES, model_width)
    shift_two_grad = jnp.sum(moe_in_grad, axis=1)
    scale_two_grad = jnp.sum(moe_in_grad * second_norm, axis=1)
    residual_grad = upstream + normalize_back(
        second_norm, second_inv, moe_in_grad * (1.0 + scale_two)
    )
    attn_grad = (gate_one * residual_grad).astype(jnp.bfloat16).reshape(local_tokens, model_width)
    gate_one_grad = jnp.sum(residual_grad * attn_out, axis=1)
    grad_rows = lax.all_gather(attn_grad, "tensor", axis=0, tiled=True)
    out_weight_grad = jnp.einsum(
        "rf,rd->fd", context, grad_rows, preferred_element_type=jnp.float32
    )
    context_grad = jnp.einsum(
        "rd,fd->rf", grad_rows, out_weight, preferred_element_type=jnp.float32
    ).astype(jnp.bfloat16)
    context_grad = context_grad.reshape(group_images, PATCHES, local_heads, HD)
    soft_grad = jnp.einsum(
        "iphd,iqhd->ihpq", context_grad, values_all, preferred_element_type=jnp.float32
    )
    value_grad = jnp.einsum(
        "ihpq,iphd->iqhd", soft_low, context_grad, preferred_element_type=jnp.float32
    ).astype(jnp.bfloat16)
    score_grad = (
        soft_weights * (soft_grad - jnp.sum(soft_grad * soft_weights, axis=-1, keepdims=True))
    ).astype(jnp.bfloat16)
    query_grad = (
        jnp.einsum("ihpq,iqhd->iphd", score_grad, keys_all, preferred_element_type=jnp.float32)
        * scale_factor
    ).astype(jnp.bfloat16)
    key_grad = (
        jnp.einsum("ihpq,iphd->iqhd", score_grad, queries, preferred_element_type=jnp.float32)
        * scale_factor
    ).astype(jnp.bfloat16)
    triple_grad = jnp.stack([query_grad, key_grad, value_grad], axis=2).reshape(
        group_rows, 3, local_width
    )
    qkv_grad = jnp.einsum("rd,rcf->dcf", attn_rows, triple_grad, preferred_element_type=jnp.float32)
    picked = triple_grad
    attn_in_grad = lax.psum_scatter(
        jnp.einsum("rcf,dcf->rd", picked, qkv_weight, preferred_element_type=jnp.float32),
        "tensor",
        scatter_dimension=0,
        tiled=True,
    ).reshape(images_dev, PATCHES, model_width)
    shift_one_grad = jnp.sum(attn_in_grad, axis=1)
    scale_one_grad = jnp.sum(attn_in_grad * first_norm, axis=1)
    tokens_grad = residual_grad + normalize_back(
        first_norm, first_inv, attn_in_grad * (1.0 + scale_one)
    )
    mod_grad = jnp.stack(
        [
            shift_one_grad,
            scale_one_grad,
            gate_one_grad,
            shift_two_grad,
            scale_two_grad,
            gate_two_grad,
        ],
        axis=1,
    )
    mod_grad_cols = lax.all_to_all(mod_grad, "tensor", split_axis=2, concat_axis=0, tiled=True)
    ada_grad = jnp.einsum(
        "id,icf->dcf", condition.astype(jnp.float32), mod_grad_cols, precision=lax.Precision.HIGHEST
    )
    ada_bias_grad = jnp.sum(mod_grad_cols, axis=0)
    counts_local = jnp.sum(pair_hot, axis=(0, 1))
    dense_sums = lax.psum(
        (ada_grad, ada_bias_grad, qkv_grad, out_weight_grad, shared_up_grad, shared_down_grad),
        ("dp", "expert"),
    )
    expert_sums = lax.psum((expert_up_grad, expert_down_grad), "dp")
    router_sums = lax.psum((router_grad, counts_local), ("dp", "expert", "tensor"))
    return (
        output,
        tokens_grad.reshape(local_tokens, model_width),
        dense_sums[0],
        dense_sums[1],
        dense_sums[2],
        dense_sums[3],
        router_sums[0],
        dense_sums[4],
        dense_sums[5],
        expert_sums[0],
        expert_sums[1],
        router_sums[1].astype(jnp.int32),
    )


def solution(mesh):
    placed = (
        P(("dp", "expert", "tensor"), None),
        P(("dp", "expert", "tensor"), None),
        P(("dp", "expert")),
        P(None, None, "tensor"),
        P(None, "tensor"),
        P(None, None, "tensor"),
        P("tensor", None),
        P(),
        P(None, "tensor"),
        P("tensor", None),
        P("expert", None, "tensor"),
        P("expert", "tensor", None),
        P(("dp", "expert", "tensor"), None),
        P(("dp", "expert", "tensor"), None),
    )
    return jax.shard_map(
        local,
        mesh=mesh,
        in_specs=placed,
        out_specs=(
            P(("dp", "expert", "tensor"), None),
            P(("dp", "expert", "tensor"), None),
            P(None, None, "tensor"),
            P(None, "tensor"),
            P(None, None, "tensor"),
            P("tensor", None),
            P(),
            P(None, "tensor"),
            P("tensor", None),
            P("expert", None, "tensor"),
            P("expert", "tensor", None),
            P(),
        ),
        check_vma=False,
    )
```

profile of v0, /device:TPU:0, one launch (start us, length us, event | category | flops | bytes accessed | tf_op | source)
XLA Modules:
  0.0 1534.7 jit_solution(14079578405554964155)
XLA Ops:
  10.7 4.2 all-to-all-start
  20.1 20.6 %all-gather.7.cloned.1.call-done = bf16[1024,768]{1,0:T(8,128)(2,1)} async-done(((bf16[256,768]{1,0:T(8,128)(2,1)}), bf16[1024,768]{1,0:T(8,128)(2,1)}) %all-gather.7.cloned.1.call-update) | async-done | bytes 1572880 | tf_op jit(solution)/shard_map/all_gather | solution.py:93
  58.0 3.3 gather_fusion.2
  61.4 30.6 %reduce-scatter.7.cloned.1.call-done = f32[256,768]{1,0:T(8,128)} async-done(((f32[1024,768]{1,0:T(8,128)}), f32[256,768]{1,0:T(8,128)}) %reduce-scatter.7.cloned.1.call-update) | async-done | bytes 786448 | tf_op jit(solution)/shard_map/reduce_scatter | solution.py:117
  99.6 15.6 %all_to_all.102 = bf16[8,80,768]{2,1,0:T(8,128)(2,1)S(1)} all-to-all(bf16[8,80,768]{2,1,0:T(8,128)(2,1)S(1)} %multiply_convert_fusion.3), channel_id=1, replica_groups=mesh['dp'=4,'expert'=2,'tensor'=4] {'expert'}, dimensions={0} | all-to-all | bytes 1966080 | tf_op jit(solution)/shard_map/all_to_all | solution.py:161
  116.5 3.8 scatter_custom_fusion.1
  124.8 14.7 all_to_all.103
  141.7 6.8 all-gather.15.cloned.1.call-done
  148.5 10.1 fusion.82
  158.6 25.0 %all-gather.11.cloned.1.call-done = bf16[4,640,768]{2,1,0:T(8,128)(2,1)} async-done(((bf16[4,160,768]{2,1,0:T(8,128)(2,1)}), bf16[4,640,768]{2,1,0:T(8,128)(2,1)}) %all-gather.11.cloned.1.call-update) | async-done | bytes 3932176 | tf_op jit(solution)/shard_map/all_gather | solution.py:166
  183.6 13.6 fusion.7
  197.2 3.0 copy-done.68
  200.3 8.1 fusion.72
  208.5 10.0 fusion.83
  219.0 4.8 fusion.80
  226.6 6.5 fusion.14
  234.2 3.1 fusion.81
  238.8 6.4 fusion.70
  245.2 53.6 %reduce-scatter.11.cloned.1.call-done = f32[4,160,768]{2,1,0:T(8,128)} async-done(((f32[4,640,768]{2,1,0:T(8,128)}), f32[4,160,768]{2,1,0:T(8,128)}) %reduce-scatter.11.cloned.1.call-update) | async-done | bytes 1966096 | tf_op jit(solution)/shard_map/reduce_scatter | solution.py:178
  298.8 4.1 copy.172
  302.9 3.7 all-to-all-start.2
  306.7 64.3 %reduce-scatter.15.cloned.1.call-done = f32[4,160,768]{2,1,0:T(8,128)} async-done(((f32[4,640,768]{2,1,0:T(8,128)}), f32[4,160,768]{2,1,0:T(8,128)}) %reduce-scatter.15.cloned.1.call-update) | async-done | bytes 1966096 | tf_op jit(solution)/shard_map/reduce_scatter | solution.py:179
  371.0 4.1 copy.178
  375.1 4.8 all-to-all-start.4
  388.3 3.0 reshape.432
  391.3 12.4 all-to-all-done.4
  408.2 3.1 reshape.448
  411.4 7.6 multiply_reduce_fusion.2
  421.4 3.0 multiply_reduce_fusion.5
  425.0 27.0 %reduce-scatter.9.cloned.1.call-done = f32[256,768]{1,0:T(8,128)} async-done(((f32[1024,768]{1,0:T(8,128)}), f32[256,768]{1,0:T(8,128)}) %reduce-scatter.9.cloned.1.call-update) | async-done | bytes 786448 | tf_op jit(solution)/shard_map/reduce_scatter | solution.py:176
  452.0 3.0 fusion.39
  457.9 19.8 %all-gather.17.cloned.1.call-done = bf16[1024,768]{1,0:T(8,128)(2,1)} async-done(((bf16[256,768]{1,0:T(8,128)(2,1)}), bf16[1024,768]{1,0:T(8,128)(2,1)}) %all-gather.17.cloned.1.call-update) | async-done | bytes 1572880 | tf_op jit(solution)/shard_map/all_gather | solution.py:215
  489.5 4.3 convolution_bitcast_fusion
  494.1 11.1 fusion.86
  505.2 11.6 fusion.71
  518.3 4.4 fusion.85
  522.7 3.3 fusion.69
  528.7 3.2 reduce-scatter.17.cloned.1.call-done
  536.9 3.3 all-to-all-start.5
  545.6 3.4 fusion.47
  550.1 48.4 %all-reduce = (f32[768,8]{0,1:T(8,128)}, f32[8]{0:T(128)S(1)}) all-reduce(f32[768,8]{0,1:T(8,128)S(1)} %fusion.88, f32[8]{0:T(128)S(1)} %copy-done.59), channel_id=1, replica_groups=mesh['dp'=4,'expert'=2,'tensor'=4] {'dp','expert','tensor'}, use_global_device_ids=true, to_apply=%region_39.40 | all-reduce | flops 6152 | bytes 49216 | tf_op jit(solution)/shard_map/psum | solution.py:278
  600.2 22.2 %psum.71 = f32[6,192]{1,0:T(8,128)} all-reduce(f32[6,192]{1,0:T(8,128)S(1)} %bitcast_reduce_fusion), channel_id=1, replica_groups=mesh['dp'=4,'expert'=2,'tensor'=4] {'dp','expert'}, use_global_device_ids=true, to_apply=%region_36.37 | all-reduce | flops 1152 | bytes 9216 | tf_op jit(solution)/shard_map/psum | solution.py:273
  622.4 544.9 %all-reduce.8.cloned.1.call-done = (f32[4,768,768]{2,1,0:T(8,128)}, f32[4,768,768]{2,1,0:T(8,128)}) async-done(((f32[4,768,768]{2,1,0:T(8,128)}, f32[4,768,768]{2,1,0:T(8,128)}), (f32[4,768,768]{2,1,0:T(8,128)}, f32[4,768,768]{2,1,0:T(8,128)})) %all-reduce.8.cloned.1.call-update) | async-done | bytes 18874384 | tf_op jit(solution)/shard_map/psum | solution.py:277
  1167.3 338.6 %all-reduce.6.cloned.1.call-done = (f32[768,6,192]{0,2,1:T(8,128)}, f32[768,3,192]{0,2,1:T(8,128)}, f32[192,768]{1,0:T(8,128)}, f32[768,768]{1,0:T(8,128)}, f32[768,768]{1,0:T(8,128)}) async-done(((f32[768,6,192]{0,2,1:T(8,128)}, f32[768,3,192]{0,2,1:T(8,128)}, f32[192,768]{1,0:T(8,128)}, f32[768,768]{1,0:T(8,128)}, f32[768,768]{1,0:T(8,128)}), (f32[768,6,192]{0,2,1:T(8,128)}, f32[768,3,192]{0,2,1:T(8,128)}, ...) | async-done | bytes 10616848 | tf_op jit(solution)/shard_map/psum | solution.py:273
  1505.9 4.4 copy.231
  1510.2 3.4 copy.232
  1517.3 4.8 copy.236
  1523.9 3.8 copy.237
  (299 shorter events, 100.6 us)
Async XLA Ops:
  7.2 11.8 copy-start.4
  7.2 33.5 %copy-start.66 = (bf16[768,3,192]{0,2,1:T(8,128)(2,1)S(1)}, bf16[768,3,192]{0,2,1:T(8,128)(2,1)}, u32[]{:S(2)}) copy-start(bf16[768,3,192]{0,2,1:T(8,128)(2,1)} %param.19) | copy-start | bytes 2654212
  10.7 8.2 all-to-all-start
  14.9 25.8 %all-gather.7.cloned.1.call-start = ((), (), s32[]{:S(2)}) async-start(), calls=%async_computation.12 | async-start | bytes 1966080 | tf_op jit(solution)/shard_map/all_gather | solution.py:93
  16.0 27.2 %copy-start.47 = (f32[256]{0:T(256)}, f32[256]{0:T(256)S(1)}, u32[]{:S(2)}) copy-start(f32[256]{0:T(256)S(1)} %broadcast_multiply_fusion.6) | copy-start | bytes 3076
  17.3 25.9 %copy-start.52 = (f32[256]{0:T(256)}, f32[256]{0:T(256)S(1)}, u32[]{:S(2)}) copy-start(f32[256]{0:T(256)S(1)} %add_rsqrt_fusion.1) | copy-start | bytes 3076
  19.0 24.2 %copy-start.36 = (f32[768]{0:T(1024)}, f32[768]{0:T(1024)S(1)}, u32[]{:S(2)}) copy-start(f32[768]{0:T(1024)S(1)} %get-tuple-element.27) | copy-start | bytes 9220
  19.0 73.0 %copy-start.45 = (f32[768]{0:T(1024)}, f32[768]{0:T(1024)S(1)}, u32[]{:S(2)}) copy-start(f32[768]{0:T(1024)S(1)} %get-tuple-element.28) | copy-start | bytes 9220
  20.0 71.9 %reduce-scatter.7.cloned.1.call-start = ((), (), s32[]{:S(2)}) async-start(), calls=%async_computation.13 | async-start | bytes 3932160 | tf_op jit(solution)/shard_map/reduce_scatter | solution.py:117
  53.9 94.6 %all-gather.15.cloned.1.call-start = ((), (), s32[]{:S(2)}) async-start(), calls=%async_computation.20 | async-start | bytes 4915200 | tf_op jit(solution)/shard_map/all_gather | solution.py:167
  61.4 32.8 %copy-start.42 = (bf16[768,8]{0,1:T(8,128)(2,1)S(1)}, bf16[768,8]{0,1:T(8,128)(2,1)}, u32[]{:S(2)}) copy-start(bf16[768,8]{0,1:T(8,128)(2,1)} %param.21) | copy-start | bytes 36868
  93.8 27.2 %copy-start.2 = (bf16[256,768]{1,0:T(8,128)(2,1)}, bf16[256,768]{1,0:T(8,128)(2,1)S(1)}, u32[]{:S(2)}) copy-start(bf16[256,768]{1,0:T(8,128)(2,1)S(1)} %add_convert_fusion.1) | copy-start | bytes 1179652
  116.3 67.3 %all-gather.11.cloned.1.call-start = ((), (), s32[]{:S(2)}) async-start(), calls=%async_computation.16 | async-start | bytes 4915200 | tf_op jit(solution)/shard_map/all_gather | solution.py:166
  140.5 78.5 %all-gather.13.cloned.1.call-start = ((), (), s32[]{:S(2)}) async-start(), calls=%async_computation.18 | async-start | bytes 1966080 | tf_op jit(solution)/shard_map/all_gather | solution.py:165
  141.1 85.5 %all-gather.9.cloned.1.call-start = ((), (), s32[]{:S(2)}) async-start(), calls=%async_computation.14 | async-start | bytes 1966080 | tf_op jit(solution)/shard_map/all_gather | solution.py:164
  141.7 157.2 %reduce-scatter.11.cloned.1.call-start = ((), (), s32[]{:S(2)}) async-start(), calls=%async_computation.17 | async-start | bytes 9830400 | tf_op jit(solution)/shard_map/reduce_scatter | solution.py:178
  208.4 162.6 %reduce-scatter.15.cloned.1.call-start = ((), (), s32[]{:S(2)}) async-start(), calls=%async_computation.21 | async-start | bytes 9830400 | tf_op jit(solution)/shard_map/reduce_scatter | solution.py:179
  218.5 8.1 copy-start.64
  218.5 202.9 %reduce-scatter.13.cloned.1.call-start = ((), (), s32[]{:S(2)}) async-start(), calls=%async_computation.19 | async-start | bytes 3932160 | tf_op jit(solution)/shard_map/reduce_scatter | solution.py:177
  237.3 214.7 %reduce-scatter.9.cloned.1.call-start = ((), (), s32[]{:S(2)}) async-start(), calls=%async_computation.15 | async-start | bytes 3932160 | tf_op jit(solution)/shard_map/reduce_scatter | solution.py:176
  302.9 72.1 %all-to-all-start.2 = ((f32[4,160,768]{2,0,1:T(4,128)}), f32[4,160,768]{2,0,1:T(4,128)S(1)}, u32[]{:S(2)}, u32[]{:S(2)}) async-start(f32[4,160,768]{2,0,1:T(4,128)} %copy.172), calls=%async_computation.5 | async-start | bytes 3932160 | tf_op jit(solution)/shard_map/all_to_all | solution.py:184
  306.7 76.2 %copy-start.46 = (f32[256,2]{0,1:T(2,128)S(1)}, f32[256,2]{0,1:T(2,128)}, u32[]{:S(2)}) copy-start(f32[256,2]{0,1:T(2,128)} %get-tuple-element.43) | copy-start | bytes 6148
  375.0 8.6 copy-start.8
  375.1 28.6 %all-to-all-start.4 = ((f32[4,160,768]{2,0,1:T(4,128)}), f32[4,160,768]{2,0,1:T(4,128)}, u32[]{:S(2)}, u32[]{:S(2)}) async-start(f32[4,160,768]{2,0,1:T(4,128)} %copy.178), calls=%async_computation.9 | async-start | bytes 3932160 | tf_op jit(solution)/shard_map/all_to_all | solution.py:185
  379.9 97.8 %all-gather.17.cloned.1.call-start = ((), (), s32[]{:S(2)}) async-start(), calls=%async_computation.22 | async-start | bytes 1966080 | tf_op jit(solution)/shard_map/all_gather | solution.py:215
  418.9 33.1 %copy-start.18 = (f32[256,768]{1,0:T(8,128)S(1)}, f32[256,768]{1,0:T(8,128)}, u32[]{:S(2)}) copy-start(f32[256,768]{1,0:T(8,128)} %reduce-scatter.7.cloned.1.call-done) | copy-start | bytes 2359300
  418.9 33.1 %copy-start.20 = (f32[256,768]{1,0:T(8,128)S(1)}, f32[256,768]{1,0:T(8,128)}, u32[]{:S(2)}) copy-start(f32[256,768]{1,0:T(8,128)} %get-tuple-element.13) | copy-start | bytes 2359300
  418.9 33.1 %copy-start.25 = (bf16[256,768]{1,0:T(8,128)(2,1)S(1)}, bf16[256,768]{1,0:T(8,128)(2,1)}, u32[]{:S(2)}) copy-start(bf16[256,768]{1,0:T(8,128)(2,1)} %param.15) | copy-start | bytes 1179652
  421.4 30.6 %copy-start.43 = (bf16[256,8]{0,1:T(8,128)(2,1)}, bf16[256,8]{0,1:T(8,128)(2,1)S(1)}, u32[]{:S(2)}) copy-start(bf16[256,8]{0,1:T(8,128)(2,1)S(1)} %get-tuple-element.30) | copy-start | bytes 12292
  455.0 27.5 %copy-start.7 = (f32[4,3,256,256]{2,3,1,0:T(8,128)S(1)}, f32[4,3,256,256]{2,3,1,0:T(8,128)}, u32[]{:S(2)}) copy-start(f32[4,3,256,256]{2,3,1,0:T(8,128)} %copy-done.6) | copy-start | bytes 9437188
  455.0 27.5 %copy-start.30 = (bf16[4,256,1,3,64]{1,0,4,3,2:T(4,128)(2,1)S(1)}, bf16[4,256,1,3,64]{1,0,4,3,2:T(4,128)(2,1)}, u32[]{:S(2)}) copy-start(bf16[4,256,1,3,64]{1,0,4,3,2:T(4,128)(2,1)} %copy-done.29) | copy-start | bytes 1179652
  455.0 27.5 %copy-start.35 = (f32[4,3,256]{2,1,0:T(4,128)S(1)}, f32[4,3,256]{2,1,0:T(4,128)}, u32[]{:S(2)}) copy-start(f32[4,3,256]{2,1,0:T(4,128)} %copy-done.34) | copy-start | bytes 36868
  457.9 74.1 %reduce-scatter.17.cloned.1.call-start = ((), (), s32[]{:S(2)}) async-start(), calls=%async_computation.23 | async-start | bytes 3932160 | tf_op jit(solution)/shard_map/reduce_scatter | solution.py:245
  493.8 673.5 %all-reduce.8.cloned.1.call-start = ((), (), s32[]{:S(2)}) async-start(), calls=%async_computation.25 | async-start | bytes 37748736 | tf_op jit(solution)/shard_map/psum | solution.py:277
  494.1 11.2 copy-start.60
  528.7 11.6 copy-start.13
  528.7 11.6 copy-start.23
  528.7 16.9 %copy-start.39 = (f32[4,384]{1,0:T(4,128)S(1)}, f32[4,384]{1,0:T(4,128)}, u32[]{:S(2)}) copy-start(f32[4,384]{1,0:T(4,128)} %copy-done.38) | copy-start | bytes 18436
  528.7 16.9 %copy-start.41 = (f32[4,384]{1,0:T(4,128)S(1)}, f32[4,384]{1,0:T(4,128)}, u32[]{:S(2)}) copy-start(f32[4,384]{1,0:T(4,128)} %copy-done.40) | copy-start | bytes 18436
  536.9 7.1 all-to-all-start.5
  540.2 965.7 %all-reduce.6.cloned.1.call-start = ((), (), s32[]{:S(2)}) async-start(), calls=%async_computation.24 | async-start | bytes 21233664 | tf_op jit(solution)/shard_map/psum | solution.py:273
  549.0 50.1 %copy-start.10 = (f32[256,768]{1,0:T(8,128)S(1)}, f32[256,768]{1,0:T(8,128)}, u32[]{:S(2)}) copy-start(f32[256,768]{1,0:T(8,128)} %copy-done.9) | copy-start | bytes 2359300
  549.0 50.1 %copy-start.19 = (f32[256,768]{1,0:T(8,128)S(1)}, f32[256,768]{1,0:T(8,128)}, u32[]{:S(2)}) copy-start(f32[256,768]{1,0:T(8,128)} %reduce-scatter.17.cloned.1.call-done) | copy-start | bytes 2359300
  1505.9 7.8 copy-start.26
  1505.9 11.4 slice-start.3
  1505.9 11.4 slice-start.4
  1517.3 6.4 slice-start.1
  1517.3 6.6 slice-start.2
  (46 other events, 120.7 us)
Sparse Core Ops, SparseCore 0:
  20.2 20.4 all-gather.6
  54.0 37.9 reduce-scatter.6
  116.4 32.0 all-gather.14
  150.6 32.9 all-gather.10
  185.7 19.6 all-gather.12
  206.9 19.6 all-gather.8
  229.8 68.9 reduce-scatter.10
  302.0 68.9 reduce-scatter.14
  373.7 37.9 reduce-scatter.12
  414.1 37.9 reduce-scatter.8
  458.0 19.6 all-gather.16
  493.9 37.9 reduce-scatter.16
  535.1 632.1 all-reduce.7
  1173.9 331.9 all-reduce.5
where the time goes:
time: 1540 us; the launch traced here: 1530 us
  waiting for transfers between devices  1150 us (75%)
  matrix products  122 us (8%)
  blocking collectives  101 us (7%)
  local copies, waits for them, and re-layouts  89.8 us (6%)
  other arithmetic  34.7 us (2%)
  starting transfers between devices  17.6 us (1%)
    psum x1, waiting for transfers between devices, local(): expert_sums = lax.psum((expert_up_grad, expert_down_grad), 'dp')  545 us
    psum x1, waiting for transfers between devices, local(): lax.psum((ada_grad, ada_bias_grad, qkv_grad, out_weight_grad, shared_up_g...  339 us
    reduce_scatter x1, waiting for transfers between devices, local(): lax.psum_scatter(routed_back, 'tensor', scatter_dimension=1, tiled=True)  64.3 us
    reduce_scatter x1, waiting for transfers between devices, local(): lax.psum_scatter(routed_res, 'tensor', scatter_dimension=1, tiled=True)  53.6 us
    psum x1, blocking collectives, local(): lax.psum((router_grad, counts_local), ('dp', 'expert', 'tensor'))  48.4 us
    unnamed x165, local copies, waits for them, and re-layouts  37.3 us
  transfers between devices with their start and end apart: 18, of which 15 were waited for; matrix products, arithmetic and copies ran while one was open for 11% of the time, Pallas kernels for 0%

commit v1 on v0

v1 whole, which is shorter than its diff:
```python
import functools
import math

import jax
import jax.numpy as jnp
from jax import lax
from jax.experimental import pallas as pl
from jax.experimental.pallas import tpu as pltpu
from jax.sharding import PartitionSpec as P

HD = 64
EXPERTS = 8
TOPK = 2
PATCHES = 256
CAP = 80
EXTRA = 16
EPSILON = 1e-06
GROUP = 8
FULL_LIMIT = 32 * 1024 * 1024

f32 = jnp.float32
bf16 = jnp.bfloat16
NN = (((1,), (0,)), ((), ()))
NT = (((1,), (1,)), ((), ()))
TN = (((0,), (0,)), ((), ()))
VMEM_LIMIT = 58 * 1024 * 1024


def mm(left, right, dims):
    return lax.dot_general(left, right, dims, preferred_element_type=f32)


def normalize(values):
    center = jnp.mean(values, axis=-1, keepdims=True)
    shifted = values - center
    inverse = lax.rsqrt(jnp.mean(shifted * shifted, axis=-1, keepdims=True) + EPSILON)
    return (shifted * inverse, inverse)


def normalize_back(normed, inverse, upstream):
    return inverse * (
        upstream
        - jnp.mean(upstream, axis=-1, keepdims=True)
        - normed * jnp.mean(upstream * normed, axis=-1, keepdims=True)
    )


def embedding(steps, model_width):
    half_width = model_width // 2
    freqs_all = jnp.exp(-math.log(10000.0) * jnp.arange(half_width, dtype=f32) / half_width)
    angles = steps.astype(f32)[:, None] * freqs_all[None, :]
    return jnp.concatenate([jnp.cos(angles), jnp.sin(angles)], axis=1)


def gelu_both(pre):
    const = math.sqrt(2.0 / math.pi)
    square = pre * pre
    tanh = jnp.tanh(const * pre * (1.0 + 0.044715 * square))
    half = 0.5 + 0.5 * tanh
    slope = half + 0.5 * pre * (1.0 - tanh * tanh) * (const * (1.0 + 3.0 * 0.044715 * square))
    return pre * half, slope


def whole(shape):
    return pl.BlockSpec(shape, lambda *_: (0,) * len(shape))


def pair_masks(rows):
    lane = lax.broadcasted_iota(jnp.int32, (rows, 2 * HD), 1)
    return (lane < HD, lane >= HD)


def head_probs(query, key):
    scores = mm(query, key, NT) * (1.0 / math.sqrt(HD))
    weights = jnp.exp(scores - jnp.max(scores, axis=-1, keepdims=True))
    return weights / jnp.sum(weights, axis=-1, keepdims=True)


def shard_rows(shards, part, local_width):
    return jnp.concatenate(
        [shard[part * local_width : (part + 1) * local_width, :] for shard in shards], axis=0
    )


def attention_kernel(
    local_width, tok_ref, mod_ref, cond_ref, router_ref, pairs_ref, w0, w1, w2, w3,
    attn_in_ref, qkv_ref, context_ref, attn_out_ref, ext_ref,
):
    shards = (w0, w1, w2, w3)
    rows, width = tok_ref.shape
    mod = mod_ref[...]
    stream = tok_ref[...].astype(f32)
    attn_in = (normalize(stream)[0] * (1.0 + mod[1:2]) + mod[0:1]).astype(bf16)
    attn_in_ref[...] = attn_in
    for part in range(3):
        qkv_ref[part] = mm(attn_in, shard_rows(shards, part, local_width), NT).astype(bf16)
    masks = pair_masks(rows)
    zero = jnp.zeros((rows, 2 * HD), bf16)
    for pair in range(width // (2 * HD)):
        cols = slice(pair * 2 * HD, (pair + 1) * 2 * HD)
        query, key, value = qkv_ref[0, :, cols], qkv_ref[1, :, cols], qkv_ref[2, :, cols]
        parts = []
        for mask in masks:
            probs = head_probs(jnp.where(mask, query, zero), key)
            parts.append(mm(probs.astype(bf16), value, NN))
        context_ref[:, cols] = jnp.where(masks[0], parts[0], parts[1]).astype(bf16)
    attn_out = mm(context_ref[...], shard_rows(shards, 3, local_width), NN)
    attn_out_ref[...] = attn_out
    residual = stream + mod[2:3] * attn_out
    moe_in = (normalize(residual)[0] * (1.0 + mod[4:5]) + mod[3:4]).astype(bf16)
    ext_ref[0:rows, :] = moe_in
    logits = mm(router_ref[...], moe_in, NT)
    pairs = pairs_ref[...]
    expert_id = lax.broadcasted_iota(jnp.int32, (EXPERTS, rows), 0)
    chosen = [
        jnp.sum(jnp.where(expert_id == pairs[k : k + 1], logits, 0.0), axis=0, keepdims=True)
        for k in range(TOPK)
    ]
    top = jnp.maximum(chosen[0], chosen[1])
    powers = [jnp.exp(value - top) for value in chosen]
    gates = [power / (powers[0] + powers[1]) for power in powers]
    high = [gate.astype(bf16).astype(f32) for gate in gates]
    rest = [gate - upper for gate, upper in zip(gates, high)]
    values = pairs.astype(f32)
    packed = (
        jnp.concatenate([values[0:1], values[1:2], values[2:3]], axis=1),
        jnp.concatenate([values[3:4], high[0], high[1]], axis=1),
        jnp.concatenate([rest[0], rest[1], jnp.zeros_like(rest[0])], axis=1),
        cond_ref[...],
    )
    row_id = lax.broadcasted_iota(jnp.int32, (EXTRA, width), 0)
    extra = jnp.zeros((EXTRA, width), f32)
    for index, line in enumerate(packed):
        extra = jnp.where(row_id == index, line, extra)
    ext_ref[rows : rows + EXTRA, :] = extra.astype(bf16)


def attention_forward(tokens, mod, cond, router_t, pairs, shards, local_width):
    rows, width = tokens.shape
    return pl.pallas_call(
        functools.partial(attention_kernel, local_width),
        out_shape=(
            jax.ShapeDtypeStruct((rows, width), bf16),
            jax.ShapeDtypeStruct((3, rows, width), bf16),
            jax.ShapeDtypeStruct((rows, width), bf16),
            jax.ShapeDtypeStruct((rows, width), f32),
            jax.ShapeDtypeStruct((rows + EXTRA, width), bf16),
        ),
        compiler_params=pltpu.CompilerParams(vmem_limit_bytes=VMEM_LIMIT),
        cost_estimate=pl.CostEstimate(flops=3 * 10**9, bytes_accessed=8 * 10**6, transcendentals=0),
        name="attention_forward",
    )(tokens, mod, cond, router_t, pairs, *shards)


def read_pairs(extra):
    info = extra.astype(f32)
    count = PATCHES
    routes = (info[0:1, 0:count], info[0:1, count : 2 * count])
    places = (info[0:1, 2 * count : 3 * count], info[1:2, 0:count])
    gates = (
        info[1:2, count : 2 * count] + info[2:3, 0:count],
        info[1:2, 2 * count : 3 * count] + info[2:3, count : 2 * count],
    )
    return routes, places, gates


def slot_hits(routes, places, base, slots):
    slot_id = lax.broadcasted_iota(jnp.int32, (slots, PATCHES), 0).astype(f32)
    return [
        slot_id == jnp.where(place < CAP, (route - base) * CAP + place, -1.0)
        for route, place in zip(routes, places)
    ]


def slot_gates(hits, gates):
    return jnp.sum(
        jnp.where(hits[0], gates[0], 0.0) + jnp.where(hits[1], gates[1], 0.0), axis=1, keepdims=True
    )


def dispatch_kernel(base_ref, ext_ref, cot_ref, rows_ref, cots_ref):
    members = rows_ref.shape[0]
    base = base_ref[0].astype(f32)
    for block in range(GROUP):
        routes, places, gates = read_pairs(ext_ref[block, PATCHES:, :])
        hits = slot_hits(routes, places, base, members * CAP)
        hot = (hits[0] | hits[1]).astype(bf16)
        picked = mm(hot, ext_ref[block, 0:PATCHES, :], NN).astype(bf16)
        scaled = (mm(hot, cot_ref[block], NN) * slot_gates(hits, gates)).astype(bf16)
        for member in range(members):
            span = slice(member * CAP, (member + 1) * CAP)
            rows_ref[member, block * CAP : (block + 1) * CAP, :] = picked[span]
            cots_ref[member, block * CAP : (block + 1) * CAP, :] = scaled[span]


def dispatch(base, ext, cot, members):
    blocks, _, width = ext.shape
    steps = blocks // GROUP
    out = jax.ShapeDtypeStruct((members, blocks * CAP, width), bf16)
    out_spec = pl.BlockSpec((members, GROUP * CAP, width), lambda c, b: (0, c, 0))
    return pl.pallas_call(
        dispatch_kernel,
        grid_spec=pltpu.PrefetchScalarGridSpec(
            num_scalar_prefetch=1,
            grid=(steps,),
            in_specs=[
                pl.BlockSpec((GROUP, PATCHES + EXTRA, width), lambda c, b: (c, 0, 0)),
                pl.BlockSpec((GROUP, PATCHES, width), lambda c, b: (c, 0, 0)),
            ],
            out_specs=(out_spec, out_spec),
        ),
        out_shape=(out, out),
        compiler_params=pltpu.CompilerParams(vmem_limit_bytes=VMEM_LIMIT),
        cost_estimate=pl.CostEstimate(
            flops=4 * blocks * members * CAP * PATCHES * width,
            bytes_accessed=blocks * 2 * 10**6,
            transcendentals=0,
        ),
        name="dispatch",
    )(base, ext, cot)


def expert_kernel(
    shared_ids, base_ref, ext_ref, cot_ref, sup_ref, sdown_ref, eup_ref, edown_ref,
    first_ref, second_ref, rows_s, cots_s, gate_s, dot_s, shared_s,
):
    chunk, step = pl.program_id(0), pl.program_id(1)
    members = rows_s.shape[0]
    width = cot_ref.shape[2]
    base = base_ref[0].astype(f32)

    def block_hits(block):
        routes, places, gates = read_pairs(ext_ref[block, PATCHES:, :])
        return slot_hits(routes, places, base, members * CAP), gates

    @pl.when(step == 0)
    def _():
        for block in range(GROUP):
            hits, gates = block_hits(block)
            hot = (hits[0] | hits[1]).astype(bf16)
            picked = mm(hot, ext_ref[block, 0:PATCHES, :], NN).astype(bf16)
            cots = mm(hot, cot_ref[block], NN).astype(bf16)
            gate = slot_gates(hits, gates)
            for member in range(members):
                span = slice(member * CAP, (member + 1) * CAP)
                rows_s[member, block * CAP : (block + 1) * CAP, :] = picked[span]
                cots_s[member, block * CAP : (block + 1) * CAP, :] = cots[span]
                gate_s[member, block * CAP : (block + 1) * CAP, :] = gate[span]

    @pl.when((step == 0) & (chunk == 0))
    def _():
        for place, block in enumerate(shared_ids):
            inputs, cots = ext_ref[block, 0:PATCHES, :], cot_ref[block]
            value, slope = gelu_both(mm(inputs, sup_ref[...], NN))
            pre_grad = (mm(cots, sdown_ref[...], NT) * slope).astype(bf16)
            shared_s[place, :, 0:width] = mm(value.astype(bf16), sdown_ref[...], NN)
            shared_s[place, :, width:] = mm(pre_grad, sup_ref[...], NT)

    @pl.when(step > 0)
    def _():
        member = step - 1
        total = GROUP * CAP
        tile = total // 2
        for part in range(2):
            span = slice(part * tile, (part + 1) * tile)
            inputs, cots, gate = rows_s[member, span, :], cots_s[member, span, :], gate_s[member, span, :]
            value, slope = gelu_both(mm(inputs, eup_ref[0], NN))
            act_grad = mm(cots, edown_ref[0], NT)
            dot_s[member, span, :] = jnp.sum(value * act_grad, axis=1, keepdims=True)
            active = (gate * value).astype(bf16)
            pre_grad = (gate * act_grad * slope).astype(bf16)
            rows_s[member, span, :] = mm(active, edown_ref[0], NN).astype(bf16)
            cots_s[member, span, :] = mm(pre_grad, eup_ref[0], NT).astype(bf16)

    @pl.when(step == members)
    def _():
        half = GROUP // 2
        for block in range(GROUP):
            out_ref, place = (first_ref, block) if block < half else (second_ref, block - half)
            hits, _ = block_hits(block)
            hot = (hits[0] | hits[1]).astype(bf16)
            span = slice(block * CAP, (block + 1) * CAP)
            dots = jnp.concatenate([dot_s[m, span, :] for m in range(members)], axis=0)
            sums = [jnp.sum(jnp.where(hit, dots, 0.0), axis=0, keepdims=True) for hit in hits]
            line = jnp.concatenate(sums + [jnp.zeros_like(sums[0])], axis=1)
            row_id = lax.broadcasted_iota(jnp.int32, (EXTRA, width), 0)
            out_ref[place, 2 * PATCHES :, :] = jnp.where(row_id == 0, line, 0.0).astype(bf16)
            for index, source in enumerate((rows_s, cots_s)):
                slots = jnp.concatenate([source[m, span, :] for m in range(members)], axis=0)
                total = mm(hot, slots, TN)
                if block in shared_ids:
                    where = shared_ids.index(block)
                    own = shared_s[where, :, index * width : (index + 1) * width]
                    total = total + jnp.where(chunk == 0, own, 0.0)
                out_ref[place, index * PATCHES : (index + 1) * PATCHES, :] = total.astype(bf16)


def experts_both(base, ext, cot, shared_up, shared_down, expert_up, expert_down, shared_ids):
    blocks, _, width = ext.shape
    members, _, hidden = expert_up.shape
    steps = blocks // GROUP
    half = GROUP // 2
    out = jax.ShapeDtypeStruct((steps * half, 2 * PATCHES + EXTRA, width), bf16)
    one = pl.Buffered(1)
    out_spec = pl.BlockSpec((half, 2 * PATCHES + EXTRA, width), lambda c, e, b: (c, 0, 0), pipeline_mode=one)
    return pl.pallas_call(
        functools.partial(expert_kernel, shared_ids),
        grid_spec=pltpu.PrefetchScalarGridSpec(
            num_scalar_prefetch=1,
            grid=(steps, members + 1),
            in_specs=[
                pl.BlockSpec((GROUP, PATCHES + EXTRA, width), lambda c, e, b: (c, 0, 0), pipeline_mode=one),
                pl.BlockSpec((GROUP, PATCHES, width), lambda c, e, b: (c, 0, 0), pipeline_mode=one),
                pl.BlockSpec((width, hidden), lambda c, e, b: (0, 0), pipeline_mode=one),
                pl.BlockSpec((hidden, width), lambda c, e, b: (0, 0), pipeline_mode=one),
                pl.BlockSpec((1, width, hidden), lambda c, e, b: (jnp.maximum(e - 1, 0), 0, 0)),
                pl.BlockSpec((1, hidden, width), lambda c, e, b: (jnp.maximum(e - 1, 0), 0, 0)),
            ],
            out_specs=(out_spec, out_spec),
            scratch_shapes=[
                pltpu.VMEM((members, GROUP * CAP, width), bf16),
                pltpu.VMEM((members, GROUP * CAP, width), bf16),
                pltpu.VMEM((members, GROUP * CAP, 1), f32),
                pltpu.VMEM((members, GROUP * CAP, 1), f32),
                pltpu.VMEM((len(shared_ids), PATCHES, 2 * width), f32),
            ],
        ),
        out_shape=(out, out),
        compiler_params=pltpu.CompilerParams(vmem_limit_bytes=VMEM_LIMIT),
        cost_estimate=pl.CostEstimate(flops=25 * 10**9, bytes_accessed=30 * 10**6, transcendentals=0),
        name="experts_both",
    )(base, ext, cot, shared_up, shared_down, expert_up, expert_down)


def grads_kernel(started, rows_ref, cots_ref, up_ref, down_ref, *refs):
    up_grad_ref, down_grad_ref = refs[-2:]
    width = up_ref.shape[1]
    inputs = rows_ref[...].reshape(-1, width)
    cots = cots_ref[...].reshape(-1, width)
    value, slope = gelu_both(mm(inputs, up_ref[0], NN))
    pre_grad = (mm(cots, down_ref[0], NT) * slope).astype(bf16)
    up_grad = mm(inputs, pre_grad, TN)
    down_grad = mm(value.astype(bf16), cots, TN)

    @pl.when(pl.program_id(1) == 0)
    def _():
        if started:
            up_grad_ref[0] = refs[0][0] + up_grad
            down_grad_ref[0] = refs[1][0] + down_grad
        else:
            up_grad_ref[0] = up_grad
            down_grad_ref[0] = down_grad

    @pl.when(pl.program_id(1) > 0)
    def _():
        up_grad_ref[0] += up_grad
        down_grad_ref[0] += down_grad


def weight_grads(rows, cots, up, down, before, row_spec, cot_spec, steps, count):
    members, width, hidden = up.shape
    up_spec = pl.BlockSpec((1, width, hidden), lambda e, t: (e, 0, 0))
    down_spec = pl.BlockSpec((1, hidden, width), lambda e, t: (e, 0, 0))
    started = before is not None
    return pl.pallas_call(
        functools.partial(grads_kernel, started),
        grid=(members, steps),
        in_specs=[row_spec, cot_spec, up_spec, down_spec] + ([up_spec, down_spec] if started else []),
        out_specs=(up_spec, down_spec),
        out_shape=(
            jax.ShapeDtypeStruct(up.shape, f32),
            jax.ShapeDtypeStruct(down.shape, f32),
        ),
        input_output_aliases={4: 0, 5: 1} if started else {},
        compiler_params=pltpu.CompilerParams(vmem_limit_bytes=VMEM_LIMIT),
        cost_estimate=pl.CostEstimate(
            flops=8 * count * width * hidden, bytes_accessed=count * width * 4, transcendentals=0
        ),
        name="weight_grads",
    )(rows, cots, up, down, *(before or ()))


def routed_grads(rows, cots, up, down, before):
    members, count, width = rows.shape
    tile = GROUP * CAP
    spec = pl.BlockSpec((1, tile, width), lambda e, t: (e, t, 0))
    return weight_grads(rows, cots, up, down, before, spec, spec, count // tile, members * count)


def shared_grads(ext, cot, up, down, before):
    blocks, _, width = ext.shape
    spec = pl.BlockSpec((4, PATCHES, width), lambda e, t: (t, 0, 0))
    return weight_grads(
        ext, cot, up[None], down[None], before, spec, spec, blocks // 4, blocks * PATCHES
    )


def backward_kernel(
    local_width, moe_ref, back_ref, dots_ref, tok_ref, cot_ref, mod_ref, router_ref, pairs_ref, attn_in_ref,
    qkv_ref, context_ref, attn_out_ref, ext_ref, w0, w1, w2, w3,
    output_ref, tok_grad_ref, small_ref, weights_ref, grad_s,
):
    shards = (w0, w1, w2, w3)
    rows, width = tok_ref.shape
    mod = mod_ref[...]
    stream = tok_ref[...].astype(f32)
    attn_out = attn_out_ref[...]
    residual = stream + mod[2:3] * attn_out
    second_norm, second_inv = normalize(residual)
    moe_out = moe_ref[...].astype(f32)
    upstream = cot_ref[...].astype(f32)
    output_ref[...] = (residual + mod[5:6] * moe_out).astype(bf16)
    gate_two_grad = jnp.sum(upstream * moe_out, axis=0, keepdims=True)
    routes, places, gates = read_pairs(ext_ref[rows:, :])
    dots = dots_ref[...].astype(f32)
    dots = (dots[0:1, 0:PATCHES], dots[0:1, PATCHES : 2 * PATCHES])
    mean_dot = gates[0] * dots[0] + gates[1] * dots[1]
    pairs = pairs_ref[...]
    expert_id = lax.broadcasted_iota(jnp.int32, (EXPERTS, rows), 0)
    logits_grad = jnp.zeros((EXPERTS, rows), f32)
    for k in range(TOPK):
        logits_grad += jnp.where(expert_id == pairs[k : k + 1], gates[k] * (dots[k] - mean_dot), 0.0)
    logits_grad = logits_grad.astype(bf16)
    moe_in_grad = back_ref[...].astype(f32) + mm(logits_grad, router_ref[...], TN)
    shift_two_grad = jnp.sum(moe_in_grad, axis=0, keepdims=True)
    scale_two_grad = jnp.sum(moe_in_grad * second_norm, axis=0, keepdims=True)
    residual_grad = upstream + normalize_back(
        second_norm, second_inv, moe_in_grad * (1.0 + mod[4:5])
    )
    gate_one_grad = jnp.sum(residual_grad * attn_out, axis=0, keepdims=True)
    attn_grad = (mod[2:3] * residual_grad).astype(bf16)
    out_grad = mm(context_ref[...], attn_grad, TN).astype(bf16)
    for index in range(len(shards)):
        weights_ref[index, 3 * local_width :, :] = out_grad[index * local_width : (index + 1) * local_width]
    context_grad = mm(attn_grad, shard_rows(shards, 3, local_width), NT).astype(bf16)
    masks = pair_masks(rows)
    zero = jnp.zeros((rows, 2 * HD), bf16)
    scale = 1.0 / math.sqrt(HD)
    for pair in range(width // (2 * HD)):
        cols = slice(pair * 2 * HD, (pair + 1) * 2 * HD)
        query, key, value = qkv_ref[0, :, cols], qkv_ref[1, :, cols], qkv_ref[2, :, cols]
        upper = context_grad[:, cols]
        sums = []
        for mask in masks:
            probs = head_probs(jnp.where(mask, query, zero), key)
            probs_grad = mm(jnp.where(mask, upper, zero), value, NT)
            value_grad = mm(probs.astype(bf16), upper, TN)
            score_grad = (
                probs * (probs_grad - jnp.sum(probs_grad * probs, axis=-1, keepdims=True))
            ).astype(bf16)
            sums.append((mm(score_grad, key, NN) * scale, mm(score_grad, query, TN) * scale, value_grad))
        for part in range(3):
            grad_s[part, :, cols] = jnp.where(masks[0], sums[0][part], sums[1][part]).astype(bf16)
    attn_in = attn_in_ref[...]
    attn_in_grad = jnp.zeros((rows, width), f32)
    for part in range(3):
        grad = grad_s[part]
        attn_in_grad += mm(grad, shard_rows(shards, part, local_width), NN)
        weight_grad = mm(grad, attn_in, TN).astype(bf16)
        for index in range(len(shards)):
            weights_ref[index, part * local_width : (part + 1) * local_width, :] = weight_grad[
                index * local_width : (index + 1) * local_width
            ]
    first_norm, first_inv = normalize(stream)
    shift_one_grad = jnp.sum(attn_in_grad, axis=0, keepdims=True)
    scale_one_grad = jnp.sum(attn_in_grad * first_norm, axis=0, keepdims=True)
    tok_grad_ref[...] = residual_grad + normalize_back(
        first_norm, first_inv, attn_in_grad * (1.0 + mod[1:2])
    )
    lines = (
        shift_one_grad, scale_one_grad, gate_one_grad, shift_two_grad, scale_two_grad, gate_two_grad,
    )
    row_id = lax.broadcasted_iota(jnp.int32, (8, width), 0)
    stacked = jnp.zeros((8, width), f32)
    for index, line in enumerate(lines):
        stacked = jnp.where(row_id == index, line, stacked)
    small_ref[0:8, :] = stacked
    small_ref[8:16, :] = mm(logits_grad, ext_ref[0:rows, :], NN)


def attention_backward(
    moe_out, moe_back, dots, tokens, cotangent, mod, router_t, pairs, attn_in, qkv, context, attn_out, ext,
    shards, local_width,
):
    rows, width = tokens.shape
    return pl.pallas_call(
        functools.partial(backward_kernel, local_width),
        out_shape=(
            jax.ShapeDtypeStruct((rows, width), bf16),
            jax.ShapeDtypeStruct((rows, width), f32),
            jax.ShapeDtypeStruct((16, width), f32),
            jax.ShapeDtypeStruct((len(shards), 4 * local_width, width), bf16),
        ),
        scratch_shapes=[pltpu.VMEM((3, rows, width), bf16)],
        compiler_params=pltpu.CompilerParams(vmem_limit_bytes=VMEM_LIMIT),
        cost_estimate=pl.CostEstimate(flops=6 * 10**9, bytes_accessed=16 * 10**6, transcendentals=0),
        name="attention_backward",
    )(
        moe_out, moe_back, dots, tokens, cotangent, mod, router_t, pairs, attn_in, qkv, context, attn_out,
        ext, *shards,
    )


class Links:
    def __init__(self, mesh):
        self.dp, self.expert, self.tensor = (mesh.shape[name] for name in ("dp", "expert", "tensor"))
        self.paired = self.expert == 2 and self.tensor == 4
        self.core = [(i, i ^ 1) for i in range(self.tensor)]
        self.side = [(i, i ^ 2) for i in range(self.tensor)]
        self.cross = [(i, i ^ 3) for i in range(self.tensor)]
        self.other = [(0, 1), (1, 0)]

    def to_core(self, value):
        return lax.ppermute(value, "tensor", self.core)

    def to_side(self, value):
        return lax.ppermute(value, "tensor", self.side)

    def to_other(self, value):
        return lax.ppermute(value, "expert", self.other)

    def tensor_blocks(self, block):
        if self.tensor != 4:
            raise NotImplementedError
        across = self.to_side(block)
        near = self.to_core(block)
        return (block, near, across, self.to_core(across))

    def plane(self, blocks):
        if self.paired:
            rows = blocks.shape[1]
            cut = (rows // 2 + 15) // 16 * 16
            side, other = self.to_side(blocks), self.to_other(blocks)
            upper = self.to_side(other[:, :cut])
            lower = self.to_other(side[:, cut:])
            corner = jnp.concatenate([upper, lower], axis=1)
            mine = jnp.concatenate([blocks, side, other, corner], axis=0)
            return jnp.concatenate([mine, self.to_core(mine)], axis=0)
        everything = lax.all_gather(blocks, ("expert", "tensor"), axis=0, tiled=True)
        return jnp.roll(everything, -lax.axis_index("expert") * self.tensor * blocks.shape[0], axis=0)

    def column(self, block):
        return jnp.stack(
            [
                lax.ppermute(block, "dp", [(i, (i + hop) % self.dp) for i in range(self.dp)])
                for hop in range(1, self.dp)
            ]
        )

    def plane_sum(self, first, second):
        if self.paired:
            here = first + self.to_core(second)
            rows = here.shape[1]
            cut = PATCHES
            from_side = self.to_side(here[1::2, :cut])
            from_other = self.to_other(here[2:, cut:])
            upper = here[0, :cut] + from_side[0]
            lower = here[0, cut:] + from_other[0]
            upper_next = here[2, :cut] + from_side[1]
            lower_next = here[1, cut:] + from_other[1]
            return upper + self.to_other(upper_next), lower + self.to_side(lower_next)
        half = GROUP // 2
        blocks = jnp.concatenate(
            [part.reshape((-1, half) + part.shape[1:]) for part in (first, second)], axis=1
        ).reshape((-1,) + first.shape[1:])
        blocks = jnp.roll(blocks, lax.axis_index("expert") * self.tensor, axis=0)
        total = lax.psum_scatter(blocks, ("expert", "tensor"), scatter_dimension=0, tiled=True)[0]
        return total[:PATCHES], total[PATCHES:]

    def sum_along(self, value, axis, size):
        rows = value.shape[0]
        share = rows // size
        if rows % (size * 16):
            return lax.psum(value, axis)
        me = lax.axis_index(axis)
        piece = lambda index: lax.dynamic_slice_in_dim(value, index * share, share, axis=0)
        total = piece(me).astype(f32)
        for hop in range(1, size):
            pairs = [(i, (i + hop) % size) for i in range(size)]
            total = total + lax.ppermute(piece((me + hop) % size), axis, pairs).astype(f32)
        total = total.astype(value.dtype)
        result = jnp.zeros_like(value)
        result = lax.dynamic_update_slice_in_dim(result, total, me * share, axis=0)
        for hop in range(1, size):
            pairs = [(i, (i + hop) % size) for i in range(size)]
            result = lax.dynamic_update_slice_in_dim(
                result, lax.ppermute(total, axis, pairs), (me - hop) % size * share, axis=0
            )
        return result


def local(
    links,
    tokens,
    cotangent,
    timesteps,
    ada_weight,
    ada_bias,
    qkv_weight,
    out_weight,
    router_weight,
    shared_up,
    shared_down,
    expert_up,
    expert_down,
    routes,
    places,
):
    rows, width = tokens.shape
    local_width = qkv_weight.shape[2]
    members = expert_up.shape[0]
    me = lax.axis_index("tensor")
    base = (lax.axis_index("expert") * members).astype(jnp.int32).reshape(1)

    weight = jnp.concatenate(
        [qkv_weight.transpose(1, 2, 0).reshape(3 * local_width, width), out_weight], axis=0
    )
    shards = links.tensor_blocks(weight)

    condition = jax.nn.silu(embedding(timesteps, width)).astype(bf16)
    mod_cols = jnp.einsum("id,dcf->icf", condition, ada_weight, preferred_element_type=f32) + ada_bias[None]
    mod = lax.all_to_all(mod_cols, "tensor", split_axis=0, concat_axis=2, tiled=True)[0]
    own_condition = lax.dynamic_slice_in_dim(condition.astype(f32), me, 1, axis=0)
    shared_cot = (mod[5][None] * cotangent.astype(f32)).astype(bf16)
    router_t = router_weight.T
    pairs = jnp.concatenate([routes.T, places.T], axis=0)

    attn_in, qkv, context, attn_out, ext = attention_forward(
        tokens, mod, own_condition, router_t, pairs, shards, local_width
    )
    cot_plane = links.plane(shared_cot[None])
    ext_plane = links.plane(ext[None])
    shared_ids = (0, 1, 4, 5) if links.paired else tuple(range(links.tensor))
    first, second = experts_both(
        base, ext_plane, cot_plane, shared_up, shared_down, expert_up, expert_down, shared_ids
    )
    upper, lower = links.plane_sum(first, second)
    slot_rows, slot_cots = dispatch(base, ext_plane, cot_plane, members)
    routed = routed_grads(slot_rows, slot_cots, expert_up, expert_down, None)
    shared = shared_grads(ext_plane, cot_plane, shared_up, shared_down, None)

    output, tokens_grad, small, weights_grad = attention_backward(
        upper, lower[:PATCHES], lower[PATCHES:], tokens, cotangent, mod, router_t, pairs,
        attn_in, qkv, context, attn_out, ext, shards, local_width,
    )

    total_blocks = links.dp * links.expert * links.tensor
    full = links.paired and total_blocks * rows * width * 2 <= FULL_LIMIT
    if full:
        cot_rest = links.plane(links.column(shared_cot))
        ext_rest = links.plane(links.column(ext))
        rest_rows, rest_cots = dispatch(base, ext_rest, cot_rest, members)
        routed = routed_grads(rest_rows, rest_cots, expert_up, expert_down, routed)
        shared = shared_grads(ext_rest, cot_rest, shared_up, shared_down, shared)
        small_all = jnp.concatenate([links.plane(small[None]), links.plane(links.column(small))], axis=0)
        extra_all = jnp.concatenate([ext_plane[:, PATCHES:], ext_rest[:, PATCHES:]], axis=0)
        condition_all = extra_all[:, 3]
        routes_all = extra_all[:, 0, : TOPK * PATCHES]
        near = weights_grad[0] + links.to_core(weights_grad[1])
        far = weights_grad[2] + links.to_core(weights_grad[3])
        dense = near + links.to_side(far)
        dense = links.sum_along(links.sum_along(dense, "expert", links.expert), "dp", links.dp)
    else:
        routed = lax.psum(routed, "dp")
        shared = lax.psum(shared, "dp")
        small_all = lax.all_gather(small, ("dp", "expert", "tensor"), axis=0)
        condition_all = lax.all_gather(own_condition[0], ("dp", "expert", "tensor"), axis=0).astype(bf16)
        routes_all = lax.all_gather(routes.reshape(-1), ("dp", "expert", "tensor"), axis=0)
        order = jnp.arange(links.tensor) ^ me
        dense = lax.psum_scatter(
            weights_grad[order], "tensor", scatter_dimension=0, tiled=True
        )[0]
        dense = lax.psum(dense, ("dp", "expert"))

    mod_grad = lax.dynamic_slice_in_dim(small_all[:, 0:6], me * local_width, local_width, axis=2)
    ada_grad = jnp.einsum(
        "id,icf->dcf", condition_all.astype(f32), mod_grad, precision=lax.Precision.HIGHEST
    )
    ada_bias_grad = jnp.sum(mod_grad, axis=0)
    router_grad = jnp.sum(small_all[:, 8:16], axis=0).T
    counts = jnp.sum(
        (routes_all[:, :, None] == jnp.arange(EXPERTS).astype(routes_all.dtype)).astype(jnp.int32),
        axis=(0, 1),
    )
    dense = dense.astype(f32)
    qkv_grad = dense[: 3 * local_width].reshape(3, local_width, width).transpose(2, 0, 1)
    return (
        output,
        tokens_grad,
        ada_grad,
        ada_bias_grad,
        qkv_grad,
        dense[3 * local_width :],
        router_grad,
        shared[0][0],
        shared[1][0],
        routed[0],
        routed[1],
        counts,
    )


def solution(mesh):
    rows = P(("dp", "expert", "tensor"), None)
    placed = (
        rows,
        rows,
        P(("dp", "expert")),
        P(None, None, "tensor"),
        P(None, "tensor"),
        P(None, None, "tensor"),
        P("tensor", None),
        P(),
        P(None, "tensor"),
        P("tensor", None),
        P("expert", None, "tensor"),
        P("expert", "tensor", None),
        rows,
        rows,
    )
    return jax.shard_map(
        functools.partial(local, Links(mesh)),
        mesh=mesh,
        in_specs=placed,
        out_specs=(
            rows,
            rows,
            P(None, None, "tensor"),
            P(None, "tensor"),
            P(None, None, "tensor"),
            P("tensor", None),
            P(),
            P(None, "tensor"),
            P("tensor", None),
            P("expert", None, "tensor"),
            P("expert", "tensor", None),
            P(),
        ),
        check_vma=False,
    )
```

time: 1540 us -> 524 us (0.34)
  waiting for transfers between devices: 1150 us -> 158 us
  Pallas kernels: 0 us -> 219 us
  matrix products: 122 us -> 4.65 us
  blocking collectives: 101 us -> 0 us
  starting transfers between devices: 17.6 us -> 54.3 us
  local copies, waits for them, and re-layouts: 89.8 us -> 55.5 us
    psum x2 -> x0, waiting for transfers between devices: 883 us -> none  [the longest x1 545 us: local(): expert_sums = lax.psum((expert_up_grad, expert_down_grad), 'dp')]
    pallas_call x0 -> x9, Pallas kernels: none -> 219 us  [the longest x4 136 us: weight_grads(): pl.pallas_call(functools.partial(grads_kernel, started), grid=(members, s...]
    reduce_scatter x6 -> x0, waiting for transfers between devices: 179 us -> none  [the longest x1 64.3 us: local(): lax.psum_scatter(routed_back, 'tensor', scatter_dimension=1, tiled=True)]
    ppermute x0 -> x56, waiting for transfers between devices: none -> 158 us  [the longest x16 54.7 us: to_side(): return lax.ppermute(value, 'tensor', self.side)]
    dot_general x27 -> x2, matrix products: 117 us -> 4.65 us  [the longest x1 3.4 us: local(): jnp.einsum('id,icf->dcf', condition_all.astype(f32), mod_grad, precision=...]
    all_gather x6 -> x0, waiting for transfers between devices: 74.8 us -> none  [the longest x1 25 us: local(): lax.all_gather(recv_rows, 'tensor', axis=1, tiled=True)]
    psum x2 -> x0, blocking collectives: 70.6 us -> none  [the longest x1 48.4 us: local(): lax.psum((router_grad, counts_local), ('dp', 'expert', 'tensor'))]
    ppermute x0 -> x56, starting transfers between devices: none -> 51 us  [the longest x16 17.4 us: to_side(): return lax.ppermute(value, 'tensor', self.side)]
  transfers between devices with their start and end apart: 18 -> 57, of which waited for: 15 -> 25; matrix products, arithmetic and copies ran while one was open for 11% -> 15% of each run, Pallas kernels for 0% -> 42%
where the time goes in v1:
time: 524 us; the launch traced here: 518 us
  Pallas kernels  219 us (42%)
  waiting for transfers between devices  158 us (30%)
  local copies, waits for them, and re-layouts  55.5 us (11%)
  starting transfers between devices  54.3 us (10%)
  other arithmetic  24.8 us (5%)
    pallas_call x4, Pallas kernels, weight_grads(): pl.pallas_call(functools.partial(grads_kernel, started), grid=(members, s...  136 us
    ppermute x16, waiting for transfers between devices, to_side(): return lax.ppermute(value, 'tensor', self.side)  54.7 us
    pallas_call x1, Pallas kernels, experts_both(): pl.pallas_call(functools.partial(expert_kernel, shared_ids), grid_spec=pl...  34 us
    ppermute x12, waiting for transfers between devices, to_other(): return lax.ppermute(value, 'expert', self.other)  34 us
    ppermute x9, waiting for transfers between devices, column(): lax.ppermute(block, 'dp', [(i, (i + hop) % self.dp) for i in range(self.d...  32.3 us
    pallas_call x2, Pallas kernels, dispatch(): pl.pallas_call(dispatch_kernel, grid_spec=pltpu.PrefetchScalarGridSpec(nu...  26.8 us
    unnamed x68, local copies, waits for them, and re-layouts  26.3 us
    ppermute x4, waiting for transfers between devices, sum_along(): lax.ppermute(piece((me + hop) % size), axis, pairs).astype(f32)  20.8 us
  transfers between devices with their start and end apart: 57, of which 25 were waited for; matrix products, arithmetic and copies ran while one was open for 15% of the time, Pallas kernels for 42%

profile of v1, /device:TPU:0, one launch (start us, length us, event | category | flops | bytes accessed | tf_op | source)
XLA Modules:
  0.0 518.0 jit_solution(800973510721991440)
XLA Ops:
  0.7 2.5 pad_maximum_fusion.1.w0
  3.2 2.9 collective-permute-start.1
  8.9 3.3 all-to-all-start
  12.6 20.0 %collective-permute-done.1.w2 = bf16[768,768]{1,0:T(8,128)(2,1)} collective-permute-done((bf16[768,768]{1,0:T(8,128)(2,1)}, bf16[768,768]{1,0:T(8,128)(2,1)}, u32[]{:S(2)}, u32[]{:S(2)}) %collective-permute-start.1) | collective-permute-done | bytes 1179680 | tf_op jit(solution)/shard_map/ppermute | solution.py:517
  33.6 3.9 collective-permute-start.50
  38.4 8.5 %collective-permute-done.50 = bf16[256,768]{1,0:T(8,128)(2,1)S(1)} collective-permute-done((bf16[256,768]{1,0:T(8,128)(2,1)S(1)}, bf16[256,768]{1,0:T(8,128)(2,1)S(1)}, u32[]{:S(2)}, u32[]{:S(2)}) %collective-permute-start.50) | collective-permute-done | bytes 393248 | tf_op jit(solution)/shard_map/ppermute | solution.py:545
  48.5 23.1 %collective-permute-done.49 = bf16[256,768]{1,0:T(8,128)(2,1)S(1)} collective-permute-done((bf16[256,768]{1,0:T(8,128)(2,1)S(1)}, bf16[256,768]{1,0:T(8,128)(2,1)S(1)}, u32[]{:S(2)}, u32[]{:S(2)}) %collective-permute-start.49) | collective-permute-done | bytes 393248 | tf_op jit(solution)/shard_map/ppermute | solution.py:545
  78.2 5.4 %collective-permute-done.8 = bf16[1,256,768]{2,1,0:T(8,128)(2,1)S(1)} collective-permute-done((bf16[1,256,768]{2,1,0:T(8,128)(2,1)S(1)}, bf16[1,256,768]{2,1,0:T(8,128)(2,1)S(1)}, u32[]{:S(2)}, u32[]{:S(2)}) %collective-permute-start.8) | collective-permute-done | bytes 393248 | tf_op jit(solution)/shard_map/ppermute | solution.py:517
  87.4 7.4 %attention_forward.1 = (bf16[256,768]{1,0:T(8,128)(2,1)}, bf16[3,256,768]{2,1,0:T(8,128)(2,1)}, bf16[256,768]{1,0:T(8,128)(2,1)}, f32[256,768]{1,0:T(8,128)}, bf16[272,768]{1,0:T(8,128)(2,1)}) custom-call(bf16[256,768]{1,0:T(8,128)(2,1)} %tok_ref.3, f32[6,768]{1,0:T(8,128)} %squeeze.32.mod_ref, f32[1,768]{1,0:T(1,128)} %fusion.13.cond_ref, ...), custom_call_target="tpu_custom_call" | custom-call | flops 3000000000 | bytes 8000000 | tf_op jit(solution)/shard_map/attention_forward/pallas_call | solution.py:140
  95.4 16.4 %collective-permute-done.10 = bf16[1,128,768]{2,1,0:T(8,128)(2,1)S(1)} collective-permute-done((bf16[1,128,768]{2,1,0:T(8,128)(2,1)S(1)}, bf16[1,128,768]{2,1,0:T(8,128)(2,1)S(1)}, u32[]{:S(2)}, u32[]{:S(2)}) %collective-permute-start.10) | collective-permute-done | bytes 196640 | tf_op jit(solution)/shard_map/ppermute | solution.py:517
  113.5 3.2 collective-permute-done.4
  117.4 7.2 %collective-permute-done.3 = bf16[1,272,768]{2,1,0:T(8,128)(2,1)S(1)} collective-permute-done((bf16[1,272,768]{2,1,0:T(8,128)(2,1)}, bf16[1,272,768]{2,1,0:T(8,128)(2,1)S(1)}, u32[]{:S(2)}, u32[]{:S(2)}) %collective-permute-start.3) | collective-permute-done | bytes 417824 | tf_op jit(solution)/shard_map/ppermute | solution.py:517
  126.2 4.1 collective-permute-done.6
  143.8 34.0 %experts_both.1 = (bf16[4,528,768]{2,1,0:T(8,128)(2,1)}, bf16[4,528,768]{2,1,0:T(8,128)(2,1)}) custom-call(s32[1]{0:T(128)} %bitcast.base_ref, bf16[8,272,768]{2,1,0:T(8,128)(2,1)} %constant_dynamic-update-slice_fusion.ext_ref.rows_ref, bf16[8,256,768]{2,1,0:T(8,128)(2,1)} %copy-done.12, bf16[768,768]{1,0:T(8,128)(2,1)} %sup_ref.1, ...), custom_call_target="tpu_custom_call" | custom-call | flops 24999999488 | bytes 30000000 | tf_op jit(solution)/shard_map/experts_both/pallas_call | solution.py:306
  180.3 2.2 maximum_dynamic-update-slice_fusion.1
  183.4 1.9 constant_dynamic-update-slice_fusion.49
  185.4 2.0 constant_dynamic-update-slice_fusion.16
  189.3 20.1 %collective-permute-done.22 = bf16[3,272,768]{2,1,0:T(8,128)(2,1)S(1)} collective-permute-done((bf16[3,272,768]{2,1,0:T(8,128)(2,1)}, bf16[3,272,768]{2,1,0:T(8,128)(2,1)S(1)}, u32[]{:S(2)}, u32[]{:S(2)}) %collective-permute-start.22) | collective-permute-done | bytes 1253408 | tf_op jit(solution)/shard_map/ppermute | solution.py:520
  214.5 8.3 %dispatch.3 = (bf16[4,640,768]{2,1,0:T(8,128)(2,1)}, bf16[4,640,768]{2,1,0:T(8,128)(2,1)}) custom-call(s32[1]{0:T(128)} %bitcast.base_ref, bf16[8,272,768]{2,1,0:T(8,128)(2,1)} %constant_dynamic-update-slice_fusion.ext_ref.rows_ref, bf16[8,256,768]{2,1,0:T(8,128)(2,1)} %copy-done.12), custom_call_target="tpu_custom_call" | custom-call | flops 2013265920 | bytes 16000000 | tf_op jit(solution)/shard_map/dispatch/pallas_call | solution.py:201
  222.9 18.9 %weight_grads.6 = (f32[4,768,768]{2,1,0:T(8,128)}, f32[4,768,768]{2,1,0:T(8,128)}) custom-call(bf16[4,640,768]{2,1,0:T(8,128)(2,1)} %get-tuple-element.52.rows_ref, bf16[4,640,768]{2,1,0:T(8,128)(2,1)} %get-tuple-element.53.cots_ref, bf16[4,768,768]{2,1,0:T(8,128)(2,1)} %up_ref.3, bf16[4,768,768]{2,1,0:T(8,128)(2,1)} %down_ref.3), custom_call_target="tpu_custom_call" | custom-call | flops 12079595520 | bytes 7864320 | tf_op jit(solution)/shard_map/weight_grads/pallas_call | solution.py:365
  243.0 3.7 add.149
  251.0 16.9 %weight_grads.4 = (f32[1,768,768]{2,1,0:T(8,128)}, f32[1,768,768]{2,1,0:T(8,128)}) custom-call(bf16[8,272,768]{2,1,0:T(8,128)(2,1)} %constant_dynamic-update-slice_fusion.ext_ref.rows_ref, bf16[8,256,768]{2,1,0:T(8,128)(2,1)} %copy-done.12, bf16[1,768,768]{2,1,0:T(8,128)(2,1)} %bitcast.109, bf16[1,768,768]{2,1,0:T(8,128)(2,1)} %bitcast.111), custom_call_target="tpu_custom_call" | custom-call | flops 9663676416 | bytes 6291456 | tf_op jit(solution)/shard_map/weight_grads/pallas_call | solution.py:365
  273.5 4.9 constant_dynamic-update-slice_fusion.48.cots_ref.cot_ref
  278.4 4.3 collective-permute-done.15
  282.7 1.8 fusion.6.moe_ref
  286.0 15.6 %attention_backward.1 = (bf16[256,768]{1,0:T(8,128)(2,1)}, f32[256,768]{1,0:T(8,128)}, f32[16,768]{1,0:T(8,128)}, bf16[4,768,768]{2,1,0:T(8,128)(2,1)}) custom-call(bf16[256,768]{1,0:T(8,128)(2,1)} %fusion.6.moe_ref, bf16[256,768]{1,0:T(8,128)(2,1)} %slice.147.back_ref, bf16[16,768]{1,0:T(8,128)(2,1)} %slice.148.dots_ref, bf16[256,768]{1,0:T(8,128)(2,1)} %tok_ref.3, ...), custom_call_target="tpu_custom_call" | custom-call | flops 6000000000 | bytes 16000000 | tf_op jit(solution)/shard_map/attention_backward/pallas_call | solution.py:486
  301.6 3.9 collective-permute-start.32
  306.1 2.9 slice_bitcast_fusion.1
  311.6 2.3 collective-permute-done.27
  316.1 2.7 collective-permute-done.28
  328.3 1.7 collective-permute-done.35
  330.8 4.9 constant_dynamic-update-slice_fusion.17.rows_ref.ext_ref
  335.7 18.5 %dispatch.2 = (bf16[4,1920,768]{2,1,0:T(8,128)(2,1)}, bf16[4,1920,768]{2,1,0:T(8,128)(2,1)}) custom-call(s32[1]{0:T(128)} %bitcast.base_ref, bf16[24,272,768]{2,1,0:T(8,128)(2,1)} %constant_dynamic-update-slice_fusion.17.rows_ref.ext_ref, bf16[24,256,768]{2,1,0:T(8,128)(2,1)} %constant_dynamic-update-slice_fusion.48.cots_ref.cot_ref), custom_call_target="tpu_custom_call" | custom-call | flops 6039797760 | bytes 48000000 | tf_op jit(solution)/shard_map/dispatch/pallas_call | solution.py:201
  355.0 1.8 fusion
  358.1 57.1 %weight_grads.7 = (f32[4,768,768]{2,1,0:T(8,128)}, f32[4,768,768]{2,1,0:T(8,128)}) custom-call(bf16[4,1920,768]{2,1,0:T(8,128)(2,1)} %get-tuple-element.50.rows_ref, bf16[4,1920,768]{2,1,0:T(8,128)(2,1)} %get-tuple-element.51.cots_ref, bf16[4,768,768]{2,1,0:T(8,128)(2,1)} %up_ref.3, ...), custom_call_target="tpu_custom_call", output_to_operand_aliasing={{0}: (4, {}), {1}: (5, {})} | custom-call | flops 36238786560 | bytes 23592960 | tf_op jit(solution)/shard_map/weight_grads/pallas_call | solution.py:365
  416.3 42.8 %weight_grads.5 = (f32[1,768,768]{2,1,0:T(8,128)}, f32[1,768,768]{2,1,0:T(8,128)}) custom-call(bf16[24,272,768]{2,1,0:T(8,128)(2,1)} %constant_dynamic-update-slice_fusion.17.rows_ref.ext_ref, bf16[24,256,768]{2,1,0:T(8,128)(2,1)} %constant_dynamic-update-slice_fusion.48.cots_ref.cot_ref, ...), custom_call_target="tpu_custom_call", output_to_operand_aliasing={{0}: (4, {}), {1}: (5, {})} | custom-call | flops 28991029248 | bytes 18874368 | tf_op jit(solution)/shard_map/weight_grads/pallas_call | solution.py:365
  461.3 2.6 collective-permute-start.42
  465.5 1.9 constant_dynamic-update-slice_fusion.31
  469.3 3.8 collective-permute-done.42
  473.1 4.6 collective-permute-done.44
  477.7 12.5 %collective-permute-done.43 = bf16[192,768]{1,0:T(8,128)(2,1)S(1)} collective-permute-done((bf16[192,768]{1,0:T(8,128)(2,1)S(1)}, bf16[192,768]{1,0:T(8,128)(2,1)S(1)}, u32[]{:S(2)}, u32[]{:S(2)}) %collective-permute-start.43) | collective-permute-done | bytes 294944 | tf_op jit(solution)/shard_map/ppermute | solution.py:580
  490.5 1.9 collective-permute-start.45
  492.4 3.4 fusion.7
  495.7 2.0 collective-permute-start.47
  497.7 1.8 slice_reduce_fusion
  499.5 6.6 %collective-permute-done.45 = bf16[192,768]{1,0:T(8,128)(2,1)S(1)} collective-permute-done((bf16[192,768]{1,0:T(8,128)(2,1)S(1)}, bf16[192,768]{1,0:T(8,128)(2,1)S(1)}, u32[]{:S(2)}, u32[]{:S(2)}) %collective-permute-start.45) | collective-permute-done | bytes 294944 | tf_op jit(solution)/shard_map/ppermute | solution.py:587
  506.2 4.1 collective-permute-done.46
  510.3 5.1 collective-permute-done.47
  (213 shorter events, 85.2 us)
Async XLA Ops:
  3.2 29.4 %collective-permute-start.1 = (bf16[768,768]{1,0:T(8,128)(2,1)}, bf16[768,768]{1,0:T(8,128)(2,1)}, u32[]{:S(2)}, u32[]{:S(2)}) collective-permute-start(bf16[768,768]{1,0:T(8,128)(2,1)} %pad_maximum_fusion.1.w0), channel_id=1, source_target_pairs={{0,2},{1,3},{2,0},{3,1},{4,6},{5,7},{6,4},{7,5},{8,10},{9,11},{10,... | collective-permute-start | bytes 3538952 | tf_op jit(solution)/shard_map/ppermute | solution.py:517
  8.9 23.8 %all-to-all-start = ((f32[4,6,192]{2,1,0:T(8,128)}), f32[4,6,192]{2,1,0:T(8,128)S(1)}, u32[]{:S(2)}, u32[]{:S(2)}) async-start(f32[4,6,192]{2,1,0:T(8,128)} %copy.35), calls=%async_computation | async-start | bytes 65536 | tf_op jit(solution)/shard_map/all_to_all | solution.py:622
  12.1 73.8 %collective-permute-start = (bf16[768,768]{1,0:T(8,128)(2,1)}, bf16[768,768]{1,0:T(8,128)(2,1)}, u32[]{:S(2)}, u32[]{:S(2)}) collective-permute-start(bf16[768,768]{1,0:T(8,128)(2,1)} %pad_maximum_fusion.1.w0), channel_id=1, source_target_pairs={{0,1},{1,0},{2,3},{3,2},{4,5},{5,4},{6,7},{7,6},{8,9},{9,8},{10,11... | collective-permute-start | bytes 3538952 | tf_op jit(solution)/shard_map/ppermute | solution.py:514
  32.6 54.8 %collective-permute-start.2 = (bf16[768,768]{1,0:T(8,128)(2,1)}, bf16[768,768]{1,0:T(8,128)(2,1)}, u32[]{:S(2)}, u32[]{:S(2)}) collective-permute-start(bf16[768,768]{1,0:T(8,128)(2,1)} %collective-permute-done.1.w2), channel_id=1, source_target_pairs={{0,1},{1,0},{2,3},{3,2},{4,5},{5,4},{6,7},{7,6},{8,9},{9,8},{10,11... | collective-permute-start | bytes 3538952 | tf_op jit(solution)/shard_map/ppermute | solution.py:514
  33.6 13.4 %collective-permute-start.50 = (bf16[256,768]{1,0:T(8,128)(2,1)S(1)}, bf16[256,768]{1,0:T(8,128)(2,1)S(1)}, u32[]{:S(2)}, u32[]{:S(2)}) collective-permute-start(bf16[256,768]{1,0:T(8,128)(2,1)S(1)} %get-tuple-element.65), channel_id=1, source_target_pairs={{0,24},{8,0},{16,8},{24,16},{1,25},{9,1},{17,9},{25,17},{2,26},{10... | collective-permute-start | bytes 1179656 | tf_op jit(solution)/shard_map/ppermute | solution.py:545
  37.4 34.2 %collective-permute-start.49 = (bf16[256,768]{1,0:T(8,128)(2,1)S(1)}, bf16[256,768]{1,0:T(8,128)(2,1)S(1)}, u32[]{:S(2)}, u32[]{:S(2)}) collective-permute-start(bf16[256,768]{1,0:T(8,128)(2,1)S(1)} %get-tuple-element.65), channel_id=1, source_target_pairs={{0,16},{8,24},{16,0},{24,8},{1,17},{9,25},{17,1},{25,9},{2,18},{10... | collective-permute-start | bytes 1179656 | tf_op jit(solution)/shard_map/ppermute | solution.py:545
  37.4 37.5 %collective-permute-start.48 = (bf16[256,768]{1,0:T(8,128)(2,1)S(1)}, bf16[256,768]{1,0:T(8,128)(2,1)S(1)}, u32[]{:S(2)}, u32[]{:S(2)}) collective-permute-start(bf16[256,768]{1,0:T(8,128)(2,1)S(1)} %get-tuple-element.65), channel_id=1, source_target_pairs={{0,8},{8,16},{16,24},{24,0},{1,9},{9,17},{17,25},{25,1},{2,10},{10... | collective-permute-start | bytes 1179656 | tf_op jit(solution)/shard_map/ppermute | solution.py:545
  47.0 30.7 %collective-permute-start.9 = (bf16[1,256,768]{2,1,0:T(8,128)(2,1)S(1)}, bf16[1,256,768]{2,1,0:T(8,128)(2,1)S(1)}, u32[]{:S(2)}, u32[]{:S(2)}) collective-permute-start(bf16[1,256,768]{2,1,0:T(8,128)(2,1)S(1)} %bitcast.92), channel_id=1, source_target_pairs={{0,4},{4,0},{1,5},{5,1},{2,6},{6,2},{3,7},{7,3},{8,12},{12,8},{9,1... | collective-permute-start | bytes 1179656 | tf_op jit(solution)/shard_map/ppermute | solution.py:520
  71.6 12.0 %collective-permute-start.8 = (bf16[1,256,768]{2,1,0:T(8,128)(2,1)S(1)}, bf16[1,256,768]{2,1,0:T(8,128)(2,1)S(1)}, u32[]{:S(2)}, u32[]{:S(2)}) collective-permute-start(bf16[1,256,768]{2,1,0:T(8,128)(2,1)S(1)} %bitcast.93), channel_id=1, source_target_pairs={{0,2},{1,3},{2,0},{3,1},{4,6},{5,7},{6,4},{7,5},{8,10},{9,11},{10,... | collective-permute-start | bytes 1179656 | tf_op jit(solution)/shard_map/ppermute | solution.py:517
  76.1 54.5 %collective-permute-start.52 = (bf16[3,256,768]{2,1,0:T(8,128)(2,1)}, bf16[3,256,768]{2,1,0:T(8,128)(2,1)S(1)}, u32[]{:S(2)}, u32[]{:S(2)}) collective-permute-start(bf16[3,256,768]{2,1,0:T(8,128)(2,1)} %pad_maximum_fusion.2), channel_id=1, source_target_pairs={{0,4},{4,0},{1,5},{5,1},{2,6},{6,2},{3,7},{7,3},{8,12},{12,8},{9,1... | collective-permute-start | bytes 3538952 | tf_op jit(solution)/shard_map/ppermute | solution.py:520
  77.6 55.3 %collective-permute-start.51 = (bf16[3,256,768]{2,1,0:T(8,128)(2,1)}, bf16[3,256,768]{2,1,0:T(8,128)(2,1)S(1)}, u32[]{:S(2)}, u32[]{:S(2)}) collective-permute-start(bf16[3,256,768]{2,1,0:T(8,128)(2,1)} %pad_maximum_fusion.2), channel_id=1, source_target_pairs={{0,2},{1,3},{2,0},{3,1},{4,6},{5,7},{6,4},{7,5},{8,10},{9,11},{10,... | collective-permute-start | bytes 3538952 | tf_op jit(solution)/shard_map/ppermute | solution.py:517
  83.6 28.1 %collective-permute-start.10 = (bf16[1,128,768]{2,1,0:T(8,128)(2,1)S(1)}, bf16[1,128,768]{2,1,0:T(8,128)(2,1)S(1)}, u32[]{:S(2)}, u32[]{:S(2)}) collective-permute-start(bf16[1,128,768]{2,1,0:T(8,128)(2,1)S(1)} %slice.136), channel_id=1, source_target_pairs={{0,2},{1,3},{2,0},{3,1},{4,6},{5,7},{6,4},{7,5},{8,10},{9,11},{10,... | collective-permute-start | bytes 589832 | tf_op jit(solution)/shard_map/ppermute | solution.py:517
  85.9 27.4 %collective-permute-start.11 = (bf16[1,128,768]{2,1,0:T(8,128)(2,1)S(1)}, bf16[1,128,768]{2,1,0:T(8,128)(2,1)S(1)}, u32[]{:S(2)}, u32[]{:S(2)}) collective-permute-start(bf16[1,128,768]{2,1,0:T(8,128)(2,1)S(1)} %slice.137), channel_id=1, source_target_pairs={{0,4},{4,0},{1,5},{5,1},{2,6},{6,2},{3,7},{7,3},{8,12},{12,8},{9,1... | collective-permute-start | bytes 589832 | tf_op jit(solution)/shard_map/ppermute | solution.py:520
  94.8 21.9 %collective-permute-start.4 = (bf16[1,272,768]{2,1,0:T(8,128)(2,1)}, bf16[1,272,768]{2,1,0:T(8,128)(2,1)S(1)}, u32[]{:S(2)}, u32[]{:S(2)}) collective-permute-start(bf16[1,272,768]{2,1,0:T(8,128)(2,1)} %bitcast.87), channel_id=1, source_target_pairs={{0,4},{4,0},{1,5},{5,1},{2,6},{6,2},{3,7},{7,3},{8,12},{12,8},{9,1... | collective-permute-start | bytes 1253384 | tf_op jit(solution)/shard_map/ppermute | solution.py:520
  111.8 12.8 %collective-permute-start.3 = (bf16[1,272,768]{2,1,0:T(8,128)(2,1)}, bf16[1,272,768]{2,1,0:T(8,128)(2,1)S(1)}, u32[]{:S(2)}, u32[]{:S(2)}) collective-permute-start(bf16[1,272,768]{2,1,0:T(8,128)(2,1)} %bitcast.88), channel_id=1, source_target_pairs={{0,2},{1,3},{2,0},{3,1},{4,6},{5,7},{6,4},{7,5},{8,10},{9,11},{10,... | collective-permute-start | bytes 1253384 | tf_op jit(solution)/shard_map/ppermute | solution.py:517
  113.4 22.3 %collective-permute-start.12 = (bf16[4,256,768]{2,1,0:T(8,128)(2,1)S(1)}, bf16[4,256,768]{2,1,0:T(8,128)(2,1)S(1)}, u32[]{:S(2)}, u32[]{:S(2)}) collective-permute-start(bf16[4,256,768]{2,1,0:T(8,128)(2,1)S(1)} %maximum_maximum_fusion.1), channel_id=1, source_target_pairs={{0,1},{1,0},{2,3},{3,2},{4,5},{5,4},{6,7},{7,6},{8,9},{9,8},{10,11... | collective-permute-start | bytes 4718600 | tf_op jit(solution)/shard_map/ppermute | solution.py:514
  116.8 13.5 %collective-permute-start.5 = (bf16[1,144,768]{2,1,0:T(8,128)(2,1)S(1)}, bf16[1,144,768]{2,1,0:T(8,128)(2,1)S(1)}, u32[]{:S(2)}, u32[]{:S(2)}) collective-permute-start(bf16[1,144,768]{2,1,0:T(8,128)(2,1)S(1)} %slice.133), channel_id=1, source_target_pairs={{0,2},{1,3},{2,0},{3,1},{4,6},{5,7},{6,4},{7,5},{8,10},{9,11},{10,... | collective-permute-start | bytes 663560 | tf_op jit(solution)/shard_map/ppermute | solution.py:517
  130.4 12.1 %collective-permute-start.7 = (bf16[4,272,768]{2,1,0:T(8,128)(2,1)S(1)}, bf16[4,272,768]{2,1,0:T(8,128)(2,1)S(1)}, u32[]{:S(2)}, u32[]{:S(2)}) collective-permute-start(bf16[4,272,768]{2,1,0:T(8,128)(2,1)S(1)} %maximum_maximum_fusion), channel_id=1, source_target_pairs={{0,1},{1,0},{2,3},{3,2},{4,5},{5,4},{6,7},{7,6},{8,9},{9,8},{10,11... | collective-permute-start | bytes 5013512 | tf_op jit(solution)/shard_map/ppermute | solution.py:514
  131.5 48.8 %collective-permute-start.53 = (bf16[3,128,768]{2,1,0:T(8,128)(2,1)}, bf16[3,128,768]{2,1,0:T(8,128)(2,1)S(1)}, u32[]{:S(2)}, u32[]{:S(2)}) collective-permute-start(bf16[3,128,768]{2,1,0:T(8,128)(2,1)} %slice.157), channel_id=1, source_target_pairs={{0,2},{1,3},{2,0},{3,1},{4,6},{5,7},{6,4},{7,5},{8,10},{9,11},{10,... | collective-permute-start | bytes 1769480 | tf_op jit(solution)/shard_map/ppermute | solution.py:517
  133.8 46.5 %collective-permute-start.54 = (bf16[3,128,768]{2,1,0:T(8,128)(2,1)}, bf16[3,128,768]{2,1,0:T(8,128)(2,1)}, u32[]{:S(2)}, u32[]{:S(2)}) collective-permute-start(bf16[3,128,768]{2,1,0:T(8,128)(2,1)} %slice.158), channel_id=1, source_target_pairs={{0,4},{4,0},{1,5},{5,1},{2,6},{6,2},{3,7},{7,3},{8,12},{12,8},{9,1... | collective-permute-start | bytes 1769480 | tf_op jit(solution)/shard_map/ppermute | solution.py:520
  135.8 42.0 %collective-permute-start.20 = (bf16[272,768]{1,0:T(8,128)(2,1)S(1)}, bf16[272,768]{1,0:T(8,128)(2,1)S(1)}, u32[]{:S(2)}, u32[]{:S(2)}) collective-permute-start(bf16[272,768]{1,0:T(8,128)(2,1)S(1)} %copy-done.8), channel_id=1, source_target_pairs={{0,24},{8,0},{16,8},{24,16},{1,25},{9,1},{17,9},{25,17},{2,26},{10... | collective-permute-start | bytes 1253384 | tf_op jit(solution)/shard_map/ppermute | solution.py:545
  135.9 42.1 %collective-permute-start.19 = (bf16[272,768]{1,0:T(8,128)(2,1)S(1)}, bf16[272,768]{1,0:T(8,128)(2,1)S(1)}, u32[]{:S(2)}, u32[]{:S(2)}) collective-permute-start(bf16[272,768]{1,0:T(8,128)(2,1)S(1)} %copy-done.8), channel_id=1, source_target_pairs={{0,16},{8,24},{16,0},{24,8},{1,17},{9,25},{17,1},{25,9},{2,18},{10... | collective-permute-start | bytes 1253384 | tf_op jit(solution)/shard_map/ppermute | solution.py:545
  142.5 35.5 %collective-permute-start.18 = (bf16[272,768]{1,0:T(8,128)(2,1)S(1)}, bf16[272,768]{1,0:T(8,128)(2,1)S(1)}, u32[]{:S(2)}, u32[]{:S(2)}) collective-permute-start(bf16[272,768]{1,0:T(8,128)(2,1)S(1)} %copy-done.8), channel_id=1, source_target_pairs={{0,8},{8,16},{16,24},{24,0},{1,9},{9,17},{17,25},{25,1},{2,10},{10... | collective-permute-start | bytes 1253384 | tf_op jit(solution)/shard_map/ppermute | solution.py:545
  177.9 65.1 %collective-permute-start.13 = (bf16[4,528,768]{2,1,0:T(8,128)(2,1)}, bf16[4,528,768]{2,1,0:T(8,128)(2,1)}, u32[]{:S(2)}, u32[]{:S(2)}) collective-permute-start(bf16[4,528,768]{2,1,0:T(8,128)(2,1)} %get-tuple-element.37), channel_id=1, source_target_pairs={{0,1},{1,0},{2,3},{3,2},{4,5},{5,4},{6,7},{7,6},{8,9},{9,8},{10,11... | collective-permute-start | bytes 9732104 | tf_op jit(solution)/shard_map/ppermute | solution.py:514
  179.3 30.1 %collective-permute-start.22 = (bf16[3,272,768]{2,1,0:T(8,128)(2,1)}, bf16[3,272,768]{2,1,0:T(8,128)(2,1)S(1)}, u32[]{:S(2)}, u32[]{:S(2)}) collective-permute-start(bf16[3,272,768]{2,1,0:T(8,128)(2,1)} %pad_maximum_fusion), channel_id=1, source_target_pairs={{0,4},{4,0},{1,5},{5,1},{2,6},{6,2},{3,7},{7,3},{8,12},{12,8},{9,1... | collective-permute-start | bytes 3760136 | tf_op jit(solution)/shard_map/ppermute | solution.py:520
  179.8 30.3 %collective-permute-start.21 = (bf16[3,272,768]{2,1,0:T(8,128)(2,1)}, bf16[3,272,768]{2,1,0:T(8,128)(2,1)S(1)}, u32[]{:S(2)}, u32[]{:S(2)}) collective-permute-start(bf16[3,272,768]{2,1,0:T(8,128)(2,1)} %pad_maximum_fusion), channel_id=1, source_target_pairs={{0,2},{1,3},{2,0},{3,1},{4,6},{5,7},{6,4},{7,5},{8,10},{9,11},{10,... | collective-permute-start | bytes 3760136 | tf_op jit(solution)/shard_map/ppermute | solution.py:517
  182.5 91.0 %collective-permute-start.55 = (bf16[12,256,768]{2,1,0:T(8,128)(2,1)}, bf16[12,256,768]{2,1,0:T(8,128)(2,1)}, u32[]{:S(2)}, u32[]{:S(2)}) collective-permute-start(bf16[12,256,768]{2,1,0:T(8,128)(2,1)} %maximum_dynamic-update-slice_fusion.1), channel_id=1, source_target_pairs={{0,1},{1,0},{2,3},{3,2},{4,5},{5,4},{6,7},{7,6},{8,9},{9,8},{10,11... | collective-permute-start | bytes 14155784 | tf_op jit(solution)/shard_map/ppermute | solution.py:514
  209.5 32.3 %collective-permute-start.23 = (bf16[3,144,768]{2,1,0:T(8,128)(2,1)S(1)}, bf16[3,144,768]{2,1,0:T(8,128)(2,1)S(1)}, u32[]{:S(2)}, u32[]{:S(2)}) collective-permute-start(bf16[3,144,768]{2,1,0:T(8,128)(2,1)S(1)} %slice.150), channel_id=1, source_target_pairs={{0,2},{1,3},{2,0},{3,1},{4,6},{5,7},{6,4},{7,5},{8,10},{9,11},{10,... | collective-permute-start | bytes 1990664 | tf_op jit(solution)/shard_map/ppermute | solution.py:517
  210.1 31.6 %collective-permute-start.24 = (bf16[3,128,768]{2,1,0:T(8,128)(2,1)S(1)}, bf16[3,128,768]{2,1,0:T(8,128)(2,1)S(1)}, u32[]{:S(2)}, u32[]{:S(2)}) collective-permute-start(bf16[3,128,768]{2,1,0:T(8,128)(2,1)S(1)} %slice.151), channel_id=1, source_target_pairs={{0,4},{4,0},{1,5},{5,1},{2,6},{6,2},{3,7},{7,3},{8,12},{12,8},{9,1... | collective-permute-start | bytes 1769480 | tf_op jit(solution)/shard_map/ppermute | solution.py:520
  243.0 87.8 %collective-permute-start.25 = (bf16[12,272,768]{2,1,0:T(8,128)(2,1)}, bf16[12,272,768]{2,1,0:T(8,128)(2,1)}, u32[]{:S(2)}, u32[]{:S(2)}) collective-permute-start(bf16[12,272,768]{2,1,0:T(8,128)(2,1)} %maximum_dynamic-update-slice_fusion), channel_id=1, source_target_pairs={{0,1},{1,0},{2,3},{3,2},{4,5},{5,4},{6,7},{7,6},{8,9},{9,8},{10,11... | collective-permute-start | bytes 15040520 | tf_op jit(solution)/shard_map/ppermute | solution.py:514
  248.6 22.1 %collective-permute-start.14 = (bf16[2,256,768]{2,1,0:T(8,128)(2,1)}, bf16[2,256,768]{2,1,0:T(8,128)(2,1)}, u32[]{:S(2)}, u32[]{:S(2)}) collective-permute-start(bf16[2,256,768]{2,1,0:T(8,128)(2,1)} %slice.106), channel_id=1, source_target_pairs={{0,2},{1,3},{2,0},{3,1},{4,6},{5,7},{6,4},{7,5},{8,10},{9,11},{10,... | collective-permute-start | bytes 2359304 | tf_op jit(solution)/shard_map/ppermute | solution.py:517
  249.5 22.8 %collective-permute-start.16 = (bf16[2,272,768]{2,1,0:T(8,128)(2,1)}, bf16[2,272,768]{2,1,0:T(8,128)(2,1)S(1)}, u32[]{:S(2)}, u32[]{:S(2)}) collective-permute-start(bf16[2,272,768]{2,1,0:T(8,128)(2,1)} %slice.143), channel_id=1, source_target_pairs={{0,4},{4,0},{1,5},{5,1},{2,6},{6,2},{3,7},{7,3},{8,12},{12,8},{9,1... | collective-permute-start | bytes 2506760 | tf_op jit(solution)/shard_map/ppermute | solution.py:520
  271.7 11.0 %collective-permute-start.15 = (bf16[256,768]{1,0:T(8,128)(2,1)S(1)}, bf16[256,768]{1,0:T(8,128)(2,1)S(1)}, u32[]{:S(2)}, u32[]{:S(2)}) collective-permute-start(bf16[256,768]{1,0:T(8,128)(2,1)S(1)} %fusion.4), channel_id=1, source_target_pairs={{0,4},{4,0},{1,5},{5,1},{2,6},{6,2},{3,7},{7,3},{8,12},{12,8},{9,1... | collective-permute-start | bytes 1179656 | tf_op jit(solution)/shard_map/ppermute | solution.py:520
  272.3 12.2 %collective-permute-start.17 = (bf16[272,768]{1,0:T(8,128)(2,1)S(1)}, bf16[272,768]{1,0:T(8,128)(2,1)S(1)}, u32[]{:S(2)}, u32[]{:S(2)}) collective-permute-start(bf16[272,768]{1,0:T(8,128)(2,1)S(1)} %fusion.1), channel_id=1, source_target_pairs={{0,2},{1,3},{2,0},{3,1},{4,6},{5,7},{6,4},{7,5},{8,10},{9,11},{10,... | collective-permute-start | bytes 1253384 | tf_op jit(solution)/shard_map/ppermute | solution.py:517
  301.6 8.1 %collective-permute-start.32 = (f32[16,768]{1,0:T(8,128)}, f32[16,768]{1,0:T(8,128)S(1)}, u32[]{:S(2)}, u32[]{:S(2)}) collective-permute-start(f32[16,768]{1,0:T(8,128)} %get-tuple-element.44), channel_id=1, source_target_pairs={{0,24},{8,0},{16,8},{24,16},{1,25},{9,1},{17,9},{25,17},{2,26},{10... | collective-permute-start | bytes 147464 | tf_op jit(solution)/shard_map/ppermute | solution.py:545
  309.1 15.2 %collective-permute-start.38 = (bf16[768,768]{1,0:T(8,128)(2,1)S(1)}, bf16[768,768]{1,0:T(8,128)(2,1)S(1)}, u32[]{:S(2)}, u32[]{:S(2)}) collective-permute-start(bf16[768,768]{1,0:T(8,128)(2,1)S(1)} %get-tuple-element.67), channel_id=1, source_target_pairs={{0,1},{1,0},{2,3},{3,2},{4,5},{5,4},{6,7},{7,6},{8,9},{9,8},{10,11... | collective-permute-start | bytes 3538952 | tf_op jit(solution)/shard_map/ppermute | solution.py:514
  311.6 42.6 %collective-permute-start.37 = (bf16[768,768]{1,0:T(8,128)(2,1)}, bf16[768,768]{1,0:T(8,128)(2,1)}, u32[]{:S(2)}, u32[]{:S(2)}) collective-permute-start(bf16[768,768]{1,0:T(8,128)(2,1)} %get-tuple-element.66), channel_id=1, source_target_pairs={{0,1},{1,0},{2,3},{3,2},{4,5},{5,4},{6,7},{7,6},{8,9},{9,8},{10,11... | collective-permute-start | bytes 3538952 | tf_op jit(solution)/shard_map/ppermute | solution.py:514
  321.0 9.1 %collective-permute-start.35 = (f32[3,16,768]{2,1,0:T(8,128)S(1)}, f32[3,16,768]{2,1,0:T(8,128)S(1)}, u32[]{:S(2)}, u32[]{:S(2)}) collective-permute-start(f32[3,16,768]{2,1,0:T(8,128)S(1)} %collective-permute-done.34), channel_id=1, source_target_pairs={{0,2},{1,3},{2,0},{3,1},{4,6},{5,7},{6,4},{7,5},{8,10},{9,11},{10,... | collective-permute-start | bytes 442376 | tf_op jit(solution)/shard_map/ppermute | solution.py:517
  325.4 29.6 %collective-permute-start.39 = (bf16[768,768]{1,0:T(8,128)(2,1)}, bf16[768,768]{1,0:T(8,128)(2,1)}, u32[]{:S(2)}, u32[]{:S(2)}) collective-permute-start(bf16[768,768]{1,0:T(8,128)(2,1)} %bitcast_add_fusion), channel_id=1, source_target_pairs={{0,2},{1,3},{2,0},{3,1},{4,6},{5,7},{6,4},{7,5},{8,10},{9,11},{10,... | collective-permute-start | bytes 3538952 | tf_op jit(solution)/shard_map/ppermute | solution.py:517
  330.8 134.7 %collective-permute-start.36 = (f32[12,16,768]{2,1,0:T(8,128)}, f32[12,16,768]{2,1,0:T(8,128)}, u32[]{:S(2)}, u32[]{:S(2)}) collective-permute-start(f32[12,16,768]{2,1,0:T(8,128)} %get-tuple-element.91), channel_id=1, source_target_pairs={{0,1},{1,0},{2,3},{3,2},{4,5},{5,4},{6,7},{7,6},{8,9},{9,8},{10,11... | collective-permute-start | bytes 1769480 | tf_op jit(solution)/shard_map/ppermute | solution.py:514
  356.9 58.2 %collective-permute-start.40 = (bf16[384,768]{1,0:T(8,128)(2,1)S(1)}, bf16[384,768]{1,0:T(8,128)(2,1)S(1)}, u32[]{:S(2)}, u32[]{:S(2)}) collective-permute-start(bf16[384,768]{1,0:T(8,128)(2,1)S(1)} %constant_dynamic-slice_fusion.3), channel_id=1, source_target_pairs={{0,4},{4,0},{1,5},{5,1},{2,6},{6,2},{3,7},{7,3},{8,12},{12,8},{9,1... | collective-permute-start | bytes 1769480 | tf_op jit(solution)/shard_map/ppermute | solution.py:580
  415.4 45.8 %collective-permute-start.41 = (bf16[384,768]{1,0:T(8,128)(2,1)S(1)}, bf16[384,768]{1,0:T(8,128)(2,1)S(1)}, u32[]{:S(2)}, u32[]{:S(2)}) collective-permute-start(bf16[384,768]{1,0:T(8,128)(2,1)S(1)} %get-tuple-element.61), channel_id=1, source_target_pairs={{0,4},{4,0},{1,5},{5,1},{2,6},{6,2},{3,7},{7,3},{8,12},{12,8},{9,1... | collective-permute-start | bytes 1769480 | tf_op jit(solution)/shard_map/ppermute | solution.py:587
  461.3 11.8 %collective-permute-start.42 = (bf16[192,768]{1,0:T(8,128)(2,1)S(1)}, bf16[192,768]{1,0:T(8,128)(2,1)S(1)}, u32[]{:S(2)}, u32[]{:S(2)}) collective-permute-start(bf16[192,768]{1,0:T(8,128)(2,1)S(1)} %get-tuple-element.76), channel_id=1, source_target_pairs={{0,8},{8,16},{16,24},{24,0},{1,9},{9,17},{17,25},{25,1},{2,10},{10... | collective-permute-start | bytes 884744 | tf_op jit(solution)/shard_map/ppermute | solution.py:580
  463.8 13.8 %collective-permute-start.44 = (bf16[192,768]{1,0:T(8,128)(2,1)S(1)}, bf16[192,768]{1,0:T(8,128)(2,1)S(1)}, u32[]{:S(2)}, u32[]{:S(2)}) collective-permute-start(bf16[192,768]{1,0:T(8,128)(2,1)S(1)} %get-tuple-element.77), channel_id=1, source_target_pairs={{0,24},{8,0},{16,8},{24,16},{1,25},{9,1},{17,9},{25,17},{2,26},{10... | collective-permute-start | bytes 884744 | tf_op jit(solution)/shard_map/ppermute | solution.py:580
  465.1 25.0 %collective-permute-start.43 = (bf16[192,768]{1,0:T(8,128)(2,1)S(1)}, bf16[192,768]{1,0:T(8,128)(2,1)S(1)}, u32[]{:S(2)}, u32[]{:S(2)}) collective-permute-start(bf16[192,768]{1,0:T(8,128)(2,1)S(1)} %get-tuple-element.78), channel_id=1, source_target_pairs={{0,16},{8,24},{16,0},{24,8},{1,17},{9,25},{17,1},{25,9},{2,18},{10... | collective-permute-start | bytes 884744 | tf_op jit(solution)/shard_map/ppermute | solution.py:580
  490.4 19.9 %collective-permute-start.46 = (bf16[192,768]{1,0:T(8,128)(2,1)S(1)}, bf16[192,768]{1,0:T(8,128)(2,1)S(1)}, u32[]{:S(2)}, u32[]{:S(2)}) collective-permute-start(bf16[192,768]{1,0:T(8,128)(2,1)S(1)} %get-tuple-element.59), channel_id=1, source_target_pairs={{0,16},{8,24},{16,0},{24,8},{1,17},{9,25},{17,1},{25,9},{2,18},{10... | collective-permute-start | bytes 884744 | tf_op jit(solution)/shard_map/ppermute | solution.py:587
  490.5 15.7 %collective-permute-start.45 = (bf16[192,768]{1,0:T(8,128)(2,1)S(1)}, bf16[192,768]{1,0:T(8,128)(2,1)S(1)}, u32[]{:S(2)}, u32[]{:S(2)}) collective-permute-start(bf16[192,768]{1,0:T(8,128)(2,1)S(1)} %get-tuple-element.59), channel_id=1, source_target_pairs={{0,8},{8,16},{16,24},{24,0},{1,9},{9,17},{17,25},{25,1},{2,10},{10... | collective-permute-start | bytes 884744 | tf_op jit(solution)/shard_map/ppermute | solution.py:587
  495.7 19.6 %collective-permute-start.47 = (bf16[192,768]{1,0:T(8,128)(2,1)S(1)}, bf16[192,768]{1,0:T(8,128)(2,1)S(1)}, u32[]{:S(2)}, u32[]{:S(2)}) collective-permute-start(bf16[192,768]{1,0:T(8,128)(2,1)S(1)} %get-tuple-element.59), channel_id=1, source_target_pairs={{0,24},{8,0},{16,8},{24,16},{1,25},{9,1},{17,9},{25,17},{2,26},{10... | collective-permute-start | bytes 884744 | tf_op jit(solution)/shard_map/ppermute | solution.py:587
  (26 other events, 372.4 us)

commit v2 on v1

v2 whole, which is shorter than its diff:
```python
import functools
import math

import jax
import jax.numpy as jnp
from jax import lax
from jax.experimental import pallas as pl
from jax.experimental.pallas import tpu as pltpu
from jax.sharding import PartitionSpec as P

HD = 64
EXPERTS = 8
TOPK = 2
PATCHES = 256
CAP = 80
EXTRA = 16
EPSILON = 1e-06
HALF = 4
FULL_LIMIT = 32 * 1024 * 1024

f32 = jnp.float32
bf16 = jnp.bfloat16
NN = (((1,), (0,)), ((), ()))
NT = (((1,), (1,)), ((), ()))
TN = (((0,), (0,)), ((), ()))
TT = (((0,), (1,)), ((), ()))
VMEM_LIMIT = 58 * 1024 * 1024


def mm(left, right, dims):
    return lax.dot_general(left, right, dims, preferred_element_type=f32)


def normalize(values):
    center = jnp.mean(values, axis=-1, keepdims=True)
    shifted = values - center
    inverse = lax.rsqrt(jnp.mean(shifted * shifted, axis=-1, keepdims=True) + EPSILON)
    return (shifted * inverse, inverse)


def normalize_back(normed, inverse, upstream):
    return inverse * (
        upstream
        - jnp.mean(upstream, axis=-1, keepdims=True)
        - normed * jnp.mean(upstream * normed, axis=-1, keepdims=True)
    )


def embedding(steps, model_width):
    half_width = model_width // 2
    freqs_all = jnp.exp(-math.log(10000.0) * jnp.arange(half_width, dtype=f32) / half_width)
    angles = steps.astype(f32)[:, None] * freqs_all[None, :]
    return jnp.concatenate([jnp.cos(angles), jnp.sin(angles)], axis=1)


def gelu_both(pre):
    const = math.sqrt(2.0 / math.pi)
    square = pre * pre
    tanh = jnp.tanh(const * pre * (1.0 + 0.044715 * square))
    half = 0.5 + 0.5 * tanh
    value = pre * half
    return value, half + value * (1.0 - tanh) * (const + 3.0 * 0.044715 * const * square)


def params():
    return pltpu.CompilerParams(vmem_limit_bytes=VMEM_LIMIT)


def cost(flops, moved):
    return pl.CostEstimate(flops=int(flops), bytes_accessed=int(moved), transcendentals=0)


def copy_kernel(plan, count, *refs):
    sources, out, sems = refs[:count], refs[-2], refs[-1]
    copies = [
        pltpu.make_async_copy(sources[index].at[take], out.at[put], sems.at[order])
        for order, (index, take, put) in enumerate(plan)
    ]
    for copy in copies:
        copy.start()
    for copy in copies:
        copy.wait()


def assemble(shape, dtype, sources, plan, after=()):
    anywhere = pl.BlockSpec(memory_space=pl.ANY)
    operands = (*sources, *after)
    return pl.pallas_call(
        functools.partial(copy_kernel, plan, len(sources)),
        in_specs=[anywhere] * len(operands),
        out_specs=anywhere,
        out_shape=jax.ShapeDtypeStruct(shape, dtype),
        scratch_shapes=[pltpu.SemaphoreType.DMA((len(plan),))],
        compiler_params=params(),
        cost_estimate=cost(0, 2 * math.prod(shape) * jnp.dtype(dtype).itemsize),
        name="assemble",
    )(*operands)


def cotangent_kernel(mod_ref, cot_ref, after_ref, out_ref):
    out_ref[...] = (mod_ref[5:6] * cot_ref[...].astype(f32)).astype(bf16)


def moe_cotangent(mod, cotangent, after):
    vmem = pl.BlockSpec(memory_space=pltpu.VMEM)
    return pl.pallas_call(
        cotangent_kernel,
        in_specs=[vmem, vmem, pl.BlockSpec(memory_space=pl.ANY)],
        out_specs=vmem,
        out_shape=jax.ShapeDtypeStruct(cotangent.shape, bf16),
        compiler_params=params(),
        name="moe_cotangent",
    )(mod, cotangent, after)


def pair_masks(rows):
    lane = lax.broadcasted_iota(jnp.int32, (rows, 2 * HD), 1)
    return (lane < HD, lane >= HD)


def head_probs(query, key):
    scores = mm(query, key, NT) * (1.0 / math.sqrt(HD))
    weights = jnp.exp(scores - jnp.max(scores, axis=-1, keepdims=True))
    return weights / jnp.sum(weights, axis=-1, keepdims=True)


def shard_rows(shards, part, local_width):
    return jnp.concatenate(
        [shard[part * local_width : (part + 1) * local_width, :] for shard in shards], axis=0
    )


def attention_kernel(
    local_width, tok_ref, mod_ref, cond_ref, router_ref, pairs_ref, cot_ref, w0, w1, w2, w3,
    attn_in_ref, qkv_ref, context_ref, attn_out_ref, ext_ref, both_ref,
):
    shards = (w0, w1, w2, w3)
    rows, width = tok_ref.shape
    mod = mod_ref[...]
    stream = tok_ref[...].astype(f32)
    attn_in = (normalize(stream)[0] * (1.0 + mod[1:2]) + mod[0:1]).astype(bf16)
    attn_in_ref[...] = attn_in
    for part in range(3):
        qkv_ref[part] = mm(attn_in, shard_rows(shards, part, local_width), NT).astype(bf16)
    masks = pair_masks(rows)
    zero = jnp.zeros((rows, 2 * HD), bf16)
    for pair in range(width // (2 * HD)):
        cols = slice(pair * 2 * HD, (pair + 1) * 2 * HD)
        query, key, value = qkv_ref[0, :, cols], qkv_ref[1, :, cols], qkv_ref[2, :, cols]
        parts = []
        for mask in masks:
            probs = head_probs(jnp.where(mask, query, zero), key)
            parts.append(mm(probs.astype(bf16), value, NN))
        context_ref[:, cols] = jnp.where(masks[0], parts[0], parts[1]).astype(bf16)
    attn_out = mm(context_ref[...], shard_rows(shards, 3, local_width), NN)
    attn_out_ref[...] = attn_out
    residual = stream + mod[2:3] * attn_out
    moe_in = (normalize(residual)[0] * (1.0 + mod[4:5]) + mod[3:4]).astype(bf16)
    ext_ref[0:rows, :] = moe_in
    logits = mm(router_ref[...], moe_in, NT)
    pairs = pairs_ref[...]
    expert_id = lax.broadcasted_iota(jnp.int32, (EXPERTS, rows), 0)
    chosen = [
        jnp.sum(jnp.where(expert_id == pairs[k : k + 1], logits, 0.0), axis=0, keepdims=True)
        for k in range(TOPK)
    ]
    top = jnp.maximum(chosen[0], chosen[1])
    powers = [jnp.exp(value - top) for value in chosen]
    gates = [power / (powers[0] + powers[1]) for power in powers]
    high = [gate.astype(bf16).astype(f32) for gate in gates]
    rest = [gate - upper for gate, upper in zip(gates, high)]
    values = pairs.astype(f32)
    packed = (
        jnp.concatenate([values[0:1], values[1:2], values[2:3]], axis=1),
        jnp.concatenate([values[3:4], high[0], high[1]], axis=1),
        jnp.concatenate([rest[0], rest[1], jnp.zeros_like(rest[0])], axis=1),
        cond_ref[...],
    )
    row_id = lax.broadcasted_iota(jnp.int32, (EXTRA, width), 0)
    extra = jnp.zeros((EXTRA, width), f32)
    for index, line in enumerate(packed):
        extra = jnp.where(row_id == index, line, extra)
    ext_ref[rows : rows + EXTRA, :] = extra.astype(bf16)
    both_ref[0:rows, :] = cot_ref[...]
    both_ref[rows : 2 * rows, :] = moe_in
    both_ref[2 * rows :, :] = extra.astype(bf16)


def attention_forward(tokens, mod, cond, router_t, pairs, cot, shards, local_width):
    rows, width = tokens.shape
    return pl.pallas_call(
        functools.partial(attention_kernel, local_width),
        out_shape=(
            jax.ShapeDtypeStruct((rows, width), bf16),
            jax.ShapeDtypeStruct((3, rows, width), bf16),
            jax.ShapeDtypeStruct((rows, width), bf16),
            jax.ShapeDtypeStruct((rows, width), f32),
            jax.ShapeDtypeStruct((rows + EXTRA, width), bf16),
            jax.ShapeDtypeStruct((2 * rows + EXTRA, width), bf16),
        ),
        compiler_params=params(),
        cost_estimate=cost(5 * 10**9, 9 * 10**6),
        name="attention_forward",
    )(tokens, mod, cond, router_t, pairs, cot, *shards)


def read_pairs(extra):
    info = extra.astype(f32)
    count = PATCHES
    routes = (info[0:1, 0:count], info[0:1, count : 2 * count])
    places = (info[0:1, 2 * count : 3 * count], info[1:2, 0:count])
    gates = (
        info[1:2, count : 2 * count] + info[2:3, 0:count],
        info[1:2, 2 * count : 3 * count] + info[2:3, count : 2 * count],
    )
    return routes, places, gates


def slot_hits(routes, places, base, slots):
    slot_id = lax.broadcasted_iota(jnp.int32, (slots, PATCHES), 0).astype(f32)
    return [
        slot_id == jnp.where(place < CAP, (route - base) * CAP + place, -1.0)
        for route, place in zip(routes, places)
    ]


def slot_gates(hits, gates):
    return jnp.sum(
        jnp.where(hits[0], gates[0], 0.0) + jnp.where(hits[1], gates[1], 0.0), axis=1, keepdims=True
    )


class Blocks:
    def __init__(self, rows, rows_at, extra_at, cots, cots_at):
        self.rows, self.rows_at, self.extra_at, self.cots, self.cots_at = rows, rows_at, extra_at, cots, cots_at

    @classmethod
    def apart(cls, ext, cots):
        return cls(ext, 0, PATCHES // EXTRA, cots, 0)

    @classmethod
    def joined(cls, both):
        return cls(both, 1, 2 * PATCHES // EXTRA, both, 0)

    def operands(self):
        return [self.rows, self.rows, self.cots]

    def specs(self):
        width = self.rows.shape[2]
        places = ((PATCHES, self.rows_at), (EXTRA, self.extra_at), (PATCHES, self.cots_at))
        return [
            pl.BlockSpec((HALF, count, width), lambda *_, at=at: (0, at, 0)) for count, at in places
        ]

    def extra(self):
        return self.rows[:, self.extra_at * EXTRA : (self.extra_at + 1) * EXTRA]


def dispatch_kernel(base_ref, *refs):
    rows_ref, cots_ref = refs[-2:]
    members = rows_ref.shape[0]
    base = base_ref[0].astype(f32)
    for part in range(2):
        rows_in, extra_in, cots_in = refs[3 * part : 3 * part + 3]

        @pl.when(pl.program_id(0) == part)
        def _():
            for block in range(HALF):
                routes, places, gates = read_pairs(extra_in[block])
                hits = slot_hits(routes, places, base, members * CAP)
                hot = (hits[0] | hits[1]).astype(bf16)
                picked = mm(hot, rows_in[block], NN).astype(bf16)
                scaled = (mm(hot, cots_in[block], NN) * slot_gates(hits, gates)).astype(bf16)
                for member in range(members):
                    span = slice(member * CAP, (member + 1) * CAP)
                    rows_ref[member, block * CAP : (block + 1) * CAP, :] = picked[span]
                    cots_ref[member, block * CAP : (block + 1) * CAP, :] = scaled[span]


def dispatch(base, blocks, members):
    width = blocks[0].rows.shape[2]
    out = jax.ShapeDtypeStruct((members, 2 * HALF * CAP, width), bf16)
    out_spec = pl.BlockSpec((members, HALF * CAP, width), lambda c, b: (0, c, 0))
    return pl.pallas_call(
        dispatch_kernel,
        grid_spec=pltpu.PrefetchScalarGridSpec(
            num_scalar_prefetch=1,
            grid=(2,),
            in_specs=[spec for part in blocks for spec in part.specs()],
            out_specs=(out_spec, out_spec),
        ),
        out_shape=(out, out),
        compiler_params=params(),
        cost_estimate=cost(8 * 10**9, 16 * 10**6),
        name="dispatch",
    )(base, *[operand for part in blocks for operand in part.operands()])


def expert_kernel(
    shared_ids, base_ref, rows0, extra0, cots0, rows1, extra1, cots1, sup_ref, sdown_ref, eup_ref, edown_ref,
    first_ref, second_ref, rows_s, cots_s, gate_s, dot_s, shared_s,
):
    step = pl.program_id(0)
    members = rows_s.shape[0]
    width = sup_ref.shape[0]
    base = base_ref[0].astype(f32)
    halves = ((rows0, extra0, cots0), (rows1, extra1, cots1))
    total_rows = 2 * HALF * CAP

    def block_hits(block):
        routes, places, gates = read_pairs(halves[block // HALF][1][block % HALF])
        return slot_hits(routes, places, base, members * CAP), gates

    @pl.when(step == 0)
    def _():
        for block in range(2 * HALF):
            rows_in, _, cots_in = halves[block // HALF]
            hits, gates = block_hits(block)
            hot = (hits[0] | hits[1]).astype(bf16)
            picked = mm(hot, rows_in[block % HALF], NN).astype(bf16)
            cots = mm(hot, cots_in[block % HALF], NN).astype(bf16)
            gate = slot_gates(hits, gates)
            for member in range(members):
                span = slice(member * CAP, (member + 1) * CAP)
                rows_s[member, block * CAP : (block + 1) * CAP, :] = picked[span]
                cots_s[member, block * CAP : (block + 1) * CAP, :] = cots[span]
                gate_s[member, block * CAP : (block + 1) * CAP, :] = gate[span]
        for start in range(0, len(shared_ids), 2):
            pair = shared_ids[start : start + 2]
            inputs = jnp.concatenate([halves[b // HALF][0][b % HALF] for b in pair], axis=0)
            cots = jnp.concatenate([halves[b // HALF][2][b % HALF] for b in pair], axis=0)
            value, slope = gelu_both(mm(inputs, sup_ref[...], NN))
            pre_grad = (mm(cots, sdown_ref[...], NT) * slope).astype(bf16)
            result = mm(value.astype(bf16), sdown_ref[...], NN)
            back = mm(pre_grad, sup_ref[...], NT)
            for place in range(len(pair)):
                span = slice(place * PATCHES, (place + 1) * PATCHES)
                shared_s[start + place, :, 0:width] = result[span]
                shared_s[start + place, :, width:] = back[span]

    @pl.when(step > 0)
    def _():
        member = step - 1
        tile = total_rows // 2
        for part in range(2):
            span = slice(part * tile, (part + 1) * tile)
            inputs, cots, gate = rows_s[member, span, :], cots_s[member, span, :], gate_s[member, span, :]
            value, slope = gelu_both(mm(inputs, eup_ref[0], NN))
            act_grad = mm(cots, edown_ref[0], NT)
            dot_s[member, span, :] = jnp.sum(value * act_grad, axis=1, keepdims=True)
            active = (gate * value).astype(bf16)
            pre_grad = (gate * act_grad * slope).astype(bf16)
            rows_s[member, span, :] = mm(active, edown_ref[0], NN).astype(bf16)
            cots_s[member, span, :] = mm(pre_grad, eup_ref[0], NT).astype(bf16)

    @pl.when(step == members)
    def _():
        for block in range(2 * HALF):
            out_ref = (first_ref, second_ref)[block // HALF]
            place = block % HALF
            hits, _ = block_hits(block)
            hot = (hits[0] | hits[1]).astype(bf16)
            span = slice(block * CAP, (block + 1) * CAP)
            dots = jnp.concatenate([dot_s[m, span, :] for m in range(members)], axis=0)
            sums = [jnp.sum(jnp.where(hit, dots, 0.0), axis=0, keepdims=True) for hit in hits]
            line = jnp.concatenate(sums + [jnp.zeros_like(sums[0])], axis=1)
            row_id = lax.broadcasted_iota(jnp.int32, (EXTRA, width), 0)
            out_ref[place, 2 * PATCHES :, :] = jnp.where(row_id == 0, line, 0.0).astype(bf16)
            for index, source in enumerate((rows_s, cots_s)):
                slots = jnp.concatenate([source[m, span, :] for m in range(members)], axis=0)
                total = mm(hot, slots, TN)
                if block in shared_ids:
                    where = shared_ids.index(block)
                    total = total + shared_s[where, :, index * width : (index + 1) * width]
                out_ref[place, index * PATCHES : (index + 1) * PATCHES, :] = total.astype(bf16)


def experts_both(base, blocks, shared_up, shared_down, expert_up, expert_down, shared_ids):
    members, width, hidden = expert_up.shape
    out = jax.ShapeDtypeStruct((HALF, 2 * PATCHES + EXTRA, width), bf16)
    out_spec = pl.BlockSpec(out.shape, lambda e, b: (0, 0, 0))
    return pl.pallas_call(
        functools.partial(expert_kernel, shared_ids),
        grid_spec=pltpu.PrefetchScalarGridSpec(
            num_scalar_prefetch=1,
            grid=(members + 1,),
            in_specs=[spec for part in blocks for spec in part.specs()]
            + [
                pl.BlockSpec((width, hidden), lambda e, b: (0, 0)),
                pl.BlockSpec((hidden, width), lambda e, b: (0, 0)),
                pl.BlockSpec((1, width, hidden), lambda e, b: (jnp.maximum(e - 1, 0), 0, 0)),
                pl.BlockSpec((1, hidden, width), lambda e, b: (jnp.maximum(e - 1, 0), 0, 0)),
            ],
            out_specs=(out_spec, out_spec),
            scratch_shapes=[
                pltpu.VMEM((members, 2 * HALF * CAP, width), bf16),
                pltpu.VMEM((members, 2 * HALF * CAP, width), bf16),
                pltpu.VMEM((members, 2 * HALF * CAP, 1), f32),
                pltpu.VMEM((members, 2 * HALF * CAP, 1), f32),
                pltpu.VMEM((max(len(shared_ids), 1), PATCHES, 2 * width), f32),
            ],
        ),
        out_shape=(out, out),
        compiler_params=params(),
        cost_estimate=cost(30 * 10**9, 30 * 10**6),
        name="experts_both",
    )(
        base, *[operand for part in blocks for operand in part.operands()],
        shared_up, shared_down, expert_up, expert_down,
    )


def grads_kernel(count, tile, started, *refs):
    row_refs, cot_refs = refs[:count], refs[count : 2 * count]
    up_ref, down_ref = refs[2 * count : 2 * count + 2]
    up_grad_ref, down_grad_ref = refs[-2:]
    width = up_ref.shape[1]
    inputs = [ref[...].reshape(-1, width) for ref in row_refs]
    cots = [ref[...].reshape(-1, width) for ref in cot_refs]
    groups = max(1, count * inputs[0].shape[0] // tile)
    each = count // groups
    for group in range(groups):
        part = slice(group * each, (group + 1) * each)
        rows, cot = jnp.concatenate(inputs[part], axis=0), jnp.concatenate(cots[part], axis=0)
        value, slope = gelu_both(mm(up_ref[0], rows, TT))
        pre_grad = (mm(down_ref[0], cot, NT) * slope).astype(bf16)
        up_grad = mm(rows, pre_grad, TT)
        down_grad = mm(value.astype(bf16), cot, NN)
        if group == 0 and started:
            up_grad_ref[0] = refs[2 * count + 2][0] + up_grad
            down_grad_ref[0] = refs[2 * count + 3][0] + down_grad
        elif group == 0:
            up_grad_ref[0] = up_grad
            down_grad_ref[0] = down_grad
        else:
            up_grad_ref[0] += up_grad
            down_grad_ref[0] += down_grad


def weight_grads(rows, cots, specs, up, down, before, tile, total):
    members, width, hidden = up.shape
    up_spec = pl.BlockSpec((1, width, hidden), lambda e: (e, 0, 0))
    down_spec = pl.BlockSpec((1, hidden, width), lambda e: (e, 0, 0))
    started = before is not None
    count = len(rows)
    return pl.pallas_call(
        functools.partial(grads_kernel, count, tile, started),
        grid=(members,),
        in_specs=specs + [up_spec, down_spec] + ([up_spec, down_spec] if started else []),
        out_specs=(up_spec, down_spec),
        out_shape=(
            jax.ShapeDtypeStruct(up.shape, f32),
            jax.ShapeDtypeStruct(down.shape, f32),
        ),
        input_output_aliases={2 * count + 2: 0, 2 * count + 3: 1} if started else {},
        compiler_params=params(),
        cost_estimate=cost(12 * total * width * hidden, total * width * 4),
        name="weight_grads",
    )(*rows, *cots, up, down, *(before or ()))


def routed_grads(slots, up, down, before):
    members, count, width = slots[0][0].shape
    spec = pl.BlockSpec((1, count, width), lambda e: (e, 0, 0))
    rows, cots = [pair[0] for pair in slots], [pair[1] for pair in slots]
    specs = [spec] * (2 * len(slots))
    return weight_grads(
        rows, cots, specs, up, down, before, len(slots) * count, len(slots) * members * count
    )


def shared_grads(blocks, up, down, before):
    rows, cots = [part.rows for part in blocks], [part.cots for part in blocks]
    all_specs = [part.specs() for part in blocks]
    specs = [spec[0] for spec in all_specs] + [spec[2] for spec in all_specs]
    return weight_grads(
        rows, cots, specs, up[None], down[None], before, 2 * HALF * PATCHES, len(blocks) * HALF * PATCHES
    )


def backward_kernel(
    local_width, moe_ref, moe_more_ref, back_ref, back_more_ref, tok_ref, cot_ref, mod_ref, router_ref, pairs_ref, attn_in_ref,
    qkv_ref, context_ref, attn_out_ref, ext_ref, w0, w1, w2, w3,
    output_ref, tok_grad_ref, small_ref, near_ref, far_ref, grad_s,
):
    def put_weight_grad(first, grad):
        for index in range(len(shards)):
            out_ref = (near_ref, far_ref)[index % 2]
            out_ref[index // 2, first : first + local_width, :] = grad[
                index * local_width : (index + 1) * local_width
            ]

    shards = (w0, w1, w2, w3)
    rows, width = tok_ref.shape
    mod = mod_ref[...]
    stream = tok_ref[...].astype(f32)
    attn_out = attn_out_ref[...]
    residual = stream + mod[2:3] * attn_out
    second_norm, second_inv = normalize(residual)
    moe_out = moe_ref[...] + moe_more_ref[...].astype(f32)
    back = back_ref[...] + back_more_ref[...].astype(f32)
    upstream = cot_ref[...].astype(f32)
    output_ref[...] = (residual + mod[5:6] * moe_out).astype(bf16)
    gate_two_grad = jnp.sum(upstream * moe_out, axis=0, keepdims=True)
    routes, places, gates = read_pairs(ext_ref[rows:, :])
    dots = (back[rows : rows + 1, 0:PATCHES], back[rows : rows + 1, PATCHES : 2 * PATCHES])
    mean_dot = gates[0] * dots[0] + gates[1] * dots[1]
    pairs = pairs_ref[...]
    expert_id = lax.broadcasted_iota(jnp.int32, (EXPERTS, rows), 0)
    logits_grad = jnp.zeros((EXPERTS, rows), f32)
    for k in range(TOPK):
        logits_grad += jnp.where(expert_id == pairs[k : k + 1], gates[k] * (dots[k] - mean_dot), 0.0)
    logits_grad = logits_grad.astype(bf16)
    moe_in_grad = back[0:rows] + mm(logits_grad, router_ref[...], TN)
    shift_two_grad = jnp.sum(moe_in_grad, axis=0, keepdims=True)
    scale_two_grad = jnp.sum(moe_in_grad * second_norm, axis=0, keepdims=True)
    residual_grad = upstream + normalize_back(
        second_norm, second_inv, moe_in_grad * (1.0 + mod[4:5])
    )
    gate_one_grad = jnp.sum(residual_grad * attn_out, axis=0, keepdims=True)
    attn_grad = (mod[2:3] * residual_grad).astype(bf16)
    out_grad = mm(context_ref[...], attn_grad, TN).astype(bf16)
    put_weight_grad(3 * local_width, out_grad)
    context_grad = mm(attn_grad, shard_rows(shards, 3, local_width), NT).astype(bf16)
    masks = pair_masks(rows)
    zero = jnp.zeros((rows, 2 * HD), bf16)
    scale = 1.0 / math.sqrt(HD)
    for pair in range(width // (2 * HD)):
        cols = slice(pair * 2 * HD, (pair + 1) * 2 * HD)
        query, key, value = qkv_ref[0, :, cols], qkv_ref[1, :, cols], qkv_ref[2, :, cols]
        upper = context_grad[:, cols]
        sums = []
        for mask in masks:
            probs = head_probs(jnp.where(mask, query, zero), key)
            probs_grad = mm(jnp.where(mask, upper, zero), value, NT)
            value_grad = mm(probs.astype(bf16), upper, TN)
            score_grad = (
                probs * (probs_grad - jnp.sum(probs_grad * probs, axis=-1, keepdims=True))
            ).astype(bf16)
            sums.append((mm(score_grad, key, NN) * scale, mm(score_grad, query, TN) * scale, value_grad))
        for part in range(3):
            grad_s[part, :, cols] = jnp.where(masks[0], sums[0][part], sums[1][part]).astype(bf16)
    attn_in = attn_in_ref[...]
    attn_in_grad = jnp.zeros((rows, width), f32)
    for part in range(3):
        grad = grad_s[part]
        attn_in_grad += mm(grad, shard_rows(shards, part, local_width), NN)
        put_weight_grad(part * local_width, mm(grad, attn_in, TN).astype(bf16))
    first_norm, first_inv = normalize(stream)
    shift_one_grad = jnp.sum(attn_in_grad, axis=0, keepdims=True)
    scale_one_grad = jnp.sum(attn_in_grad * first_norm, axis=0, keepdims=True)
    tok_grad_ref[...] = residual_grad + normalize_back(
        first_norm, first_inv, attn_in_grad * (1.0 + mod[1:2])
    )
    lines = (
        shift_one_grad, scale_one_grad, gate_one_grad, shift_two_grad, scale_two_grad, gate_two_grad,
    )
    row_id = lax.broadcasted_iota(jnp.int32, (8, width), 0)
    stacked = jnp.zeros((8, width), f32)
    for index, line in enumerate(lines):
        stacked = jnp.where(row_id == index, line, stacked)
    small_ref[0:8, :] = stacked
    small_ref[8:16, :] = mm(logits_grad, ext_ref[0:rows, :], NN)


def attention_backward(
    moe, moe_more, back, back_more, tokens, cotangent, mod, router_t, pairs, attn_in, qkv, context, attn_out,
    ext, shards, local_width,
):
    rows, width = tokens.shape
    halves = jax.ShapeDtypeStruct((len(shards) // 2, 4 * local_width, width), bf16)
    return pl.pallas_call(
        functools.partial(backward_kernel, local_width),
        out_shape=(
            jax.ShapeDtypeStruct((rows, width), bf16),
            jax.ShapeDtypeStruct((rows, width), f32),
            jax.ShapeDtypeStruct((16, width), f32),
            halves,
            halves,
        ),
        scratch_shapes=[pltpu.VMEM((3, rows, width), bf16)],
        compiler_params=params(),
        cost_estimate=cost(10 * 10**9, 16 * 10**6),
        name="attention_backward",
    )(
        moe, moe_more, back, back_more, tokens, cotangent, mod, router_t, pairs, attn_in, qkv, context,
        attn_out, ext, *shards,
    )


def local_call(kernel, name, outs, operands, scalars=None, moved=4 * 10**6):
    count = 0 if scalars is None else 1
    vmem = pl.BlockSpec(memory_space=pltpu.VMEM)
    smem = pl.BlockSpec(memory_space=pltpu.SMEM)
    return pl.pallas_call(
        kernel,
        in_specs=[smem] * count + [vmem] * len(operands),
        out_specs=tuple(vmem for _ in outs),
        out_shape=tuple(jax.ShapeDtypeStruct(*out) for out in outs),
        compiler_params=params(),
        cost_estimate=cost(0, moved),
        name=name,
    )(*([] if scalars is None else [scalars]), *operands)


def plane_first_kernel(first, more, side, other, keep_upper, keep_lower):
    cut = PATCHES
    upper = lambda block: first[block, 0:cut, :].astype(f32) + more[block, 0:cut, :].astype(f32)
    lower = lambda block: first[block, cut:, :].astype(f32) + more[block, cut:, :].astype(f32)
    side[0], side[1] = upper(1).astype(bf16), upper(3).astype(bf16)
    other[0], other[1] = lower(2).astype(bf16), lower(3).astype(bf16)
    keep_upper[0], keep_upper[1] = upper(0), upper(2)
    keep_lower[0], keep_lower[1] = lower(0), lower(1)


def plane_second_kernel(keep_upper, keep_lower, side, other, upper, lower, upper_next, lower_next):
    upper[...] = keep_upper[0] + side[0].astype(f32)
    upper_next[...] = (keep_upper[1] + side[1].astype(f32)).astype(bf16)
    lower[...] = keep_lower[0] + other[0].astype(f32)
    lower_next[...] = (keep_lower[1] + other[1].astype(f32)).astype(bf16)


def span_of(index, size):
    return pl.ds(pl.multiple_of(index * size, size), size)


def dense_first_kernel(place, near, more, side, other, keep_upper, keep_lower):
    cut = near.shape[1] // 2
    half = cut // 2
    mine = place[0]
    side[...] = (near[1, 0:cut, :].astype(f32) + more[1, 0:cut, :].astype(f32)).astype(bf16)
    keep_upper[...] = near[0, 0:cut, :].astype(f32) + more[0, 0:cut, :].astype(f32)
    for index in range(2):
        for out, who in ((keep_lower, mine), (other, 1 - mine)):
            rows = pl.ds(pl.multiple_of(cut + who * half, half), half)
            total = near[index, rows, :].astype(f32) + more[index, rows, :].astype(f32)
            out[index] = total.astype(out.dtype)


def dense_second_kernel(place, keep_upper, keep_lower, from_side, from_other, side, other, upper, lower):
    half = upper.shape[0]
    mine = place[0]
    for out, who in ((upper, mine), (other, 1 - mine)):
        rows = span_of(who, half)
        out[...] = (keep_upper[rows, :] + from_side[rows, :].astype(f32)).astype(out.dtype)
    lower[...] = keep_lower[0] + from_other[0].astype(f32)
    side[...] = (keep_lower[1] + from_other[1].astype(f32)).astype(bf16)


def dense_third_kernel(size, place, upper, lower, from_side, from_other, own, sent, total):
    half = upper.shape[0]
    share = 2 * half // size
    total[0:half, :] = upper[...] + from_other[...].astype(f32)
    total[half:, :] = lower[...] + from_side[...].astype(f32)
    own[...] = total[span_of(place[1], share), :]
    for hop in range(1, size):
        sent[hop - 1] = total[span_of(lax.rem(place[1] + hop, size), share), :].astype(bf16)


def dense_fourth_kernel(own, *refs):
    out = refs[-1]
    total = own[...]
    for ref in refs[:-1]:
        total = total + ref[...].astype(f32)
    out[...] = total.astype(bf16)


def dense_fifth_kernel(size, place, own, *refs):
    out = refs[-1]
    share = own.shape[0]
    out[span_of(place[1], share), :] = own[...]
    for hop in range(1, size):
        out[span_of(lax.rem(place[1] + size - hop, size), share), :] = refs[hop - 1][...]


def dense_last_kernel(place, own, more, out):
    half = own.shape[0] // 2
    for ref, who in ((own, place[0]), (more, 1 - place[0])):
        for index in range(2):
            rows = pl.ds(pl.multiple_of(2 * half * index + who * half, half), half)
            out[rows, :] = ref[index * half : (index + 1) * half, :].astype(f32)


class Links:
    def __init__(self, mesh):
        self.dp, self.expert, self.tensor = (mesh.shape[name] for name in ("dp", "expert", "tensor"))
        self.paired = self.expert == 2 and self.tensor == 4
        self.core = [(i, i ^ 1) for i in range(self.tensor)]
        self.side = [(i, i ^ 2) for i in range(self.tensor)]
        self.other = [(0, 1), (1, 0)]

    def to_core(self, value):
        return lax.ppermute(value, "tensor", self.core)

    def to_side(self, value):
        return lax.ppermute(value, "tensor", self.side)

    def to_other(self, value):
        return lax.ppermute(value, "expert", self.other)

    def along(self, value, hop):
        return lax.ppermute(value, "dp", [(i, (i + hop) % self.dp) for i in range(self.dp)])

    def plane(self, block, after=()):
        rows, width = block.shape
        cut = (rows // 2 + 15) // 16 * 16
        side, other = self.to_side(block), self.to_other(block)
        upper, lower = self.to_side(other[:cut]), self.to_other(side[cut:])
        everything = slice(None)
        plan = [(index, everything, index) for index in range(3)]
        plan += [(3, everything, (3, pl.ds(0, cut))), (4, everything, (3, pl.ds(cut, rows - cut)))]
        mine = assemble((HALF, rows, width), block.dtype, (block, side, other, upper, lower), plan, after)
        return mine, self.to_core(mine)

    def everywhere(self, small):
        stack = jnp.stack([small] + [self.along(small, hop) for hop in range(1, self.dp)])
        side, other = self.to_side(stack), self.to_other(stack)
        chips = jnp.stack([stack, side, other, self.to_side(other)])
        cores = jnp.stack([chips, self.to_core(chips)])
        return cores.transpose((2, 0, 1) + tuple(range(3, cores.ndim)))

    def plane_sum(self, first, second):
        width = first.shape[2]
        low = first.shape[1] - PATCHES
        side, other, keep_upper, keep_lower = local_call(
            plane_first_kernel,
            "plane_first",
            [((2, PATCHES, width), bf16), ((2, low, width), bf16), ((2, PATCHES, width), f32), ((2, low, width), f32)],
            [first, self.to_core(second)],
        )
        upper, lower, upper_next, lower_next = local_call(
            plane_second_kernel,
            "plane_second",
            [((PATCHES, width), f32), ((low, width), f32), ((PATCHES, width), bf16), ((low, width), bf16)],
            [keep_upper, keep_lower, self.to_side(side), self.to_other(other)],
        )
        return upper, self.to_other(upper_next), lower, self.to_side(lower_next)

    def dense_sum(self, near, far):
        _, rows, width = near.shape
        cut, half, share = rows // 2, rows // 4, rows // 2 // self.dp
        place = jnp.stack([lax.axis_index("expert"), lax.axis_index("dp")]).astype(jnp.int32)
        side, other, keep_upper, keep_lower = local_call(
            dense_first_kernel,
            "dense_first",
            [((cut, width), bf16), ((2, half, width), bf16), ((cut, width), f32), ((2, half, width), f32)],
            [near, self.to_core(far)],
            place,
        )
        side, other, upper, lower = local_call(
            dense_second_kernel,
            "dense_second",
            [((half, width), bf16), ((half, width), bf16), ((half, width), f32), ((half, width), f32)],
            [keep_upper, keep_lower, self.to_side(side), self.to_other(other)],
            place,
        )
        own, sent, _ = local_call(
            functools.partial(dense_third_kernel, self.dp),
            "dense_third",
            [((share, width), f32), ((self.dp - 1, share, width), bf16), ((cut, width), f32)],
            [upper, lower, self.to_side(side), self.to_other(other)],
            place,
        )
        hops = range(1, self.dp)
        (total,) = local_call(
            dense_fourth_kernel,
            "dense_fourth",
            [((share, width), bf16)],
            [own] + [self.along(sent[hop - 1], hop) for hop in hops],
        )
        (column,) = local_call(
            functools.partial(dense_fifth_kernel, self.dp),
            "dense_fifth",
            [((cut, width), bf16)],
            [total] + [self.along(total, hop) for hop in hops],
            place,
        )
        (result,) = local_call(
            dense_last_kernel, "dense_last", [((rows, width), f32)], [column, self.to_other(column)], place
        )
        return result


def local(
    links,
    tokens,
    cotangent,
    timesteps,
    ada_weight,
    ada_bias,
    qkv_weight,
    out_weight,
    router_weight,
    shared_up,
    shared_down,
    expert_up,
    expert_down,
    routes,
    places,
):
    rows, width = tokens.shape
    local_width = qkv_weight.shape[2]
    members = expert_up.shape[0]
    me = lax.axis_index("tensor")
    base = (lax.axis_index("expert") * members).astype(jnp.int32).reshape(1)
    everyone = ("dp", "expert", "tensor")
    total_blocks = links.dp * links.expert * links.tensor
    full = links.paired and total_blocks * rows * width * 2 <= FULL_LIMIT

    weight = jnp.concatenate(
        [qkv_weight.transpose(1, 2, 0).reshape(3 * local_width, width), out_weight], axis=0
    )
    across = links.to_side(weight)
    shards = (weight, links.to_core(weight), across, links.to_core(across))

    condition = jax.nn.silu(embedding(timesteps, width)).astype(bf16)
    mod_cols = jnp.einsum("id,dcf->icf", condition, ada_weight, preferred_element_type=f32) + ada_bias[None]
    mod = lax.all_to_all(mod_cols, "tensor", split_axis=0, concat_axis=2, tiled=True)[0]
    own_condition = lax.dynamic_slice_in_dim(condition.astype(f32), me, 1, axis=0)
    shared_cot = moe_cotangent(mod, cotangent, across)
    router_t = router_weight.T
    pairs = jnp.concatenate([routes.T, places.T], axis=0)

    attn_in, qkv, context, attn_out, ext, both = attention_forward(
        tokens, mod, own_condition, router_t, pairs, shared_cot, shards, local_width
    )
    feed = (shared_up, shared_down, expert_up, expert_down)
    if links.paired:
        cots = links.plane(shared_cot)
        exts = links.plane(ext)
        planes = [tuple(Blocks.apart(*pair) for pair in zip(exts, cots))]
        first, second = experts_both(base, planes[0], *feed, (0, 1, 4, 5))
        upper, upper_more, lower, lower_more = links.plane_sum(first, second)
    else:
        shift = lax.axis_index("expert") * links.tensor
        gather = lambda block: jnp.roll(
            lax.all_gather(block, ("expert", "tensor"), axis=0), -shift, axis=0
        )
        all_ext, all_cot = gather(ext), gather(shared_cot)
        planes, sums = [], []
        for start in range(0, links.expert * links.tensor, 2 * HALF):
            spans = [slice(start + HALF * part, start + HALF * (part + 1)) for part in range(2)]
            planes.append(tuple(Blocks.apart(all_ext[span], all_cot[span]) for span in spans))
            shared_ids = tuple(range(links.tensor)) if start == 0 else ()
            sums += experts_both(base, planes[-1], *feed, shared_ids)
        blocks = jnp.roll(jnp.concatenate(sums, axis=0), shift, axis=0)
        total = lax.psum_scatter(blocks, ("expert", "tensor"), scatter_dimension=0, tiled=True)[0]
        upper, lower = total[:PATCHES].astype(f32), total[PATCHES:].astype(f32)
        upper_more, lower_more = jnp.zeros_like(total[:PATCHES]), jnp.zeros_like(total[PATCHES:])

    output, tokens_grad, small, near, far = attention_backward(
        upper, upper_more, lower, lower_more, tokens, cotangent, mod, router_t, pairs,
        attn_in, qkv, context, attn_out, ext, shards, local_width,
    )

    if full:
        hops = [links.plane(links.along(both, hop)) for hop in range(1, links.dp)]
        planes += [tuple(Blocks.joined(part) for part in parts) for parts in hops]
    slots = [dispatch(base, plane, members) for plane in planes]
    routed, shared = None, None
    for start in range(0, len(planes), 2):
        routed = routed_grads(slots[start : start + 2], expert_up, expert_down, routed)
        parts = [part for plane in planes[start : start + 2] for part in plane]
        shared = shared_grads(parts, shared_up, shared_down, shared)

    if full:
        small_all = links.everywhere(small).reshape(-1, 16, width)
        extra_all = jnp.concatenate([part.extra() for plane in planes for part in plane], axis=0)
        condition_all = extra_all[:, 3]
        routes_all = extra_all[:, 0, : TOPK * PATCHES]
        dense = links.dense_sum(near, far)
    else:
        routed = lax.psum(routed, "dp")
        shared = lax.psum(shared, "dp")
        small_all = lax.all_gather(small, everyone, axis=0)
        condition_all = lax.all_gather(own_condition[0], everyone, axis=0).astype(bf16)
        routes_all = lax.all_gather(routes.reshape(-1), everyone, axis=0)
        order = jnp.arange(links.tensor) ^ me
        grads = jnp.stack([near, far], axis=1).reshape((-1,) + near.shape[1:])[order]
        dense = lax.psum_scatter(grads, "tensor", scatter_dimension=0, tiled=True)[0]
        dense = lax.psum(dense, ("dp", "expert")).astype(f32)

    mod_grad = lax.dynamic_slice_in_dim(small_all[:, 0:6], me * local_width, local_width, axis=2)
    ada_grad = jnp.einsum(
        "id,icf->dcf", condition_all.astype(f32), mod_grad, precision=lax.Precision.HIGHEST
    )
    ada_bias_grad = jnp.sum(mod_grad, axis=0)
    router_grad = jnp.sum(small_all[:, 8:16], axis=0).T
    counts = jnp.sum(
        (routes_all[:, :, None] == jnp.arange(EXPERTS).astype(routes_all.dtype)).astype(jnp.int32),
        axis=(0, 1),
    )
    qkv_grad = dense[: 3 * local_width].reshape(3, local_width, width).transpose(2, 0, 1)
    return (
        output,
        tokens_grad,
        ada_grad,
        ada_bias_grad,
        qkv_grad,
        dense[3 * local_width :],
        router_grad,
        shared[0][0],
        shared[1][0],
        routed[0],
        routed[1],
        counts,
    )


def solution(mesh):
    rows = P(("dp", "expert", "tensor"), None)
    placed = (
        rows,
        rows,
        P(("dp", "expert")),
        P(None, None, "tensor"),
        P(None, "tensor"),
        P(None, None, "tensor"),
        P("tensor", None),
        P(),
        P(None, "tensor"),
        P("tensor", None),
        P("expert", None, "tensor"),
        P("expert", "tensor", None),
        rows,
        rows,
    )
    return jax.shard_map(
        functools.partial(local, Links(mesh)),
        mesh=mesh,
        in_specs=placed,
        out_specs=(
            rows,
            rows,
            P(None, None, "tensor"),
            P(None, "tensor"),
            P(None, None, "tensor"),
            P("tensor", None),
            P(),
            P(None, "tensor"),
            P("tensor", None),
            P("expert", None, "tensor"),
            P("expert", "tensor", None),
            P(),
        ),
        check_vma=False,
    )
```

time: 524 us -> 902 us (1.72)
  Pallas kernels: 219 us -> 633 us
  local copies, waits for them, and re-layouts: 55.5 us -> 31.2 us
  other arithmetic: 24.8 us -> 6.57 us
  starting transfers between devices: 54.3 us -> 71.3 us
  waiting for transfers between devices: 158 us -> 148 us
    pallas_call x4 -> x18, Pallas kernels: 136 us -> 546 us  [the longest x5 399 us: assemble(): pl.pallas_call(functools.partial(copy_kernel, plan, len(sources)), in_spe...]
    ppermute x17 -> x12, waiting for transfers between devices: 68.8 us -> 39.6 us  [along(): lax.ppermute(value, 'dp', [(i, (i + hop) % self.dp) for i in range(self.d...]
    ppermute x17 -> x12, starting transfers between devices: 19.7 us -> 34.7 us  [along(): lax.ppermute(value, 'dp', [(i, (i + hop) % self.dp) for i in range(self.d...]
    concatenate x6 -> x1, local copies, waits for them, and re-layouts: 13.8 us -> 0.9 us  [local(): jnp.concatenate([part.extra() for plane in planes for part in plane], axi...]
    add x7 -> x0, other arithmetic: 9.62 us -> none  [the longest x1 3.72 us: plane_sum(): here = first + self.to_core(second)]
    ppermute x12 -> x16, waiting for transfers between devices: 34 us -> 42.8 us  [to_other(): return lax.ppermute(value, 'expert', self.other)]
    ppermute x16 -> x17, waiting for transfers between devices: 54.7 us -> 62.8 us  [to_side(): return lax.ppermute(value, 'tensor', self.side)]
    unnamed x68 -> x102, local copies, waits for them, and re-layouts: 26.3 us -> 20.4 us
  transfers between devices with their start and end apart: 57 -> 56, of which waited for: 25 -> 23; matrix products, arithmetic and copies ran while one was open for 15% -> 3% of each run, Pallas kernels for 42% -> 67%
where the time goes in v2:
time: 902 us; the launch traced here: 896 us
  Pallas kernels  633 us (70%)
  waiting for transfers between devices  148 us (16%)
  starting transfers between devices  71.3 us (8%)
  local copies, waits for them, and re-layouts  31.2 us (3%)
    pallas_call x5, Pallas kernels, assemble(): pl.pallas_call(functools.partial(copy_kernel, plan, len(sources)), in_spe...  399 us
    pallas_call x4, Pallas kernels, weight_grads(): pl.pallas_call(functools.partial(grads_kernel, count, tile, started), gri...  119 us
    ppermute x17, waiting for transfers between devices, to_side(): return lax.ppermute(value, 'tensor', self.side)  62.8 us
    ppermute x16, waiting for transfers between devices, to_other(): return lax.ppermute(value, 'expert', self.other)  42.8 us
    ppermute x12, waiting for transfers between devices, along(): lax.ppermute(value, 'dp', [(i, (i + hop) % self.dp) for i in range(self.d...  39.6 us
    ppermute x12, starting transfers between devices, along(): lax.ppermute(value, 'dp', [(i, (i + hop) % self.dp) for i in range(self.d...  34.7 us
    pallas_call x1, Pallas kernels, experts_both(): pl.pallas_call(functools.partial(expert_kernel, shared_ids), grid_spec=pl...  33.3 us
    pallas_call x4, Pallas kernels, dispatch(): pl.pallas_call(dispatch_kernel, grid_spec=pltpu.PrefetchScalarGridSpec(nu...  29.9 us
  transfers between devices with their start and end apart: 56, of which 23 were waited for; matrix products, arithmetic and copies ran while one was open for 3% of the time, Pallas kernels for 67%

profile of v2, /device:TPU:0, one launch (start us, length us, event | category | flops | bytes accessed | tf_op | source)
XLA Modules:
  0.0 895.7 jit_solution(5511378300345391820)
XLA Ops:
  2.2 3.0 collective-permute-start
  5.2 26.1 %collective-permute-done.after_ref.w2 = bf16[768,768]{1,0:T(8,128)(2,1)} collective-permute-done((bf16[768,768]{1,0:T(8,128)(2,1)S(1)}, bf16[768,768]{1,0:T(8,128)(2,1)}, u32[]{:S(2)}, u32[]{:S(2)}) %collective-permute-start) | collective-permute-done | bytes 1179680 | tf_op jit(solution)/shard_map/ppermute | solution.py:696
  32.7 3.3 all-to-all-start
  37.1 2.7 all-to-all-done
  42.4 7.8 attention_forward.1
  52.0 2.6 collective-permute-start.24
  58.2 6.6 collective-permute-done.8.refs_2_
  65.0 3.2 collective-permute-done.7.refs_1_
  68.8 10.4 %collective-permute-done.9.refs_3_ = bf16[128,768]{1,0:T(8,128)(2,1)S(1)} collective-permute-done((bf16[128,768]{1,0:T(8,128)(2,1)S(1)}, bf16[128,768]{1,0:T(8,128)(2,1)S(1)}, u32[]{:S(2)}, u32[]{:S(2)}) %collective-permute-start.9) | collective-permute-done | bytes 196640 | tf_op jit(solution)/shard_map/ppermute | solution.py:696
  82.9 24.3 %collective-permute-done.24.refs_0_ = bf16[528,768]{1,0:T(8,128)(2,1)} collective-permute-done((bf16[528,768]{1,0:T(8,128)(2,1)}, bf16[528,768]{1,0:T(8,128)(2,1)}, u32[]{:S(2)}, u32[]{:S(2)}) %collective-permute-start.24) | collective-permute-done | bytes 811040 | tf_op jit(solution)/shard_map/ppermute | solution.py:702
  109.0 5.2 collective-permute-done.6.refs_4_
  115.9 16.1 %collective-permute-done.5.refs_3_ = bf16[144,768]{1,0:T(8,128)(2,1)S(1)} collective-permute-done((bf16[144,768]{1,0:T(8,128)(2,1)S(1)}, bf16[144,768]{1,0:T(8,128)(2,1)S(1)}, u32[]{:S(2)}, u32[]{:S(2)}) %collective-permute-start.5) | collective-permute-done | bytes 221216 | tf_op jit(solution)/shard_map/ppermute | solution.py:696
  133.6 51.8 %assemble.5.rows0.extra0.refs_0_.refs_1_ = bf16[4,272,768]{2,1,0:T(8,128)(2,1)} custom-call(bf16[272,768]{1,0:T(8,128)(2,1)} %get-tuple-element.59.refs_0_.ext_ref, bf16[272,768]{1,0:T(8,128)(2,1)} %copy-done.13, bf16[272,768]{1,0:T(8,128)(2,1)} %copy-done.12, bf16[144,768]{1,0:T(8,128)(2,1)} %copy-done.29, bf16[128,768]{1,0:T(8,128)(2,1)} %collective-permute-done.6.refs_4_), custom_call_target="tpu_custom_call" | custom-call | bytes 3342336 | tf_op jit(solution)/shard_map/assemble/pallas_call | solution.py:88
  187.3 48.8 %assemble.6.cots0.refs_4_.refs_2_ = bf16[4,256,768]{2,1,0:T(8,128)(2,1)} custom-call(bf16[256,768]{1,0:T(8,128)(2,1)} %moe_cotangent.1.cot_ref.refs_0_, bf16[256,768]{1,0:T(8,128)(2,1)} %copy-done.15, bf16[256,768]{1,0:T(8,128)(2,1)} %copy-done.14, bf16[128,768]{1,0:T(8,128)(2,1)} %copy-done.30, bf16[128,768]{1,0:T(8,128)(2,1)} %copy-done.31), custom_call_target="tpu_custom_call" | custom-call | bytes 3145728 | tf_op jit(solution)/shard_map/assemble/pallas_call | solution.py:88
  242.6 7.6 collective-permute-done.22.refs_4_
  250.4 7.4 collective-permute-done.28.refs_4_
  262.7 99.4 %assemble.7.refs_2_.refs_6_.refs_0_.refs_1_ = bf16[4,528,768]{2,1,0:T(8,128)(2,1)} custom-call(bf16[528,768]{1,0:T(8,128)(2,1)} %collective-permute-done.18.refs_0_, bf16[528,768]{1,0:T(8,128)(2,1)} %copy-done.7, bf16[528,768]{1,0:T(8,128)(2,1)} %copy-done.4, bf16[272,768]{1,0:T(8,128)(2,1)} %copy-done.22, bf16[256,768]{1,0:T(8,128)(2,1)} %copy-done.26), custom_call_target="tpu_custom_call" | custom-call | bytes 6488064 | tf_op jit(solution)/shard_map/assemble/pallas_call | solution.py:88
  362.9 99.4 %assemble.8.refs_0_.refs_4_.refs_1_.refs_2_ = bf16[4,528,768]{2,1,0:T(8,128)(2,1)} custom-call(bf16[528,768]{1,0:T(8,128)(2,1)} %collective-permute-done.24.refs_0_, bf16[528,768]{1,0:T(8,128)(2,1)} %copy-done.8, bf16[528,768]{1,0:T(8,128)(2,1)} %copy-done.5, bf16[272,768]{1,0:T(8,128)(2,1)} %copy-done.24, bf16[256,768]{1,0:T(8,128)(2,1)} %copy-done.25), custom_call_target="tpu_custom_call" | custom-call | bytes 6488064 | tf_op jit(solution)/shard_map/assemble/pallas_call | solution.py:88
  463.2 99.4 %assemble.9.refs_2_.refs_6_.refs_0_.refs_1_ = bf16[4,528,768]{2,1,0:T(8,128)(2,1)} custom-call(bf16[528,768]{1,0:T(8,128)(2,1)} %copy-done.17, bf16[528,768]{1,0:T(8,128)(2,1)} %copy-done.9, bf16[528,768]{1,0:T(8,128)(2,1)} %copy-done.6, bf16[272,768]{1,0:T(8,128)(2,1)} %copy-done.23, bf16[256,768]{1,0:T(8,128)(2,1)} %collective-permute-done.34.refs_4_), custom_call_target="tpu_custom_call" | custom-call | bytes 6488064 | tf_op jit(solution)/shard_map/assemble/pallas_call | solution.py:88
  563.1 33.3 %experts_both.1 = (bf16[4,528,768]{2,1,0:T(8,128)(2,1)}, bf16[4,528,768]{2,1,0:T(8,128)(2,1)}) custom-call(s32[1]{0:T(128)} %bitcast.base_ref, bf16[4,272,768]{2,1,0:T(8,128)(2,1)} %assemble.5.rows0.extra0.refs_0_.refs_1_, bf16[4,272,768]{2,1,0:T(8,128)(2,1)} %assemble.5.rows0.extra0.refs_0_.refs_1_, bf16[4,256,768]{2,1,0:T(8,128)(2,1)} %assemble.6.cots0.refs_4_.refs_2_, ...), custom_call_target="tpu_custom_call" | custom-call | flops 30000001024 | bytes 30000000 | tf_op jit(solution)/shard_map/experts_both/pallas_call | solution.py:382
  599.6 7.4 dispatch.6
  607.0 7.4 dispatch.7
  614.5 30.3 %weight_grads.6 = (f32[4,768,768]{2,1,0:T(8,128)}, f32[4,768,768]{2,1,0:T(8,128)}) custom-call(bf16[4,640,768]{2,1,0:T(8,128)(2,1)} %get-tuple-element.98.refs_0_, bf16[4,640,768]{2,1,0:T(8,128)(2,1)} %get-tuple-element.99.refs_1_, bf16[4,640,768]{2,1,0:T(8,128)(2,1)} %get-tuple-element.100.refs_2_, bf16[4,640,768]{2,1,0:T(8,128)(2,1)} %get-tuple-element.101.refs_3_, ...), custom_call_target="tpu_custom_call" | custom-call | flops 36238786560 | bytes 15728640 | tf_op jit(solution)/shard_map/weight_grads/pallas_call | solution.py:446
  646.5 5.3 plane_first.1
  653.8 7.7 dispatch.4
  661.5 7.4 dispatch.5
  668.9 3.0 collective-permute-done.14.side
  674.9 3.9 plane_second.1
  680.2 32.2 %weight_grads.7 = (f32[4,768,768]{2,1,0:T(8,128)}, f32[4,768,768]{2,1,0:T(8,128)}) custom-call(bf16[4,640,768]{2,1,0:T(8,128)(2,1)} %get-tuple-element.94.refs_0_, bf16[4,640,768]{2,1,0:T(8,128)(2,1)} %get-tuple-element.95.refs_1_, bf16[4,640,768]{2,1,0:T(8,128)(2,1)} %get-tuple-element.96.refs_2_, ...), custom_call_target="tpu_custom_call", output_to_operand_aliasing={{0}: (6, {}), {1}: (7, {})} | custom-call | flops 36238786560 | bytes 15728640 | tf_op jit(solution)/shard_map/weight_grads/pallas_call | solution.py:446
  713.3 16.1 %attention_backward.1 = (bf16[256,768]{1,0:T(8,128)(2,1)}, f32[256,768]{1,0:T(8,128)}, f32[16,768]{1,0:T(8,128)}, bf16[2,768,768]{2,1,0:T(8,128)(2,1)}, bf16[2,768,768]{2,1,0:T(8,128)(2,1)}) custom-call(f32[256,768]{1,0:T(8,128)} %get-tuple-element.66.moe_ref, bf16[256,768]{1,0:T(8,128)(2,1)} %copy-done.45, f32[272,768]{1,0:T(8,128)} %get-tuple-element.68.back_ref, ...), custom_call_target="tpu_custom_call" | custom-call | flops 10000000000 | bytes 16000000 | tf_op jit(solution)/shard_map/attention_backward/pallas_call | solution.py:572
  729.4 27.4 %weight_grads.4 = (f32[1,768,768]{2,1,0:T(8,128)}, f32[1,768,768]{2,1,0:T(8,128)}) custom-call(bf16[4,272,768]{2,1,0:T(8,128)(2,1)} %assemble.5.rows0.extra0.refs_0_.refs_1_, bf16[4,272,768]{2,1,0:T(8,128)(2,1)} %collective-permute-done.11.rows1.extra1.refs_1_.refs_3_.refs_4_, bf16[4,528,768]{2,1,0:T(8,128)(2,1)} %assemble.7.refs_2_.refs_6_.refs_0_.refs_1_, ...), custom_call_target="tpu_custom_call" | custom-call | flops 28991029248 | bytes 12582912 | tf_op jit(solution)/shard_map/weight_grads/pallas_call | solution.py:446
  758.2 4.3 dense_first.1
  765.2 28.8 %weight_grads.5 = (f32[1,768,768]{2,1,0:T(8,128)}, f32[1,768,768]{2,1,0:T(8,128)}) custom-call(bf16[4,528,768]{2,1,0:T(8,128)(2,1)} %assemble.8.refs_0_.refs_4_.refs_1_.refs_2_, bf16[4,528,768]{2,1,0:T(8,128)(2,1)} %collective-permute-done.29.refs_1_.refs_5_.refs_3_.refs_4_, ...), custom_call_target="tpu_custom_call", output_to_operand_aliasing={{0}: (10, {}), {1}: (11, {})} | custom-call | flops 28991029248 | bytes 12582912 | tf_op jit(solution)/shard_map/weight_grads/pallas_call | solution.py:446
  794.0 17.8 %collective-permute-start.38 = (f32[16,768]{1,0:T(8,128)S(1)}, f32[16,768]{1,0:T(8,128)S(1)}, u32[]{:S(2)}, u32[]{:S(2)}) collective-permute-start(f32[16,768]{1,0:T(8,128)S(1)} %copy-done.39), channel_id=1, source_target_pairs={{0,24},{8,0},{16,8},{24,16},{1,25},{9,1},{17,9},{25,17},{2,26},{10... | collective-permute-start | bytes 147464 | tf_op jit(solution)/shard_map/ppermute | solution.py:702
  813.9 2.9 collective-permute-done.37
  820.0 3.4 collective-permute-done.40
  825.2 3.3 dense_second.1
  831.6 3.9 collective-permute-done.46.from_side
  837.4 2.9 dense_third.1
  843.8 2.8 collective-permute-start.50
  849.1 3.3 collective-permute-done.49.refs_1_
  854.9 2.7 collective-permute-start.51
  857.6 2.6 collective-permute-start.52
  864.7 3.6 collective-permute-done.52.refs_1_
  874.1 3.4 fusion
  877.5 9.3 %collective-permute-done.54.more = bf16[384,768]{1,0:T(8,128)(2,1)S(1)} collective-permute-done((bf16[384,768]{1,0:T(8,128)(2,1)}, bf16[384,768]{1,0:T(8,128)(2,1)S(1)}, u32[]{:S(2)}, u32[]{:S(2)}) %collective-permute-start.54) | collective-permute-done | bytes 589856 | tf_op jit(solution)/shard_map/ppermute | solution.py:699
  887.6 2.9 dense_last.1
  890.5 2.8 slice.128
  (229 shorter events, 86.6 us)
Async XLA Ops:
  2.2 29.1 %collective-permute-start = (bf16[768,768]{1,0:T(8,128)(2,1)S(1)}, bf16[768,768]{1,0:T(8,128)(2,1)}, u32[]{:S(2)}, u32[]{:S(2)}) collective-permute-start(bf16[768,768]{1,0:T(8,128)(2,1)S(1)} %pad_maximum_fusion.w0), channel_id=1, source_target_pairs={{0,2},{1,3},{2,0},{3,1},{4,6},{5,7},{6,4},{7,5},{8,10},{9,11},{10,... | collective-permute-start | bytes 3538952 | tf_op jit(solution)/shard_map/ppermute | solution.py:696
  5.2 37.2 %collective-permute-start.1 = (bf16[768,768]{1,0:T(8,128)(2,1)S(1)}, bf16[768,768]{1,0:T(8,128)(2,1)}, u32[]{:S(2)}, u32[]{:S(2)}) collective-permute-start(bf16[768,768]{1,0:T(8,128)(2,1)S(1)} %pad_maximum_fusion.w0), channel_id=1, source_target_pairs={{0,1},{1,0},{2,3},{3,2},{4,5},{5,4},{6,7},{7,6},{8,9},{9,8},{10,11... | collective-permute-start | bytes 3538952 | tf_op jit(solution)/shard_map/ppermute | solution.py:693
  31.2 11.1 %collective-permute-start.2 = (bf16[768,768]{1,0:T(8,128)(2,1)}, bf16[768,768]{1,0:T(8,128)(2,1)}, u32[]{:S(2)}, u32[]{:S(2)}) collective-permute-start(bf16[768,768]{1,0:T(8,128)(2,1)} %collective-permute-done.after_ref.w2), channel_id=1, source_target_pairs={{0,1},{1,0},{2,3},{3,2},{4,5},{5,4},{6,7},{7,6},{8,9},{9,8},{10,11... | collective-permute-start | bytes 3538952 | tf_op jit(solution)/shard_map/ppermute | solution.py:693
  50.2 30.9 %collective-permute-start.18 = (bf16[528,768]{1,0:T(8,128)(2,1)}, bf16[528,768]{1,0:T(8,128)(2,1)}, u32[]{:S(2)}, u32[]{:S(2)}) collective-permute-start(bf16[528,768]{1,0:T(8,128)(2,1)} %get-tuple-element.76), channel_id=1, source_target_pairs={{0,8},{8,16},{16,24},{24,0},{1,9},{9,17},{17,25},{25,1},{2,10},{10... | collective-permute-start | bytes 2433032 | tf_op jit(solution)/shard_map/ppermute | solution.py:702
  52.0 55.2 %collective-permute-start.24 = (bf16[528,768]{1,0:T(8,128)(2,1)}, bf16[528,768]{1,0:T(8,128)(2,1)}, u32[]{:S(2)}, u32[]{:S(2)}) collective-permute-start(bf16[528,768]{1,0:T(8,128)(2,1)} %get-tuple-element.76), channel_id=1, source_target_pairs={{0,16},{8,24},{16,0},{24,8},{1,17},{9,25},{17,1},{25,9},{2,18},{10... | collective-permute-start | bytes 2433032 | tf_op jit(solution)/shard_map/ppermute | solution.py:702
  54.6 10.2 %collective-permute-start.8 = (bf16[256,768]{1,0:T(8,128)(2,1)S(1)}, bf16[256,768]{1,0:T(8,128)(2,1)S(1)}, u32[]{:S(2)}, u32[]{:S(2)}) collective-permute-start(bf16[256,768]{1,0:T(8,128)(2,1)S(1)} %copy-done.10), channel_id=1, source_target_pairs={{0,4},{4,0},{1,5},{5,1},{2,6},{6,2},{3,7},{7,3},{8,12},{12,8},{9,1... | collective-permute-start | bytes 1179656 | tf_op jit(solution)/shard_map/ppermute | solution.py:699
  56.2 12.1 %collective-permute-start.7 = (bf16[256,768]{1,0:T(8,128)(2,1)S(1)}, bf16[256,768]{1,0:T(8,128)(2,1)S(1)}, u32[]{:S(2)}, u32[]{:S(2)}) collective-permute-start(bf16[256,768]{1,0:T(8,128)(2,1)S(1)} %copy-done.10), channel_id=1, source_target_pairs={{0,2},{1,3},{2,0},{3,1},{4,6},{5,7},{6,4},{7,5},{8,10},{9,11},{10,... | collective-permute-start | bytes 1179656 | tf_op jit(solution)/shard_map/ppermute | solution.py:696
  56.2 25.2 %collective-permute-start.3 = (bf16[272,768]{1,0:T(8,128)(2,1)}, bf16[272,768]{1,0:T(8,128)(2,1)S(1)}, u32[]{:S(2)}, u32[]{:S(2)}) collective-permute-start(bf16[272,768]{1,0:T(8,128)(2,1)} %get-tuple-element.59.refs_0_.ext_ref), channel_id=1, source_target_pairs={{0,2},{1,3},{2,0},{3,1},{4,6},{5,7},{6,4},{7,5},{8,10},{9,11},{10,... | collective-permute-start | bytes 1253384 | tf_op jit(solution)/shard_map/ppermute | solution.py:696
  64.8 14.4 %collective-permute-start.9 = (bf16[128,768]{1,0:T(8,128)(2,1)S(1)}, bf16[128,768]{1,0:T(8,128)(2,1)S(1)}, u32[]{:S(2)}, u32[]{:S(2)}) collective-permute-start(bf16[128,768]{1,0:T(8,128)(2,1)S(1)} %slice.110), channel_id=1, source_target_pairs={{0,2},{1,3},{2,0},{3,1},{4,6},{5,7},{6,4},{7,5},{8,10},{9,11},{10,... | collective-permute-start | bytes 589832 | tf_op jit(solution)/shard_map/ppermute | solution.py:696
  68.2 11.5 %collective-permute-start.10 = (bf16[128,768]{1,0:T(8,128)(2,1)S(1)}, bf16[128,768]{1,0:T(8,128)(2,1)S(1)}, u32[]{:S(2)}, u32[]{:S(2)}) collective-permute-start(bf16[128,768]{1,0:T(8,128)(2,1)S(1)} %slice.111), channel_id=1, source_target_pairs={{0,4},{4,0},{1,5},{5,1},{2,6},{6,2},{3,7},{7,3},{8,12},{12,8},{9,1... | collective-permute-start | bytes 589832 | tf_op jit(solution)/shard_map/ppermute | solution.py:699
  79.2 28.2 %collective-permute-start.4 = (bf16[272,768]{1,0:T(8,128)(2,1)}, bf16[272,768]{1,0:T(8,128)(2,1)S(1)}, u32[]{:S(2)}, u32[]{:S(2)}) collective-permute-start(bf16[272,768]{1,0:T(8,128)(2,1)} %get-tuple-element.59.refs_0_.ext_ref), channel_id=1, source_target_pairs={{0,4},{4,0},{1,5},{5,1},{2,6},{6,2},{3,7},{7,3},{8,12},{12,8},{9,1... | collective-permute-start | bytes 1253384 | tf_op jit(solution)/shard_map/ppermute | solution.py:699
  79.7 105.7 %collective-permute-start.30 = (bf16[528,768]{1,0:T(8,128)(2,1)}, bf16[528,768]{1,0:T(8,128)(2,1)S(1)}, u32[]{:S(2)}, u32[]{:S(2)}) collective-permute-start(bf16[528,768]{1,0:T(8,128)(2,1)} %get-tuple-element.76), channel_id=1, source_target_pairs={{0,24},{8,0},{16,8},{24,16},{1,25},{9,1},{17,9},{25,17},{2,26},{10... | collective-permute-start | bytes 2433032 | tf_op jit(solution)/shard_map/ppermute | solution.py:702
  81.1 105.2 %collective-permute-start.19 = (bf16[528,768]{1,0:T(8,128)(2,1)}, bf16[528,768]{1,0:T(8,128)(2,1)S(1)}, u32[]{:S(2)}, u32[]{:S(2)}) collective-permute-start(bf16[528,768]{1,0:T(8,128)(2,1)} %collective-permute-done.18.refs_0_), channel_id=1, source_target_pairs={{0,2},{1,3},{2,0},{3,1},{4,6},{5,7},{6,4},{7,5},{8,10},{9,11},{10,... | collective-permute-start | bytes 2433032 | tf_op jit(solution)/shard_map/ppermute | solution.py:696
  81.4 105.2 %collective-permute-start.20 = (bf16[528,768]{1,0:T(8,128)(2,1)}, bf16[528,768]{1,0:T(8,128)(2,1)S(1)}, u32[]{:S(2)}, u32[]{:S(2)}) collective-permute-start(bf16[528,768]{1,0:T(8,128)(2,1)} %collective-permute-done.18.refs_0_), channel_id=1, source_target_pairs={{0,4},{4,0},{1,5},{5,1},{2,6},{6,2},{3,7},{7,3},{8,12},{12,8},{9,1... | collective-permute-start | bytes 2433032 | tf_op jit(solution)/shard_map/ppermute | solution.py:699
  107.2 128.8 %collective-permute-start.25 = (bf16[528,768]{1,0:T(8,128)(2,1)}, bf16[528,768]{1,0:T(8,128)(2,1)S(1)}, u32[]{:S(2)}, u32[]{:S(2)}) collective-permute-start(bf16[528,768]{1,0:T(8,128)(2,1)} %collective-permute-done.24.refs_0_), channel_id=1, source_target_pairs={{0,2},{1,3},{2,0},{3,1},{4,6},{5,7},{6,4},{7,5},{8,10},{9,11},{10,... | collective-permute-start | bytes 2433032 | tf_op jit(solution)/shard_map/ppermute | solution.py:696
  114.2 17.9 %collective-permute-start.5 = (bf16[144,768]{1,0:T(8,128)(2,1)S(1)}, bf16[144,768]{1,0:T(8,128)(2,1)S(1)}, u32[]{:S(2)}, u32[]{:S(2)}) collective-permute-start(bf16[144,768]{1,0:T(8,128)(2,1)S(1)} %slice.108), channel_id=1, source_target_pairs={{0,2},{1,3},{2,0},{3,1},{4,6},{5,7},{6,4},{7,5},{8,10},{9,11},{10,... | collective-permute-start | bytes 663560 | tf_op jit(solution)/shard_map/ppermute | solution.py:696
  132.1 104.1 %collective-permute-start.26 = (bf16[528,768]{1,0:T(8,128)(2,1)}, bf16[528,768]{1,0:T(8,128)(2,1)S(1)}, u32[]{:S(2)}, u32[]{:S(2)}) collective-permute-start(bf16[528,768]{1,0:T(8,128)(2,1)} %collective-permute-done.24.refs_0_), channel_id=1, source_target_pairs={{0,4},{4,0},{1,5},{5,1},{2,6},{6,2},{3,7},{7,3},{8,12},{12,8},{9,1... | collective-permute-start | bytes 2433032 | tf_op jit(solution)/shard_map/ppermute | solution.py:699
  185.4 377.7 %collective-permute-start.11 = (bf16[4,272,768]{2,1,0:T(8,128)(2,1)}, bf16[4,272,768]{2,1,0:T(8,128)(2,1)}, u32[]{:S(2)}, u32[]{:S(2)}) collective-permute-start(bf16[4,272,768]{2,1,0:T(8,128)(2,1)} %assemble.5.rows0.extra0.refs_0_.refs_1_), channel_id=1, source_target_pairs={{0,1},{1,0},{2,3},{3,2},{4,5},{5,4},{6,7},{7,6},{8,9},{9,8},{10,11... | collective-permute-start | bytes 5013512 | tf_op jit(solution)/shard_map/ppermute | solution.py:693
  186.3 51.8 %collective-permute-start.31 = (bf16[528,768]{1,0:T(8,128)(2,1)}, bf16[528,768]{1,0:T(8,128)(2,1)S(1)}, u32[]{:S(2)}, u32[]{:S(2)}) collective-permute-start(bf16[528,768]{1,0:T(8,128)(2,1)} %copy-done.17), channel_id=1, source_target_pairs={{0,2},{1,3},{2,0},{3,1},{4,6},{5,7},{6,4},{7,5},{8,10},{9,11},{10,... | collective-permute-start | bytes 2433032 | tf_op jit(solution)/shard_map/ppermute | solution.py:696
  186.6 53.0 %collective-permute-start.32 = (bf16[528,768]{1,0:T(8,128)(2,1)}, bf16[528,768]{1,0:T(8,128)(2,1)S(1)}, u32[]{:S(2)}, u32[]{:S(2)}) collective-permute-start(bf16[528,768]{1,0:T(8,128)(2,1)} %copy-done.17), channel_id=1, source_target_pairs={{0,4},{4,0},{1,5},{5,1},{2,6},{6,2},{3,7},{7,3},{8,12},{12,8},{9,1... | collective-permute-start | bytes 2433032 | tf_op jit(solution)/shard_map/ppermute | solution.py:699
  236.1 327.1 %collective-permute-start.12 = (bf16[4,256,768]{2,1,0:T(8,128)(2,1)}, bf16[4,256,768]{2,1,0:T(8,128)(2,1)}, u32[]{:S(2)}, u32[]{:S(2)}) collective-permute-start(bf16[4,256,768]{2,1,0:T(8,128)(2,1)} %assemble.6.cots0.refs_4_.refs_2_), channel_id=1, source_target_pairs={{0,1},{1,0},{2,3},{3,2},{4,5},{5,4},{6,7},{7,6},{8,9},{9,8},{10,11... | collective-permute-start | bytes 4718600 | tf_op jit(solution)/shard_map/ppermute | solution.py:693
  236.2 21.9 %collective-permute-start.21 = (bf16[272,768]{1,0:T(8,128)(2,1)S(1)}, bf16[272,768]{1,0:T(8,128)(2,1)S(1)}, u32[]{:S(2)}, u32[]{:S(2)}) collective-permute-start(bf16[272,768]{1,0:T(8,128)(2,1)S(1)} %slice.114), channel_id=1, source_target_pairs={{0,2},{1,3},{2,0},{3,1},{4,6},{5,7},{6,4},{7,5},{8,10},{9,11},{10,... | collective-permute-start | bytes 1253384 | tf_op jit(solution)/shard_map/ppermute | solution.py:696
  238.1 12.0 %collective-permute-start.22 = (bf16[256,768]{1,0:T(8,128)(2,1)S(1)}, bf16[256,768]{1,0:T(8,128)(2,1)S(1)}, u32[]{:S(2)}, u32[]{:S(2)}) collective-permute-start(bf16[256,768]{1,0:T(8,128)(2,1)S(1)} %slice.115), channel_id=1, source_target_pairs={{0,4},{4,0},{1,5},{5,1},{2,6},{6,2},{3,7},{7,3},{8,12},{12,8},{9,1... | collective-permute-start | bytes 1179656 | tf_op jit(solution)/shard_map/ppermute | solution.py:699
  239.6 18.3 %collective-permute-start.28 = (bf16[256,768]{1,0:T(8,128)(2,1)S(1)}, bf16[256,768]{1,0:T(8,128)(2,1)S(1)}, u32[]{:S(2)}, u32[]{:S(2)}) collective-permute-start(bf16[256,768]{1,0:T(8,128)(2,1)S(1)} %slice.119), channel_id=1, source_target_pairs={{0,4},{4,0},{1,5},{5,1},{2,6},{6,2},{3,7},{7,3},{8,12},{12,8},{9,1... | collective-permute-start | bytes 1179656 | tf_op jit(solution)/shard_map/ppermute | solution.py:699
  250.2 112.0 %collective-permute-start.27 = (bf16[272,768]{1,0:T(8,128)(2,1)}, bf16[272,768]{1,0:T(8,128)(2,1)S(1)}, u32[]{:S(2)}, u32[]{:S(2)}) collective-permute-start(bf16[272,768]{1,0:T(8,128)(2,1)} %slice.118), channel_id=1, source_target_pairs={{0,2},{1,3},{2,0},{3,1},{4,6},{5,7},{6,4},{7,5},{8,10},{9,11},{10,... | collective-permute-start | bytes 1253384 | tf_op jit(solution)/shard_map/ppermute | solution.py:696
  257.9 204.5 %collective-permute-start.33 = (bf16[272,768]{1,0:T(8,128)(2,1)}, bf16[272,768]{1,0:T(8,128)(2,1)S(1)}, u32[]{:S(2)}, u32[]{:S(2)}) collective-permute-start(bf16[272,768]{1,0:T(8,128)(2,1)} %slice.122), channel_id=1, source_target_pairs={{0,2},{1,3},{2,0},{3,1},{4,6},{5,7},{6,4},{7,5},{8,10},{9,11},{10,... | collective-permute-start | bytes 1253384 | tf_op jit(solution)/shard_map/ppermute | solution.py:696
  258.6 203.7 %collective-permute-start.34 = (bf16[256,768]{1,0:T(8,128)(2,1)}, bf16[256,768]{1,0:T(8,128)(2,1)}, u32[]{:S(2)}, u32[]{:S(2)}) collective-permute-start(bf16[256,768]{1,0:T(8,128)(2,1)} %slice.123), channel_id=1, source_target_pairs={{0,4},{4,0},{1,5},{5,1},{2,6},{6,2},{3,7},{7,3},{8,12},{12,8},{9,1... | collective-permute-start | bytes 1179656 | tf_op jit(solution)/shard_map/ppermute | solution.py:699
  362.1 244.9 %collective-permute-start.23 = (bf16[4,528,768]{2,1,0:T(8,128)(2,1)}, bf16[4,528,768]{2,1,0:T(8,128)(2,1)}, u32[]{:S(2)}, u32[]{:S(2)}) collective-permute-start(bf16[4,528,768]{2,1,0:T(8,128)(2,1)} %assemble.7.refs_2_.refs_6_.refs_0_.refs_1_), channel_id=1, source_target_pairs={{0,1},{1,0},{2,3},{3,2},{4,5},{5,4},{6,7},{7,6},{8,9},{9,8},{10,11... | collective-permute-start | bytes 9732104 | tf_op jit(solution)/shard_map/ppermute | solution.py:693
  462.3 191.5 %collective-permute-start.29 = (bf16[4,528,768]{2,1,0:T(8,128)(2,1)}, bf16[4,528,768]{2,1,0:T(8,128)(2,1)}, u32[]{:S(2)}, u32[]{:S(2)}) collective-permute-start(bf16[4,528,768]{2,1,0:T(8,128)(2,1)} %assemble.8.refs_0_.refs_4_.refs_1_.refs_2_), channel_id=1, source_target_pairs={{0,1},{1,0},{2,3},{3,2},{4,5},{5,4},{6,7},{7,6},{8,9},{9,8},{10,11... | collective-permute-start | bytes 9732104 | tf_op jit(solution)/shard_map/ppermute | solution.py:693
  562.6 98.9 %collective-permute-start.35 = (bf16[4,528,768]{2,1,0:T(8,128)(2,1)}, bf16[4,528,768]{2,1,0:T(8,128)(2,1)}, u32[]{:S(2)}, u32[]{:S(2)}) collective-permute-start(bf16[4,528,768]{2,1,0:T(8,128)(2,1)} %assemble.9.refs_2_.refs_6_.refs_0_.refs_1_), channel_id=1, source_target_pairs={{0,1},{1,0},{2,3},{3,2},{4,5},{5,4},{6,7},{7,6},{8,9},{9,8},{10,11... | collective-permute-start | bytes 9732104 | tf_op jit(solution)/shard_map/ppermute | solution.py:693
  596.4 48.4 %collective-permute-start.13 = (bf16[4,528,768]{2,1,0:T(8,128)(2,1)}, bf16[4,528,768]{2,1,0:T(8,128)(2,1)S(1)}, u32[]{:S(2)}, u32[]{:S(2)}) collective-permute-start(bf16[4,528,768]{2,1,0:T(8,128)(2,1)} %get-tuple-element.61), channel_id=1, source_target_pairs={{0,1},{1,0},{2,3},{3,2},{4,5},{5,4},{6,7},{7,6},{8,9},{9,8},{10,11... | collective-permute-start | bytes 9732104 | tf_op jit(solution)/shard_map/ppermute | solution.py:693
  651.8 20.1 %collective-permute-start.14 = (bf16[2,256,768]{2,1,0:T(8,128)(2,1)}, bf16[2,256,768]{2,1,0:T(8,128)(2,1)S(1)}, u32[]{:S(2)}, u32[]{:S(2)}) collective-permute-start(bf16[2,256,768]{2,1,0:T(8,128)(2,1)} %get-tuple-element.64), channel_id=1, source_target_pairs={{0,2},{1,3},{2,0},{3,1},{4,6},{5,7},{6,4},{7,5},{8,10},{9,11},{10,... | collective-permute-start | bytes 2359304 | tf_op jit(solution)/shard_map/ppermute | solution.py:696
  653.2 20.9 %collective-permute-start.15 = (bf16[2,272,768]{2,1,0:T(8,128)(2,1)}, bf16[2,272,768]{2,1,0:T(8,128)(2,1)S(1)}, u32[]{:S(2)}, u32[]{:S(2)}) collective-permute-start(bf16[2,272,768]{2,1,0:T(8,128)(2,1)} %get-tuple-element.65), channel_id=1, source_target_pairs={{0,4},{4,0},{1,5},{5,1},{2,6},{6,2},{3,7},{7,3},{8,12},{12,8},{9,1... | collective-permute-start | bytes 2506760 | tf_op jit(solution)/shard_map/ppermute | solution.py:699
  678.8 33.6 %collective-permute-start.16 = (bf16[256,768]{1,0:T(8,128)(2,1)}, bf16[256,768]{1,0:T(8,128)(2,1)S(1)}, u32[]{:S(2)}, u32[]{:S(2)}) collective-permute-start(bf16[256,768]{1,0:T(8,128)(2,1)} %get-tuple-element.67), channel_id=1, source_target_pairs={{0,4},{4,0},{1,5},{5,1},{2,6},{6,2},{3,7},{7,3},{8,12},{12,8},{9,1... | collective-permute-start | bytes 1179656 | tf_op jit(solution)/shard_map/ppermute | solution.py:699
  679.5 32.9 %collective-permute-start.17 = (bf16[272,768]{1,0:T(8,128)(2,1)}, bf16[272,768]{1,0:T(8,128)(2,1)S(1)}, u32[]{:S(2)}, u32[]{:S(2)}) collective-permute-start(bf16[272,768]{1,0:T(8,128)(2,1)} %get-tuple-element.69), channel_id=1, source_target_pairs={{0,2},{1,3},{2,0},{3,1},{4,6},{5,7},{6,4},{7,5},{8,10},{9,11},{10,... | collective-permute-start | bytes 1253384 | tf_op jit(solution)/shard_map/ppermute | solution.py:696
  729.4 27.4 %collective-permute-start.43 = (bf16[2,768,768]{2,1,0:T(8,128)(2,1)}, bf16[2,768,768]{2,1,0:T(8,128)(2,1)S(1)}, u32[]{:S(2)}, u32[]{:S(2)}) collective-permute-start(bf16[2,768,768]{2,1,0:T(8,128)(2,1)} %get-tuple-element.79), channel_id=1, source_target_pairs={{0,1},{1,0},{2,3},{3,2},{4,5},{5,4},{6,7},{7,6},{8,9},{9,8},{10,11... | collective-permute-start | bytes 7077896 | tf_op jit(solution)/shard_map/ppermute | solution.py:693
  762.6 61.6 %collective-permute-start.44 = (bf16[384,768]{1,0:T(8,128)(2,1)}, bf16[384,768]{1,0:T(8,128)(2,1)S(1)}, u32[]{:S(2)}, u32[]{:S(2)}) collective-permute-start(bf16[384,768]{1,0:T(8,128)(2,1)} %get-tuple-element.82), channel_id=1, source_target_pairs={{0,2},{1,3},{2,0},{3,1},{4,6},{5,7},{6,4},{7,5},{8,10},{9,11},{10,... | collective-permute-start | bytes 1769480 | tf_op jit(solution)/shard_map/ppermute | solution.py:696
  763.9 60.3 %collective-permute-start.45 = (bf16[2,192,768]{2,1,0:T(8,128)(2,1)}, bf16[2,192,768]{2,1,0:T(8,128)(2,1)S(1)}, u32[]{:S(2)}, u32[]{:S(2)}) collective-permute-start(bf16[2,192,768]{2,1,0:T(8,128)(2,1)} %get-tuple-element.83), channel_id=1, source_target_pairs={{0,4},{4,0},{1,5},{5,1},{2,6},{6,2},{3,7},{7,3},{8,12},{12,8},{9,1... | collective-permute-start | bytes 1769480 | tf_op jit(solution)/shard_map/ppermute | solution.py:699
  794.0 19.9 %collective-permute-start.38 = (f32[16,768]{1,0:T(8,128)S(1)}, f32[16,768]{1,0:T(8,128)S(1)}, u32[]{:S(2)}, u32[]{:S(2)}) collective-permute-start(f32[16,768]{1,0:T(8,128)S(1)} %copy-done.39), channel_id=1, source_target_pairs={{0,24},{8,0},{16,8},{24,16},{1,25},{9,1},{17,9},{25,17},{2,26},{10... | collective-permute-start | bytes 147464 | tf_op jit(solution)/shard_map/ppermute | solution.py:702
  819.3 12.0 %collective-permute-start.39 = (f32[4,16,768]{2,1,0:T(8,128)S(1)}, f32[4,16,768]{2,1,0:T(8,128)S(1)}, u32[]{:S(2)}, u32[]{:S(2)}) collective-permute-start(f32[4,16,768]{2,1,0:T(8,128)S(1)} %get-tuple-element.114), channel_id=1, source_target_pairs={{0,2},{1,3},{2,0},{3,1},{4,6},{5,7},{6,4},{7,5},{8,10},{9,11},{10,... | collective-permute-start | bytes 589832 | tf_op jit(solution)/shard_map/ppermute | solution.py:696
  823.5 7.9 collective-permute-start.41
  831.5 40.8 %collective-permute-start.42 = (f32[4,4,16,768]{3,2,1,0:T(8,128)S(1)}, f32[4,4,16,768]{3,2,1,0:T(8,128)S(1)}, u32[]{:S(2)}, u32[]{:S(2)}) collective-permute-start(f32[4,4,16,768]{3,2,1,0:T(8,128)S(1)} %get-tuple-element.109), channel_id=1, source_target_pairs={{0,1},{1,0},{2,3},{3,2},{4,5},{5,4},{6,7},{7,6},{8,9},{9,8},{10,11... | collective-permute-start | bytes 2359304 | tf_op jit(solution)/shard_map/ppermute | solution.py:693
  841.4 10.9 %collective-permute-start.49 = (bf16[96,768]{1,0:T(8,128)(2,1)S(1)}, bf16[96,768]{1,0:T(8,128)(2,1)S(1)}, u32[]{:S(2)}, u32[]{:S(2)}) collective-permute-start(bf16[96,768]{1,0:T(8,128)(2,1)S(1)} %get-tuple-element.111), channel_id=1, source_target_pairs={{0,16},{8,24},{16,0},{24,8},{1,17},{9,25},{17,1},{25,9},{2,18},{10... | collective-permute-start | bytes 442376 | tf_op jit(solution)/shard_map/ppermute | solution.py:702
  843.8 8.6 collective-permute-start.50
  854.9 9.8 %collective-permute-start.51 = (bf16[96,768]{1,0:T(8,128)(2,1)}, bf16[96,768]{1,0:T(8,128)(2,1)S(1)}, u32[]{:S(2)}, u32[]{:S(2)}) collective-permute-start(bf16[96,768]{1,0:T(8,128)(2,1)} %dense_fourth.1.own), channel_id=1, source_target_pairs={{0,8},{8,16},{16,24},{24,0},{1,9},{9,17},{17,25},{25,1},{2,10},{10... | collective-permute-start | bytes 442376 | tf_op jit(solution)/shard_map/ppermute | solution.py:702
  857.6 10.7 %collective-permute-start.52 = (bf16[96,768]{1,0:T(8,128)(2,1)}, bf16[96,768]{1,0:T(8,128)(2,1)S(1)}, u32[]{:S(2)}, u32[]{:S(2)}) collective-permute-start(bf16[96,768]{1,0:T(8,128)(2,1)} %dense_fourth.1.own), channel_id=1, source_target_pairs={{0,16},{8,24},{16,0},{24,8},{1,17},{9,25},{17,1},{25,9},{2,18},{10... | collective-permute-start | bytes 442376 | tf_op jit(solution)/shard_map/ppermute | solution.py:702
  860.2 8.1 collective-permute-start.53
  871.6 15.2 %collective-permute-start.54 = (bf16[384,768]{1,0:T(8,128)(2,1)}, bf16[384,768]{1,0:T(8,128)(2,1)S(1)}, u32[]{:S(2)}, u32[]{:S(2)}) collective-permute-start(bf16[384,768]{1,0:T(8,128)(2,1)} %dense_fifth.1.own), channel_id=1, source_target_pairs={{0,4},{4,0},{1,5},{5,1},{2,6},{6,2},{3,7},{7,3},{8,12},{12,8},{9,1... | collective-permute-start | bytes 1769480 | tf_op jit(solution)/shard_map/ppermute | solution.py:699
  (55 other events, 1165.4 us)

commit v3 on v2

--- a/solution.py
+++ b/solution.py
@@ -17,6 +17,7 @@
 EPSILON = 1e-06
 HALF = 4
 FULL_LIMIT = 32 * 1024 * 1024
+VMEM_LIMIT = 58 * 1024 * 1024
 
 f32 = jnp.float32
 bf16 = jnp.bfloat16
@@ -24,7 +25,6 @@
 NT = (((1,), (1,)), ((), ()))
 TN = (((0,), (0,)), ((), ()))
 TT = (((0,), (1,)), ((), ()))
-VMEM_LIMIT = 58 * 1024 * 1024
 
 
 def mm(left, right, dims):
@@ -62,12 +62,39 @@
     return value, half + value * (1.0 - tanh) * (const + 3.0 * 0.044715 * const * square)
 
 
-def params():
-    return pltpu.CompilerParams(vmem_limit_bytes=VMEM_LIMIT)
-
-
-def cost(flops, moved):
-    return pl.CostEstimate(flops=int(flops), bytes_accessed=int(moved), transcendentals=0)
+def launch(
+    kernel, name, outs, operands, *, in_specs=None, out_specs=None, grid=(), scalars=(), scratch=(), aliases=None,
+    after=(), flops=0, moved=0,
+):
+    lead = len(scalars)
+    count = lead + len(operands)
+    waits = len(after)
+    on_chip = pl.BlockSpec(memory_space=pltpu.VMEM)
+    anywhere = pl.BlockSpec(memory_space=pl.ANY)
+    in_specs = list(in_specs or [on_chip] * len(operands)) + [anywhere] * waits
+    out_specs = tuple(out_specs or [on_chip] * len(outs))
+
+    def body(*refs):
+        kernel(*refs[:count], *refs[count + waits :])
+
+    if scalars and grid:
+        shape = dict(
+            grid_spec=pltpu.PrefetchScalarGridSpec(
+                num_scalar_prefetch=lead, grid=grid, in_specs=in_specs, out_specs=out_specs, scratch_shapes=scratch
+            )
+        )
+    else:
+        in_specs = [pl.BlockSpec(memory_space=pltpu.SMEM)] * lead + in_specs
+        shape = dict(grid=grid, in_specs=in_specs, out_specs=out_specs, scratch_shapes=scratch)
+    return pl.pallas_call(
+        body,
+        out_shape=tuple(jax.ShapeDtypeStruct(*out) for out in outs),
+        input_output_aliases=aliases or {},
+        compiler_params=pltpu.CompilerParams(vmem_limit_bytes=VMEM_LIMIT),
+        cost_estimate=pl.CostEstimate(flops=int(flops), bytes_accessed=int(moved), transcendentals=0),
+        name=name,
+        **shape,
+    )(*scalars, *operands, *after)
 
 
 def copy_kernel(plan, count, *refs):
@@ -83,34 +110,24 @@
 
 
 def assemble(shape, dtype, sources, plan, after=()):
-    anywhere = pl.BlockSpec(memory_space=pl.ANY)
-    operands = (*sources, *after)
-    return pl.pallas_call(
-        functools.partial(copy_kernel, plan, len(sources)),
-        in_specs=[anywhere] * len(operands),
-        out_specs=anywhere,
-        out_shape=jax.ShapeDtypeStruct(shape, dtype),
-        scratch_shapes=[pltpu.SemaphoreType.DMA((len(plan),))],
-        compiler_params=params(),
-        cost_estimate=cost(0, 2 * math.prod(shape) * jnp.dtype(dtype).itemsize),
-        name="assemble",
-    )(*operands)
-
-
-def cotangent_kernel(mod_ref, cot_ref, after_ref, out_ref):
-    out_ref[...] = (mod_ref[5:6] * cot_ref[...].astype(f32)).astype(bf16)
-
-
-def moe_cotangent(mod, cotangent, after):
-    vmem = pl.BlockSpec(memory_space=pltpu.VMEM)
-    return pl.pallas_call(
-        cotangent_kernel,
-        in_specs=[vmem, vmem, pl.BlockSpec(memory_space=pl.ANY)],
-        out_specs=vmem,
-        out_shape=jax.ShapeDtypeStruct(cotangent.shape, bf16),
-        compiler_params=params(),
-        name="moe_cotangent",
-    )(mod, cotangent, after)
+    size = math.prod(shape) * jnp.dtype(dtype).itemsize
+    return launch(
+        functools.partial(copy_kernel, plan, len(sources)), "assemble", [(shape, dtype)], sources,
+        in_specs=[pl.BlockSpec(memory_space=pl.ANY)] * len(sources),
+        scratch=[pltpu.SemaphoreType.DMA((len(plan),))], after=after, moved=2 * size,
+    )[0]
+
+
+def order_kernel(*refs):
+    pass
+
+
+def ordered(values, after):
+    anywhere = [pl.BlockSpec(memory_space=pl.ANY)] * len(values)
+    return launch(
+        order_kernel, "ordered", [(value.shape, value.dtype) for value in values], values, in_specs=anywhere,
+        out_specs=anywhere, aliases={index: index for index in range(len(values))}, after=after,
+    )
 
 
 def pair_masks(rows):
@@ -131,8 +148,8 @@
 
 
 def attention_kernel(
-    local_width, tok_ref, mod_ref, cond_ref, router_ref, pairs_ref, cot_ref, w0, w1, w2, w3,
-    attn_in_ref, qkv_ref, context_ref, attn_out_ref, ext_ref, both_ref,
+    local_width, tok_ref, mod_ref, router_ref, pairs_ref, w0, w1, w2, w3,
+    attn_in_ref, qkv_ref, context_ref, attn_out_ref, ext_ref,
 ):
     shards = (w0, w1, w2, w3)
     rows, width = tok_ref.shape
@@ -174,34 +191,27 @@
         jnp.concatenate([values[0:1], values[1:2], values[2:3]], axis=1),
         jnp.concatenate([values[3:4], high[0], high[1]], axis=1),
         jnp.concatenate([rest[0], rest[1], jnp.zeros_like(rest[0])], axis=1),
-        cond_ref[...],
     )
     row_id = lax.broadcasted_iota(jnp.int32, (EXTRA, width), 0)
     extra = jnp.zeros((EXTRA, width), f32)
     for index, line in enumerate(packed):
         extra = jnp.where(row_id == index, line, extra)
     ext_ref[rows : rows + EXTRA, :] = extra.astype(bf16)
-    both_ref[0:rows, :] = cot_ref[...]
-    both_ref[rows : 2 * rows, :] = moe_in
-    both_ref[2 * rows :, :] = extra.astype(bf16)
-
-
-def attention_forward(tokens, mod, cond, router_t, pairs, cot, shards, local_width):
+
+
+def attention_forward(tokens, mod, router_t, pairs, shards, local_width):
     rows, width = tokens.shape
-    return pl.pallas_call(
-        functools.partial(attention_kernel, local_width),
-        out_shape=(
-            jax.ShapeDtypeStruct((rows, width), bf16),
-            jax.ShapeDtypeStruct((3, rows, width), bf16),
-            jax.ShapeDtypeStruct((rows, width), bf16),
-            jax.ShapeDtypeStruct((rows, width), f32),
-            jax.ShapeDtypeStruct((rows + EXTRA, width), bf16),
-            jax.ShapeDtypeStruct((2 * rows + EXTRA, width), bf16),
-        ),
-        compiler_params=params(),
-        cost_estimate=cost(5 * 10**9, 9 * 10**6),
-        name="attention_forward",
-    )(tokens, mod, cond, router_t, pairs, cot, *shards)
+    outs = [
+        ((rows, width), bf16),
+        ((3, rows, width), bf16),
+        ((rows, width), bf16),
+        ((rows, width), f32),
+        ((rows + EXTRA, width), bf16),
+    ]
+    return launch(
+        functools.partial(attention_kernel, local_width), "attention_forward", outs,
+        [tokens, mod, router_t, pairs, *shards], flops=5 * 10**9, moved=9 * 10**6,
+    )
 
 
 def read_pairs(extra):
@@ -238,18 +248,14 @@
     def apart(cls, ext, cots):
         return cls(ext, 0, PATCHES // EXTRA, cots, 0)
 
-    @classmethod
-    def joined(cls, both):
-        return cls(both, 1, 2 * PATCHES // EXTRA, both, 0)
-
     def operands(self):
         return [self.rows, self.rows, self.cots]
 
-    def specs(self):
+    def specs(self, taken=HALF):
         width = self.rows.shape[2]
         places = ((PATCHES, self.rows_at), (EXTRA, self.extra_at), (PATCHES, self.cots_at))
         return [
-            pl.BlockSpec((HALF, count, width), lambda *_, at=at: (0, at, 0)) for count, at in places
+            pl.BlockSpec((taken, count, width), lambda *_, at=at: (0, at, 0)) for count, at in places
         ]
 
     def extra(self):
@@ -266,34 +272,59 @@
         @pl.when(pl.program_id(0) == part)
         def _():
             for block in range(HALF):
-                routes, places, gates = read_pairs(extra_in[block])
-                hits = slot_hits(routes, places, base, members * CAP)
-                hot = (hits[0] | hits[1]).astype(bf16)
-                picked = mm(hot, rows_in[block], NN).astype(bf16)
-                scaled = (mm(hot, cots_in[block], NN) * slot_gates(hits, gates)).astype(bf16)
-                for member in range(members):
-                    span = slice(member * CAP, (member + 1) * CAP)
-                    rows_ref[member, block * CAP : (block + 1) * CAP, :] = picked[span]
-                    cots_ref[member, block * CAP : (block + 1) * CAP, :] = scaled[span]
-
-
-def dispatch(base, blocks, members):
+                dispatch_block(
+                    base, members, rows_in[block], extra_in[block], cots_in[block], rows_ref, cots_ref, block
+                )
+
+
+def dispatch_block(base, members, rows, extra, cots, rows_ref, cots_ref, block):
+    routes, places, gates = read_pairs(extra)
+    hits = slot_hits(routes, places, base, members * CAP)
+    hot = (hits[0] | hits[1]).astype(bf16)
+    picked = mm(hot, rows, NN).astype(bf16)
+    scaled = (mm(hot, cots, NN) * slot_gates(hits, gates)).astype(bf16)
+    for member in range(members):
+        span = slice(member * CAP, (member + 1) * CAP)
+        rows_ref[member, block * CAP : (block + 1) * CAP, :] = picked[span]
+        cots_ref[member, block * CAP : (block + 1) * CAP, :] = scaled[span]
+
+
+def hops_kernel(place_ref, ext, cots, rows_ref, cots_ref):
+    base = place_ref[0].astype(f32)
+    for block in range(ext.shape[1]):
+        dispatch_block(
+            base, rows_ref.shape[0], ext[0, block, :PATCHES], ext[0, block, PATCHES:], cots[0, block], rows_ref,
+            cots_ref, block,
+        )
+
+
+def plane_of(hop, place, planes):
+    return lax.rem(place[2] + hop + 1, planes)
+
+
+def dispatch_hops(place, ext, cots, members, after=()):
+    planes, blocks, rows, width = ext.shape
+    out = ((members, (planes - 1) * blocks * CAP, width), bf16)
+    out_spec = pl.BlockSpec((members, blocks * CAP, width), lambda h, p: (0, h, 0))
+    specs = [
+        pl.BlockSpec((1, blocks, count, width), lambda h, p: (plane_of(h, p, planes), 0, 0, 0))
+        for count in (rows, PATCHES)
+    ]
+    return launch(
+        hops_kernel, "dispatch_hops", [out, out], [ext, cots], in_specs=specs, out_specs=[out_spec, out_spec],
+        grid=(planes - 1,), scalars=[place], after=after, flops=24 * 10**9, moved=48 * 10**6,
+    )
+
+
+def dispatch(base, blocks, members, after=()):
     width = blocks[0].rows.shape[2]
-    out = jax.ShapeDtypeStruct((members, 2 * HALF * CAP, width), bf16)
-    out_spec = pl.BlockSpec((members, HALF * CAP, width), lambda c, b: (0, c, 0))
-    return pl.pallas_call(
-        dispatch_kernel,
-        grid_spec=pltpu.PrefetchScalarGridSpec(
-            num_scalar_prefetch=1,
-            grid=(2,),
-            in_specs=[spec for part in blocks for spec in part.specs()],
-            out_specs=(out_spec, out_spec),
-        ),
-        out_shape=(out, out),
-        compiler_params=params(),
-        cost_estimate=cost(8 * 10**9, 16 * 10**6),
-        name="dispatch",
-    )(base, *[operand for part in blocks for operand in part.operands()])
+    out = ((members, 2 * HALF * CAP, width), bf16)
+    out_spec = pl.BlockSpec((members, HALF * CAP, width), lambda c, *_: (0, c, 0))
+    return launch(
+        dispatch_kernel, "dispatch", [out, out], [operand for part in blocks for operand in part.operands()],
+        in_specs=[spec for part in blocks for spec in part.specs()], out_specs=[out_spec, out_spec],
+        grid=(2,), scalars=[base], after=after, flops=8 * 10**9, moved=16 * 10**6,
+    )
 
 
 def expert_kernel(
@@ -375,45 +406,40 @@
                 out_ref[place, index * PATCHES : (index + 1) * PATCHES, :] = total.astype(bf16)
 
 
-def experts_both(base, blocks, shared_up, shared_down, expert_up, expert_down, shared_ids):
+def experts_both(base, blocks, shared_up, shared_down, expert_up, expert_down, shared_ids, after=()):
     members, width, hidden = expert_up.shape
-    out = jax.ShapeDtypeStruct((HALF, 2 * PATCHES + EXTRA, width), bf16)
-    out_spec = pl.BlockSpec(out.shape, lambda e, b: (0, 0, 0))
-    return pl.pallas_call(
-        functools.partial(expert_kernel, shared_ids),
-        grid_spec=pltpu.PrefetchScalarGridSpec(
-            num_scalar_prefetch=1,
-            grid=(members + 1,),
-            in_specs=[spec for part in blocks for spec in part.specs()]
-            + [
-                pl.BlockSpec((width, hidden), lambda e, b: (0, 0)),
-                pl.BlockSpec((hidden, width), lambda e, b: (0, 0)),
-                pl.BlockSpec((1, width, hidden), lambda e, b: (jnp.maximum(e - 1, 0), 0, 0)),
-                pl.BlockSpec((1, hidden, width), lambda e, b: (jnp.maximum(e - 1, 0), 0, 0)),
-            ],
-            out_specs=(out_spec, out_spec),
-            scratch_shapes=[
-                pltpu.VMEM((members, 2 * HALF * CAP, width), bf16),
-                pltpu.VMEM((members, 2 * HALF * CAP, width), bf16),
-                pltpu.VMEM((members, 2 * HALF * CAP, 1), f32),
-                pltpu.VMEM((members, 2 * HALF * CAP, 1), f32),
-                pltpu.VMEM((max(len(shared_ids), 1), PATCHES, 2 * width), f32),
-            ],
-        ),
-        out_shape=(out, out),
-        compiler_params=params(),
-        cost_estimate=cost(30 * 10**9, 30 * 10**6),
-        name="experts_both",
-    )(
-        base, *[operand for part in blocks for operand in part.operands()],
-        shared_up, shared_down, expert_up, expert_down,
-    )
-
-
-def grads_kernel(count, tile, started, *refs):
+    shape = (HALF, 2 * PATCHES + EXTRA, width)
+    out_spec = pl.BlockSpec(shape, lambda e, b: (0, 0, 0))
+    slots = (members, 2 * HALF * CAP)
+    return launch(
+        functools.partial(expert_kernel, shared_ids), "experts_both", [(shape, bf16)] * 2,
+        [operand for part in blocks for operand in part.operands()]
+        + [shared_up, shared_down, expert_up, expert_down],
+        in_specs=[spec for part in blocks for spec in part.specs()]
+        + [
+            pl.BlockSpec((width, hidden), lambda e, b: (0, 0)),
+            pl.BlockSpec((hidden, width), lambda e, b: (0, 0)),
+            pl.BlockSpec((1, width, hidden), lambda e, b: (jnp.maximum(e - 1, 0), 0, 0)),
+            pl.BlockSpec((1, hidden, width), lambda e, b: (jnp.maximum(e - 1, 0), 0, 0)),
+        ],
+        out_specs=[out_spec, out_spec],
+        grid=(members + 1,),
+        scalars=[base],
+        after=after,
+        scratch=[
+            pltpu.VMEM((*slots, width), bf16),
+            pltpu.VMEM((*slots, width), bf16),
+            pltpu.VMEM((*slots, 1), f32),
+            pltpu.VMEM((*slots, 1), f32),
+            pltpu.VMEM((max(len(shared_ids), 1), PATCHES, 2 * width), f32),
+        ], flops=30 * 10**9, moved=30 * 10**6,
+    )
+
+
+def grads_kernel(count, tile, started, low, *refs):
     row_refs, cot_refs = refs[:count], refs[count : 2 * count]
     up_ref, down_ref = refs[2 * count : 2 * count + 2]
-    up_grad_ref, down_grad_ref = refs[-2:]
+    up_grad_ref, down_grad_ref = refs[-3:-1] if low else refs[-2:]
     width = up_ref.shape[1]
     inputs = [ref[...].reshape(-1, width) for ref in row_refs]
     cots = [ref[...].reshape(-1, width) for ref in cot_refs]
@@ -435,51 +461,73 @@
         else:
             up_grad_ref[0] += up_grad
             down_grad_ref[0] += down_grad
-
-
-def weight_grads(rows, cots, specs, up, down, before, tile, total):
+    if low:
+        refs[-1][0] = up_grad_ref[0].astype(bf16)
+        refs[-1][1] = down_grad_ref[0].astype(bf16)
+
+
+def weight_grads(rows, cots, specs, up, down, before, tile, total, low=False, after=(), scalars=(), span=None):
     members, width, hidden = up.shape
-    up_spec = pl.BlockSpec((1, width, hidden), lambda e: (e, 0, 0))
-    down_spec = pl.BlockSpec((1, hidden, width), lambda e: (e, 0, 0))
+    start, stop = span or (0, members)
+    up_spec = pl.BlockSpec((1, width, hidden), lambda e, *_: (e + start, 0, 0))
+    down_spec = pl.BlockSpec((1, hidden, width), lambda e, *_: (e + start, 0, 0))
     started = before is not None
     count = len(rows)
-    return pl.pallas_call(
-        functools.partial(grads_kernel, count, tile, started),
-        grid=(members,),
-        in_specs=specs + [up_spec, down_spec] + ([up_spec, down_spec] if started else []),
-        out_specs=(up_spec, down_spec),
-        out_shape=(
-            jax.ShapeDtypeStruct(up.shape, f32),
-            jax.ShapeDtypeStruct(down.shape, f32),
-        ),
-        input_output_aliases={2 * count + 2: 0, 2 * count + 3: 1} if started else {},
-        compiler_params=params(),
-        cost_estimate=cost(12 * total * width * hidden, total * width * 4),
-        name="weight_grads",
-    )(*rows, *cots, up, down, *(before or ()))
-
-
-def routed_grads(slots, up, down, before):
+    first = len(scalars) + 2 * count + 2
+    low_spec = [pl.BlockSpec((2, width, hidden), lambda *_: (0, 0, 0))] if low else []
+    kernel = functools.partial(grads_kernel, count, tile, started, low)
+    return launch(
+        (lambda place_ref, *refs: kernel(*refs)) if scalars else kernel, "weight_grads",
+        [(up.shape, f32), (down.shape, f32)] + ([((2, width, hidden), bf16)] if low else []),
+        [*rows, *cots, up, down, *(before or ())],
+        in_specs=specs + [up_spec, down_spec] * (2 if started else 1), out_specs=[up_spec, down_spec] + low_spec,
+        grid=(stop - start,), aliases={first: 0, first + 1: 1} if started else None, after=after, scalars=scalars,
+        flops=12 * total * width * hidden, moved=total * width * 4,
+    )
+
+
+def routed_grads(slots, up, down, before, after=(), span=None):
     members, count, width = slots[0][0].shape
-    spec = pl.BlockSpec((1, count, width), lambda e: (e, 0, 0))
+    start, stop = span or (0, members)
+    spec = pl.BlockSpec((1, count, width), lambda e: (e + start, 0, 0))
     rows, cots = [pair[0] for pair in slots], [pair[1] for pair in slots]
     specs = [spec] * (2 * len(slots))
+    each = len(slots) * count
     return weight_grads(
-        rows, cots, specs, up, down, before, len(slots) * count, len(slots) * members * count
-    )
-
-
-def shared_grads(blocks, up, down, before):
+        rows, cots, specs, up, down, before, each, (stop - start) * each, after=after, span=span
+    )
+
+
+def shared_grads(blocks, taken, up, down, before, after=()):
     rows, cots = [part.rows for part in blocks], [part.cots for part in blocks]
-    all_specs = [part.specs() for part in blocks]
+    all_specs = [part.specs(taken) for part in blocks]
     specs = [spec[0] for spec in all_specs] + [spec[2] for spec in all_specs]
+    total = len(blocks) * taken * PATCHES
+    tile = total if total <= 8 * PATCHES else total // 2
+    return weight_grads(rows, cots, specs, up[None], down[None], before, tile, total, after=after)
+
+
+def shared_grads_hops(place, ext, cots, up, down, before, after=()):
+    planes, blocks, _, width = ext.shape
+    taken = blocks // 2
+    specs = [
+        pl.BlockSpec((1, taken, PATCHES, width), lambda e, p, hop=hop: (plane_of(hop, p, planes), p[1], 0, 0))
+        for hop in range(planes - 1)
+    ]
+    total = (planes - 1) * taken * PATCHES
     return weight_grads(
-        rows, cots, specs, up[None], down[None], before, 2 * HALF * PATCHES, len(blocks) * HALF * PATCHES
-    )
+        [ext] * len(specs), [cots] * len(specs), specs * 2, up[None], down[None], before, taken * PATCHES, total, True,
+        after, [place],
+    )
+
+
+def shared_last_kernel(up, down, more, up_out, down_out):
+    up_out[...] = up[0] + more[0].astype(f32)
+    down_out[...] = down[0] + more[1].astype(f32)
 
 
 def backward_kernel(
-    local_width, moe_ref, moe_more_ref, back_ref, back_more_ref, tok_ref, cot_ref, mod_ref, router_ref, pairs_ref, attn_in_ref,
+    local_width, moe_ref, moe_more_ref, back_ref, back_more_ref, cond_ref, tok_ref, cot_ref, mod_ref, router_ref, pairs_ref, attn_in_ref,
     qkv_ref, context_ref, attn_out_ref, ext_ref, w0, w1, w2, w3,
     output_ref, tok_grad_ref, small_ref, near_ref, far_ref, grad_s,
 ):
@@ -554,6 +602,7 @@
     )
     lines = (
         shift_one_grad, scale_one_grad, gate_one_grad, shift_two_grad, scale_two_grad, gate_two_grad,
+        cond_ref[...],
     )
     row_id = lax.broadcasted_iota(jnp.int32, (8, width), 0)
     stacked = jnp.zeros((8, width), f32)
@@ -564,43 +613,20 @@
 
 
 def attention_backward(
-    moe, moe_more, back, back_more, tokens, cotangent, mod, router_t, pairs, attn_in, qkv, context, attn_out,
-    ext, shards, local_width,
+    moe, moe_more, back, back_more, cond, tokens, cotangent, mod, router_t, pairs, attn_in, qkv, context,
+    attn_out, ext, shards, local_width, after=(),
 ):
     rows, width = tokens.shape
-    halves = jax.ShapeDtypeStruct((len(shards) // 2, 4 * local_width, width), bf16)
-    return pl.pallas_call(
-        functools.partial(backward_kernel, local_width),
-        out_shape=(
-            jax.ShapeDtypeStruct((rows, width), bf16),
-            jax.ShapeDtypeStruct((rows, width), f32),
-            jax.ShapeDtypeStruct((16, width), f32),
-            halves,
-            halves,
-        ),
-        scratch_shapes=[pltpu.VMEM((3, rows, width), bf16)],
-        compiler_params=params(),
-        cost_estimate=cost(10 * 10**9, 16 * 10**6),
-        name="attention_backward",
-    )(
-        moe, moe_more, back, back_more, tokens, cotangent, mod, router_t, pairs, attn_in, qkv, context,
-        attn_out, ext, *shards,
-    )
-
-
-def local_call(kernel, name, outs, operands, scalars=None, moved=4 * 10**6):
-    count = 0 if scalars is None else 1
-    vmem = pl.BlockSpec(memory_space=pltpu.VMEM)
-    smem = pl.BlockSpec(memory_space=pltpu.SMEM)
-    return pl.pallas_call(
-        kernel,
-        in_specs=[smem] * count + [vmem] * len(operands),
-        out_specs=tuple(vmem for _ in outs),
-        out_shape=tuple(jax.ShapeDtypeStruct(*out) for out in outs),
-        compiler_params=params(),
-        cost_estimate=cost(0, moved),
-        name=name,
-    )(*([] if scalars is None else [scalars]), *operands)
+    halves = ((len(shards) // 2, 4 * local_width, width), bf16)
+    return launch(
+        functools.partial(backward_kernel, local_width), "attention_backward",
+        [((rows, width), bf16), ((rows, width), f32), ((16, width), f32), halves, halves],
+        [
+            moe, moe_more, back, back_more, cond, tokens, cotangent, mod, router_t, pairs, attn_in, qkv,
+            context, attn_out, ext, *shards,
+        ],
+        scratch=[pltpu.VMEM((3, rows, width), bf16)], after=after, flops=10 * 10**9, moved=16 * 10**6,
+    )
 
 
 def plane_first_kernel(first, more, side, other, keep_upper, keep_lower):
@@ -647,14 +673,15 @@
     side[...] = (keep_lower[1] + from_other[1].astype(f32)).astype(bf16)
 
 
-def dense_third_kernel(size, place, upper, lower, from_side, from_other, own, sent, total):
+def dense_third_kernel(size, place, upper, lower, from_side, from_other, own, *outs):
+    sent, total = outs[:-1], outs[-1]
     half = upper.shape[0]
     share = 2 * half // size
     total[0:half, :] = upper[...] + from_other[...].astype(f32)
     total[half:, :] = lower[...] + from_side[...].astype(f32)
     own[...] = total[span_of(place[1], share), :]
     for hop in range(1, size):
-        sent[hop - 1] = total[span_of(lax.rem(place[1] + hop, size), share), :].astype(bf16)
+        sent[hop - 1][...] = total[span_of(lax.rem(place[1] + hop, size), share), :].astype(bf16)
 
 
 def dense_fourth_kernel(own, *refs):
@@ -673,12 +700,15 @@
         out[span_of(lax.rem(place[1] + size - hop, size), share), :] = refs[hop - 1][...]
 
 
-def dense_last_kernel(place, own, more, out):
+def dense_last_kernel(place, own, more, qkv_out, out_out, total):
     half = own.shape[0] // 2
     for ref, who in ((own, place[0]), (more, 1 - place[0])):
         for index in range(2):
             rows = pl.ds(pl.multiple_of(2 * half * index + who * half, half), half)
-            out[rows, :] = ref[index * half : (index + 1) * half, :].astype(f32)
+            total[rows, :] = ref[index * half : (index + 1) * half, :].astype(f32)
+    count = qkv_out.shape[0]
+    qkv_out[...] = total[0:count, :]
+    out_out[...] = total[count:, :]
 
 
 class Links:
@@ -701,84 +731,69 @@
     def along(self, value, hop):
         return lax.ppermute(value, "dp", [(i, (i + hop) % self.dp) for i in range(self.dp)])
 
-    def plane(self, block, after=()):
-        rows, width = block.shape
-        cut = (rows // 2 + 15) // 16 * 16
-        side, other = self.to_side(block), self.to_other(block)
-        upper, lower = self.to_side(other[:cut]), self.to_other(side[cut:])
-        everything = slice(None)
-        plan = [(index, everything, index) for index in range(3)]
-        plan += [(3, everything, (3, pl.ds(0, cut))), (4, everything, (3, pl.ds(cut, rows - cut)))]
-        mine = assemble((HALF, rows, width), block.dtype, (block, side, other, upper, lower), plan, after)
-        return mine, self.to_core(mine)
-
-    def everywhere(self, small):
-        stack = jnp.stack([small] + [self.along(small, hop) for hop in range(1, self.dp)])
-        side, other = self.to_side(stack), self.to_other(stack)
-        chips = jnp.stack([stack, side, other, self.to_side(other)])
-        cores = jnp.stack([chips, self.to_core(chips)])
-        return cores.transpose((2, 0, 1) + tuple(range(3, cores.ndim)))
-
-    def plane_sum(self, first, second):
+    def plane_sum_first(self, first, more, after):
         width = first.shape[2]
         low = first.shape[1] - PATCHES
-        side, other, keep_upper, keep_lower = local_call(
-            plane_first_kernel,
-            "plane_first",
+        return launch(
+            plane_first_kernel, "plane_first",
             [((2, PATCHES, width), bf16), ((2, low, width), bf16), ((2, PATCHES, width), f32), ((2, low, width), f32)],
-            [first, self.to_core(second)],
-        )
-        upper, lower, upper_next, lower_next = local_call(
-            plane_second_kernel,
-            "plane_second",
+            [first, more], after=after, moved=10 * 10**6,
+        )
+
+    def plane_sum_second(self, keep_upper, keep_lower, side, other, after):
+        _, low, width = keep_lower.shape
+        return launch(
+            plane_second_kernel, "plane_second",
             [((PATCHES, width), f32), ((low, width), f32), ((PATCHES, width), bf16), ((low, width), bf16)],
-            [keep_upper, keep_lower, self.to_side(side), self.to_other(other)],
-        )
-        return upper, self.to_other(upper_next), lower, self.to_side(lower_next)
+            [keep_upper, keep_lower, side, other], after=after, moved=6 * 10**6,
+        )
 
     def dense_sum(self, near, far):
         _, rows, width = near.shape
         cut, half, share = rows // 2, rows // 4, rows // 2 // self.dp
-        place = jnp.stack([lax.axis_index("expert"), lax.axis_index("dp")]).astype(jnp.int32)
-        side, other, keep_upper, keep_lower = local_call(
-            dense_first_kernel,
-            "dense_first",
+        place = [jnp.stack([lax.axis_index("expert"), lax.axis_index("dp")]).astype(jnp.int32)]
+        more = self.to_core(far)
+        after = yield None
+        side, other, keep_upper, keep_lower = launch(
+            dense_first_kernel, "dense_first",
             [((cut, width), bf16), ((2, half, width), bf16), ((cut, width), f32), ((2, half, width), f32)],
-            [near, self.to_core(far)],
-            place,
-        )
-        side, other, upper, lower = local_call(
-            dense_second_kernel,
-            "dense_second",
+            [near, more], scalars=place, after=after, moved=8 * 10**6,
+        )
+        from_side, from_other = self.to_side(side), self.to_other(other)
+        after = yield keep_upper
+        side, other, upper, lower = launch(
+            dense_second_kernel, "dense_second",
             [((half, width), bf16), ((half, width), bf16), ((half, width), f32), ((half, width), f32)],
-            [keep_upper, keep_lower, self.to_side(side), self.to_other(other)],
-            place,
-        )
-        own, sent, _ = local_call(
-            functools.partial(dense_third_kernel, self.dp),
-            "dense_third",
-            [((share, width), f32), ((self.dp - 1, share, width), bf16), ((cut, width), f32)],
-            [upper, lower, self.to_side(side), self.to_other(other)],
-            place,
-        )
+            [keep_upper, keep_lower, from_side, from_other], scalars=place, after=after, moved=5 * 10**6,
+        )
+        from_side, from_other = self.to_side(side), self.to_other(other)
+        after = yield upper
         hops = range(1, self.dp)
-        (total,) = local_call(
-            dense_fourth_kernel,
-            "dense_fourth",
-            [((share, width), bf16)],
-            [own] + [self.along(sent[hop - 1], hop) for hop in hops],
-        )
-        (column,) = local_call(
-            functools.partial(dense_fifth_kernel, self.dp),
-            "dense_fifth",
-            [((cut, width), bf16)],
-            [total] + [self.along(total, hop) for hop in hops],
-            place,
-        )
-        (result,) = local_call(
-            dense_last_kernel, "dense_last", [((rows, width), f32)], [column, self.to_other(column)], place
-        )
-        return result
+        outs = launch(
+            functools.partial(dense_third_kernel, self.dp), "dense_third",
+            [((share, width), f32)] + [((share, width), bf16)] * len(hops),
+            [upper, lower, from_side, from_other], scalars=place, scratch=[pltpu.VMEM((cut, width), f32)],
+            after=after, moved=3 * 10**6,
+        )
+        moved = [self.along(outs[hop], hop) for hop in hops]
+        after = yield outs[0]
+        (total,) = launch(
+            dense_fourth_kernel, "dense_fourth", [((share, width), bf16)], [outs[0], *moved], after=after,
+            moved=10**6,
+        )
+        moved = [self.along(total, hop) for hop in hops]
+        after = yield total
+        (column,) = launch(
+            functools.partial(dense_fifth_kernel, self.dp), "dense_fifth", [((cut, width), bf16)], [total, *moved],
+            scalars=place, after=after, moved=10**6,
+        )
+        more = self.to_other(column)
+        after = yield column
+        yield launch(
+            dense_last_kernel, "dense_last", [((rows * 3 // 4, width), f32), ((rows // 4, width), f32)],
+            [column, more], scalars=place, scratch=[pltpu.VMEM((rows, width), f32)], after=after,
+            moved=4 * 10**6,
+        )
 
 
 def local(
@@ -807,30 +822,92 @@
     total_blocks = links.dp * links.expert * links.tensor
     full = links.paired and total_blocks * rows * width * 2 <= FULL_LIMIT
 
-    weight = jnp.concatenate(
-        [qkv_weight.transpose(1, 2, 0).reshape(3 * local_width, width), out_weight], axis=0
-    )
-    across = links.to_side(weight)
-    shards = (weight, links.to_core(weight), across, links.to_core(across))
-
     condition = jax.nn.silu(embedding(timesteps, width)).astype(bf16)
     mod_cols = jnp.einsum("id,dcf->icf", condition, ada_weight, preferred_element_type=f32) + ada_bias[None]
     mod = lax.all_to_all(mod_cols, "tensor", split_axis=0, concat_axis=2, tiled=True)[0]
     own_condition = lax.dynamic_slice_in_dim(condition.astype(f32), me, 1, axis=0)
-    shared_cot = moe_cotangent(mod, cotangent, across)
+    shared_cot = (mod[5][None] * cotangent.astype(f32)).astype(bf16)
+
+    weight = jnp.concatenate(
+        [qkv_weight.transpose(1, 2, 0).reshape(3 * local_width, width), out_weight], axis=0
+    )
+    across = links.to_side(weight)
+    near_shard = links.to_core(weight)
+    (across,) = ordered([across], [mod])
+    shards = (weight, near_shard, across, links.to_core(across))
     router_t = router_weight.T
     pairs = jnp.concatenate([routes.T, places.T], axis=0)
 
-    attn_in, qkv, context, attn_out, ext, both = attention_forward(
-        tokens, mod, own_condition, router_t, pairs, shared_cot, shards, local_width
+    attn_in, qkv, context, attn_out, ext = attention_forward(
+        tokens, mod, router_t, pairs, shards, local_width
     )
     feed = (shared_up, shared_down, expert_up, expert_down)
-    if links.paired:
-        cots = links.plane(shared_cot)
-        exts = links.plane(ext)
-        planes = [tuple(Blocks.apart(*pair) for pair in zip(exts, cots))]
-        first, second = experts_both(base, planes[0], *feed, (0, 1, 4, 5))
-        upper, upper_more, lower, lower_more = links.plane_sum(first, second)
+    backward = functools.partial(
+        attention_backward, cond=own_condition, tokens=tokens, cotangent=cotangent, mod=mod, router_t=router_t,
+        pairs=pairs, attn_in=attn_in, qkv=qkv, context=context, attn_out=attn_out, ext=ext, shards=shards,
+        local_width=local_width,
+    )
+    whole = slice(None)
+    if full:
+        place = jnp.stack([base[0], *(lax.axis_index(axis) for axis in ("expert", "dp"))]).astype(jnp.int32)
+        cots = lax.all_gather(shared_cot, everyone, axis=0)
+        cot_side, cot_other = links.to_side(shared_cot), links.to_other(shared_cot)
+        ext_side, ext_other = links.to_side(ext), links.to_other(ext)
+        everything = lax.all_gather(ext, everyone, axis=0)
+        cut = PATCHES // 2 + EXTRA
+        ext_corner = (links.to_side(ext_other[:cut]), links.to_other(ext_side[cut:]))
+        cot_corner = links.to_other(ordered([cot_side], [ext])[0])
+        cot_mine = assemble(
+            (HALF, PATCHES, width), bf16, [shared_cot, cot_side, cot_other, cot_corner],
+            [(index, whole, index) for index in range(HALF)], after=[ext_side],
+        )
+        cot_near = links.to_core(cot_mine)
+        ext_mine = assemble(
+            (HALF, PATCHES + EXTRA, width), bf16, [ext, ext_side, ext_other, *ext_corner],
+            [(index, whole, index) for index in range(3)]
+            + [(3, whole, (3, pl.ds(0, cut))), (4, whole, (3, pl.ds(cut, PATCHES // 2)))],
+        )
+        ext_near = links.to_core(ext_mine)
+        own = (Blocks.apart(ext_mine, cot_mine), Blocks.apart(ext_near, cot_near))
+        first, second = experts_both(base, own, *feed, (0, 1, 4, 5))
+        moved = links.to_core(second)
+        slots = dispatch(base, own, members, after=[first])
+        side, other, keep_upper, keep_lower = links.plane_sum_first(first, moved, after=[slots[0]])
+        from_side, from_other = links.to_side(side), links.to_other(other)
+        routed = routed_grads([slots], expert_up, expert_down, None, after=[side])
+        upper, lower, upper_next, lower_next = links.plane_sum_second(
+            keep_upper, keep_lower, from_side, from_other, after=[routed[0]]
+        )
+        upper_more, lower_more = links.to_other(upper_next), links.to_side(lower_next)
+        shared = shared_grads(own, 2, shared_up, shared_down, None, after=[upper])
+        output, tokens_grad, small, near, far = backward(
+            upper, upper_more, lower, lower_more, after=[shared[0]]
+        )
+        dense = links.dense_sum(near, far)
+        next(dense)
+        small_all = lax.all_gather(small, everyone, axis=0)
+        everything, cots = ordered([everything, cots], [small])
+        everything, cots = (
+            value.reshape(links.dp, links.expert * links.tensor, *value.shape[1:]) for value in (everything, cots)
+        )
+        slots = dispatch_hops(place, everything, cots, members)
+        step = dense.send([slots[0]])
+        *shared, sent = shared_grads_hops(place, everything, cots, shared_up, shared_down, shared, after=[step])
+        step = dense.send([sent])
+        middle = members // 2
+        routed = routed_grads([slots], expert_up, expert_down, routed, after=[step], span=(0, middle))
+        step = dense.send([routed[0]])
+        shared_more = links.to_other(ordered([sent], [step])[0])
+        routed = routed_grads([slots], expert_up, expert_down, routed, after=[step], span=(middle, members))
+        step = dense.send([routed[0]])
+        step = dense.send([step])
+        shared = launch(
+            shared_last_kernel, "shared_last", [(shared_up.shape, f32), (shared_down.shape, f32)],
+            [*shared, shared_more], after=[step], moved=12 * 10**6,
+        )
+        qkv_grad, out_grad = dense.send([shared[0]])
+        (small_all,) = ordered([small_all], [routed[0]])
+        routes_all = everything[:, :, PATCHES, : TOPK * PATCHES].reshape(-1, TOPK * PATCHES)
     else:
         shift = lax.axis_index("expert") * links.tensor
         gather = lambda block: jnp.roll(
@@ -846,40 +923,25 @@
         blocks = jnp.roll(jnp.concatenate(sums, axis=0), shift, axis=0)
         total = lax.psum_scatter(blocks, ("expert", "tensor"), scatter_dimension=0, tiled=True)[0]
         upper, lower = total[:PATCHES].astype(f32), total[PATCHES:].astype(f32)
-        upper_more, lower_more = jnp.zeros_like(total[:PATCHES]), jnp.zeros_like(total[PATCHES:])
-
-    output, tokens_grad, small, near, far = attention_backward(
-        upper, upper_more, lower, lower_more, tokens, cotangent, mod, router_t, pairs,
-        attn_in, qkv, context, attn_out, ext, shards, local_width,
-    )
-
-    if full:
-        hops = [links.plane(links.along(both, hop)) for hop in range(1, links.dp)]
-        planes += [tuple(Blocks.joined(part) for part in parts) for parts in hops]
-    slots = [dispatch(base, plane, members) for plane in planes]
-    routed, shared = None, None
-    for start in range(0, len(planes), 2):
-        routed = routed_grads(slots[start : start + 2], expert_up, expert_down, routed)
-        parts = [part for plane in planes[start : start + 2] for part in plane]
-        shared = shared_grads(parts, shared_up, shared_down, shared)
-
-    if full:
-        small_all = links.everywhere(small).reshape(-1, 16, width)
-        extra_all = jnp.concatenate([part.extra() for plane in planes for part in plane], axis=0)
-        condition_all = extra_all[:, 3]
-        routes_all = extra_all[:, 0, : TOPK * PATCHES]
-        dense = links.dense_sum(near, far)
-    else:
+        output, tokens_grad, small, near, far = backward(
+            upper, jnp.zeros_like(total[:PATCHES]), lower, jnp.zeros_like(total[PATCHES:])
+        )
+        small_all = lax.all_gather(small, everyone, axis=0)
+        slots = [dispatch(base, plane, members) for plane in planes]
+        routed = None
+        for start in range(0, len(planes), 2):
+            routed = routed_grads(slots[start : start + 2], expert_up, expert_down, routed)
+        shared = shared_grads(planes[0][:1], HALF, shared_up, shared_down, None)
         routed = lax.psum(routed, "dp")
-        shared = lax.psum(shared, "dp")
-        small_all = lax.all_gather(small, everyone, axis=0)
-        condition_all = lax.all_gather(own_condition[0], everyone, axis=0).astype(bf16)
+        shared = lax.psum(tuple(part[0] for part in shared), ("dp", "expert"))
         routes_all = lax.all_gather(routes.reshape(-1), everyone, axis=0)
-        order = jnp.arange(links.tensor) ^ me
-        grads = jnp.stack([near, far], axis=1).reshape((-1,) + near.shape[1:])[order]
+        turn = jnp.arange(links.tensor) ^ me
+        grads = jnp.stack([near, far], axis=1).reshape((-1,) + near.shape[1:])[turn]
         dense = lax.psum_scatter(grads, "tensor", scatter_dimension=0, tiled=True)[0]
         dense = lax.psum(dense, ("dp", "expert")).astype(f32)
-
+        qkv_grad, out_grad = dense[: 3 * local_width], dense[3 * local_width :]
+
+    condition_all = small_all[:, 6].astype(bf16)
     mod_grad = lax.dynamic_slice_in_dim(small_all[:, 0:6], me * local_width, local_width, axis=2)
     ada_grad = jnp.einsum(
         "id,icf->dcf", condition_all.astype(f32), mod_grad, precision=lax.Precision.HIGHEST
@@ -890,17 +952,17 @@
         (routes_all[:, :, None] == jnp.arange(EXPERTS).astype(routes_all.dtype)).astype(jnp.int32),
         axis=(0, 1),
     )
-    qkv_grad = dense[: 3 * local_width].reshape(3, local_width, width).transpose(2, 0, 1)
+    qkv_grad = qkv_grad.reshape(3, local_width, width).transpose(2, 0, 1)
     return (
         output,
         tokens_grad,
         ada_grad,
         ada_bias_grad,
         qkv_grad,
-        dense[3 * local_width :],
+        out_grad,
         router_grad,
-        shared[0][0],
-        shared[1][0],
+        shared[0],
+        shared[1],
         routed[0],
         routed[1],
         counts,

time: 902 us -> 428 us (0.47)
  Pallas kernels: 633 us -> 241 us
  waiting for transfers between devices: 148 us -> 101 us
  starting transfers between devices: 71.3 us -> 33.3 us
  local copies, waits for them, and re-layouts: 31.2 us -> 18.4 us
  between operations: 1.77 us -> 14.4 us
    pallas_call x25 -> x26, Pallas kernels: 633 us -> 241 us  [launch(): pl.pallas_call(body, out_shape=tuple((jax.ShapeDtypeStruct(*out) for out...]
    ppermute x12 -> x6, waiting for transfers between devices: 39.6 us -> 7.71 us  [along(): lax.ppermute(value, 'dp', [(i, (i + hop) % self.dp) for i in range(self.d...]
    ppermute x12 -> x6, starting transfers between devices: 34.7 us -> 10.6 us  [along(): lax.ppermute(value, 'dp', [(i, (i + hop) % self.dp) for i in range(self.d...]
    ppermute x16 -> x10, waiting for transfers between devices: 42.8 us -> 23.9 us  [to_other(): return lax.ppermute(value, 'expert', self.other)]
    unnamed x102 -> x74, local copies, waits for them, and re-layouts: 20.4 us -> 13.9 us
    ppermute x17 -> x8, waiting for transfers between devices: 62.8 us -> 63.2 us  [to_side(): return lax.ppermute(value, 'tensor', self.side)]
  transfers between devices with their start and end apart: 56 -> 33, of which waited for: 23 -> 9; matrix products, arithmetic and copies ran while one was open for 3% -> 3% of each run, Pallas kernels for 67% -> 55%
where the time goes in v3:
time: 428 us; the launch traced here: 430 us
  Pallas kernels  241 us (56%)
  waiting for transfers between devices  101 us (24%)
  starting transfers between devices  33.3 us (8%)
  local copies, waits for them, and re-layouts  18.4 us (4%)
  between operations  14.4 us (3%)
  other arithmetic  8.69 us (2%)
  blocking collectives  7.95 us (2%)
  matrix products  4.64 us (1%)
    pallas_call x26, Pallas kernels, launch(): pl.pallas_call(body, out_shape=tuple((jax.ShapeDtypeStruct(*out) for out...  241 us
    ppermute x8, waiting for transfers between devices, to_side(): return lax.ppermute(value, 'tensor', self.side)  63.2 us
    ppermute x10, waiting for transfers between devices, to_other(): return lax.ppermute(value, 'expert', self.other)  23.9 us
    unnamed x74, local copies, waits for them, and re-layouts  13.9 us
    ppermute x10, starting transfers between devices, to_other(): return lax.ppermute(value, 'expert', self.other)  11.6 us
    ppermute x6, starting transfers between devices, along(): lax.ppermute(value, 'dp', [(i, (i + hop) % self.dp) for i in range(self.d...  10.6 us
    ppermute x8, starting transfers between devices, to_side(): return lax.ppermute(value, 'tensor', self.side)  9.95 us
  transfers between devices with their start and end apart: 33, of which 9 were waited for; matrix products, arithmetic and copies ran while one was open for 3% of the time, Pallas kernels for 55%

profile of v3, /device:TPU:0, one launch (start us, length us, event | category | flops | bytes accessed | tf_op | source)
XLA Modules:
  0.0 430.0 jit_solution(5579238024884763556)
XLA Ops:
  10.0 8.0 %all_to_all.15 = f32[4,6,192]{2,1,0:T(8,128)S(1)} all-to-all(f32[4,6,192]{2,1,0:T(8,128)S(1)} %copy.43), channel_id=1, replica_groups=mesh['dp'=4,'expert'=2,'tensor'=4] {'tensor'}, dimensions={0} | all-to-all | bytes 36864 | tf_op jit(solution)/shard_map/all_to_all | solution.py:827
  18.0 1.8 multiply_convert_fusion.refs_0_
  22.2 29.5 %collective-permute-done.1.refs_0_ = bf16[768,768]{1,0:T(8,128)(2,1)S(1)} collective-permute-done((bf16[768,768]{1,0:T(8,128)(2,1)S(1)}, bf16[768,768]{1,0:T(8,128)(2,1)S(1)}, u32[]{:S(2)}, u32[]{:S(2)}) %collective-permute-start.1) | collective-permute-done | bytes 1179680 | tf_op jit(solution)/shard_map/ppermute | solution.py:726
  53.3 2.4 collective-permute-done.2.refs_7_.refs_18_
  56.8 7.4 %attention_forward.1 = (bf16[256,768]{1,0:T(8,128)(2,1)}, bf16[3,256,768]{2,1,0:T(8,128)(2,1)}, bf16[256,768]{1,0:T(8,128)(2,1)}, f32[256,768]{1,0:T(8,128)}, bf16[272,768]{1,0:T(8,128)(2,1)}) custom-call(bf16[256,768]{1,0:T(8,128)(2,1)} %refs_5_.1, f32[6,768]{1,0:T(8,128)} %squeeze.4.refs_1_.refs_7_, bf16[8,768]{1,0:T(8,128)(2,1)} %bitcast.57, ...), custom_call_target="tpu_custom_call" | custom-call | flops 5000000000 | bytes 9000000 | tf_op jit(solution)/shard_map/attention_forward/pallas_call | solution.py:89
  64.7 1.5 collective-permute-start.4
  66.2 1.7 collective-permute-start.3
  68.4 7.9 %collective-permute-done.7.refs_1_ = bf16[256,768]{1,0:T(8,128)(2,1)S(1)} collective-permute-done((bf16[256,768]{1,0:T(8,128)(2,1)S(1)}, bf16[256,768]{1,0:T(8,128)(2,1)S(1)}, u32[]{:S(2)}, u32[]{:S(2)}) %collective-permute-start.7) | collective-permute-done | bytes 393248 | tf_op jit(solution)/shard_map/ppermute | solution.py:726
  77.1 1.5 collective-permute-start.9
  79.2 12.2 %collective-permute-done.3.refs_1_.refs_4_ = bf16[272,768]{1,0:T(8,128)(2,1)S(1)} collective-permute-done((bf16[272,768]{1,0:T(8,128)(2,1)}, bf16[272,768]{1,0:T(8,128)(2,1)S(1)}, u32[]{:S(2)}, u32[]{:S(2)}) %collective-permute-start.3) | collective-permute-done | bytes 417824 | tf_op jit(solution)/shard_map/ppermute | solution.py:726
  91.4 1.7 collective-permute-start.6
  93.1 23.9 %collective-permute-done.6.refs_4_ = bf16[128,768]{1,0:T(8,128)(2,1)S(1)} collective-permute-done((bf16[128,768]{1,0:T(8,128)(2,1)S(1)}, bf16[128,768]{1,0:T(8,128)(2,1)S(1)}, u32[]{:S(2)}, u32[]{:S(2)}) %collective-permute-start.6) | collective-permute-done | bytes 196640 | tf_op jit(solution)/shard_map/ppermute | solution.py:729
  118.3 2.6 assemble.2.refs_1_.refs_2_.refs_0_
  122.5 2.5 assemble.3.refs_3_.refs_2_
  125.6 3.8 collective-permute-done.11.refs_6_.refs_3_
  130.5 46.1 %experts_both.1 = (bf16[4,528,768]{2,1,0:T(8,128)(2,1)}, bf16[4,528,768]{2,1,0:T(8,128)(2,1)}) custom-call(s32[1]{0:T(128)} %bitcast.refs_0_, bf16[4,272,768]{2,1,0:T(8,128)(2,1)} %assemble.2.refs_1_.refs_2_.refs_0_, bf16[4,272,768]{2,1,0:T(8,128)(2,1)} %assemble.2.refs_1_.refs_2_.refs_0_, bf16[4,256,768]{2,1,0:T(8,128)(2,1)} %assemble.3.refs_3_.refs_2_, ...), custom_call_target="tpu_custom_call" | custom-call | flops 30000001024 | bytes 30000000 | tf_op jit(solution)/shard_map/experts_both/pallas_call | solution.py:89
  178.1 7.4 %dispatch.1 = (bf16[4,640,768]{2,1,0:T(8,128)(2,1)}, bf16[4,640,768]{2,1,0:T(8,128)(2,1)}) custom-call(s32[1]{0:T(128)} %bitcast.refs_0_, bf16[4,272,768]{2,1,0:T(8,128)(2,1)} %assemble.2.refs_1_.refs_2_.refs_0_, bf16[4,272,768]{2,1,0:T(8,128)(2,1)} %assemble.2.refs_1_.refs_2_.refs_0_, bf16[4,256,768]{2,1,0:T(8,128)(2,1)} %assemble.3.refs_3_.refs_2_, ...), custom_call_target="tpu_custom_call" | custom-call | flops 8000000000 | bytes 16000000 | tf_op jit(solution)/shard_map/dispatch/pallas_call | solution.py:89
  185.6 5.3 %plane_first.1 = (bf16[2,256,768]{2,1,0:T(8,128)(2,1)}, bf16[2,272,768]{2,1,0:T(8,128)(2,1)}, f32[2,256,768]{2,1,0:T(8,128)}, f32[2,272,768]{2,1,0:T(8,128)}) custom-call(bf16[4,528,768]{2,1,0:T(8,128)(2,1)} %get-tuple-element.66.refs_7_.refs_0_, bf16[4,528,768]{2,1,0:T(8,128)(2,1)} %collective-permute-done.12.refs_1_, ...), custom_call_target="tpu_custom_call" | custom-call | bytes 10000000 | tf_op jit(solution)/shard_map/plane_first/pallas_call | solution.py:89
  190.9 2.0 collective-permute-start.14
  192.9 1.7 collective-permute-start.13
  194.6 20.2 %weight_grads.5 = (f32[4,768,768]{2,1,0:T(8,128)}, f32[4,768,768]{2,1,0:T(8,128)}) custom-call(bf16[4,640,768]{2,1,0:T(8,128)(2,1)} %get-tuple-element.68.refs_2_.refs_0_, bf16[4,640,768]{2,1,0:T(8,128)(2,1)} %get-tuple-element.73.refs_1_, bf16[4,768,768]{2,1,0:T(8,128)(2,1)} %refs_2_.5, bf16[4,768,768]{2,1,0:T(8,128)(2,1)} %refs_3_.5, ...), custom_call_target="tpu_custom_call" | custom-call | flops 18119393280 | bytes 7864320 | tf_op jit(solution)/shard_map/weight_grads/pallas_call | solution.py:89
  214.8 13.6 %collective-permute-done.13.refs_2_ = bf16[2,256,768]{2,1,0:T(8,128)(2,1)S(1)} collective-permute-done((bf16[2,256,768]{2,1,0:T(8,128)(2,1)}, bf16[2,256,768]{2,1,0:T(8,128)(2,1)S(1)}, u32[]{:S(2)}, u32[]{:S(2)}) %collective-permute-start.13) | collective-permute-done | bytes 786464 | tf_op jit(solution)/shard_map/ppermute | solution.py:726
  229.5 3.9 plane_second.1
  233.4 2.4 collective-permute-start.16
  236.0 9.4 %weight_grads.6 = (f32[1,768,768]{2,1,0:T(8,128)}, f32[1,768,768]{2,1,0:T(8,128)}) custom-call(bf16[4,272,768]{2,1,0:T(8,128)(2,1)} %assemble.2.refs_1_.refs_2_.refs_0_, bf16[4,272,768]{2,1,0:T(8,128)(2,1)} %collective-permute-done.10.refs_4_.refs_5_.refs_1_, bf16[4,256,768]{2,1,0:T(8,128)(2,1)} %assemble.3.refs_3_.refs_2_, bf16[4,256,768]{2,1,0:T(8,128)(2,1)} %copy-done.29, ...), custom_call_target="tpu_custom_call" | custom-call | flops 7247757312 | bytes 3145728 | tf_op jit(solution)/shard_map/weight_grads/pallas_call | solution.py:89
  246.3 16.8 %attention_backward.1 = (bf16[256,768]{1,0:T(8,128)(2,1)}, f32[256,768]{1,0:T(8,128)}, f32[16,768]{1,0:T(8,128)}, bf16[2,768,768]{2,1,0:T(8,128)(2,1)}, bf16[2,768,768]{2,1,0:T(8,128)(2,1)}) custom-call(f32[256,768]{1,0:T(8,128)} %get-tuple-element.75.refs_6_.refs_0_, bf16[256,768]{1,0:T(8,128)(2,1)} %copy-done.32, f32[272,768]{1,0:T(8,128)} %get-tuple-element.77.refs_2_, ...), custom_call_target="tpu_custom_call" | custom-call | flops 10000000000 | bytes 16000000 | tf_op jit(solution)/shard_map/attention_backward/pallas_call | solution.py:89
  263.8 19.0 %dispatch_hops.1 = (bf16[4,1920,768]{2,1,0:T(8,128)(2,1)}, bf16[4,1920,768]{2,1,0:T(8,128)(2,1)}) custom-call(s32[3]{0:T(128)} %pad_add_fusion.1.refs_0_, bf16[4,8,272,768]{3,2,1,0:T(8,128)(2,1)} %bitcast.34, bf16[4,8,256,768]{3,2,1,0:T(8,128)(2,1)} %bitcast.40), custom_call_target="tpu_custom_call" | custom-call | flops 24000000000 | bytes 48000000 | tf_op jit(solution)/shard_map/dispatch_hops/pallas_call | solution.py:89
  282.8 4.3 %dense_first.1 = (bf16[384,768]{1,0:T(8,128)(2,1)}, bf16[2,192,768]{2,1,0:T(8,128)(2,1)}, f32[384,768]{1,0:T(8,128)}, f32[2,192,768]{2,1,0:T(8,128)}) custom-call(s32[2]{0:T(128)} %pad_add_fusion.2.refs_0_, bf16[2,768,768]{2,1,0:T(8,128)(2,1)} %get-tuple-element.92.refs_1_, bf16[2,768,768]{2,1,0:T(8,128)(2,1)} %collective-permute-done.17.refs_2_, ...), custom_call_target="tpu_custom_call" | custom-call | bytes 8000000 | tf_op jit(solution)/shard_map/dense_first/pallas_call | solution.py:89
  287.2 1.4 collective-permute-start.18
  289.7 24.5 %weight_grads.7 = (f32[1,768,768]{2,1,0:T(8,128)}, f32[1,768,768]{2,1,0:T(8,128)}, bf16[2,768,768]{2,1,0:T(8,128)(2,1)}) custom-call(s32[3]{0:T(128)} %pad_add_fusion.1.refs_0_, bf16[4,8,272,768]{3,2,1,0:T(8,128)(2,1)} %bitcast.35, bf16[4,8,272,768]{3,2,1,0:T(8,128)(2,1)} %bitcast.36, ...), custom_call_target="tpu_custom_call", output_to_operand_aliasing={{0}: (9, {}), {1}: (10, {})} | custom-call | flops 21743271936 | bytes 9437184 | tf_op jit(solution)/shard_map/weight_grads/pallas_call | solution.py:89
  315.2 3.3 dense_second.1
  318.4 1.7 collective-permute-start.20
  320.2 26.9 %weight_grads.8 = (f32[4,768,768]{2,1,0:T(8,128)}, f32[4,768,768]{2,1,0:T(8,128)}) custom-call(bf16[4,1920,768]{2,1,0:T(8,128)(2,1)} %get-tuple-element.89.refs_3_.refs_0_, bf16[4,1920,768]{2,1,0:T(8,128)(2,1)} %get-tuple-element.90.refs_1_, bf16[4,768,768]{2,1,0:T(8,128)(2,1)} %refs_2_.5, ...), custom_call_target="tpu_custom_call", output_to_operand_aliasing={{0}: (4, {}), {1}: (5, {})} | custom-call | flops 27179089920 | bytes 11796480 | tf_op jit(solution)/shard_map/weight_grads/pallas_call | solution.py:89
  347.9 2.4 dense_third.1
  350.4 2.1 collective-permute-start.29
  352.5 2.4 collective-permute-start.22
  354.8 2.3 collective-permute-start.23
  357.2 2.0 collective-permute-start.24
  359.2 26.9 %weight_grads.9 = (f32[4,768,768]{2,1,0:T(8,128)}, f32[4,768,768]{2,1,0:T(8,128)}) custom-call(bf16[4,1920,768]{2,1,0:T(8,128)(2,1)} %get-tuple-element.89.refs_3_.refs_0_, bf16[4,1920,768]{2,1,0:T(8,128)(2,1)} %get-tuple-element.90.refs_1_, bf16[4,768,768]{2,1,0:T(8,128)(2,1)} %refs_2_.5, ...), custom_call_target="tpu_custom_call", output_to_operand_aliasing={{0}: (4, {}), {1}: (5, {})} | custom-call | flops 27179089920 | bytes 11796480 | tf_op jit(solution)/shard_map/weight_grads/pallas_call | solution.py:89
  386.9 1.9 dense_fourth.1.refs_1_.refs_5_
  389.4 3.2 collective-permute-start.27
  393.6 4.0 collective-permute-done.25.refs_2_
  397.6 3.7 collective-permute-done.26.refs_3_
  402.6 2.0 dense_fifth.1.refs_3_.refs_1_
  406.5 1.3 slice.34
  410.5 3.4 fusion
  413.9 5.6 %shared_last.1 = (f32[768,768]{1,0:T(8,128)}, f32[768,768]{1,0:T(8,128)}) custom-call(f32[1,768,768]{2,1,0:T(8,128)} %get-tuple-element.111.refs_0_, f32[1,768,768]{2,1,0:T(8,128)} %get-tuple-element.112.refs_1_, bf16[2,768,768]{2,1,0:T(8,128)(2,1)} %collective-permute-done.29.refs_2_, bf16[384,768]{1,0:T(8,128)(2,1)} %dense_fifth.1.refs_3_.refs_1_), custom_call_target="tpu_custom_call" | custom-call | bytes 12000000 | tf_op jit(solution)/shard_map/shared_last/pallas_call | solution.py:89
  420.3 2.9 dense_last.1
  (148 shorter events, 31.0 us)
Async XLA Ops:
  7.2 1.5 copy-start
  7.2 12.7 %copy-start.16 = (bf16[192,768]{1,0:T(8,128)(2,1)S(1)}, bf16[192,768]{1,0:T(8,128)(2,1)}, u32[]{:S(2)}) copy-start(bf16[192,768]{1,0:T(8,128)(2,1)} %param.20) | copy-start | bytes 884740
  7.2 256.6 %all-gather.11.cloned.1.call-start = ((), (), s32[]{:S(2)}) async-start(), calls=%async_computation.3 | async-start | bytes 12976128 | tf_op jit(solution)/shard_map/all_gather | solution.py:853
  19.9 243.9 %all-gather.9.cloned.1.call-start = ((), (), s32[]{:S(2)}) async-start(), calls=%async_computation.2 | async-start | bytes 13787136 | tf_op jit(solution)/shard_map/all_gather | solution.py:856
  19.9 32.8 %copy-start.27 = (s32[256,2]{0,1:T(2,128)S(1)}, s32[256,2]{0,1:T(2,128)}, u32[]{:S(2)}) copy-start(s32[256,2]{0,1:T(2,128)} %param.27) | copy-start | bytes 6148
  19.9 32.8 %copy-start.28 = (s32[256,2]{0,1:T(2,128)S(1)}, s32[256,2]{0,1:T(2,128)}, u32[]{:S(2)}) copy-start(s32[256,2]{0,1:T(2,128)} %param.26) | copy-start | bytes 6148
  21.2 34.6 %copy-start.6 = (bf16[768,768]{1,0:T(8,128)(2,1)}, bf16[768,768]{1,0:T(8,128)(2,1)S(1)}, u32[]{:S(2)}) copy-start(bf16[768,768]{1,0:T(8,128)(2,1)S(1)} %pad_maximum_fusion.refs_4_.refs_15_) | copy-start | bytes 3538948
  21.2 30.5 %collective-permute-start.1 = (bf16[768,768]{1,0:T(8,128)(2,1)S(1)}, bf16[768,768]{1,0:T(8,128)(2,1)S(1)}, u32[]{:S(2)}, u32[]{:S(2)}) collective-permute-start(bf16[768,768]{1,0:T(8,128)(2,1)S(1)} %pad_maximum_fusion.refs_4_.refs_15_), channel_id=1, source_target_pairs={{0,2},{1,3},{2,0},{3,1},{4,6},{5,7},{6,4},{7,5},{8,10},{9,11},{10,... | collective-permute-start | bytes 3538952 | tf_op jit(solution)/shard_map/ppermute | solution.py:726
  21.3 32.0 %collective-permute-start = (bf16[768,768]{1,0:T(8,128)(2,1)S(1)}, bf16[768,768]{1,0:T(8,128)(2,1)}, u32[]{:S(2)}, u32[]{:S(2)}) collective-permute-start(bf16[768,768]{1,0:T(8,128)(2,1)S(1)} %pad_maximum_fusion.refs_4_.refs_15_), channel_id=1, source_target_pairs={{0,1},{1,0},{2,3},{3,2},{4,5},{5,4},{6,7},{7,6},{8,9},{9,8},{10,11... | collective-permute-start | bytes 3538952 | tf_op jit(solution)/shard_map/ppermute | solution.py:723
  52.7 3.1 collective-permute-start.2
  56.8 7.5 %copy-start.3 = (bf16[256,768]{1,0:T(8,128)(2,1)S(1)}, bf16[256,768]{1,0:T(8,128)(2,1)}, u32[]{:S(2)}) copy-start(bf16[256,768]{1,0:T(8,128)(2,1)} %multiply_convert_fusion.refs_0_) | copy-start | bytes 1179652
  64.2 342.3 %all-gather.7.cloned.1.call-start = ((), (), s32[]{:S(2)}) async-start(), calls=%async_computation.1 | async-start | bytes 1622016 | tf_op jit(solution)/shard_map/all_gather | solution.py:888
  64.3 12.0 %collective-permute-start.7 = (bf16[256,768]{1,0:T(8,128)(2,1)S(1)}, bf16[256,768]{1,0:T(8,128)(2,1)S(1)}, u32[]{:S(2)}, u32[]{:S(2)}) collective-permute-start(bf16[256,768]{1,0:T(8,128)(2,1)S(1)} %copy-done.3), channel_id=1, source_target_pairs={{0,2},{1,3},{2,0},{3,1},{4,6},{5,7},{6,4},{7,5},{8,10},{9,11},{10,... | collective-permute-start | bytes 1179656 | tf_op jit(solution)/shard_map/ppermute | solution.py:726
  64.7 13.9 %collective-permute-start.4 = (bf16[272,768]{1,0:T(8,128)(2,1)}, bf16[272,768]{1,0:T(8,128)(2,1)S(1)}, u32[]{:S(2)}, u32[]{:S(2)}) collective-permute-start(bf16[272,768]{1,0:T(8,128)(2,1)} %get-tuple-element.65.refs_0_.refs_1_.refs_14_), channel_id=1, source_target_pairs={{0,4},{4,0},{1,5},{5,1},{2,6},{6,2},{3,7},{7,3},{8,12},{12,8},{9,1... | collective-permute-start | bytes 1253384 | tf_op jit(solution)/shard_map/ppermute | solution.py:729
  66.2 25.2 %collective-permute-start.3 = (bf16[272,768]{1,0:T(8,128)(2,1)}, bf16[272,768]{1,0:T(8,128)(2,1)S(1)}, u32[]{:S(2)}, u32[]{:S(2)}) collective-permute-start(bf16[272,768]{1,0:T(8,128)(2,1)} %get-tuple-element.65.refs_0_.refs_1_.refs_14_), channel_id=1, source_target_pairs={{0,2},{1,3},{2,0},{3,1},{4,6},{5,7},{6,4},{7,5},{8,10},{9,11},{10,... | collective-permute-start | bytes 1253384 | tf_op jit(solution)/shard_map/ppermute | solution.py:726
  67.9 53.1 %collective-permute-start.8 = (bf16[256,768]{1,0:T(8,128)(2,1)S(1)}, bf16[256,768]{1,0:T(8,128)(2,1)S(1)}, u32[]{:S(2)}, u32[]{:S(2)}) collective-permute-start(bf16[256,768]{1,0:T(8,128)(2,1)S(1)} %copy-done.3), channel_id=1, source_target_pairs={{0,4},{4,0},{1,5},{5,1},{2,6},{6,2},{3,7},{7,3},{8,12},{12,8},{9,1... | collective-permute-start | bytes 1179656 | tf_op jit(solution)/shard_map/ppermute | solution.py:729
  76.3 44.6 %copy-start.5 = (bf16[256,768]{1,0:T(8,128)(2,1)}, bf16[256,768]{1,0:T(8,128)(2,1)S(1)}, u32[]{:S(2)}) copy-start(bf16[256,768]{1,0:T(8,128)(2,1)S(1)} %collective-permute-done.7.refs_1_) | copy-start | bytes 1179652
  77.1 43.9 %collective-permute-start.9 = (bf16[256,768]{1,0:T(8,128)(2,1)}, bf16[256,768]{1,0:T(8,128)(2,1)S(1)}, u32[]{:S(2)}, u32[]{:S(2)}) collective-permute-start(bf16[256,768]{1,0:T(8,128)(2,1)} %ordered.6), channel_id=1, source_target_pairs={{0,4},{4,0},{1,5},{5,1},{2,6},{6,2},{3,7},{7,3},{8,12},{12,8},{9,1... | collective-permute-start | bytes 1179656 | tf_op jit(solution)/shard_map/ppermute | solution.py:729
  78.6 38.3 %copy-start.8 = (bf16[272,768]{1,0:T(8,128)(2,1)}, bf16[272,768]{1,0:T(8,128)(2,1)S(1)}, u32[]{:S(2)}) copy-start(bf16[272,768]{1,0:T(8,128)(2,1)S(1)} %collective-permute-done.4.refs_2_) | copy-start | bytes 1253380
  78.6 38.3 %collective-permute-start.5 = (bf16[144,768]{1,0:T(8,128)(2,1)S(1)}, bf16[144,768]{1,0:T(8,128)(2,1)S(1)}, u32[]{:S(2)}, u32[]{:S(2)}) collective-permute-start(bf16[144,768]{1,0:T(8,128)(2,1)S(1)} %slice.30), channel_id=1, source_target_pairs={{0,2},{1,3},{2,0},{3,1},{4,6},{5,7},{6,4},{7,5},{8,10},{9,11},{10,... | collective-permute-start | bytes 663560 | tf_op jit(solution)/shard_map/ppermute | solution.py:726
  91.4 25.6 %copy-start.4 = (bf16[272,768]{1,0:T(8,128)(2,1)}, bf16[272,768]{1,0:T(8,128)(2,1)S(1)}, u32[]{:S(2)}) copy-start(bf16[272,768]{1,0:T(8,128)(2,1)S(1)} %collective-permute-done.3.refs_1_.refs_4_) | copy-start | bytes 1253380
  91.4 25.5 %collective-permute-start.6 = (bf16[128,768]{1,0:T(8,128)(2,1)S(1)}, bf16[128,768]{1,0:T(8,128)(2,1)S(1)}, u32[]{:S(2)}, u32[]{:S(2)}) collective-permute-start(bf16[128,768]{1,0:T(8,128)(2,1)S(1)} %slice.31), channel_id=1, source_target_pairs={{0,4},{4,0},{1,5},{5,1},{2,6},{6,2},{3,7},{7,3},{8,12},{12,8},{9,1... | collective-permute-start | bytes 589832 | tf_op jit(solution)/shard_map/ppermute | solution.py:729
  120.9 8.5 %collective-permute-start.10 = (bf16[4,272,768]{2,1,0:T(8,128)(2,1)}, bf16[4,272,768]{2,1,0:T(8,128)(2,1)}, u32[]{:S(2)}, u32[]{:S(2)}) collective-permute-start(bf16[4,272,768]{2,1,0:T(8,128)(2,1)} %assemble.2.refs_1_.refs_2_.refs_0_), channel_id=1, source_target_pairs={{0,1},{1,0},{2,3},{3,2},{4,5},{5,4},{6,7},{7,6},{8,9},{9,8},{10,11... | collective-permute-start | bytes 5013512 | tf_op jit(solution)/shard_map/ppermute | solution.py:723
  125.0 4.4 %collective-permute-start.11 = (bf16[4,256,768]{2,1,0:T(8,128)(2,1)}, bf16[4,256,768]{2,1,0:T(8,128)(2,1)S(1)}, u32[]{:S(2)}, u32[]{:S(2)}) collective-permute-start(bf16[4,256,768]{2,1,0:T(8,128)(2,1)} %assemble.3.refs_3_.refs_2_), channel_id=1, source_target_pairs={{0,1},{1,0},{2,3},{3,2},{4,5},{5,4},{6,7},{7,6},{8,9},{9,8},{10,11... | collective-permute-start | bytes 4718600 | tf_op jit(solution)/shard_map/ppermute | solution.py:723
  176.6 9.0 %collective-permute-start.12 = (bf16[4,528,768]{2,1,0:T(8,128)(2,1)}, bf16[4,528,768]{2,1,0:T(8,128)(2,1)}, u32[]{:S(2)}, u32[]{:S(2)}) collective-permute-start(bf16[4,528,768]{2,1,0:T(8,128)(2,1)} %get-tuple-element.67), channel_id=1, source_target_pairs={{0,1},{1,0},{2,3},{3,2},{4,5},{5,4},{6,7},{7,6},{8,9},{9,8},{10,11... | collective-permute-start | bytes 9732104 | tf_op jit(solution)/shard_map/ppermute | solution.py:723
  190.9 37.5 %collective-permute-start.14 = (bf16[2,272,768]{2,1,0:T(8,128)(2,1)}, bf16[2,272,768]{2,1,0:T(8,128)(2,1)S(1)}, u32[]{:S(2)}, u32[]{:S(2)}) collective-permute-start(bf16[2,272,768]{2,1,0:T(8,128)(2,1)} %get-tuple-element.72), channel_id=1, source_target_pairs={{0,4},{4,0},{1,5},{5,1},{2,6},{6,2},{3,7},{7,3},{8,12},{12,8},{9,1... | collective-permute-start | bytes 2506760 | tf_op jit(solution)/shard_map/ppermute | solution.py:729
  192.9 35.5 %collective-permute-start.13 = (bf16[2,256,768]{2,1,0:T(8,128)(2,1)}, bf16[2,256,768]{2,1,0:T(8,128)(2,1)S(1)}, u32[]{:S(2)}, u32[]{:S(2)}) collective-permute-start(bf16[2,256,768]{2,1,0:T(8,128)(2,1)} %get-tuple-element.71.refs_4_), channel_id=1, source_target_pairs={{0,2},{1,3},{2,0},{3,1},{4,6},{5,7},{6,4},{7,5},{8,10},{9,11},{10,... | collective-permute-start | bytes 2359304 | tf_op jit(solution)/shard_map/ppermute | solution.py:726
  233.4 12.0 %collective-permute-start.16 = (bf16[272,768]{1,0:T(8,128)(2,1)}, bf16[272,768]{1,0:T(8,128)(2,1)S(1)}, u32[]{:S(2)}, u32[]{:S(2)}) collective-permute-start(bf16[272,768]{1,0:T(8,128)(2,1)} %get-tuple-element.78), channel_id=1, source_target_pairs={{0,2},{1,3},{2,0},{3,1},{4,6},{5,7},{6,4},{7,5},{8,10},{9,11},{10,... | collective-permute-start | bytes 1253384 | tf_op jit(solution)/shard_map/ppermute | solution.py:726
  235.9 9.5 %collective-permute-start.15 = (bf16[256,768]{1,0:T(8,128)(2,1)}, bf16[256,768]{1,0:T(8,128)(2,1)S(1)}, u32[]{:S(2)}, u32[]{:S(2)}) collective-permute-start(bf16[256,768]{1,0:T(8,128)(2,1)} %get-tuple-element.76), channel_id=1, source_target_pairs={{0,4},{4,0},{1,5},{5,1},{2,6},{6,2},{3,7},{7,3},{8,12},{12,8},{9,1... | collective-permute-start | bytes 1179656 | tf_op jit(solution)/shard_map/ppermute | solution.py:729
  263.1 19.8 %collective-permute-start.17 = (bf16[2,768,768]{2,1,0:T(8,128)(2,1)}, bf16[2,768,768]{2,1,0:T(8,128)(2,1)}, u32[]{:S(2)}, u32[]{:S(2)}) collective-permute-start(bf16[2,768,768]{2,1,0:T(8,128)(2,1)} %get-tuple-element.93), channel_id=1, source_target_pairs={{0,1},{1,0},{2,3},{3,2},{4,5},{5,4},{6,7},{7,6},{8,9},{9,8},{10,11... | collective-permute-start | bytes 7077896 | tf_op jit(solution)/shard_map/ppermute | solution.py:723
  287.2 27.0 %collective-permute-start.18 = (bf16[384,768]{1,0:T(8,128)(2,1)}, bf16[384,768]{1,0:T(8,128)(2,1)S(1)}, u32[]{:S(2)}, u32[]{:S(2)}) collective-permute-start(bf16[384,768]{1,0:T(8,128)(2,1)} %get-tuple-element.96), channel_id=1, source_target_pairs={{0,2},{1,3},{2,0},{3,1},{4,6},{5,7},{6,4},{7,5},{8,10},{9,11},{10,... | collective-permute-start | bytes 1769480 | tf_op jit(solution)/shard_map/ppermute | solution.py:726
  288.6 25.6 %collective-permute-start.19 = (bf16[2,192,768]{2,1,0:T(8,128)(2,1)}, bf16[2,192,768]{2,1,0:T(8,128)(2,1)S(1)}, u32[]{:S(2)}, u32[]{:S(2)}) collective-permute-start(bf16[2,192,768]{2,1,0:T(8,128)(2,1)} %get-tuple-element.97), channel_id=1, source_target_pairs={{0,4},{4,0},{1,5},{5,1},{2,6},{6,2},{3,7},{7,3},{8,12},{12,8},{9,1... | collective-permute-start | bytes 1769480 | tf_op jit(solution)/shard_map/ppermute | solution.py:729
  318.4 28.6 %collective-permute-start.20 = (bf16[192,768]{1,0:T(8,128)(2,1)}, bf16[192,768]{1,0:T(8,128)(2,1)S(1)}, u32[]{:S(2)}, u32[]{:S(2)}) collective-permute-start(bf16[192,768]{1,0:T(8,128)(2,1)} %get-tuple-element.104), channel_id=1, source_target_pairs={{0,2},{1,3},{2,0},{3,1},{4,6},{5,7},{6,4},{7,5},{8,10},{9,11},{10,... | collective-permute-start | bytes 884744 | tf_op jit(solution)/shard_map/ppermute | solution.py:726
  320.2 26.9 %collective-permute-start.21 = (bf16[192,768]{1,0:T(8,128)(2,1)}, bf16[192,768]{1,0:T(8,128)(2,1)S(1)}, u32[]{:S(2)}, u32[]{:S(2)}) collective-permute-start(bf16[192,768]{1,0:T(8,128)(2,1)} %get-tuple-element.105), channel_id=1, source_target_pairs={{0,4},{4,0},{1,5},{5,1},{2,6},{6,2},{3,7},{7,3},{8,12},{12,8},{9,1... | collective-permute-start | bytes 884744 | tf_op jit(solution)/shard_map/ppermute | solution.py:729
  350.3 2.1 copy-start.35
  350.3 4.5 %copy-start.34 = (bf16[96,768]{1,0:T(8,128)(2,1)S(1)}, bf16[96,768]{1,0:T(8,128)(2,1)}, u32[]{:S(2)}) copy-start(bf16[96,768]{1,0:T(8,128)(2,1)} %get-tuple-element.109) | copy-start | bytes 442372
  350.3 6.8 %copy-start.33 = (bf16[96,768]{1,0:T(8,128)(2,1)S(1)}, bf16[96,768]{1,0:T(8,128)(2,1)}, u32[]{:S(2)}) copy-start(bf16[96,768]{1,0:T(8,128)(2,1)} %get-tuple-element.110) | copy-start | bytes 442372
  350.4 63.5 %collective-permute-start.29 = (bf16[2,768,768]{2,1,0:T(8,128)(2,1)}, bf16[2,768,768]{2,1,0:T(8,128)(2,1)}, u32[]{:S(2)}, u32[]{:S(2)}) collective-permute-start(bf16[2,768,768]{2,1,0:T(8,128)(2,1)} %ordered.9), channel_id=1, source_target_pairs={{0,4},{4,0},{1,5},{5,1},{2,6},{6,2},{3,7},{7,3},{8,12},{12,8},{9,1... | collective-permute-start | bytes 7077896 | tf_op jit(solution)/shard_map/ppermute | solution.py:729
  352.5 33.7 %collective-permute-start.22 = (bf16[96,768]{1,0:T(8,128)(2,1)S(1)}, bf16[96,768]{1,0:T(8,128)(2,1)S(1)}, u32[]{:S(2)}, u32[]{:S(2)}) collective-permute-start(bf16[96,768]{1,0:T(8,128)(2,1)S(1)} %copy-done.35), channel_id=1, source_target_pairs={{0,8},{8,16},{16,24},{24,0},{1,9},{9,17},{17,25},{25,1},{2,10},{10... | collective-permute-start | bytes 442376 | tf_op jit(solution)/shard_map/ppermute | solution.py:732
  354.8 31.3 %collective-permute-start.23 = (bf16[96,768]{1,0:T(8,128)(2,1)S(1)}, bf16[96,768]{1,0:T(8,128)(2,1)S(1)}, u32[]{:S(2)}, u32[]{:S(2)}) collective-permute-start(bf16[96,768]{1,0:T(8,128)(2,1)S(1)} %copy-done.34), channel_id=1, source_target_pairs={{0,16},{8,24},{16,0},{24,8},{1,17},{9,25},{17,1},{25,9},{2,18},{10... | collective-permute-start | bytes 442376 | tf_op jit(solution)/shard_map/ppermute | solution.py:732
  357.2 29.0 %collective-permute-start.24 = (bf16[96,768]{1,0:T(8,128)(2,1)S(1)}, bf16[96,768]{1,0:T(8,128)(2,1)S(1)}, u32[]{:S(2)}, u32[]{:S(2)}) collective-permute-start(bf16[96,768]{1,0:T(8,128)(2,1)S(1)} %copy-done.33), channel_id=1, source_target_pairs={{0,24},{8,0},{16,8},{24,16},{1,25},{9,1},{17,9},{25,17},{2,26},{10... | collective-permute-start | bytes 442376 | tf_op jit(solution)/shard_map/ppermute | solution.py:732
  388.7 8.8 %collective-permute-start.25 = (bf16[96,768]{1,0:T(8,128)(2,1)}, bf16[96,768]{1,0:T(8,128)(2,1)S(1)}, u32[]{:S(2)}, u32[]{:S(2)}) collective-permute-start(bf16[96,768]{1,0:T(8,128)(2,1)} %dense_fourth.1.refs_1_.refs_5_), channel_id=1, source_target_pairs={{0,8},{8,16},{16,24},{24,0},{1,9},{9,17},{17,25},{25,1},{2,10},{10... | collective-permute-start | bytes 442376 | tf_op jit(solution)/shard_map/ppermute | solution.py:732
  388.7 12.5 %collective-permute-start.26 = (bf16[96,768]{1,0:T(8,128)(2,1)}, bf16[96,768]{1,0:T(8,128)(2,1)S(1)}, u32[]{:S(2)}, u32[]{:S(2)}) collective-permute-start(bf16[96,768]{1,0:T(8,128)(2,1)} %dense_fourth.1.refs_1_.refs_5_), channel_id=1, source_target_pairs={{0,16},{8,24},{16,0},{24,8},{1,17},{9,25},{17,1},{25,9},{2,18},{10... | collective-permute-start | bytes 442376 | tf_op jit(solution)/shard_map/ppermute | solution.py:732
  389.4 11.9 %collective-permute-start.27 = (bf16[96,768]{1,0:T(8,128)(2,1)}, bf16[96,768]{1,0:T(8,128)(2,1)S(1)}, u32[]{:S(2)}, u32[]{:S(2)}) collective-permute-start(bf16[96,768]{1,0:T(8,128)(2,1)} %dense_fourth.1.refs_1_.refs_5_), channel_id=1, source_target_pairs={{0,24},{8,0},{16,8},{24,16},{1,25},{9,1},{17,9},{25,17},{2,26},{10... | collective-permute-start | bytes 442376 | tf_op jit(solution)/shard_map/ppermute | solution.py:732
  397.6 3.7 copy-start.21
  404.6 14.8 %collective-permute-start.28 = (bf16[384,768]{1,0:T(8,128)(2,1)}, bf16[384,768]{1,0:T(8,128)(2,1)S(1)}, u32[]{:S(2)}, u32[]{:S(2)}) collective-permute-start(bf16[384,768]{1,0:T(8,128)(2,1)} %dense_fifth.1.refs_3_.refs_1_), channel_id=1, source_target_pairs={{0,4},{4,0},{1,5},{5,1},{2,6},{6,2},{3,7},{7,3},{8,12},{12,8},{9,1... | collective-permute-start | bytes 1769480 | tf_op jit(solution)/shard_map/ppermute | solution.py:729
  406.5 3.3 copy-start.2
  413.9 9.4 %copy-start.1 = (bf16[768,6,192]{0,2,1:T(8,128)(2,1)S(1)}, bf16[768,6,192]{0,2,1:T(8,128)(2,1)}, u32[]{:S(2)}) copy-start(bf16[768,6,192]{0,2,1:T(8,128)(2,1)} %param.17) | copy-start | bytes 5308420
  (21 other events, 17.2 us)
Sparse Core Ops, SparseCore 0:
  20.0 117.4 all-gather.10
  141.0 114.6 all-gather.8
  263.9 57.3 all-gather.6

commit v4 on v3

--- a/solution.py
+++ b/solution.py
@@ -289,31 +289,30 @@
         cots_ref[member, block * CAP : (block + 1) * CAP, :] = scaled[span]
 
 
-def hops_kernel(place_ref, ext, cots, rows_ref, cots_ref):
-    base = place_ref[0].astype(f32)
-    for block in range(ext.shape[1]):
+def hops_kernel(base_ref, ext, cots, rows_ref, cots_ref):
+    base = base_ref[0].astype(f32)
+    for block in range(ext.shape[0]):
         dispatch_block(
-            base, rows_ref.shape[0], ext[0, block, :PATCHES], ext[0, block, PATCHES:], cots[0, block], rows_ref,
+            base, rows_ref.shape[0], ext[block, 0, :PATCHES], ext[block, 0, PATCHES:], cots[block, 0], rows_ref,
             cots_ref, block,
         )
 
 
-def plane_of(hop, place, planes):
-    return lax.rem(place[2] + hop + 1, planes)
-
-
-def dispatch_hops(place, ext, cots, members, after=()):
-    planes, blocks, rows, width = ext.shape
-    out = ((members, (planes - 1) * blocks * CAP, width), bf16)
-    out_spec = pl.BlockSpec((members, blocks * CAP, width), lambda h, p: (0, h, 0))
-    specs = [
-        pl.BlockSpec((1, blocks, count, width), lambda h, p: (plane_of(h, p, planes), 0, 0, 0))
-        for count in (rows, PATCHES)
-    ]
+def dispatch_hops(base, ext, cots, members, after=()):
+    blocks, hops, rows, width = ext.shape
+    out = ((members, hops * blocks * CAP, width), bf16)
+    out_spec = pl.BlockSpec((members, blocks * CAP, width), lambda h, b: (0, h, 0))
+    specs = [pl.BlockSpec((blocks, 1, count, width), lambda h, b: (0, h, 0, 0)) for count in (rows, PATCHES)]
     return launch(
         hops_kernel, "dispatch_hops", [out, out], [ext, cots], in_specs=specs, out_specs=[out_spec, out_spec],
-        grid=(planes - 1,), scalars=[place], after=after, flops=24 * 10**9, moved=48 * 10**6,
-    )
+        grid=(hops,), scalars=[base], after=after, flops=24 * 10**9, moved=48 * 10**6,
+    )
+
+
+def pick_kernel(place_ref, source, out):
+    planes = source.shape[0]
+    for hop in range(planes - 1):
+        out[hop] = source[lax.rem(place_ref[2] + hop + 1, planes)]
 
 
 def dispatch(base, blocks, members, after=()):
@@ -436,10 +435,16 @@
     )
 
 
-def grads_kernel(count, tile, started, low, *refs):
+def both_grads(inputs, cots, up, down):
+    value, slope = gelu_both(mm(up, inputs, TT))
+    pre_grad = (mm(down, cots, NT) * slope).astype(bf16)
+    return mm(inputs, pre_grad, TT), mm(value.astype(bf16), cots, NN)
+
+
+def grads_kernel(count, tile, started, *refs):
     row_refs, cot_refs = refs[:count], refs[count : 2 * count]
     up_ref, down_ref = refs[2 * count : 2 * count + 2]
-    up_grad_ref, down_grad_ref = refs[-3:-1] if low else refs[-2:]
+    up_grad_ref, down_grad_ref = refs[-2:]
     width = up_ref.shape[1]
     inputs = [ref[...].reshape(-1, width) for ref in row_refs]
     cots = [ref[...].reshape(-1, width) for ref in cot_refs]
@@ -448,10 +453,7 @@
     for group in range(groups):
         part = slice(group * each, (group + 1) * each)
         rows, cot = jnp.concatenate(inputs[part], axis=0), jnp.concatenate(cots[part], axis=0)
-        value, slope = gelu_both(mm(up_ref[0], rows, TT))
-        pre_grad = (mm(down_ref[0], cot, NT) * slope).astype(bf16)
-        up_grad = mm(rows, pre_grad, TT)
-        down_grad = mm(value.astype(bf16), cot, NN)
+        up_grad, down_grad = both_grads(rows, cot, up_ref[0], down_ref[0])
         if group == 0 and started:
             up_grad_ref[0] = refs[2 * count + 2][0] + up_grad
             down_grad_ref[0] = refs[2 * count + 3][0] + down_grad
@@ -461,27 +463,41 @@
         else:
             up_grad_ref[0] += up_grad
             down_grad_ref[0] += down_grad
-    if low:
-        refs[-1][0] = up_grad_ref[0].astype(bf16)
-        refs[-1][1] = down_grad_ref[0].astype(bf16)
-
-
-def weight_grads(rows, cots, specs, up, down, before, tile, total, low=False, after=(), scalars=(), span=None):
+
+
+def shared_other_kernel(rows, cots, up, down, up_before, down_before, up_out, down_out, low_out):
+    width = up.shape[0]
+    grads = both_grads(rows[...].reshape(-1, width), cots[...].reshape(-1, width), up[...], down[...])
+    step = pl.program_id(0)
+    for grad, before, out in zip(grads, (up_before, down_before), (up_out, down_out)):
+
+        @pl.when(step == 0)
+        def _():
+            out[...] = before[0] + grad
+
+        @pl.when(step > 0)
+        def _():
+            out[...] += grad
+
+    @pl.when(step == pl.num_programs(0) - 1)
+    def _():
+        low_out[0] = up_out[...].astype(bf16)
+        low_out[1] = down_out[...].astype(bf16)
+
+
+def weight_grads(rows, cots, specs, up, down, before, tile, total, after=(), span=None):
     members, width, hidden = up.shape
     start, stop = span or (0, members)
-    up_spec = pl.BlockSpec((1, width, hidden), lambda e, *_: (e + start, 0, 0))
-    down_spec = pl.BlockSpec((1, hidden, width), lambda e, *_: (e + start, 0, 0))
+    up_spec = pl.BlockSpec((1, width, hidden), lambda e: (e + start, 0, 0))
+    down_spec = pl.BlockSpec((1, hidden, width), lambda e: (e + start, 0, 0))
     started = before is not None
     count = len(rows)
-    first = len(scalars) + 2 * count + 2
-    low_spec = [pl.BlockSpec((2, width, hidden), lambda *_: (0, 0, 0))] if low else []
-    kernel = functools.partial(grads_kernel, count, tile, started, low)
+    first = 2 * count + 2
     return launch(
-        (lambda place_ref, *refs: kernel(*refs)) if scalars else kernel, "weight_grads",
-        [(up.shape, f32), (down.shape, f32)] + ([((2, width, hidden), bf16)] if low else []),
+        functools.partial(grads_kernel, count, tile, started), "weight_grads", [(up.shape, f32), (down.shape, f32)],
         [*rows, *cots, up, down, *(before or ())],
-        in_specs=specs + [up_spec, down_spec] * (2 if started else 1), out_specs=[up_spec, down_spec] + low_spec,
-        grid=(stop - start,), aliases={first: 0, first + 1: 1} if started else None, after=after, scalars=scalars,
+        in_specs=specs + [up_spec, down_spec] * (2 if started else 1), out_specs=[up_spec, down_spec],
+        grid=(stop - start,), aliases={first: 0, first + 1: 1} if started else None, after=after,
         flops=12 * total * width * hidden, moved=total * width * 4,
     )
 
@@ -504,26 +520,29 @@
     specs = [spec[0] for spec in all_specs] + [spec[2] for spec in all_specs]
     total = len(blocks) * taken * PATCHES
     tile = total if total <= 8 * PATCHES else total // 2
-    return weight_grads(rows, cots, specs, up[None], down[None], before, tile, total, after=after)
-
-
-def shared_grads_hops(place, ext, cots, up, down, before, after=()):
-    planes, blocks, _, width = ext.shape
-    taken = blocks // 2
-    specs = [
-        pl.BlockSpec((1, taken, PATCHES, width), lambda e, p, hop=hop: (plane_of(hop, p, planes), p[1], 0, 0))
-        for hop in range(planes - 1)
-    ]
-    total = (planes - 1) * taken * PATCHES
-    return weight_grads(
-        [ext] * len(specs), [cots] * len(specs), specs * 2, up[None], down[None], before, taken * PATCHES, total, True,
-        after, [place],
+    return weight_grads(rows, cots, specs, up[None], down[None], before, tile, total, after)
+
+
+def shared_grads_other(ext, cots, hop, up, down, before, after=()):
+    blocks, _, _, width = ext.shape
+    steps = 2
+    spec = pl.BlockSpec((blocks // steps, 1, PATCHES, width), lambda t: (t, hop, 0, 0))
+    up_spec = pl.BlockSpec(up.shape, lambda t: (0, 0))
+    down_spec = pl.BlockSpec(down.shape, lambda t: (0, 0))
+    before_specs = [pl.BlockSpec((1, *part.shape), lambda t: (0, 0, 0)) for part in (up, down)]
+    low = (2, *up.shape)
+    total = blocks * PATCHES
+    return launch(
+        shared_other_kernel, "shared_grads_other", [(up.shape, f32), (down.shape, f32), (low, bf16)],
+        [ext, cots, up, down, *before], in_specs=[spec, spec, up_spec, down_spec] + before_specs,
+        out_specs=[up_spec, down_spec, pl.BlockSpec(low, lambda t: (0, 0, 0))],
+        grid=(steps,), after=after, flops=12 * total * up.size, moved=total * width * 4,
     )
 
 
 def shared_last_kernel(up, down, more, up_out, down_out):
-    up_out[...] = up[0] + more[0].astype(f32)
-    down_out[...] = down[0] + more[1].astype(f32)
+    up_out[...] = up[...] + more[0].astype(f32)
+    down_out[...] = down[...] + more[1].astype(f32)
 
 
 def backward_kernel(
@@ -629,21 +648,47 @@
     )
 
 
-def plane_first_kernel(first, more, side, other, keep_upper, keep_lower):
+def take_all(copies):
+    for copy in copies:
+        copy.start()
+    for copy in copies:
+        copy.wait()
+
+
+def plane_first_kernel(first, more, side, other, upper_s, lower_s, sems):
     cut = PATCHES
-    upper = lambda block: first[block, 0:cut, :].astype(f32) + more[block, 0:cut, :].astype(f32)
-    lower = lambda block: first[block, cut:, :].astype(f32) + more[block, cut:, :].astype(f32)
-    side[0], side[1] = upper(1).astype(bf16), upper(3).astype(bf16)
-    other[0], other[1] = lower(2).astype(bf16), lower(3).astype(bf16)
-    keep_upper[0], keep_upper[1] = upper(0), upper(2)
-    keep_lower[0], keep_lower[1] = lower(0), lower(1)
-
-
-def plane_second_kernel(keep_upper, keep_lower, side, other, upper, lower, upper_next, lower_next):
-    upper[...] = keep_upper[0] + side[0].astype(f32)
-    upper_next[...] = (keep_upper[1] + side[1].astype(f32)).astype(bf16)
-    lower[...] = keep_lower[0] + other[0].astype(f32)
-    lower_next[...] = (keep_lower[1] + other[1].astype(f32)).astype(bf16)
+    low = first.shape[1] - cut
+    copies = []
+    for index, source in enumerate((first, more)):
+        for place, (upper, lower) in enumerate(((1, 2), (3, 3))):
+            at = 4 * index + 2 * place
+            copies += [
+                pltpu.make_async_copy(source.at[upper, pl.ds(0, cut)], upper_s.at[index, place], sems.at[at]),
+                pltpu.make_async_copy(source.at[lower, pl.ds(cut, low)], lower_s.at[index, place], sems.at[at + 1]),
+            ]
+    take_all(copies)
+    side[...] = (upper_s[0].astype(f32) + upper_s[1].astype(f32)).astype(bf16)
+    other[...] = (lower_s[0].astype(f32) + lower_s[1].astype(f32)).astype(bf16)
+
+
+def plane_second_kernel(first, more, side, other, upper, lower, upper_next, lower_next, upper_s, lower_s, sems):
+    cut = PATCHES
+    low = first.shape[1] - cut
+    copies = []
+    for index, source in enumerate((first, more)):
+        for place, (up, down) in enumerate(((0, 0), (2, 1))):
+            at = 4 * index + 2 * place
+            copies += [
+                pltpu.make_async_copy(source.at[up, pl.ds(0, cut)], upper_s.at[index, place], sems.at[at]),
+                pltpu.make_async_copy(source.at[down, pl.ds(cut, low)], lower_s.at[index, place], sems.at[at + 1]),
+            ]
+    take_all(copies)
+    uppers = [upper_s[0, p].astype(f32) + upper_s[1, p].astype(f32) + side[p].astype(f32) for p in range(2)]
+    lowers = [lower_s[0, p].astype(f32) + lower_s[1, p].astype(f32) + other[p].astype(f32) for p in range(2)]
+    upper[...] = uppers[0]
+    upper_next[...] = uppers[1].astype(bf16)
+    lower[...] = lowers[0]
+    lower_next[...] = lowers[1].astype(bf16)
 
 
 def span_of(index, size):
@@ -728,24 +773,52 @@
     def to_other(self, value):
         return lax.ppermute(value, "expert", self.other)
 
+    def to_next(self, value):
+        return lax.ppermute(value, "dp", [(i, i ^ 1) for i in range(self.dp)])
+
     def along(self, value, hop):
         return lax.ppermute(value, "dp", [(i, (i + hop) % self.dp) for i in range(self.dp)])
+
+    def column(self, block):
+        copies = jnp.broadcast_to(block[None], (self.dp, *block.shape))
+        return lax.all_to_all(copies, "dp", split_axis=0, concat_axis=0)
+
+    def column_rest(self, column, place, after):
+        planes, rows, width = column.shape
+        (rest,) = launch(
+            pick_kernel, "pick", [((planes - 1, rows, width), column.dtype)], [column], scalars=[place], after=after,
+            moved=3 * 10**6,
+        )
+        return rest, lax.all_gather(rest, ("expert", "tensor"), axis=0)
 
     def plane_sum_first(self, first, more, after):
         width = first.shape[2]
         low = first.shape[1] - PATCHES
         return launch(
-            plane_first_kernel, "plane_first",
-            [((2, PATCHES, width), bf16), ((2, low, width), bf16), ((2, PATCHES, width), f32), ((2, low, width), f32)],
-            [first, more], after=after, moved=10 * 10**6,
-        )
-
-    def plane_sum_second(self, keep_upper, keep_lower, side, other, after):
-        _, low, width = keep_lower.shape
+            plane_first_kernel, "plane_first", [((2, PATCHES, width), bf16), ((2, low, width), bf16)],
+            [first, more], in_specs=[pl.BlockSpec(memory_space=pl.ANY)] * 2,
+            scratch=[
+                pltpu.VMEM((2, 2, PATCHES, width), bf16),
+                pltpu.VMEM((2, 2, low, width), bf16),
+                pltpu.SemaphoreType.DMA((8,)),
+            ],
+            after=after, moved=5 * 10**6,
+        )
+
+    def plane_sum_second(self, first, more, side, other, after):
+        width = first.shape[2]
+        low = first.shape[1] - PATCHES
         return launch(
             plane_second_kernel, "plane_second",
             [((PATCHES, width), f32), ((low, width), f32), ((PATCHES, width), bf16), ((low, width), bf16)],
-            [keep_upper, keep_lower, side, other], after=after, moved=6 * 10**6,
+            [first, more, side, other],
+            in_specs=[pl.BlockSpec(memory_space=pl.ANY)] * 2 + [pl.BlockSpec(memory_space=pltpu.VMEM)] * 2,
+            scratch=[
+                pltpu.VMEM((2, 2, PATCHES, width), bf16),
+                pltpu.VMEM((2, 2, low, width), bf16),
+                pltpu.SemaphoreType.DMA((8,)),
+            ],
+            after=after, moved=7 * 10**6,
         )
 
     def dense_sum(self, near, far):
@@ -820,7 +893,7 @@
     base = (lax.axis_index("expert") * members).astype(jnp.int32).reshape(1)
     everyone = ("dp", "expert", "tensor")
     total_blocks = links.dp * links.expert * links.tensor
-    full = links.paired and total_blocks * rows * width * 2 <= FULL_LIMIT
+    full = links.paired and links.dp == 4 and total_blocks * rows * width * 2 <= FULL_LIMIT
 
     condition = jax.nn.silu(embedding(timesteps, width)).astype(bf16)
     mod_cols = jnp.einsum("id,dcf->icf", condition, ada_weight, preferred_element_type=f32) + ada_bias[None]
@@ -831,37 +904,42 @@
     weight = jnp.concatenate(
         [qkv_weight.transpose(1, 2, 0).reshape(3 * local_width, width), out_weight], axis=0
     )
+    if full:
+        (weight,) = ordered([weight], [shared_cot])
     across = links.to_side(weight)
     near_shard = links.to_core(weight)
-    (across,) = ordered([across], [mod])
+    if full:
+        place = jnp.stack([base[0], *(lax.axis_index(axis) for axis in ("expert", "dp"))]).astype(jnp.int32)
+        cot_column = links.column(shared_cot)
+        cot_other = links.to_other(shared_cot)
+        across, cot_other = ordered([across, cot_other], [mod])
+        cot_side = links.to_side(ordered([shared_cot], [across])[0])
+        cot_corner = links.to_other(cot_side)
+    else:
+        (across,) = ordered([across], [mod])
     shards = (weight, near_shard, across, links.to_core(across))
     router_t = router_weight.T
     pairs = jnp.concatenate([routes.T, places.T], axis=0)
 
-    attn_in, qkv, context, attn_out, ext = attention_forward(
-        tokens, mod, router_t, pairs, shards, local_width
-    )
+    whole = slice(None)
+    attn_in, qkv, context, attn_out, ext = attention_forward(tokens, mod, router_t, pairs, shards, local_width)
     feed = (shared_up, shared_down, expert_up, expert_down)
     backward = functools.partial(
         attention_backward, cond=own_condition, tokens=tokens, cotangent=cotangent, mod=mod, router_t=router_t,
         pairs=pairs, attn_in=attn_in, qkv=qkv, context=context, attn_out=attn_out, ext=ext, shards=shards,
         local_width=local_width,
     )
-    whole = slice(None)
     if full:
-        place = jnp.stack([base[0], *(lax.axis_index(axis) for axis in ("expert", "dp"))]).astype(jnp.int32)
-        cots = lax.all_gather(shared_cot, everyone, axis=0)
-        cot_side, cot_other = links.to_side(shared_cot), links.to_other(shared_cot)
         ext_side, ext_other = links.to_side(ext), links.to_other(ext)
-        everything = lax.all_gather(ext, everyone, axis=0)
         cut = PATCHES // 2 + EXTRA
-        ext_corner = (links.to_side(ext_other[:cut]), links.to_other(ext_side[cut:]))
-        cot_corner = links.to_other(ordered([cot_side], [ext])[0])
+        ext_cuts = (ext_other[:cut], ext_side[cut:])
+        ext_corner = (links.to_side(ext_cuts[0]), links.to_other(ext_cuts[1]))
         cot_mine = assemble(
             (HALF, PATCHES, width), bf16, [shared_cot, cot_side, cot_other, cot_corner],
-            [(index, whole, index) for index in range(HALF)], after=[ext_side],
+            [(index, whole, index) for index in range(HALF)], after=ext_cuts,
         )
         cot_near = links.to_core(cot_mine)
+        ext_column = links.column(ordered([ext], [ext_side, ext_other])[0])
         ext_mine = assemble(
             (HALF, PATCHES + EXTRA, width), bf16, [ext, ext_side, ext_other, *ext_corner],
             [(index, whole, index) for index in range(3)]
@@ -869,45 +947,45 @@
         )
         ext_near = links.to_core(ext_mine)
         own = (Blocks.apart(ext_mine, cot_mine), Blocks.apart(ext_near, cot_near))
-        first, second = experts_both(base, own, *feed, (0, 1, 4, 5))
+        cot_rest, cots = links.column_rest(cot_column, place, [cot_mine])
+        first, second = experts_both(base, own, *feed, (0, 1, 4, 5), after=[cot_rest])
+        ext_rest, exts = links.column_rest(ext_column, place, [first])
         moved = links.to_core(second)
-        slots = dispatch(base, own, members, after=[first])
-        side, other, keep_upper, keep_lower = links.plane_sum_first(first, moved, after=[slots[0]])
+        slots = dispatch(base, own, members, after=[first, ext_rest])
+        side, other = links.plane_sum_first(first, moved, after=[slots[0]])
         from_side, from_other = links.to_side(side), links.to_other(other)
         routed = routed_grads([slots], expert_up, expert_down, None, after=[side])
         upper, lower, upper_next, lower_next = links.plane_sum_second(
-            keep_upper, keep_lower, from_side, from_other, after=[routed[0]]
+            first, moved, from_side, from_other, after=[routed[0]]
         )
         upper_more, lower_more = links.to_other(upper_next), links.to_side(lower_next)
-        shared = shared_grads(own, 2, shared_up, shared_down, None, after=[upper])
+        shared = shared_grads(own, HALF, shared_up, shared_down, None, after=[upper, cots])
         output, tokens_grad, small, near, far = backward(
             upper, upper_more, lower, lower_more, after=[shared[0]]
         )
         dense = links.dense_sum(near, far)
         next(dense)
         small_all = lax.all_gather(small, everyone, axis=0)
-        everything, cots = ordered([everything, cots], [small])
-        everything, cots = (
-            value.reshape(links.dp, links.expert * links.tensor, *value.shape[1:]) for value in (everything, cots)
-        )
-        slots = dispatch_hops(place, everything, cots, members)
+        *shared, sent = shared_grads_other(exts, cots, 1, shared_up, shared_down, shared, after=[small])
+        shared_more = links.to_next(sent)
+        step = dense.send([sent])
+        slots = dispatch_hops(base, exts, cots, members, after=[step])
         step = dense.send([slots[0]])
-        *shared, sent = shared_grads_hops(place, everything, cots, shared_up, shared_down, shared, after=[step])
-        step = dense.send([sent])
-        middle = members // 2
-        routed = routed_grads([slots], expert_up, expert_down, routed, after=[step], span=(0, middle))
-        step = dense.send([routed[0]])
-        shared_more = links.to_other(ordered([sent], [step])[0])
-        routed = routed_grads([slots], expert_up, expert_down, routed, after=[step], span=(middle, members))
-        step = dense.send([routed[0]])
-        step = dense.send([step])
+        for span in ((0, 2), (2, 3)):
+            routed = routed_grads([slots], expert_up, expert_down, routed, after=[step], span=span)
+            step = dense.send([routed[0]])
         shared = launch(
             shared_last_kernel, "shared_last", [(shared_up.shape, f32), (shared_down.shape, f32)],
             [*shared, shared_more], after=[step], moved=12 * 10**6,
         )
-        qkv_grad, out_grad = dense.send([shared[0]])
+        routed = routed_grads([slots], expert_up, expert_down, routed, after=[shared[0]], span=(3, members))
+        step = dense.send([routed[0]])
+        qkv_grad, out_grad = dense.send([step])
         (small_all,) = ordered([small_all], [routed[0]])
-        routes_all = everything[:, :, PATCHES, : TOPK * PATCHES].reshape(-1, TOPK * PATCHES)
+        routes_all = jnp.concatenate(
+            [value[..., PATCHES, : TOPK * PATCHES].reshape(-1, TOPK * PATCHES) for value in (ext_mine, ext_near, exts)],
+            axis=0,
+        )
     else:
         shift = lax.axis_index("expert") * links.tensor
         gather = lambda block: jnp.roll(

time: 428 us -> 419 us (0.979); the launches traced: 430 us -> 413 us
  waiting for transfers between devices: 101 us -> 55.4 us
  local copies, waits for them, and re-layouts: 18.4 us -> 34.3 us
  starting transfers between devices: 33.3 us -> 44 us
  Pallas kernels: 241 us -> 250 us
  blocking collectives: 7.95 us -> 0 us
    ppermute x8, waiting for transfers between devices: 63.2 us -> 23.8 us  [to_side(): return lax.ppermute(value, 'tensor', self.side)]
    all_to_all x0 -> x3, starting transfers between devices: none -> 14 us  [the longest x2 9.83 us: column(): return lax.all_to_all(copies, 'dp', split_axis=0, concat_axis=0)]
    pallas_call x26 -> x29, Pallas kernels: 241 us -> 250 us  [launch(): pl.pallas_call(body, out_shape=tuple((jax.ShapeDtypeStruct(*out) for out...]
    all_to_all x1 -> x0, blocking collectives: 7.95 us -> none  [local(): lax.all_to_all(mod_cols, 'tensor', split_axis=0, concat_axis=2, tiled=True)]
    ppermute x6, waiting for transfers between devices: 7.71 us -> 0.02 us  [along(): lax.ppermute(value, 'dp', [(i, (i + hop) % self.dp) for i in range(self.d...]
    ppermute x6, waiting for transfers between devices: 6.27 us -> 1.16 us  [to_core(): return lax.ppermute(value, 'tensor', self.core)]
    unnamed x74 -> x84, local copies, waits for them, and re-layouts: 13.9 us -> 18.6 us
    ppermute x10 -> x9, waiting for transfers between devices: 23.9 us -> 28.5 us  [to_other(): return lax.ppermute(value, 'expert', self.other)]
  transfers between devices with their start and end apart: 33 -> 36, of which waited for: 9 -> 12; matrix products, arithmetic and copies ran while one was open for 3% -> 7% of each run, Pallas kernels for 55% -> 59%
where the time goes in v4:
time: 419 us; the launch traced here: 413 us
  Pallas kernels  250 us (60%)
  waiting for transfers between devices  55.4 us (13%)
  starting transfers between devices  44 us (11%)
  local copies, waits for them, and re-layouts  34.3 us (8%)
  between operations  14.6 us (3%)
  other arithmetic  9.18 us (2%)
  matrix products  4.64 us (1%)
    pallas_call x29, Pallas kernels, launch(): pl.pallas_call(body, out_shape=tuple((jax.ShapeDtypeStruct(*out) for out...  250 us
    ppermute x9, waiting for transfers between devices, to_other(): return lax.ppermute(value, 'expert', self.other)  28.5 us
    ppermute x8, waiting for transfers between devices, to_side(): return lax.ppermute(value, 'tensor', self.side)  23.8 us
    unnamed x84, local copies, waits for them, and re-layouts  18.6 us
    ppermute x9, starting transfers between devices, to_other(): return lax.ppermute(value, 'expert', self.other)  12.3 us
    all_to_all x2, starting transfers between devices, column(): return lax.all_to_all(copies, 'dp', split_axis=0, concat_axis=0)  9.83 us
  transfers between devices with their start and end apart: 36, of which 12 were waited for; matrix products, arithmetic and copies ran while one was open for 7% of the time, Pallas kernels for 59%

profile of v4, /device:TPU:0, one launch (start us, length us, event | category | flops | bytes accessed | tf_op | source)
XLA Modules:
  0.0 412.6 jit_solution(4696164973508283531)
XLA Ops:
  10.6 4.2 %all-to-all-start = ((f32[4,6,192]{2,1,0:T(8,128)}), f32[4,6,192]{2,1,0:T(8,128)S(1)}, u32[]{:S(2)}, u32[]{:S(2)}) async-start(f32[4,6,192]{2,1,0:T(8,128)} %copy.43), calls=%async_computation | async-start | bytes 65536 | tf_op jit(solution)/shard_map/all_to_all | solution.py:900
  14.8 2.0 pad_maximum_fusion.refs_0_
  16.8 1.9 all-to-all-done
  21.1 2.0 collective-permute-start.2
  24.4 5.0 %all-to-all-start.1 = ((bf16[4,256,768]{2,1,0:T(8,128)(2,1)}), bf16[4,256,768]{2,1,0:T(8,128)(2,1)S(1)}, u32[]{:S(2)}, u32[]{:S(2)}) async-start(bf16[4,256,768]{2,1,0:T(8,128)(2,1)} %broadcast_in_dim.8), calls=%async_computation.1 | async-start | bytes 3145728 | tf_op jit(solution)/shard_map/all_to_all | solution.py:784
  32.2 15.8 %collective-permute-done.1.refs_0_ = bf16[768,768]{1,0:T(8,128)(2,1)S(1)} collective-permute-done((bf16[768,768]{1,0:T(8,128)(2,1)}, bf16[768,768]{1,0:T(8,128)(2,1)S(1)}, u32[]{:S(2)}, u32[]{:S(2)}) %collective-permute-start.1) | collective-permute-done | bytes 1179680 | tf_op jit(solution)/shard_map/ppermute | solution.py:771
  53.1 7.4 %attention_forward.1 = (bf16[256,768]{1,0:T(8,128)(2,1)}, bf16[3,256,768]{2,1,0:T(8,128)(2,1)}, bf16[256,768]{1,0:T(8,128)(2,1)}, f32[256,768]{1,0:T(8,128)}, bf16[272,768]{1,0:T(8,128)(2,1)}) custom-call(bf16[256,768]{1,0:T(8,128)(2,1)} %refs_5_.1, f32[6,768]{1,0:T(8,128)} %squeeze.10.refs_2_.refs_1_.refs_7_, bf16[8,768]{1,0:T(8,128)(2,1)} %bitcast.52, ...), custom_call_target="tpu_custom_call" | custom-call | flops 5000000000 | bytes 9000000 | tf_op jit(solution)/shard_map/attention_forward/pallas_call | solution.py:89
  60.5 2.0 collective-permute-start.5
  64.7 8.4 %collective-permute-done.5.refs_2_ = bf16[272,768]{1,0:T(8,128)(2,1)S(1)} collective-permute-done((bf16[272,768]{1,0:T(8,128)(2,1)}, bf16[272,768]{1,0:T(8,128)(2,1)S(1)}, u32[]{:S(2)}, u32[]{:S(2)}) %collective-permute-start.5) | collective-permute-done | bytes 417824 | tf_op jit(solution)/shard_map/ppermute | solution.py:774
  74.8 6.2 %collective-permute-done.9.refs_3_ = bf16[256,768]{1,0:T(8,128)(2,1)S(1)} collective-permute-done((bf16[256,768]{1,0:T(8,128)(2,1)S(1)}, bf16[256,768]{1,0:T(8,128)(2,1)S(1)}, u32[]{:S(2)}, u32[]{:S(2)}) %collective-permute-start.9) | collective-permute-done | bytes 393248 | tf_op jit(solution)/shard_map/ppermute | solution.py:774
  81.8 2.5 assemble.3.refs_2_.refs_3_
  85.5 2.5 pick.2.refs_11_
  88.7 1.7 collective-permute-start.7
  90.4 4.6 %collective-permute-done.7.refs_4_ = bf16[128,768]{1,0:T(8,128)(2,1)S(1)} collective-permute-done((bf16[128,768]{1,0:T(8,128)(2,1)}, bf16[128,768]{1,0:T(8,128)(2,1)S(1)}, u32[]{:S(2)}, u32[]{:S(2)}) %collective-permute-start.7) | collective-permute-done | bytes 196640 | tf_op jit(solution)/shard_map/ppermute | solution.py:774
  96.4 2.7 assemble.2.refs_1_.refs_2_.refs_0_
  100.4 2.3 broadcast_in_dim.9
  102.7 4.8 %all-to-all-start.2 = ((bf16[4,272,768]{2,1,0:T(8,128)(2,1)}), bf16[4,272,768]{2,1,0:T(8,128)(2,1)S(1)}, u32[]{:S(2)}, u32[]{:S(2)}) async-start(bf16[4,272,768]{2,1,0:T(8,128)(2,1)} %broadcast_in_dim.9), calls=%async_computation.2 | async-start | bytes 3342336 | tf_op jit(solution)/shard_map/all_to_all | solution.py:784
  107.6 45.6 %experts_both.1 = (bf16[4,528,768]{2,1,0:T(8,128)(2,1)}, bf16[4,528,768]{2,1,0:T(8,128)(2,1)}) custom-call(s32[1]{0:T(128)} %bitcast.refs_0_, bf16[4,272,768]{2,1,0:T(8,128)(2,1)} %assemble.2.refs_1_.refs_2_.refs_0_, bf16[4,272,768]{2,1,0:T(8,128)(2,1)} %assemble.2.refs_1_.refs_2_.refs_0_, bf16[4,256,768]{2,1,0:T(8,128)(2,1)} %assemble.3.refs_2_.refs_3_, ...), custom_call_target="tpu_custom_call" | custom-call | flops 30000001024 | bytes 30000000 | tf_op jit(solution)/shard_map/experts_both/pallas_call | solution.py:89
  154.4 2.6 pick.3.refs_8_
  157.7 7.5 %dispatch.1 = (bf16[4,640,768]{2,1,0:T(8,128)(2,1)}, bf16[4,640,768]{2,1,0:T(8,128)(2,1)}) custom-call(s32[1]{0:T(128)} %bitcast.refs_0_, bf16[4,272,768]{2,1,0:T(8,128)(2,1)} %assemble.2.refs_1_.refs_2_.refs_0_, bf16[4,272,768]{2,1,0:T(8,128)(2,1)} %assemble.2.refs_1_.refs_2_.refs_0_, bf16[4,256,768]{2,1,0:T(8,128)(2,1)} %assemble.3.refs_2_.refs_3_, ...), custom_call_target="tpu_custom_call" | custom-call | flops 8000000000 | bytes 16000000 | tf_op jit(solution)/shard_map/dispatch/pallas_call | solution.py:89
  166.8 3.6 plane_first.1
  173.5 19.7 %weight_grads.5 = (f32[4,768,768]{2,1,0:T(8,128)}, f32[4,768,768]{2,1,0:T(8,128)}) custom-call(bf16[4,640,768]{2,1,0:T(8,128)(2,1)} %get-tuple-element.70.refs_2_.refs_0_, bf16[4,640,768]{2,1,0:T(8,128)(2,1)} %get-tuple-element.73.refs_1_, bf16[4,768,768]{2,1,0:T(8,128)(2,1)} %refs_2_.9, bf16[4,768,768]{2,1,0:T(8,128)(2,1)} %refs_3_.9, ...), custom_call_target="tpu_custom_call" | custom-call | flops 18119393280 | bytes 7864320 | tf_op jit(solution)/shard_map/weight_grads/pallas_call | solution.py:89
  193.1 6.5 %collective-permute-done.13.refs_2_ = bf16[2,256,768]{2,1,0:T(8,128)(2,1)S(1)} collective-permute-done((bf16[2,256,768]{2,1,0:T(8,128)(2,1)}, bf16[2,256,768]{2,1,0:T(8,128)(2,1)S(1)}, u32[]{:S(2)}, u32[]{:S(2)}) %collective-permute-start.13) | collective-permute-done | bytes 786464 | tf_op jit(solution)/shard_map/ppermute | solution.py:771
  199.6 3.3 collective-permute-done.14.refs_3_
  203.8 4.9 %plane_second.1 = (f32[256,768]{1,0:T(8,128)}, f32[272,768]{1,0:T(8,128)}, bf16[256,768]{1,0:T(8,128)(2,1)}, bf16[272,768]{1,0:T(8,128)(2,1)}) custom-call(bf16[4,528,768]{2,1,0:T(8,128)(2,1)} %get-tuple-element.68.refs_2_.refs_7_.refs_0_, bf16[4,528,768]{2,1,0:T(8,128)(2,1)} %copy-done.2, bf16[2,256,768]{2,1,0:T(8,128)(2,1)} %copy-done.17, ...), custom_call_target="tpu_custom_call" | custom-call | bytes 7000000 | tf_op jit(solution)/shard_map/plane_second/pallas_call | solution.py:89
  209.0 1.7 collective-permute-start.16
  210.7 15.3 %weight_grads.6 = (f32[1,768,768]{2,1,0:T(8,128)}, f32[1,768,768]{2,1,0:T(8,128)}) custom-call(bf16[4,272,768]{2,1,0:T(8,128)(2,1)} %assemble.2.refs_1_.refs_2_.refs_0_, bf16[4,272,768]{2,1,0:T(8,128)(2,1)} %collective-permute-done.10.refs_4_.refs_5_.refs_1_, bf16[4,256,768]{2,1,0:T(8,128)(2,1)} %assemble.3.refs_2_.refs_3_, ...), custom_call_target="tpu_custom_call" | custom-call | flops 14495514624 | bytes 6291456 | tf_op jit(solution)/shard_map/weight_grads/pallas_call | solution.py:89
  226.0 2.8 collective-permute-done.15.refs_1_
  230.9 16.6 %attention_backward.1 = (bf16[256,768]{1,0:T(8,128)(2,1)}, f32[256,768]{1,0:T(8,128)}, f32[16,768]{1,0:T(8,128)}, bf16[2,768,768]{2,1,0:T(8,128)(2,1)}, bf16[2,768,768]{2,1,0:T(8,128)(2,1)}) custom-call(f32[256,768]{1,0:T(8,128)} %get-tuple-element.75.refs_6_.refs_0_, bf16[256,768]{1,0:T(8,128)(2,1)} %copy-done.39, f32[272,768]{1,0:T(8,128)} %get-tuple-element.77.refs_2_, ...), custom_call_target="tpu_custom_call" | custom-call | flops 10000000000 | bytes 16000000 | tf_op jit(solution)/shard_map/attention_backward/pallas_call | solution.py:89
  249.7 19.0 %shared_grads_other.1 = (f32[768,768]{1,0:T(8,128)}, f32[768,768]{1,0:T(8,128)}, bf16[2,768,768]{2,1,0:T(8,128)(2,1)}) custom-call(bf16[8,3,272,768]{3,2,1,0:T(8,128)(2,1)} %bitcast.43, bf16[8,3,256,768]{3,2,1,0:T(8,128)(2,1)} %bitcast.47, bf16[768,768]{1,0:T(8,128)(2,1)} %refs_2_.6, bf16[768,768]{1,0:T(8,128)(2,1)} %refs_3_.6, ...), custom_call_target="tpu_custom_call" | custom-call | flops 14495514624 | bytes 6291456 | tf_op jit(solution)/shard_map/shared_grads_other/pallas_call | solution.py:89
  268.6 1.8 collective-permute-start.22
  270.4 4.3 %dense_first.1 = (bf16[384,768]{1,0:T(8,128)(2,1)}, bf16[2,192,768]{2,1,0:T(8,128)(2,1)}, f32[384,768]{1,0:T(8,128)}, f32[2,192,768]{2,1,0:T(8,128)}) custom-call(s32[2]{0:T(128)} %pad_add_fusion.2.refs_0_, bf16[2,768,768]{2,1,0:T(8,128)(2,1)} %get-tuple-element.87.refs_1_, bf16[2,768,768]{2,1,0:T(8,128)(2,1)} %collective-permute-done.17.refs_2_, ...), custom_call_target="tpu_custom_call" | custom-call | bytes 8000000 | tf_op jit(solution)/shard_map/dense_first/pallas_call | solution.py:89
  277.7 18.4 %dispatch_hops.1 = (bf16[4,1920,768]{2,1,0:T(8,128)(2,1)}, bf16[4,1920,768]{2,1,0:T(8,128)(2,1)}) custom-call(s32[1]{0:T(128)} %bitcast.refs_0_, bf16[8,3,272,768]{3,2,1,0:T(8,128)(2,1)} %bitcast.44, bf16[8,3,256,768]{3,2,1,0:T(8,128)(2,1)} %bitcast.48, f32[384,768]{1,0:T(8,128)} %get-tuple-element.91.refs_3_.refs_1_), custom_call_target="tpu_custom_call" | custom-call | flops 24000000000 | bytes 48000000 | tf_op jit(solution)/shard_map/dispatch_hops/pallas_call | solution.py:89
  296.1 1.7 slice_reduce_fusion.1
  300.9 3.3 dense_second.1
  305.4 27.0 %weight_grads.7 = (f32[4,768,768]{2,1,0:T(8,128)}, f32[4,768,768]{2,1,0:T(8,128)}) custom-call(bf16[4,1920,768]{2,1,0:T(8,128)(2,1)} %get-tuple-element.92.refs_5_.refs_0_, bf16[4,1920,768]{2,1,0:T(8,128)(2,1)} %get-tuple-element.93.refs_1_, bf16[4,768,768]{2,1,0:T(8,128)(2,1)} %refs_2_.9, ...), custom_call_target="tpu_custom_call", output_to_operand_aliasing={{0}: (4, {}), {1}: (5, {})} | custom-call | flops 27179089920 | bytes 11796480 | tf_op jit(solution)/shard_map/weight_grads/pallas_call | solution.py:89
  333.2 2.4 dense_third.1
  336.0 2.6 collective-permute-start.24
  338.6 2.4 collective-permute-start.25
  341.0 16.4 %weight_grads.8 = (f32[4,768,768]{2,1,0:T(8,128)}, f32[4,768,768]{2,1,0:T(8,128)}) custom-call(bf16[4,1920,768]{2,1,0:T(8,128)(2,1)} %get-tuple-element.92.refs_5_.refs_0_, bf16[4,1920,768]{2,1,0:T(8,128)(2,1)} %get-tuple-element.93.refs_1_, bf16[4,768,768]{2,1,0:T(8,128)(2,1)} %refs_2_.9, ...), custom_call_target="tpu_custom_call", output_to_operand_aliasing={{0}: (4, {}), {1}: (5, {})} | custom-call | flops 13589544960 | bytes 5898240 | tf_op jit(solution)/shard_map/weight_grads/pallas_call | solution.py:89
  358.2 1.9 dense_fourth.1.refs_3_.refs_1_
  361.2 1.7 collective-permute-start.26
  364.3 5.5 %shared_last.1 = (f32[768,768]{1,0:T(8,128)}, f32[768,768]{1,0:T(8,128)}) custom-call(f32[768,768]{1,0:T(8,128)} %get-tuple-element.107.refs_0_, f32[768,768]{1,0:T(8,128)} %get-tuple-element.108.refs_1_, bf16[2,768,768]{2,1,0:T(8,128)(2,1)} %copy-done.11, bf16[96,768]{1,0:T(8,128)(2,1)} %dense_fourth.1.refs_3_.refs_1_), custom_call_target="tpu_custom_call" | custom-call | bytes 12000000 | tf_op jit(solution)/shard_map/shared_last/pallas_call | solution.py:89
  369.8 16.5 %weight_grads.9 = (f32[4,768,768]{2,1,0:T(8,128)}, f32[4,768,768]{2,1,0:T(8,128)}) custom-call(bf16[4,1920,768]{2,1,0:T(8,128)(2,1)} %get-tuple-element.92.refs_5_.refs_0_, bf16[4,1920,768]{2,1,0:T(8,128)(2,1)} %get-tuple-element.93.refs_1_, bf16[4,768,768]{2,1,0:T(8,128)(2,1)} %refs_2_.9, ...), custom_call_target="tpu_custom_call", output_to_operand_aliasing={{0}: (4, {}), {1}: (5, {})} | custom-call | flops 13589544960 | bytes 5898240 | tf_op jit(solution)/shard_map/weight_grads/pallas_call | solution.py:89
  387.0 2.0 dense_fifth.1.refs_1_.refs_3_
  395.3 3.4 fusion
  398.7 3.1 collective-permute-done.29.refs_2_
  402.7 2.9 dense_last.1
  (172 shorter events, 55.6 us)
Async XLA Ops:
  7.2 7.6 %copy-start.15 = (bf16[768,3,192]{0,2,1:T(8,128)(2,1)S(1)}, bf16[768,3,192]{0,2,1:T(8,128)(2,1)}, u32[]{:S(2)}) copy-start(bf16[768,3,192]{0,2,1:T(8,128)(2,1)} %param.19) | copy-start | bytes 2654212
  7.2 12.1 %copy-start.23 = (bf16[256,768]{1,0:T(8,128)(2,1)S(1)}, bf16[256,768]{1,0:T(8,128)(2,1)}, u32[]{:S(2)}) copy-start(bf16[256,768]{1,0:T(8,128)(2,1)} %refs_6_.1) | copy-start | bytes 1179652
  10.6 8.2 %all-to-all-start = ((f32[4,6,192]{2,1,0:T(8,128)}), f32[4,6,192]{2,1,0:T(8,128)S(1)}, u32[]{:S(2)}, u32[]{:S(2)}) async-start(f32[4,6,192]{2,1,0:T(8,128)} %copy.43), calls=%async_computation | async-start | bytes 65536 | tf_op jit(solution)/shard_map/all_to_all | solution.py:900
  20.2 27.8 %collective-permute-start.1 = (bf16[768,768]{1,0:T(8,128)(2,1)}, bf16[768,768]{1,0:T(8,128)(2,1)S(1)}, u32[]{:S(2)}, u32[]{:S(2)}) collective-permute-start(bf16[768,768]{1,0:T(8,128)(2,1)} %ordered.5.refs_4_.refs_15_), channel_id=1, source_target_pairs={{0,2},{1,3},{2,0},{3,1},{4,6},{5,7},{6,4},{7,5},{8,10},{9,11},{10,... | collective-permute-start | bytes 3538952 | tf_op jit(solution)/shard_map/ppermute | solution.py:771
  21.1 11.1 %collective-permute-start.2 = (bf16[256,768]{1,0:T(8,128)(2,1)S(1)}, bf16[256,768]{1,0:T(8,128)(2,1)S(1)}, u32[]{:S(2)}, u32[]{:S(2)}) collective-permute-start(bf16[256,768]{1,0:T(8,128)(2,1)S(1)} %copy-done.3), channel_id=1, source_target_pairs={{0,4},{4,0},{1,5},{5,1},{2,6},{6,2},{3,7},{7,3},{8,12},{12,8},{9,1... | collective-permute-start | bytes 1179656 | tf_op jit(solution)/shard_map/ppermute | solution.py:774
  24.4 24.6 %copy-start.35 = (s32[256,2]{0,1:T(2,128)S(1)}, s32[256,2]{0,1:T(2,128)}, u32[]{:S(2)}) copy-start(s32[256,2]{0,1:T(2,128)} %param.27) | copy-start | bytes 6148
  24.4 24.6 %copy-start.36 = (s32[256,2]{0,1:T(2,128)S(1)}, s32[256,2]{0,1:T(2,128)}, u32[]{:S(2)}) copy-start(s32[256,2]{0,1:T(2,128)} %param.26) | copy-start | bytes 6148
  24.4 59.9 %all-to-all-start.1 = ((bf16[4,256,768]{2,1,0:T(8,128)(2,1)}), bf16[4,256,768]{2,1,0:T(8,128)(2,1)S(1)}, u32[]{:S(2)}, u32[]{:S(2)}) async-start(bf16[4,256,768]{2,1,0:T(8,128)(2,1)} %broadcast_in_dim.8), calls=%async_computation.1 | async-start | bytes 3145728 | tf_op jit(solution)/shard_map/all_to_all | solution.py:784
  29.4 181.3 %all-gather.7.cloned.1.call-start = ((), (), s32[]{:S(2)}) async-start(), calls=%async_computation.3 | async-start | bytes 10616832 | tf_op jit(solution)/shard_map/all_gather | solution.py:792
  30.8 20.2 %collective-permute-start = (bf16[768,768]{1,0:T(8,128)(2,1)}, bf16[768,768]{1,0:T(8,128)(2,1)}, u32[]{:S(2)}, u32[]{:S(2)}) collective-permute-start(bf16[768,768]{1,0:T(8,128)(2,1)} %ordered.5.refs_4_.refs_15_), channel_id=1, source_target_pairs={{0,1},{1,0},{2,3},{3,2},{4,5},{5,4},{6,7},{7,6},{8,9},{9,8},{10,11... | collective-permute-start | bytes 3538952 | tf_op jit(solution)/shard_map/ppermute | solution.py:768
  32.2 15.8 %copy-start.13 = (bf16[256,768]{1,0:T(8,128)(2,1)}, bf16[256,768]{1,0:T(8,128)(2,1)S(1)}, u32[]{:S(2)}) copy-start(bf16[256,768]{1,0:T(8,128)(2,1)S(1)} %collective-permute-done.2.refs_1_) | copy-start | bytes 1179652
  49.0 3.1 collective-permute-start.3
  50.4 12.6 %collective-permute-start.8 = (bf16[256,768]{1,0:T(8,128)(2,1)}, bf16[256,768]{1,0:T(8,128)(2,1)S(1)}, u32[]{:S(2)}, u32[]{:S(2)}) collective-permute-start(bf16[256,768]{1,0:T(8,128)(2,1)} %ordered.7), channel_id=1, source_target_pairs={{0,2},{1,3},{2,0},{3,1},{4,6},{5,7},{6,4},{7,5},{8,10},{9,11},{10,... | collective-permute-start | bytes 1179656 | tf_op jit(solution)/shard_map/ppermute | solution.py:771
  60.5 12.7 %collective-permute-start.5 = (bf16[272,768]{1,0:T(8,128)(2,1)}, bf16[272,768]{1,0:T(8,128)(2,1)S(1)}, u32[]{:S(2)}, u32[]{:S(2)}) collective-permute-start(bf16[272,768]{1,0:T(8,128)(2,1)} %get-tuple-element.66.refs_0_.refs_14_), channel_id=1, source_target_pairs={{0,4},{4,0},{1,5},{5,1},{2,6},{6,2},{3,7},{7,3},{8,12},{12,8},{9,1... | collective-permute-start | bytes 1253384 | tf_op jit(solution)/shard_map/ppermute | solution.py:774
  62.4 11.6 %collective-permute-start.4 = (bf16[272,768]{1,0:T(8,128)(2,1)}, bf16[272,768]{1,0:T(8,128)(2,1)S(1)}, u32[]{:S(2)}, u32[]{:S(2)}) collective-permute-start(bf16[272,768]{1,0:T(8,128)(2,1)} %get-tuple-element.66.refs_0_.refs_14_), channel_id=1, source_target_pairs={{0,2},{1,3},{2,0},{3,1},{4,6},{5,7},{6,4},{7,5},{8,10},{9,11},{10,... | collective-permute-start | bytes 1253384 | tf_op jit(solution)/shard_map/ppermute | solution.py:771
  63.0 18.0 %copy-start.21 = (bf16[256,768]{1,0:T(8,128)(2,1)}, bf16[256,768]{1,0:T(8,128)(2,1)S(1)}, u32[]{:S(2)}) copy-start(bf16[256,768]{1,0:T(8,128)(2,1)S(1)} %collective-permute-done.8.refs_1_) | copy-start | bytes 1179652
  63.0 18.0 %collective-permute-start.9 = (bf16[256,768]{1,0:T(8,128)(2,1)S(1)}, bf16[256,768]{1,0:T(8,128)(2,1)S(1)}, u32[]{:S(2)}, u32[]{:S(2)}) collective-permute-start(bf16[256,768]{1,0:T(8,128)(2,1)S(1)} %collective-permute-done.8.refs_1_), channel_id=1, source_target_pairs={{0,4},{4,0},{1,5},{5,1},{2,6},{6,2},{3,7},{7,3},{8,12},{12,8},{9,1... | collective-permute-start | bytes 1179656 | tf_op jit(solution)/shard_map/ppermute | solution.py:774
  73.1 11.2 %copy-start.9 = (bf16[272,768]{1,0:T(8,128)(2,1)}, bf16[272,768]{1,0:T(8,128)(2,1)S(1)}, u32[]{:S(2)}) copy-start(bf16[272,768]{1,0:T(8,128)(2,1)S(1)} %collective-permute-done.5.refs_2_) | copy-start | bytes 1253380
  74.1 10.3 %copy-start.10 = (bf16[272,768]{1,0:T(8,128)(2,1)}, bf16[272,768]{1,0:T(8,128)(2,1)S(1)}, u32[]{:S(2)}) copy-start(bf16[272,768]{1,0:T(8,128)(2,1)S(1)} %collective-permute-done.4.refs_1_) | copy-start | bytes 1253380
  84.3 3.7 copy-start.14
  88.0 11.2 %copy-start.6 = (bf16[4,256,768]{2,1,0:T(8,128)(2,1)S(1)}, bf16[4,256,768]{2,1,0:T(8,128)(2,1)}, u32[]{:S(2)}) copy-start(bf16[4,256,768]{2,1,0:T(8,128)(2,1)} %assemble.3.refs_2_.refs_3_) | copy-start | bytes 4718596
  88.0 11.7 %copy-start.12 = (bf16[272,768]{1,0:T(8,128)(2,1)S(1)}, bf16[272,768]{1,0:T(8,128)(2,1)}, u32[]{:S(2)}) copy-start(bf16[272,768]{1,0:T(8,128)(2,1)} %get-tuple-element.66.refs_0_.refs_14_) | copy-start | bytes 1253380
  88.1 7.0 %collective-permute-start.6 = (bf16[144,768]{1,0:T(8,128)(2,1)S(1)}, bf16[144,768]{1,0:T(8,128)(2,1)S(1)}, u32[]{:S(2)}, u32[]{:S(2)}) collective-permute-start(bf16[144,768]{1,0:T(8,128)(2,1)S(1)} %copy-done.14), channel_id=1, source_target_pairs={{0,2},{1,3},{2,0},{3,1},{4,6},{5,7},{6,4},{7,5},{8,10},{9,11},{10,... | collective-permute-start | bytes 663560 | tf_op jit(solution)/shard_map/ppermute | solution.py:771
  88.7 6.3 %collective-permute-start.7 = (bf16[128,768]{1,0:T(8,128)(2,1)}, bf16[128,768]{1,0:T(8,128)(2,1)S(1)}, u32[]{:S(2)}, u32[]{:S(2)}) collective-permute-start(bf16[128,768]{1,0:T(8,128)(2,1)} %slice.40.refs_5_), channel_id=1, source_target_pairs={{0,4},{4,0},{1,5},{5,1},{2,6},{6,2},{3,7},{7,3},{8,12},{12,8},{9,1... | collective-permute-start | bytes 589832 | tf_op jit(solution)/shard_map/ppermute | solution.py:774
  99.1 8.5 %collective-permute-start.10 = (bf16[4,272,768]{2,1,0:T(8,128)(2,1)}, bf16[4,272,768]{2,1,0:T(8,128)(2,1)}, u32[]{:S(2)}, u32[]{:S(2)}) collective-permute-start(bf16[4,272,768]{2,1,0:T(8,128)(2,1)} %assemble.2.refs_1_.refs_2_.refs_0_), channel_id=1, source_target_pairs={{0,1},{1,0},{2,3},{3,2},{4,5},{5,4},{6,7},{7,6},{8,9},{9,8},{10,11... | collective-permute-start | bytes 5013512 | tf_op jit(solution)/shard_map/ppermute | solution.py:768
  99.2 8.4 %collective-permute-start.11 = (bf16[4,256,768]{2,1,0:T(8,128)(2,1)S(1)}, bf16[4,256,768]{2,1,0:T(8,128)(2,1)}, u32[]{:S(2)}, u32[]{:S(2)}) collective-permute-start(bf16[4,256,768]{2,1,0:T(8,128)(2,1)S(1)} %copy-done.6), channel_id=1, source_target_pairs={{0,1},{1,0},{2,3},{3,2},{4,5},{5,4},{6,7},{7,6},{8,9},{9,8},{10,11... | collective-permute-start | bytes 4718600 | tf_op jit(solution)/shard_map/ppermute | solution.py:768
  102.7 50.5 %all-to-all-start.2 = ((bf16[4,272,768]{2,1,0:T(8,128)(2,1)}), bf16[4,272,768]{2,1,0:T(8,128)(2,1)S(1)}, u32[]{:S(2)}, u32[]{:S(2)}) async-start(bf16[4,272,768]{2,1,0:T(8,128)(2,1)} %broadcast_in_dim.9), calls=%async_computation.2 | async-start | bytes 3342336 | tf_op jit(solution)/shard_map/all_to_all | solution.py:784
  107.6 142.1 %all-gather.11.cloned.1.call-start = ((), (), s32[]{:S(2)}) async-start(), calls=%async_computation.5 | async-start | bytes 11280384 | tf_op jit(solution)/shard_map/all_gather | solution.py:792
  157.0 234.4 %all-gather.9.cloned.1.call-start = ((), (), s32[]{:S(2)}) async-start(), calls=%async_computation.4 | async-start | bytes 1622016 | tf_op jit(solution)/shard_map/all_gather | solution.py:968
  157.0 8.1 %collective-permute-start.12 = (bf16[4,528,768]{2,1,0:T(8,128)(2,1)}, bf16[4,528,768]{2,1,0:T(8,128)(2,1)S(1)}, u32[]{:S(2)}, u32[]{:S(2)}) collective-permute-start(bf16[4,528,768]{2,1,0:T(8,128)(2,1)} %get-tuple-element.69), channel_id=1, source_target_pairs={{0,1},{1,0},{2,3},{3,2},{4,5},{5,4},{6,7},{7,6},{8,9},{9,8},{10,11... | collective-permute-start | bytes 9732104 | tf_op jit(solution)/shard_map/ppermute | solution.py:768
  170.5 29.1 %collective-permute-start.13 = (bf16[2,256,768]{2,1,0:T(8,128)(2,1)}, bf16[2,256,768]{2,1,0:T(8,128)(2,1)S(1)}, u32[]{:S(2)}, u32[]{:S(2)}) collective-permute-start(bf16[2,256,768]{2,1,0:T(8,128)(2,1)} %get-tuple-element.71.refs_4_), channel_id=1, source_target_pairs={{0,2},{1,3},{2,0},{3,1},{4,6},{5,7},{6,4},{7,5},{8,10},{9,11},{10,... | collective-permute-start | bytes 2359304 | tf_op jit(solution)/shard_map/ppermute | solution.py:771
  171.9 30.9 %collective-permute-start.14 = (bf16[2,272,768]{2,1,0:T(8,128)(2,1)}, bf16[2,272,768]{2,1,0:T(8,128)(2,1)S(1)}, u32[]{:S(2)}, u32[]{:S(2)}) collective-permute-start(bf16[2,272,768]{2,1,0:T(8,128)(2,1)} %get-tuple-element.72), channel_id=1, source_target_pairs={{0,4},{4,0},{1,5},{5,1},{2,6},{6,2},{3,7},{7,3},{8,12},{12,8},{9,1... | collective-permute-start | bytes 2506760 | tf_op jit(solution)/shard_map/ppermute | solution.py:774
  208.6 20.2 %collective-permute-start.15 = (bf16[256,768]{1,0:T(8,128)(2,1)}, bf16[256,768]{1,0:T(8,128)(2,1)S(1)}, u32[]{:S(2)}, u32[]{:S(2)}) collective-permute-start(bf16[256,768]{1,0:T(8,128)(2,1)} %get-tuple-element.76), channel_id=1, source_target_pairs={{0,4},{4,0},{1,5},{5,1},{2,6},{6,2},{3,7},{7,3},{8,12},{12,8},{9,1... | collective-permute-start | bytes 1179656 | tf_op jit(solution)/shard_map/ppermute | solution.py:774
  209.0 21.1 %collective-permute-start.16 = (bf16[272,768]{1,0:T(8,128)(2,1)}, bf16[272,768]{1,0:T(8,128)(2,1)S(1)}, u32[]{:S(2)}, u32[]{:S(2)}) collective-permute-start(bf16[272,768]{1,0:T(8,128)(2,1)} %get-tuple-element.78), channel_id=1, source_target_pairs={{0,2},{1,3},{2,0},{3,1},{4,6},{5,7},{6,4},{7,5},{8,10},{9,11},{10,... | collective-permute-start | bytes 1253384 | tf_op jit(solution)/shard_map/ppermute | solution.py:771
  247.5 22.9 %collective-permute-start.17 = (bf16[2,768,768]{2,1,0:T(8,128)(2,1)}, bf16[2,768,768]{2,1,0:T(8,128)(2,1)}, u32[]{:S(2)}, u32[]{:S(2)}) collective-permute-start(bf16[2,768,768]{2,1,0:T(8,128)(2,1)} %get-tuple-element.88), channel_id=1, source_target_pairs={{0,1},{1,0},{2,3},{3,2},{4,5},{5,4},{6,7},{7,6},{8,9},{9,8},{10,11... | collective-permute-start | bytes 7077896 | tf_op jit(solution)/shard_map/ppermute | solution.py:768
  268.6 94.2 %collective-permute-start.22 = (bf16[2,768,768]{2,1,0:T(8,128)(2,1)}, bf16[2,768,768]{2,1,0:T(8,128)(2,1)S(1)}, u32[]{:S(2)}, u32[]{:S(2)}) collective-permute-start(bf16[2,768,768]{2,1,0:T(8,128)(2,1)} %get-tuple-element.90.refs_3_), channel_id=1, source_target_pairs={{0,8},{8,0},{16,24},{24,16},{1,9},{9,1},{17,25},{25,17},{2,10},{10... | collective-permute-start | bytes 7077896 | tf_op jit(solution)/shard_map/ppermute | solution.py:777
  274.7 25.2 %collective-permute-start.18 = (bf16[384,768]{1,0:T(8,128)(2,1)}, bf16[384,768]{1,0:T(8,128)(2,1)S(1)}, u32[]{:S(2)}, u32[]{:S(2)}) collective-permute-start(bf16[384,768]{1,0:T(8,128)(2,1)} %get-tuple-element.96), channel_id=1, source_target_pairs={{0,2},{1,3},{2,0},{3,1},{4,6},{5,7},{6,4},{7,5},{8,10},{9,11},{10,... | collective-permute-start | bytes 1769480 | tf_op jit(solution)/shard_map/ppermute | solution.py:771
  276.2 23.7 %collective-permute-start.19 = (bf16[2,192,768]{2,1,0:T(8,128)(2,1)}, bf16[2,192,768]{2,1,0:T(8,128)(2,1)S(1)}, u32[]{:S(2)}, u32[]{:S(2)}) collective-permute-start(bf16[2,192,768]{2,1,0:T(8,128)(2,1)} %get-tuple-element.97), channel_id=1, source_target_pairs={{0,4},{4,0},{1,5},{5,1},{2,6},{6,2},{3,7},{7,3},{8,12},{12,8},{9,1... | collective-permute-start | bytes 1769480 | tf_op jit(solution)/shard_map/ppermute | solution.py:774
  304.2 28.2 %collective-permute-start.20 = (bf16[192,768]{1,0:T(8,128)(2,1)}, bf16[192,768]{1,0:T(8,128)(2,1)S(1)}, u32[]{:S(2)}, u32[]{:S(2)}) collective-permute-start(bf16[192,768]{1,0:T(8,128)(2,1)} %get-tuple-element.102), channel_id=1, source_target_pairs={{0,2},{1,3},{2,0},{3,1},{4,6},{5,7},{6,4},{7,5},{8,10},{9,11},{10,... | collective-permute-start | bytes 884744 | tf_op jit(solution)/shard_map/ppermute | solution.py:771
  304.9 27.5 %collective-permute-start.21 = (bf16[192,768]{1,0:T(8,128)(2,1)}, bf16[192,768]{1,0:T(8,128)(2,1)S(1)}, u32[]{:S(2)}, u32[]{:S(2)}) collective-permute-start(bf16[192,768]{1,0:T(8,128)(2,1)} %get-tuple-element.103), channel_id=1, source_target_pairs={{0,4},{4,0},{1,5},{5,1},{2,6},{6,2},{3,7},{7,3},{8,12},{12,8},{9,1... | collective-permute-start | bytes 884744 | tf_op jit(solution)/shard_map/ppermute | solution.py:774
  335.7 21.8 %collective-permute-start.23 = (bf16[96,768]{1,0:T(8,128)(2,1)}, bf16[96,768]{1,0:T(8,128)(2,1)S(1)}, u32[]{:S(2)}, u32[]{:S(2)}) collective-permute-start(bf16[96,768]{1,0:T(8,128)(2,1)} %get-tuple-element.109), channel_id=1, source_target_pairs={{0,8},{8,16},{16,24},{24,0},{1,9},{9,17},{17,25},{25,1},{2,10},{10... | collective-permute-start | bytes 442376 | tf_op jit(solution)/shard_map/ppermute | solution.py:780
  336.0 21.4 %collective-permute-start.24 = (bf16[96,768]{1,0:T(8,128)(2,1)}, bf16[96,768]{1,0:T(8,128)(2,1)S(1)}, u32[]{:S(2)}, u32[]{:S(2)}) collective-permute-start(bf16[96,768]{1,0:T(8,128)(2,1)} %get-tuple-element.110), channel_id=1, source_target_pairs={{0,16},{8,24},{16,0},{24,8},{1,17},{9,25},{17,1},{25,9},{2,18},{10... | collective-permute-start | bytes 442376 | tf_op jit(solution)/shard_map/ppermute | solution.py:780
  338.6 18.8 %collective-permute-start.25 = (bf16[96,768]{1,0:T(8,128)(2,1)}, bf16[96,768]{1,0:T(8,128)(2,1)S(1)}, u32[]{:S(2)}, u32[]{:S(2)}) collective-permute-start(bf16[96,768]{1,0:T(8,128)(2,1)} %get-tuple-element.111), channel_id=1, source_target_pairs={{0,24},{8,0},{16,8},{24,16},{1,25},{9,1},{17,9},{25,17},{2,26},{10... | collective-permute-start | bytes 442376 | tf_op jit(solution)/shard_map/ppermute | solution.py:780
  360.1 26.1 %collective-permute-start.28 = (bf16[96,768]{1,0:T(8,128)(2,1)}, bf16[96,768]{1,0:T(8,128)(2,1)S(1)}, u32[]{:S(2)}, u32[]{:S(2)}) collective-permute-start(bf16[96,768]{1,0:T(8,128)(2,1)} %dense_fourth.1.refs_3_.refs_1_), channel_id=1, source_target_pairs={{0,24},{8,0},{16,8},{24,16},{1,25},{9,1},{17,9},{25,17},{2,26},{10... | collective-permute-start | bytes 442376 | tf_op jit(solution)/shard_map/ppermute | solution.py:780
  360.1 26.1 %collective-permute-start.27 = (bf16[96,768]{1,0:T(8,128)(2,1)}, bf16[96,768]{1,0:T(8,128)(2,1)S(1)}, u32[]{:S(2)}, u32[]{:S(2)}) collective-permute-start(bf16[96,768]{1,0:T(8,128)(2,1)} %dense_fourth.1.refs_3_.refs_1_), channel_id=1, source_target_pairs={{0,16},{8,24},{16,0},{24,8},{1,17},{9,25},{17,1},{25,9},{2,18},{10... | collective-permute-start | bytes 442376 | tf_op jit(solution)/shard_map/ppermute | solution.py:780
  361.2 25.0 %collective-permute-start.26 = (bf16[96,768]{1,0:T(8,128)(2,1)}, bf16[96,768]{1,0:T(8,128)(2,1)S(1)}, u32[]{:S(2)}, u32[]{:S(2)}) collective-permute-start(bf16[96,768]{1,0:T(8,128)(2,1)} %dense_fourth.1.refs_3_.refs_1_), channel_id=1, source_target_pairs={{0,8},{8,16},{16,24},{24,0},{1,9},{9,17},{17,25},{25,1},{2,10},{10... | collective-permute-start | bytes 442376 | tf_op jit(solution)/shard_map/ppermute | solution.py:780
  389.0 12.8 %collective-permute-start.29 = (bf16[384,768]{1,0:T(8,128)(2,1)}, bf16[384,768]{1,0:T(8,128)(2,1)S(1)}, u32[]{:S(2)}, u32[]{:S(2)}) collective-permute-start(bf16[384,768]{1,0:T(8,128)(2,1)} %dense_fifth.1.refs_1_.refs_3_), channel_id=1, source_target_pairs={{0,4},{4,0},{1,5},{5,1},{2,6},{6,2},{3,7},{7,3},{8,12},{12,8},{9,1... | collective-permute-start | bytes 1769480 | tf_op jit(solution)/shard_map/ppermute | solution.py:774
  395.3 10.3 %copy-start.1 = (bf16[768,6,192]{0,2,1:T(8,128)(2,1)S(1)}, bf16[768,6,192]{0,2,1:T(8,128)(2,1)}, u32[]{:S(2)}) copy-start(bf16[768,6,192]{0,2,1:T(8,128)(2,1)} %param.17) | copy-start | bytes 5308420
  (28 other events, 30.5 us)
Sparse Core Ops, SparseCore 0:
  88.2 59.3 all-gather.6
  157.1 81.4 all-gather.10
  249.7 57.9 all-gather.8

commit v5 on v4

--- a/solution.py
+++ b/solution.py
@@ -17,7 +17,7 @@
 EPSILON = 1e-06
 HALF = 4
 FULL_LIMIT = 32 * 1024 * 1024
-VMEM_LIMIT = 58 * 1024 * 1024
+VMEM_LIMIT = 63 * 1024 * 1024
 
 f32 = jnp.float32
 bf16 = jnp.bfloat16
@@ -149,7 +149,7 @@
 
 def attention_kernel(
     local_width, tok_ref, mod_ref, router_ref, pairs_ref, w0, w1, w2, w3,
-    attn_in_ref, qkv_ref, context_ref, attn_out_ref, ext_ref,
+    attn_in_ref, qkv_ref, context_ref, attn_out_ref, ext_ref, column_ref,
 ):
     shards = (w0, w1, w2, w3)
     rows, width = tok_ref.shape
@@ -197,9 +197,11 @@
     for index, line in enumerate(packed):
         extra = jnp.where(row_id == index, line, extra)
     ext_ref[rows : rows + EXTRA, :] = extra.astype(bf16)
-
-
-def attention_forward(tokens, mod, router_t, pairs, shards, local_width):
+    for copy in range(column_ref.shape[0]):
+        column_ref[copy] = ext_ref[...]
+
+
+def attention_forward(tokens, mod, router_t, pairs, shards, local_width, copies):
     rows, width = tokens.shape
     outs = [
         ((rows, width), bf16),
@@ -207,6 +209,7 @@
         ((rows, width), bf16),
         ((rows, width), f32),
         ((rows + EXTRA, width), bf16),
+        ((copies, rows + EXTRA, width), bf16),
     ]
     return launch(
         functools.partial(attention_kernel, local_width), "attention_forward", outs,
@@ -337,24 +340,34 @@
     halves = ((rows0, extra0, cots0), (rows1, extra1, cots1))
     total_rows = 2 * HALF * CAP
 
-    def block_hits(block):
-        routes, places, gates = read_pairs(halves[block // HALF][1][block % HALF])
+    def hits_of(half, place):
+        routes, places, gates = read_pairs(halves[half][1][place])
         return slot_hits(routes, places, base, members * CAP), gates
+
+    def start_of(half, place):
+        return pl.multiple_of((half * HALF + place) * CAP, CAP)
+
+    def per_block(count, body, first=0):
+        for half in range(2):
+            lax.fori_loop(first, count, lambda place, _, half=half: (body(half, place), 0)[1], 0)
 
     @pl.when(step == 0)
     def _():
-        for block in range(2 * HALF):
-            rows_in, _, cots_in = halves[block // HALF]
-            hits, gates = block_hits(block)
+        def send(half, place):
+            rows_in, _, cots_in = halves[half]
+            hits, gates = hits_of(half, place)
             hot = (hits[0] | hits[1]).astype(bf16)
-            picked = mm(hot, rows_in[block % HALF], NN).astype(bf16)
-            cots = mm(hot, cots_in[block % HALF], NN).astype(bf16)
+            picked = mm(hot, rows_in[place], NN).astype(bf16)
+            cots = mm(hot, cots_in[place], NN).astype(bf16)
             gate = slot_gates(hits, gates)
+            rows = pl.ds(start_of(half, place), CAP)
             for member in range(members):
                 span = slice(member * CAP, (member + 1) * CAP)
-                rows_s[member, block * CAP : (block + 1) * CAP, :] = picked[span]
-                cots_s[member, block * CAP : (block + 1) * CAP, :] = cots[span]
-                gate_s[member, block * CAP : (block + 1) * CAP, :] = gate[span]
+                rows_s[member, rows, :] = picked[span]
+                cots_s[member, rows, :] = cots[span]
+                gate_s[member, rows, :] = gate[span]
+
+        per_block(HALF, send)
         for start in range(0, len(shared_ids), 2):
             pair = shared_ids[start : start + 2]
             inputs = jnp.concatenate([halves[b // HALF][0][b % HALF] for b in pair], axis=0)
@@ -372,6 +385,7 @@
     def _():
         member = step - 1
         tile = total_rows // 2
+
         for part in range(2):
             span = slice(part * tile, (part + 1) * tile)
             inputs, cots, gate = rows_s[member, span, :], cots_s[member, span, :], gate_s[member, span, :]
@@ -385,12 +399,13 @@
 
     @pl.when(step == members)
     def _():
-        for block in range(2 * HALF):
-            out_ref = (first_ref, second_ref)[block // HALF]
-            place = block % HALF
-            hits, _ = block_hits(block)
+        per_half = [sum(1 for b in shared_ids if b // HALF == half) for half in range(2)]
+
+        def combine(half, place, shared):
+            out_ref = (first_ref, second_ref)[half]
+            hits, _ = hits_of(half, place)
             hot = (hits[0] | hits[1]).astype(bf16)
-            span = slice(block * CAP, (block + 1) * CAP)
+            span = pl.ds(start_of(half, place), CAP)
             dots = jnp.concatenate([dot_s[m, span, :] for m in range(members)], axis=0)
             sums = [jnp.sum(jnp.where(hit, dots, 0.0), axis=0, keepdims=True) for hit in hits]
             line = jnp.concatenate(sums + [jnp.zeros_like(sums[0])], axis=1)
@@ -399,10 +414,18 @@
             for index, source in enumerate((rows_s, cots_s)):
                 slots = jnp.concatenate([source[m, span, :] for m in range(members)], axis=0)
                 total = mm(hot, slots, TN)
-                if block in shared_ids:
-                    where = shared_ids.index(block)
+                if shared:
+                    where = half * per_half[0] + place
                     total = total + shared_s[where, :, index * width : (index + 1) * width]
                 out_ref[place, index * PATCHES : (index + 1) * PATCHES, :] = total.astype(bf16)
+
+        for half in range(2):
+            for first, last, shared in ((0, per_half[half], True), (per_half[half], HALF, False)):
+                if last > first:
+                    lax.fori_loop(
+                        first, last,
+                        lambda place, _, half=half, shared=shared: (combine(half, place, shared), 0)[1], 0,
+                    )
 
 
 def experts_both(base, blocks, shared_up, shared_down, expert_up, expert_down, shared_ids, after=()):
@@ -779,8 +802,7 @@
     def along(self, value, hop):
         return lax.ppermute(value, "dp", [(i, (i + hop) % self.dp) for i in range(self.dp)])
 
-    def column(self, block):
-        copies = jnp.broadcast_to(block[None], (self.dp, *block.shape))
+    def column(self, copies):
         return lax.all_to_all(copies, "dp", split_axis=0, concat_axis=0)
 
     def column_rest(self, column, place, after):
@@ -910,7 +932,7 @@
     near_shard = links.to_core(weight)
     if full:
         place = jnp.stack([base[0], *(lax.axis_index(axis) for axis in ("expert", "dp"))]).astype(jnp.int32)
-        cot_column = links.column(shared_cot)
+        cot_column = links.column(jnp.broadcast_to(shared_cot[None], (links.dp, *shared_cot.shape)))
         cot_other = links.to_other(shared_cot)
         across, cot_other = ordered([across, cot_other], [mod])
         cot_side = links.to_side(ordered([shared_cot], [across])[0])
@@ -922,7 +944,9 @@
     pairs = jnp.concatenate([routes.T, places.T], axis=0)
 
     whole = slice(None)
-    attn_in, qkv, context, attn_out, ext = attention_forward(tokens, mod, router_t, pairs, shards, local_width)
+    attn_in, qkv, context, attn_out, ext, ext_copies = attention_forward(
+        tokens, mod, router_t, pairs, shards, local_width, links.dp if full else 1
+    )
     feed = (shared_up, shared_down, expert_up, expert_down)
     backward = functools.partial(
         attention_backward, cond=own_condition, tokens=tokens, cotangent=cotangent, mod=mod, router_t=router_t,
@@ -939,7 +963,7 @@
             [(index, whole, index) for index in range(HALF)], after=ext_cuts,
         )
         cot_near = links.to_core(cot_mine)
-        ext_column = links.column(ordered([ext], [ext_side, ext_other])[0])
+        ext_column = links.column(ordered([ext_copies], [ext_side, ext_other])[0])
         ext_mine = assemble(
             (HALF, PATCHES + EXTRA, width), bf16, [ext, ext_side, ext_other, *ext_corner],
             [(index, whole, index) for index in range(3)]
@@ -951,10 +975,10 @@
         first, second = experts_both(base, own, *feed, (0, 1, 4, 5), after=[cot_rest])
         ext_rest, exts = links.column_rest(ext_column, place, [first])
         moved = links.to_core(second)
-        slots = dispatch(base, own, members, after=[first, ext_rest])
-        side, other = links.plane_sum_first(first, moved, after=[slots[0]])
+        side, other = links.plane_sum_first(first, moved, after=[ext_rest])
+        slots = dispatch(base, own, members, after=[side])
         from_side, from_other = links.to_side(side), links.to_other(other)
-        routed = routed_grads([slots], expert_up, expert_down, None, after=[side])
+        routed = routed_grads([slots], expert_up, expert_down, None)
         upper, lower, upper_next, lower_next = links.plane_sum_second(
             first, moved, from_side, from_other, after=[routed[0]]
         )

time: 419 us -> 399 us (0.952)
  local copies, waits for them, and re-layouts: 34.3 us -> 17.6 us
  waiting for transfers between devices: 55.4 us -> 63.9 us
  Pallas kernels: 250 us -> 242 us
    unnamed x84 -> x51, local copies, waits for them, and re-layouts: 18.6 us -> 8.26 us
    pallas_call x29, Pallas kernels: 250 us -> 242 us  [launch(): pl.pallas_call(body, out_shape=tuple((jax.ShapeDtypeStruct(*out) for out...]
    ppermute x6, waiting for transfers between devices: 1.16 us -> 7.44 us  [to_core(): return lax.ppermute(value, 'tensor', self.core)]
  transfers between devices with their start and end apart: 36 -> 36, of which waited for: 12 -> 17; matrix products, arithmetic and copies ran while one was open for 7% -> 5% of each run, Pallas kernels for 59% -> 60%
where the time goes in v5:
time: 399 us; the launch traced here: 393 us
  Pallas kernels  242 us (61%)
  waiting for transfers between devices  63.9 us (16%)
  starting transfers between devices  41.9 us (11%)
  local copies, waits for them, and re-layouts  17.6 us (4%)
  between operations  14.3 us (4%)
  other arithmetic  8.48 us (2%)
  matrix products  5.43 us (1%)
    pallas_call x29, Pallas kernels, launch(): pl.pallas_call(body, out_shape=tuple((jax.ShapeDtypeStruct(*out) for out...  242 us
    ppermute x9, waiting for transfers between devices, to_other(): return lax.ppermute(value, 'expert', self.other)  31.1 us
    ppermute x8, waiting for transfers between devices, to_side(): return lax.ppermute(value, 'tensor', self.side)  20.2 us
    ppermute x9, starting transfers between devices, to_other(): return lax.ppermute(value, 'expert', self.other)  13 us
    all_to_all x2, starting transfers between devices, column(): return lax.all_to_all(copies, 'dp', split_axis=0, concat_axis=0)  9.84 us
    unnamed x51, local copies, waits for them, and re-layouts  8.26 us
    ppermute x6, starting transfers between devices, along(): lax.ppermute(value, 'dp', [(i, (i + hop) % self.dp) for i in range(self.d...  8.03 us
  transfers between devices with their start and end apart: 36, of which 17 were waited for; matrix products, arithmetic and copies ran while one was open for 5% of the time, Pallas kernels for 60%

profile of v5, /device:TPU:0, one launch (start us, length us, event | category | flops | bytes accessed | tf_op | source)
XLA Modules:
  0.0 393.5 jit_solution(16726003293854925164)
XLA Ops:
  8.1 2.0 convolution_add_fusion
  10.8 4.2 %all-to-all-start = ((f32[4,6,192]{2,1,0:T(8,128)}), f32[4,6,192]{2,1,0:T(8,128)S(1)}, u32[]{:S(2)}, u32[]{:S(2)}) async-start(f32[4,6,192]{2,1,0:T(8,128)} %copy.43), calls=%async_computation | async-start | bytes 65536 | tf_op jit(solution)/shard_map/all_to_all | solution.py:922
  15.0 2.0 pad_maximum_fusion.refs_0_
  17.0 1.9 all-to-all-done
  20.9 2.0 collective-permute-start.2
  24.1 5.0 %all-to-all-start.1 = ((bf16[4,256,768]{2,1,0:T(8,128)(2,1)}), bf16[4,256,768]{2,1,0:T(8,128)(2,1)}, u32[]{:S(2)}, u32[]{:S(2)}) async-start(bf16[4,256,768]{2,1,0:T(8,128)(2,1)} %broadcast_in_dim.6), calls=%async_computation.1 | async-start | bytes 3145728 | tf_op jit(solution)/shard_map/all_to_all | solution.py:806
  29.9 2.0 collective-permute-done.2.refs_1_
  31.9 15.9 %collective-permute-done.1.refs_0_ = bf16[768,768]{1,0:T(8,128)(2,1)} collective-permute-done((bf16[768,768]{1,0:T(8,128)(2,1)}, bf16[768,768]{1,0:T(8,128)(2,1)}, u32[]{:S(2)}, u32[]{:S(2)}) %collective-permute-start.1) | collective-permute-done | bytes 1179680 | tf_op jit(solution)/shard_map/ppermute | solution.py:794
  51.0 7.9 %attention_forward.1 = (bf16[256,768]{1,0:T(8,128)(2,1)}, bf16[3,256,768]{2,1,0:T(8,128)(2,1)}, bf16[256,768]{1,0:T(8,128)(2,1)}, f32[256,768]{1,0:T(8,128)}, bf...) custom-call(bf16[256,768]{1,0:T(8,128)(2,1)} %refs_5_.1, f32[6,768]{1,0:T(8,128)} %squeeze.10.refs_2_.refs_1_.refs_7_, ...), custom_call_target="tpu_custom_call" | custom-call | flops 5000000000 | bytes 9000000 | tf_op jit(solution)/shard_map/attention_forward/pallas_call | solution.py:89
  58.9 2.0 collective-permute-start.5
  63.7 8.0 %collective-permute-done.5.refs_2_ = bf16[272,768]{1,0:T(8,128)(2,1)S(1)} collective-permute-done((bf16[272,768]{1,0:T(8,128)(2,1)}, bf16[272,768]{1,0:T(8,128)(2,1)S(1)}, u32[]{:S(2)}, u32[]{:S(2)}) %collective-permute-start.5) | collective-permute-done | bytes 417824 | tf_op jit(solution)/shard_map/ppermute | solution.py:797
  73.3 6.3 %collective-permute-done.9.refs_3_ = bf16[256,768]{1,0:T(8,128)(2,1)} collective-permute-done((bf16[256,768]{1,0:T(8,128)(2,1)}, bf16[256,768]{1,0:T(8,128)(2,1)}, u32[]{:S(2)}, u32[]{:S(2)}) %collective-permute-start.9) | collective-permute-done | bytes 393248 | tf_op jit(solution)/shard_map/ppermute | solution.py:797
  79.6 2.5 assemble.3.refs_2_.refs_3_
  82.2 2.5 pick.2.refs_11_
  85.3 1.7 collective-permute-start.7
  87.1 4.6 %collective-permute-done.7.refs_4_ = bf16[128,768]{1,0:T(8,128)(2,1)S(1)} collective-permute-done((bf16[128,768]{1,0:T(8,128)(2,1)}, bf16[128,768]{1,0:T(8,128)(2,1)S(1)}, u32[]{:S(2)}, u32[]{:S(2)}) %collective-permute-start.7) | collective-permute-done | bytes 196640 | tf_op jit(solution)/shard_map/ppermute | solution.py:797
  93.0 2.8 assemble.2.refs_1_.refs_2_.refs_0_
  96.4 4.8 %all-to-all-start.2 = ((bf16[4,272,768]{2,1,0:T(8,128)(2,1)}), bf16[4,272,768]{2,1,0:T(8,128)(2,1)}, u32[]{:S(2)}, u32[]{:S(2)}) async-start(bf16[4,272,768]{2,1,0:T(8,128)(2,1)} %ordered.8), calls=%async_computation.2 | async-start | bytes 3342336 | tf_op jit(solution)/shard_map/all_to_all | solution.py:806
  102.1 35.4 %experts_both.1 = (bf16[4,528,768]{2,1,0:T(8,128)(2,1)}, bf16[4,528,768]{2,1,0:T(8,128)(2,1)}) custom-call(s32[1]{0:T(128)} %bitcast.refs_0_, bf16[4,272,768]{2,1,0:T(8,128)(2,1)} %assemble.2.refs_1_.refs_2_.refs_0_, bf16[4,272,768]{2,1,0:T(8,128)(2,1)} %assemble.2.refs_1_.refs_2_.refs_0_, bf16[4,256,768]{2,1,0:T(8,128)(2,1)} %assemble.3.refs_2_.refs_3_, ...), custom_call_target="tpu_custom_call" | custom-call | flops 30000001024 | bytes 30000000 | tf_op jit(solution)/shard_map/experts_both/pallas_call | solution.py:89
  137.4 3.2 all-to-all-done.2.refs_1_
  140.7 2.6 pick.3.refs_2_
  144.2 5.5 %collective-permute-done.12.refs_1_ = bf16[4,528,768]{2,1,0:T(8,128)(2,1)} collective-permute-done((bf16[4,528,768]{2,1,0:T(8,128)(2,1)}, bf16[4,528,768]{2,1,0:T(8,128)(2,1)}, u32[]{:S(2)}, u32[]{:S(2)}) %collective-permute-start.12) | collective-permute-done | bytes 3244064 | tf_op jit(solution)/shard_map/ppermute | solution.py:791
  149.8 3.3 plane_first.1
  156.1 8.2 %dispatch.1 = (bf16[4,640,768]{2,1,0:T(8,128)(2,1)}, bf16[4,640,768]{2,1,0:T(8,128)(2,1)}) custom-call(s32[1]{0:T(128)} %bitcast.refs_0_, bf16[4,272,768]{2,1,0:T(8,128)(2,1)} %assemble.2.refs_1_.refs_2_.refs_0_, bf16[4,272,768]{2,1,0:T(8,128)(2,1)} %assemble.2.refs_1_.refs_2_.refs_0_, bf16[4,256,768]{2,1,0:T(8,128)(2,1)} %assemble.3.refs_2_.refs_3_, ...), custom_call_target="tpu_custom_call" | custom-call | flops 8000000000 | bytes 16000000 | tf_op jit(solution)/shard_map/dispatch/pallas_call | solution.py:89
  164.3 20.1 %weight_grads.5 = (f32[4,768,768]{2,1,0:T(8,128)}, f32[4,768,768]{2,1,0:T(8,128)}) custom-call(bf16[4,640,768]{2,1,0:T(8,128)(2,1)} %get-tuple-element.74.refs_0_, bf16[4,640,768]{2,1,0:T(8,128)(2,1)} %get-tuple-element.75.refs_1_, bf16[4,768,768]{2,1,0:T(8,128)(2,1)} %refs_2_.9, bf16[4,768,768]{2,1,0:T(8,128)(2,1)} %refs_3_.9), custom_call_target="tpu_custom_call" | custom-call | flops 18119393280 | bytes 7864320 | tf_op jit(solution)/shard_map/weight_grads/pallas_call | solution.py:89
  185.4 3.1 collective-permute-done.14.refs_3_
  189.5 4.9 %plane_second.1 = (f32[256,768]{1,0:T(8,128)}, f32[272,768]{1,0:T(8,128)}, bf16[256,768]{1,0:T(8,128)(2,1)}, bf16[272,768]{1,0:T(8,128)(2,1)}) custom-call(bf16[4,528,768]{2,1,0:T(8,128)(2,1)} %get-tuple-element.69.refs_2_.refs_0_, bf16[4,528,768]{2,1,0:T(8,128)(2,1)} %collective-permute-done.12.refs_1_, ...), custom_call_target="tpu_custom_call" | custom-call | bytes 7000000 | tf_op jit(solution)/shard_map/plane_second/pallas_call | solution.py:89
  194.4 1.7 collective-permute-start.15
  196.5 15.2 %weight_grads.6 = (f32[1,768,768]{2,1,0:T(8,128)}, f32[1,768,768]{2,1,0:T(8,128)}) custom-call(bf16[4,272,768]{2,1,0:T(8,128)(2,1)} %assemble.2.refs_1_.refs_2_.refs_0_, bf16[4,272,768]{2,1,0:T(8,128)(2,1)} %collective-permute-done.10.refs_4_.refs_5_.refs_1_, bf16[4,256,768]{2,1,0:T(8,128)(2,1)} %assemble.3.refs_2_.refs_3_, ...), custom_call_target="tpu_custom_call" | custom-call | flops 14495514624 | bytes 6291456 | tf_op jit(solution)/shard_map/weight_grads/pallas_call | solution.py:89
  211.7 2.5 collective-permute-done.15.refs_1_
  214.2 2.7 collective-permute-done.16.refs_3_
  217.7 16.4 %attention_backward.1 = (bf16[256,768]{1,0:T(8,128)(2,1)}, f32[256,768]{1,0:T(8,128)}, f32[16,768]{1,0:T(8,128)}, bf16[2,768,768]{2,1,0:T(8,128)(2,1)}, bf16[2,768,768]{2,1,0:T(8,128)(2,1)}) custom-call(f32[256,768]{1,0:T(8,128)} %get-tuple-element.77.refs_6_.refs_0_, bf16[256,768]{1,0:T(8,128)(2,1)} %copy-done.23, f32[272,768]{1,0:T(8,128)} %get-tuple-element.79.refs_2_, ...), custom_call_target="tpu_custom_call" | custom-call | flops 10000000000 | bytes 16000000 | tf_op jit(solution)/shard_map/attention_backward/pallas_call | solution.py:89
  236.3 19.0 %shared_grads_other.1 = (f32[768,768]{1,0:T(8,128)}, f32[768,768]{1,0:T(8,128)}, bf16[2,768,768]{2,1,0:T(8,128)(2,1)}) custom-call(bf16[8,3,272,768]{3,2,1,0:T(8,128)(2,1)} %bitcast.43, bf16[8,3,256,768]{3,2,1,0:T(8,128)(2,1)} %bitcast.47, bf16[768,768]{1,0:T(8,128)(2,1)} %refs_2_.6, bf16[768,768]{1,0:T(8,128)(2,1)} %refs_3_.6, ...), custom_call_target="tpu_custom_call" | custom-call | flops 14495514624 | bytes 6291456 | tf_op jit(solution)/shard_map/shared_grads_other/pallas_call | solution.py:89
  255.4 4.3 %dense_first.1 = (bf16[384,768]{1,0:T(8,128)(2,1)}, bf16[2,192,768]{2,1,0:T(8,128)(2,1)}, f32[384,768]{1,0:T(8,128)}, f32[2,192,768]{2,1,0:T(8,128)}) custom-call(s32[2]{0:T(128)} %pad_add_fusion.2.refs_0_, bf16[2,768,768]{2,1,0:T(8,128)(2,1)} %get-tuple-element.89.refs_1_, bf16[2,768,768]{2,1,0:T(8,128)(2,1)} %collective-permute-done.17.refs_2_, ...), custom_call_target="tpu_custom_call" | custom-call | bytes 8000000 | tf_op jit(solution)/shard_map/dense_first/pallas_call | solution.py:89
  260.5 18.4 %dispatch_hops.1 = (bf16[4,1920,768]{2,1,0:T(8,128)(2,1)}, bf16[4,1920,768]{2,1,0:T(8,128)(2,1)}) custom-call(s32[1]{0:T(128)} %bitcast.refs_0_, bf16[8,3,272,768]{3,2,1,0:T(8,128)(2,1)} %bitcast.44, bf16[8,3,256,768]{3,2,1,0:T(8,128)(2,1)} %bitcast.48, f32[384,768]{1,0:T(8,128)} %get-tuple-element.93.refs_3_.refs_1_), custom_call_target="tpu_custom_call" | custom-call | flops 24000000000 | bytes 48000000 | tf_op jit(solution)/shard_map/dispatch_hops/pallas_call | solution.py:89
  280.9 3.3 dense_second.1
  287.4 27.2 %weight_grads.7 = (f32[4,768,768]{2,1,0:T(8,128)}, f32[4,768,768]{2,1,0:T(8,128)}) custom-call(bf16[4,1920,768]{2,1,0:T(8,128)(2,1)} %get-tuple-element.94.refs_5_.refs_0_, bf16[4,1920,768]{2,1,0:T(8,128)(2,1)} %get-tuple-element.95.refs_1_, bf16[4,768,768]{2,1,0:T(8,128)(2,1)} %refs_2_.9, ...), custom_call_target="tpu_custom_call", output_to_operand_aliasing={{0}: (4, {}), {1}: (5, {})} | custom-call | flops 27179089920 | bytes 11796480 | tf_op jit(solution)/shard_map/weight_grads/pallas_call | solution.py:89
  315.5 2.4 dense_third.1
  317.9 2.0 collective-permute-start.23
  319.9 2.9 collective-permute-start.25
  322.8 16.6 %weight_grads.8 = (f32[4,768,768]{2,1,0:T(8,128)}, f32[4,768,768]{2,1,0:T(8,128)}) custom-call(bf16[4,1920,768]{2,1,0:T(8,128)(2,1)} %get-tuple-element.94.refs_5_.refs_0_, bf16[4,1920,768]{2,1,0:T(8,128)(2,1)} %get-tuple-element.95.refs_1_, bf16[4,768,768]{2,1,0:T(8,128)(2,1)} %refs_2_.9, ...), custom_call_target="tpu_custom_call", output_to_operand_aliasing={{0}: (4, {}), {1}: (5, {})} | custom-call | flops 13589544960 | bytes 5898240 | tf_op jit(solution)/shard_map/weight_grads/pallas_call | solution.py:89
  340.1 1.9 dense_fourth.1.refs_3_.refs_1_
  345.1 5.5 %shared_last.1 = (f32[768,768]{1,0:T(8,128)}, f32[768,768]{1,0:T(8,128)}) custom-call(f32[768,768]{1,0:T(8,128)} %get-tuple-element.109.refs_0_, f32[768,768]{1,0:T(8,128)} %get-tuple-element.110.refs_1_, bf16[2,768,768]{2,1,0:T(8,128)(2,1)} %collective-permute-done.22.refs_2_, bf16[96,768]{1,0:T(8,128)(2,1)} %dense_fourth.1.refs_3_.refs_1_), custom_call_target="tpu_custom_call" | custom-call | bytes 12000000 | tf_op jit(solution)/shard_map/shared_last/pallas_call | solution.py:89
  350.6 16.4 %weight_grads.9 = (f32[4,768,768]{2,1,0:T(8,128)}, f32[4,768,768]{2,1,0:T(8,128)}) custom-call(bf16[4,1920,768]{2,1,0:T(8,128)(2,1)} %get-tuple-element.94.refs_5_.refs_0_, bf16[4,1920,768]{2,1,0:T(8,128)(2,1)} %get-tuple-element.95.refs_1_, bf16[4,768,768]{2,1,0:T(8,128)(2,1)} %refs_2_.9, ...), custom_call_target="tpu_custom_call", output_to_operand_aliasing={{0}: (4, {}), {1}: (5, {})} | custom-call | flops 13589544960 | bytes 5898240 | tf_op jit(solution)/shard_map/weight_grads/pallas_call | solution.py:89
  367.8 2.0 dense_fifth.1.refs_1_.refs_3_
  375.1 3.4 fusion
  378.4 4.6 %collective-permute-done.29.refs_2_ = bf16[384,768]{1,0:T(8,128)(2,1)S(1)} collective-permute-done((bf16[384,768]{1,0:T(8,128)(2,1)}, bf16[384,768]{1,0:T(8,128)(2,1)S(1)}, u32[]{:S(2)}, u32[]{:S(2)}) %collective-permute-start.29) | collective-permute-done | bytes 589856 | tf_op jit(solution)/shard_map/ppermute | solution.py:797
  383.9 2.9 dense_last.1
  (138 shorter events, 43.2 us)
Async XLA Ops:
  7.2 7.8 %copy-start.5 = (bf16[768,3,192]{0,2,1:T(8,128)(2,1)S(1)}, bf16[768,3,192]{0,2,1:T(8,128)(2,1)}, u32[]{:S(2)}) copy-start(bf16[768,3,192]{0,2,1:T(8,128)(2,1)} %param.19) | copy-start | bytes 2654212
  7.2 11.9 %copy-start.9 = (bf16[256,768]{1,0:T(8,128)(2,1)S(1)}, bf16[256,768]{1,0:T(8,128)(2,1)}, u32[]{:S(2)}) copy-start(bf16[256,768]{1,0:T(8,128)(2,1)} %refs_6_.1) | copy-start | bytes 1179652
  10.8 8.2 %all-to-all-start = ((f32[4,6,192]{2,1,0:T(8,128)}), f32[4,6,192]{2,1,0:T(8,128)S(1)}, u32[]{:S(2)}, u32[]{:S(2)}) async-start(f32[4,6,192]{2,1,0:T(8,128)} %copy.43), calls=%async_computation | async-start | bytes 65536 | tf_op jit(solution)/shard_map/all_to_all | solution.py:922
  19.9 1.0 copy-start
  19.9 27.9 %collective-permute-start.1 = (bf16[768,768]{1,0:T(8,128)(2,1)}, bf16[768,768]{1,0:T(8,128)(2,1)}, u32[]{:S(2)}, u32[]{:S(2)}) collective-permute-start(bf16[768,768]{1,0:T(8,128)(2,1)} %ordered.5.refs_4_.refs_15_), channel_id=1, source_target_pairs={{0,2},{1,3},{2,0},{3,1},{4,6},{5,7},{6,4},{7,5},{8,10},{9,11},{10,... | collective-permute-start | bytes 3538952 | tf_op jit(solution)/shard_map/ppermute | solution.py:794
  20.9 11.0 %collective-permute-start.2 = (bf16[256,768]{1,0:T(8,128)(2,1)S(1)}, bf16[256,768]{1,0:T(8,128)(2,1)S(1)}, u32[]{:S(2)}, u32[]{:S(2)}) collective-permute-start(bf16[256,768]{1,0:T(8,128)(2,1)S(1)} %copy-done), channel_id=1, source_target_pairs={{0,4},{4,0},{1,5},{5,1},{2,6},{6,2},{3,7},{7,3},{8,12},{12,8},{9,1... | collective-permute-start | bytes 1179656 | tf_op jit(solution)/shard_map/ppermute | solution.py:797
  24.1 23.7 %copy-start.20 = (s32[256,2]{0,1:T(2,128)S(1)}, s32[256,2]{0,1:T(2,128)}, u32[]{:S(2)}) copy-start(s32[256,2]{0,1:T(2,128)} %param.27) | copy-start | bytes 6148
  24.1 23.7 %copy-start.21 = (s32[256,2]{0,1:T(2,128)S(1)}, s32[256,2]{0,1:T(2,128)}, u32[]{:S(2)}) copy-start(s32[256,2]{0,1:T(2,128)} %param.26) | copy-start | bytes 6148
  24.1 58.1 %all-to-all-start.1 = ((bf16[4,256,768]{2,1,0:T(8,128)(2,1)}), bf16[4,256,768]{2,1,0:T(8,128)(2,1)}, u32[]{:S(2)}, u32[]{:S(2)}) async-start(bf16[4,256,768]{2,1,0:T(8,128)(2,1)} %broadcast_in_dim.6), calls=%async_computation.1 | async-start | bytes 3145728 | tf_op jit(solution)/shard_map/all_to_all | solution.py:806
  29.1 167.3 %all-gather.7.cloned.1.call-start = ((), (), s32[]{:S(2)}) async-start(), calls=%async_computation.3 | async-start | bytes 10616832 | tf_op jit(solution)/shard_map/all_gather | solution.py:814
  29.1 20.6 %collective-permute-start = (bf16[768,768]{1,0:T(8,128)(2,1)}, bf16[768,768]{1,0:T(8,128)(2,1)}, u32[]{:S(2)}, u32[]{:S(2)}) collective-permute-start(bf16[768,768]{1,0:T(8,128)(2,1)} %ordered.5.refs_4_.refs_15_), channel_id=1, source_target_pairs={{0,1},{1,0},{2,3},{3,2},{4,5},{5,4},{6,7},{7,6},{8,9},{9,8},{10,11... | collective-permute-start | bytes 3538952 | tf_op jit(solution)/shard_map/ppermute | solution.py:791
  31.9 15.9 %copy-start.4 = (bf16[256,768]{1,0:T(8,128)(2,1)}, bf16[256,768]{1,0:T(8,128)(2,1)S(1)}, u32[]{:S(2)}) copy-start(bf16[256,768]{1,0:T(8,128)(2,1)S(1)} %collective-permute-done.2.refs_1_) | copy-start | bytes 1179652
  47.8 3.2 collective-permute-start.3
  49.2 12.3 %collective-permute-start.8 = (bf16[256,768]{1,0:T(8,128)(2,1)}, bf16[256,768]{1,0:T(8,128)(2,1)}, u32[]{:S(2)}, u32[]{:S(2)}) collective-permute-start(bf16[256,768]{1,0:T(8,128)(2,1)} %ordered.7), channel_id=1, source_target_pairs={{0,2},{1,3},{2,0},{3,1},{4,6},{5,7},{6,4},{7,5},{8,10},{9,11},{10,... | collective-permute-start | bytes 1179656 | tf_op jit(solution)/shard_map/ppermute | solution.py:794
  58.9 12.7 %collective-permute-start.5 = (bf16[272,768]{1,0:T(8,128)(2,1)}, bf16[272,768]{1,0:T(8,128)(2,1)S(1)}, u32[]{:S(2)}, u32[]{:S(2)}) collective-permute-start(bf16[272,768]{1,0:T(8,128)(2,1)} %get-tuple-element.67.refs_0_.refs_14_), channel_id=1, source_target_pairs={{0,4},{4,0},{1,5},{5,1},{2,6},{6,2},{3,7},{7,3},{8,12},{12,8},{9,1... | collective-permute-start | bytes 1253384 | tf_op jit(solution)/shard_map/ppermute | solution.py:797
  60.9 11.6 %collective-permute-start.4 = (bf16[272,768]{1,0:T(8,128)(2,1)}, bf16[272,768]{1,0:T(8,128)(2,1)S(1)}, u32[]{:S(2)}, u32[]{:S(2)}) collective-permute-start(bf16[272,768]{1,0:T(8,128)(2,1)} %get-tuple-element.67.refs_0_.refs_14_), channel_id=1, source_target_pairs={{0,2},{1,3},{2,0},{3,1},{4,6},{5,7},{6,4},{7,5},{8,10},{9,11},{10,... | collective-permute-start | bytes 1253384 | tf_op jit(solution)/shard_map/ppermute | solution.py:794
  61.5 18.2 %collective-permute-start.9 = (bf16[256,768]{1,0:T(8,128)(2,1)}, bf16[256,768]{1,0:T(8,128)(2,1)}, u32[]{:S(2)}, u32[]{:S(2)}) collective-permute-start(bf16[256,768]{1,0:T(8,128)(2,1)} %collective-permute-done.8.refs_1_), channel_id=1, source_target_pairs={{0,4},{4,0},{1,5},{5,1},{2,6},{6,2},{3,7},{7,3},{8,12},{12,8},{9,1... | collective-permute-start | bytes 1179656 | tf_op jit(solution)/shard_map/ppermute | solution.py:797
  71.6 13.1 %copy-start.2 = (bf16[272,768]{1,0:T(8,128)(2,1)}, bf16[272,768]{1,0:T(8,128)(2,1)S(1)}, u32[]{:S(2)}) copy-start(bf16[272,768]{1,0:T(8,128)(2,1)S(1)} %collective-permute-done.5.refs_2_) | copy-start | bytes 1253380
  72.6 12.1 %copy-start.3 = (bf16[272,768]{1,0:T(8,128)(2,1)}, bf16[272,768]{1,0:T(8,128)(2,1)S(1)}, u32[]{:S(2)}) copy-start(bf16[272,768]{1,0:T(8,128)(2,1)S(1)} %collective-permute-done.4.refs_1_) | copy-start | bytes 1253380
  84.7 7.2 %collective-permute-start.6 = (bf16[144,768]{1,0:T(8,128)(2,1)}, bf16[144,768]{1,0:T(8,128)(2,1)S(1)}, u32[]{:S(2)}, u32[]{:S(2)}) collective-permute-start(bf16[144,768]{1,0:T(8,128)(2,1)} %slice.39.refs_4_), channel_id=1, source_target_pairs={{0,2},{1,3},{2,0},{3,1},{4,6},{5,7},{6,4},{7,5},{8,10},{9,11},{10,... | collective-permute-start | bytes 663560 | tf_op jit(solution)/shard_map/ppermute | solution.py:794
  85.3 6.3 %collective-permute-start.7 = (bf16[128,768]{1,0:T(8,128)(2,1)}, bf16[128,768]{1,0:T(8,128)(2,1)S(1)}, u32[]{:S(2)}, u32[]{:S(2)}) collective-permute-start(bf16[128,768]{1,0:T(8,128)(2,1)} %slice.40.refs_5_), channel_id=1, source_target_pairs={{0,4},{4,0},{1,5},{5,1},{2,6},{6,2},{3,7},{7,3},{8,12},{12,8},{9,1... | collective-permute-start | bytes 589832 | tf_op jit(solution)/shard_map/ppermute | solution.py:797
  95.8 6.2 %collective-permute-start.10 = (bf16[4,272,768]{2,1,0:T(8,128)(2,1)}, bf16[4,272,768]{2,1,0:T(8,128)(2,1)}, u32[]{:S(2)}, u32[]{:S(2)}) collective-permute-start(bf16[4,272,768]{2,1,0:T(8,128)(2,1)} %assemble.2.refs_1_.refs_2_.refs_0_), channel_id=1, source_target_pairs={{0,1},{1,0},{2,3},{3,2},{4,5},{5,4},{6,7},{7,6},{8,9},{9,8},{10,11... | collective-permute-start | bytes 5013512 | tf_op jit(solution)/shard_map/ppermute | solution.py:791
  95.9 6.1 %collective-permute-start.11 = (bf16[4,256,768]{2,1,0:T(8,128)(2,1)}, bf16[4,256,768]{2,1,0:T(8,128)(2,1)}, u32[]{:S(2)}, u32[]{:S(2)}) collective-permute-start(bf16[4,256,768]{2,1,0:T(8,128)(2,1)} %assemble.3.refs_2_.refs_3_), channel_id=1, source_target_pairs={{0,1},{1,0},{2,3},{3,2},{4,5},{5,4},{6,7},{7,6},{8,9},{9,8},{10,11... | collective-permute-start | bytes 4718600 | tf_op jit(solution)/shard_map/ppermute | solution.py:791
  96.4 44.3 %all-to-all-start.2 = ((bf16[4,272,768]{2,1,0:T(8,128)(2,1)}), bf16[4,272,768]{2,1,0:T(8,128)(2,1)}, u32[]{:S(2)}, u32[]{:S(2)}) async-start(bf16[4,272,768]{2,1,0:T(8,128)(2,1)} %ordered.8), calls=%async_computation.2 | async-start | bytes 3342336 | tf_op jit(solution)/shard_map/all_to_all | solution.py:806
  101.3 135.0 %all-gather.11.cloned.1.call-start = ((), (), s32[]{:S(2)}) async-start(), calls=%async_computation.5 | async-start | bytes 11280384 | tf_op jit(solution)/shard_map/all_gather | solution.py:814
  143.3 227.8 %all-gather.9.cloned.1.call-start = ((), (), s32[]{:S(2)}) async-start(), calls=%async_computation.4 | async-start | bytes 1622016 | tf_op jit(solution)/shard_map/all_gather | solution.py:992
  143.5 6.2 %collective-permute-start.12 = (bf16[4,528,768]{2,1,0:T(8,128)(2,1)}, bf16[4,528,768]{2,1,0:T(8,128)(2,1)}, u32[]{:S(2)}, u32[]{:S(2)}) collective-permute-start(bf16[4,528,768]{2,1,0:T(8,128)(2,1)} %get-tuple-element.70), channel_id=1, source_target_pairs={{0,1},{1,0},{2,3},{3,2},{4,5},{5,4},{6,7},{7,6},{8,9},{9,8},{10,11... | collective-permute-start | bytes 9732104 | tf_op jit(solution)/shard_map/ppermute | solution.py:791
  153.0 32.4 %collective-permute-start.13 = (bf16[2,256,768]{2,1,0:T(8,128)(2,1)}, bf16[2,256,768]{2,1,0:T(8,128)(2,1)}, u32[]{:S(2)}, u32[]{:S(2)}) collective-permute-start(bf16[2,256,768]{2,1,0:T(8,128)(2,1)} %get-tuple-element.72.refs_7_), channel_id=1, source_target_pairs={{0,2},{1,3},{2,0},{3,1},{4,6},{5,7},{6,4},{7,5},{8,10},{9,11},{10,... | collective-permute-start | bytes 2359304 | tf_op jit(solution)/shard_map/ppermute | solution.py:794
  154.6 34.0 %collective-permute-start.14 = (bf16[2,272,768]{2,1,0:T(8,128)(2,1)}, bf16[2,272,768]{2,1,0:T(8,128)(2,1)S(1)}, u32[]{:S(2)}, u32[]{:S(2)}) collective-permute-start(bf16[2,272,768]{2,1,0:T(8,128)(2,1)} %get-tuple-element.73), channel_id=1, source_target_pairs={{0,4},{4,0},{1,5},{5,1},{2,6},{6,2},{3,7},{7,3},{8,12},{12,8},{9,1... | collective-permute-start | bytes 2506760 | tf_op jit(solution)/shard_map/ppermute | solution.py:797
  188.6 0.9 copy-start.6
  194.4 19.8 %collective-permute-start.15 = (bf16[256,768]{1,0:T(8,128)(2,1)}, bf16[256,768]{1,0:T(8,128)(2,1)S(1)}, u32[]{:S(2)}, u32[]{:S(2)}) collective-permute-start(bf16[256,768]{1,0:T(8,128)(2,1)} %get-tuple-element.78), channel_id=1, source_target_pairs={{0,4},{4,0},{1,5},{5,1},{2,6},{6,2},{3,7},{7,3},{8,12},{12,8},{9,1... | collective-permute-start | bytes 1179656 | tf_op jit(solution)/shard_map/ppermute | solution.py:797
  196.1 20.8 %collective-permute-start.16 = (bf16[272,768]{1,0:T(8,128)(2,1)}, bf16[272,768]{1,0:T(8,128)(2,1)S(1)}, u32[]{:S(2)}, u32[]{:S(2)}) collective-permute-start(bf16[272,768]{1,0:T(8,128)(2,1)} %get-tuple-element.80), channel_id=1, source_target_pairs={{0,2},{1,3},{2,0},{3,1},{4,6},{5,7},{6,4},{7,5},{8,10},{9,11},{10,... | collective-permute-start | bytes 1253384 | tf_op jit(solution)/shard_map/ppermute | solution.py:794
  214.2 2.7 copy-start.23
  234.1 21.3 %collective-permute-start.17 = (bf16[2,768,768]{2,1,0:T(8,128)(2,1)}, bf16[2,768,768]{2,1,0:T(8,128)(2,1)}, u32[]{:S(2)}, u32[]{:S(2)}) collective-permute-start(bf16[2,768,768]{2,1,0:T(8,128)(2,1)} %get-tuple-element.90), channel_id=1, source_target_pairs={{0,1},{1,0},{2,3},{3,2},{4,5},{5,4},{6,7},{7,6},{8,9},{9,8},{10,11... | collective-permute-start | bytes 7077896 | tf_op jit(solution)/shard_map/ppermute | solution.py:791
  255.3 89.8 %collective-permute-start.22 = (bf16[2,768,768]{2,1,0:T(8,128)(2,1)}, bf16[2,768,768]{2,1,0:T(8,128)(2,1)}, u32[]{:S(2)}, u32[]{:S(2)}) collective-permute-start(bf16[2,768,768]{2,1,0:T(8,128)(2,1)} %get-tuple-element.92.refs_3_), channel_id=1, source_target_pairs={{0,8},{8,0},{16,24},{24,16},{1,9},{9,1},{17,25},{25,17},{2,10},{10... | collective-permute-start | bytes 7077896 | tf_op jit(solution)/shard_map/ppermute | solution.py:800
  259.7 20.3 %collective-permute-start.18 = (bf16[384,768]{1,0:T(8,128)(2,1)}, bf16[384,768]{1,0:T(8,128)(2,1)S(1)}, u32[]{:S(2)}, u32[]{:S(2)}) collective-permute-start(bf16[384,768]{1,0:T(8,128)(2,1)} %get-tuple-element.98), channel_id=1, source_target_pairs={{0,2},{1,3},{2,0},{3,1},{4,6},{5,7},{6,4},{7,5},{8,10},{9,11},{10,... | collective-permute-start | bytes 1769480 | tf_op jit(solution)/shard_map/ppermute | solution.py:794
  260.0 20.0 %collective-permute-start.19 = (bf16[2,192,768]{2,1,0:T(8,128)(2,1)}, bf16[2,192,768]{2,1,0:T(8,128)(2,1)}, u32[]{:S(2)}, u32[]{:S(2)}) collective-permute-start(bf16[2,192,768]{2,1,0:T(8,128)(2,1)} %get-tuple-element.99), channel_id=1, source_target_pairs={{0,4},{4,0},{1,5},{5,1},{2,6},{6,2},{3,7},{7,3},{8,12},{12,8},{9,1... | collective-permute-start | bytes 1769480 | tf_op jit(solution)/shard_map/ppermute | solution.py:797
  284.1 30.5 %collective-permute-start.20 = (bf16[192,768]{1,0:T(8,128)(2,1)}, bf16[192,768]{1,0:T(8,128)(2,1)S(1)}, u32[]{:S(2)}, u32[]{:S(2)}) collective-permute-start(bf16[192,768]{1,0:T(8,128)(2,1)} %get-tuple-element.104), channel_id=1, source_target_pairs={{0,2},{1,3},{2,0},{3,1},{4,6},{5,7},{6,4},{7,5},{8,10},{9,11},{10,... | collective-permute-start | bytes 884744 | tf_op jit(solution)/shard_map/ppermute | solution.py:794
  285.8 28.9 %collective-permute-start.21 = (bf16[192,768]{1,0:T(8,128)(2,1)}, bf16[192,768]{1,0:T(8,128)(2,1)S(1)}, u32[]{:S(2)}, u32[]{:S(2)}) collective-permute-start(bf16[192,768]{1,0:T(8,128)(2,1)} %get-tuple-element.105), channel_id=1, source_target_pairs={{0,4},{4,0},{1,5},{5,1},{2,6},{6,2},{3,7},{7,3},{8,12},{12,8},{9,1... | collective-permute-start | bytes 884744 | tf_op jit(solution)/shard_map/ppermute | solution.py:797
  317.9 21.4 %collective-permute-start.23 = (bf16[96,768]{1,0:T(8,128)(2,1)}, bf16[96,768]{1,0:T(8,128)(2,1)S(1)}, u32[]{:S(2)}, u32[]{:S(2)}) collective-permute-start(bf16[96,768]{1,0:T(8,128)(2,1)} %get-tuple-element.111), channel_id=1, source_target_pairs={{0,8},{8,16},{16,24},{24,0},{1,9},{9,17},{17,25},{25,1},{2,10},{10... | collective-permute-start | bytes 442376 | tf_op jit(solution)/shard_map/ppermute | solution.py:803
  319.9 19.4 %collective-permute-start.24 = (bf16[96,768]{1,0:T(8,128)(2,1)}, bf16[96,768]{1,0:T(8,128)(2,1)S(1)}, u32[]{:S(2)}, u32[]{:S(2)}) collective-permute-start(bf16[96,768]{1,0:T(8,128)(2,1)} %get-tuple-element.112), channel_id=1, source_target_pairs={{0,16},{8,24},{16,0},{24,8},{1,17},{9,25},{17,1},{25,9},{2,18},{10... | collective-permute-start | bytes 442376 | tf_op jit(solution)/shard_map/ppermute | solution.py:803
  319.9 19.5 %collective-permute-start.25 = (bf16[96,768]{1,0:T(8,128)(2,1)}, bf16[96,768]{1,0:T(8,128)(2,1)S(1)}, u32[]{:S(2)}, u32[]{:S(2)}) collective-permute-start(bf16[96,768]{1,0:T(8,128)(2,1)} %get-tuple-element.113), channel_id=1, source_target_pairs={{0,24},{8,0},{16,8},{24,16},{1,25},{9,1},{17,9},{25,17},{2,26},{10... | collective-permute-start | bytes 442376 | tf_op jit(solution)/shard_map/ppermute | solution.py:803
  341.9 25.1 %collective-permute-start.28 = (bf16[96,768]{1,0:T(8,128)(2,1)}, bf16[96,768]{1,0:T(8,128)(2,1)S(1)}, u32[]{:S(2)}, u32[]{:S(2)}) collective-permute-start(bf16[96,768]{1,0:T(8,128)(2,1)} %dense_fourth.1.refs_3_.refs_1_), channel_id=1, source_target_pairs={{0,24},{8,0},{16,8},{24,16},{1,25},{9,1},{17,9},{25,17},{2,26},{10... | collective-permute-start | bytes 442376 | tf_op jit(solution)/shard_map/ppermute | solution.py:803
  343.5 23.6 %collective-permute-start.27 = (bf16[96,768]{1,0:T(8,128)(2,1)}, bf16[96,768]{1,0:T(8,128)(2,1)S(1)}, u32[]{:S(2)}, u32[]{:S(2)}) collective-permute-start(bf16[96,768]{1,0:T(8,128)(2,1)} %dense_fourth.1.refs_3_.refs_1_), channel_id=1, source_target_pairs={{0,16},{8,24},{16,0},{24,8},{1,17},{9,25},{17,1},{25,9},{2,18},{10... | collective-permute-start | bytes 442376 | tf_op jit(solution)/shard_map/ppermute | solution.py:803
  343.5 23.6 %collective-permute-start.26 = (bf16[96,768]{1,0:T(8,128)(2,1)}, bf16[96,768]{1,0:T(8,128)(2,1)S(1)}, u32[]{:S(2)}, u32[]{:S(2)}) collective-permute-start(bf16[96,768]{1,0:T(8,128)(2,1)} %dense_fourth.1.refs_3_.refs_1_), channel_id=1, source_target_pairs={{0,8},{8,16},{16,24},{24,0},{1,9},{9,17},{17,25},{25,1},{2,10},{10... | collective-permute-start | bytes 442376 | tf_op jit(solution)/shard_map/ppermute | solution.py:803
  369.8 13.2 %collective-permute-start.29 = (bf16[384,768]{1,0:T(8,128)(2,1)}, bf16[384,768]{1,0:T(8,128)(2,1)S(1)}, u32[]{:S(2)}, u32[]{:S(2)}) collective-permute-start(bf16[384,768]{1,0:T(8,128)(2,1)} %dense_fifth.1.refs_1_.refs_3_), channel_id=1, source_target_pairs={{0,4},{4,0},{1,5},{5,1},{2,6},{6,2},{3,7},{7,3},{8,12},{12,8},{9,1... | collective-permute-start | bytes 1769480 | tf_op jit(solution)/shard_map/ppermute | solution.py:797
  371.1 3.3 copy-start.1
  383.0 0.8 copy-start.8
  (12 other events, 8.6 us)
Sparse Core Ops, SparseCore 0:
  84.8 59.3 all-gather.6
  146.7 85.4 all-gather.10
  236.4 54.4 all-gather.8

commit v6 on v5

--- a/solution.py
+++ b/solution.py
@@ -318,6 +318,23 @@
         out[hop] = source[lax.rem(place_ref[2] + hop + 1, planes)]
 
 
+def pick_both_kernel(place_ref, *refs):
+    sources, column, rest, stack, sems = refs[:HALF], refs[HALF], refs[-3], refs[-2], refs[-1]
+    planes = column.shape[0]
+    copies = [
+        pltpu.make_async_copy(column.at[lax.rem(place_ref[2] + hop + 1, planes)], rest.at[hop], sems.at[hop])
+        for hop in range(planes - 1)
+    ]
+    copies += [
+        pltpu.make_async_copy(source, stack.at[index], sems.at[planes - 1 + index])
+        for index, source in enumerate(sources)
+    ]
+    for copy in copies:
+        copy.start()
+    for copy in copies:
+        copy.wait()
+
+
 def dispatch(base, blocks, members, after=()):
     width = blocks[0].rows.shape[2]
     out = ((members, 2 * HALF * CAP, width), bf16)
@@ -718,27 +735,37 @@
     return pl.ds(pl.multiple_of(index * size, size), size)
 
 
-def dense_first_kernel(place, near, more, side, other, keep_upper, keep_lower):
-    cut = near.shape[1] // 2
-    half = cut // 2
+def dense_copies(near, more, index, who, whole_s, half_s, sems):
+    cut = whole_s.shape[1]
+    half = half_s.shape[2]
+    rows = pl.ds(pl.multiple_of(cut + who * half, half), half)
+    copies = []
+    for term, source in enumerate((near, more)):
+        copies.append(pltpu.make_async_copy(source.at[index, pl.ds(0, cut)], whole_s.at[term], sems.at[3 * term]))
+        for shard in range(2):
+            copies.append(
+                pltpu.make_async_copy(source.at[shard, rows], half_s.at[term, shard], sems.at[3 * term + 1 + shard])
+            )
+    take_all(copies)
+
+
+def dense_first_kernel(place, near, more, side, other, whole_s, half_s, sems):
+    dense_copies(near, more, 1, 1 - place[0], whole_s, half_s, sems)
+    side[...] = (whole_s[0].astype(f32) + whole_s[1].astype(f32)).astype(bf16)
+    other[...] = (half_s[0].astype(f32) + half_s[1].astype(f32)).astype(bf16)
+
+
+def dense_second_kernel(place, near, more, from_side, from_other, side, other, upper, lower, whole_s, half_s, sems):
     mine = place[0]
-    side[...] = (near[1, 0:cut, :].astype(f32) + more[1, 0:cut, :].astype(f32)).astype(bf16)
-    keep_upper[...] = near[0, 0:cut, :].astype(f32) + more[0, 0:cut, :].astype(f32)
-    for index in range(2):
-        for out, who in ((keep_lower, mine), (other, 1 - mine)):
-            rows = pl.ds(pl.multiple_of(cut + who * half, half), half)
-            total = near[index, rows, :].astype(f32) + more[index, rows, :].astype(f32)
-            out[index] = total.astype(out.dtype)
-
-
-def dense_second_kernel(place, keep_upper, keep_lower, from_side, from_other, side, other, upper, lower):
+    dense_copies(near, more, 0, mine, whole_s, half_s, sems)
     half = upper.shape[0]
-    mine = place[0]
     for out, who in ((upper, mine), (other, 1 - mine)):
         rows = span_of(who, half)
-        out[...] = (keep_upper[rows, :] + from_side[rows, :].astype(f32)).astype(out.dtype)
-    lower[...] = keep_lower[0] + from_other[0].astype(f32)
-    side[...] = (keep_lower[1] + from_other[1].astype(f32)).astype(bf16)
+        total = whole_s[0, rows, :].astype(f32) + whole_s[1, rows, :].astype(f32) + from_side[rows, :].astype(f32)
+        out[...] = total.astype(out.dtype)
+    total = half_s[0].astype(f32) + half_s[1].astype(f32) + from_other[...].astype(f32)
+    lower[...] = total[0]
+    side[...] = total[1].astype(bf16)
 
 
 def dense_third_kernel(size, place, upper, lower, from_side, from_other, own, *outs):
@@ -849,17 +876,21 @@
         place = [jnp.stack([lax.axis_index("expert"), lax.axis_index("dp")]).astype(jnp.int32)]
         more = self.to_core(far)
         after = yield None
-        side, other, keep_upper, keep_lower = launch(
-            dense_first_kernel, "dense_first",
-            [((cut, width), bf16), ((2, half, width), bf16), ((cut, width), f32), ((2, half, width), f32)],
-            [near, more], scalars=place, after=after, moved=8 * 10**6,
+        anywhere, on_chip = pl.BlockSpec(memory_space=pl.ANY), pl.BlockSpec(memory_space=pltpu.VMEM)
+        scratch = [
+            pltpu.VMEM((2, cut, width), bf16), pltpu.VMEM((2, 2, half, width), bf16), pltpu.SemaphoreType.DMA((6,)),
+        ]
+        side, other = launch(
+            dense_first_kernel, "dense_first", [((cut, width), bf16), ((2, half, width), bf16)], [near, more],
+            in_specs=[anywhere] * 2, scalars=place, scratch=scratch, after=after, moved=4 * 10**6,
         )
         from_side, from_other = self.to_side(side), self.to_other(other)
-        after = yield keep_upper
+        after = yield side
         side, other, upper, lower = launch(
             dense_second_kernel, "dense_second",
             [((half, width), bf16), ((half, width), bf16), ((half, width), f32), ((half, width), f32)],
-            [keep_upper, keep_lower, from_side, from_other], scalars=place, after=after, moved=5 * 10**6,
+            [near, more, from_side, from_other], in_specs=[anywhere] * 2 + [on_chip] * 2, scalars=place,
+            scratch=scratch, after=after, moved=5 * 10**6,
         )
         from_side, from_other = self.to_side(side), self.to_other(other)
         after = yield upper
@@ -958,20 +989,23 @@
         cut = PATCHES // 2 + EXTRA
         ext_cuts = (ext_other[:cut], ext_side[cut:])
         ext_corner = (links.to_side(ext_cuts[0]), links.to_other(ext_cuts[1]))
-        cot_mine = assemble(
-            (HALF, PATCHES, width), bf16, [shared_cot, cot_side, cot_other, cot_corner],
-            [(index, whole, index) for index in range(HALF)], after=ext_cuts,
-        )
-        cot_near = links.to_core(cot_mine)
-        ext_column = links.column(ordered([ext_copies], [ext_side, ext_other])[0])
         ext_mine = assemble(
             (HALF, PATCHES + EXTRA, width), bf16, [ext, ext_side, ext_other, *ext_corner],
             [(index, whole, index) for index in range(3)]
             + [(3, whole, (3, pl.ds(0, cut))), (4, whole, (3, pl.ds(cut, PATCHES // 2)))],
         )
         ext_near = links.to_core(ext_mine)
+        pieces = [shared_cot, cot_side, cot_other, cot_corner]
+        cot_rest, cot_mine = launch(
+            pick_both_kernel, "pick_both",
+            [((links.dp - 1, PATCHES, width), bf16), ((HALF, PATCHES, width), bf16)], [*pieces, cot_column],
+            in_specs=[pl.BlockSpec(memory_space=pl.ANY)] * (HALF + 1), scalars=[place],
+            scratch=[pltpu.SemaphoreType.DMA((links.dp - 1 + HALF,))], after=[ext_mine], moved=5 * 10**6,
+        )
+        cots = lax.all_gather(cot_rest, ("expert", "tensor"), axis=0)
+        cot_near = links.to_core(cot_mine)
+        ext_column = links.column(ordered([ext_copies], [ext_side, ext_other])[0])
         own = (Blocks.apart(ext_mine, cot_mine), Blocks.apart(ext_near, cot_near))
-        cot_rest, cots = links.column_rest(cot_column, place, [cot_mine])
         first, second = experts_both(base, own, *feed, (0, 1, 4, 5), after=[cot_rest])
         ext_rest, exts = links.column_rest(ext_column, place, [first])
         moved = links.to_core(second)

time: 399 us -> 390 us (0.977)
  waiting for transfers between devices: 63.9 us -> 56 us
    ppermute x9, waiting for transfers between devices: 31.1 us -> 23.7 us  [to_other(): return lax.ppermute(value, 'expert', self.other)]
    pallas_call x29 -> x28, Pallas kernels: 242 us -> 243 us  [launch(): pl.pallas_call(body, out_shape=tuple((jax.ShapeDtypeStruct(*out) for out...]
    unnamed x51 -> x47, local copies, waits for them, and re-layouts: 8.26 us -> 7.16 us
  transfers between devices with their start and end apart: 36 -> 36, of which waited for: 17 -> 14; matrix products, arithmetic and copies ran while one was open for 5% -> 5% of each run, Pallas kernels for 60% -> 61%
where the time goes in v6:
time: 390 us; the launch traced here: 385 us
  Pallas kernels  243 us (62%)
  waiting for transfers between devices  56 us (14%)
  starting transfers between devices  41.8 us (11%)
  local copies, waits for them, and re-layouts  15 us (4%)
  between operations  14.3 us (4%)
  other arithmetic  8.54 us (2%)
  matrix products  5.43 us (1%)
    pallas_call x28, Pallas kernels, launch(): pl.pallas_call(body, out_shape=tuple((jax.ShapeDtypeStruct(*out) for out...  243 us
    ppermute x9, waiting for transfers between devices, to_other(): return lax.ppermute(value, 'expert', self.other)  23.7 us
    ppermute x8, waiting for transfers between devices, to_side(): return lax.ppermute(value, 'tensor', self.side)  18.1 us
    ppermute x9, starting transfers between devices, to_other(): return lax.ppermute(value, 'expert', self.other)  13.8 us
    all_to_all x2, starting transfers between devices, column(): return lax.all_to_all(copies, 'dp', split_axis=0, concat_axis=0)  10.1 us
    ppermute x6, starting transfers between devices, along(): lax.ppermute(value, 'dp', [(i, (i + hop) % self.dp) for i in range(self.d...  8.02 us
  transfers between devices with their start and end apart: 36, of which 14 were waited for; matrix products, arithmetic and copies ran while one was open for 5% of the time, Pallas kernels for 61%

profile of v6, /device:TPU:0, one launch (start us, length us, event | category | flops | bytes accessed | tf_op | source)
XLA Modules:
  0.0 384.6 jit_solution(801073754652095184)
XLA Ops:
  8.1 2.0 convolution_add_fusion
  10.8 4.2 %all-to-all-start = ((f32[4,6,192]{2,1,0:T(8,128)}), f32[4,6,192]{2,1,0:T(8,128)S(1)}, u32[]{:S(2)}, u32[]{:S(2)}) async-start(f32[4,6,192]{2,1,0:T(8,128)} %copy.43), calls=%async_computation | async-start | bytes 65536 | tf_op jit(solution)/shard_map/all_to_all | solution.py:953
  15.0 2.1 pad_maximum_fusion.refs_0_
  17.1 1.9 all-to-all-done
  20.9 2.0 collective-permute-start.2
  24.1 5.0 %all-to-all-start.1 = ((bf16[4,256,768]{2,1,0:T(8,128)(2,1)}), bf16[4,256,768]{2,1,0:T(8,128)(2,1)}, u32[]{:S(2)}, u32[]{:S(2)}) async-start(bf16[4,256,768]{2,1,0:T(8,128)(2,1)} %broadcast_in_dim.6), calls=%async_computation.1 | async-start | bytes 3145728 | tf_op jit(solution)/shard_map/all_to_all | solution.py:833
  29.9 2.0 collective-permute-done.2.refs_1_
  31.9 15.9 %collective-permute-done.1.refs_0_ = bf16[768,768]{1,0:T(8,128)(2,1)} collective-permute-done((bf16[768,768]{1,0:T(8,128)(2,1)}, bf16[768,768]{1,0:T(8,128)(2,1)}, u32[]{:S(2)}, u32[]{:S(2)}) %collective-permute-start.1) | collective-permute-done | bytes 1179680 | tf_op jit(solution)/shard_map/ppermute | solution.py:821
  51.0 7.9 %attention_forward.1 = (bf16[256,768]{1,0:T(8,128)(2,1)}, bf16[3,256,768]{2,1,0:T(8,128)(2,1)}, bf16[256,768]{1,0:T(8,128)(2,1)}, f32[256,768]{1,0:T(8,128)}, bf...) custom-call(bf16[256,768]{1,0:T(8,128)(2,1)} %refs_5_.1, f32[6,768]{1,0:T(8,128)} %squeeze.10.refs_2_.refs_1_.refs_7_, ...), custom_call_target="tpu_custom_call" | custom-call | flops 5000000000 | bytes 9000000 | tf_op jit(solution)/shard_map/attention_forward/pallas_call | solution.py:89
  58.9 2.0 collective-permute-start.5
  63.0 8.6 %collective-permute-done.5.refs_2_ = bf16[272,768]{1,0:T(8,128)(2,1)S(1)} collective-permute-done((bf16[272,768]{1,0:T(8,128)(2,1)}, bf16[272,768]{1,0:T(8,128)(2,1)S(1)}, u32[]{:S(2)}, u32[]{:S(2)}) %collective-permute-start.5) | collective-permute-done | bytes 417824 | tf_op jit(solution)/shard_map/ppermute | solution.py:824
  72.6 1.8 collective-permute-start.7
  75.0 8.9 %collective-permute-done.7.refs_4_ = bf16[128,768]{1,0:T(8,128)(2,1)} collective-permute-done((bf16[128,768]{1,0:T(8,128)(2,1)S(1)}, bf16[128,768]{1,0:T(8,128)(2,1)}, u32[]{:S(2)}, u32[]{:S(2)}) %collective-permute-start.7) | collective-permute-done | bytes 196640 | tf_op jit(solution)/shard_map/ppermute | solution.py:824
  83.9 2.6 assemble.1.refs_6_.refs_1_.refs_2_.refs_0_
  86.5 4.1 %pick_both.1 = (bf16[3,256,768]{2,1,0:T(8,128)(2,1)}, bf16[4,256,768]{2,1,0:T(8,128)(2,1)}) custom-call(s32[3]{0:T(128)} %pad_add_fusion.1.refs_0_, bf16[256,768]{1,0:T(8,128)(2,1)} %multiply_convert_fusion.refs_1_, bf16[256,768]{1,0:T(8,128)(2,1)} %collective-permute-done.8.refs_2_, bf16[256,768]{1,0:T(8,128)(2,1)} %get-tuple-element.68.refs_3_, ...), custom_call_target="tpu_custom_call" | custom-call | bytes 5000000 | tf_op jit(solution)/shard_map/pick_both/pallas_call | solution.py:89
  91.2 5.1 %all-to-all-start.2 = ((bf16[4,272,768]{2,1,0:T(8,128)(2,1)}), bf16[4,272,768]{2,1,0:T(8,128)(2,1)}, u32[]{:S(2)}, u32[]{:S(2)}) async-start(bf16[4,272,768]{2,1,0:T(8,128)(2,1)} %ordered.8), calls=%async_computation.2 | async-start | bytes 3342336 | tf_op jit(solution)/shard_map/all_to_all | solution.py:833
  96.8 36.5 %experts_both.1 = (bf16[4,528,768]{2,1,0:T(8,128)(2,1)}, bf16[4,528,768]{2,1,0:T(8,128)(2,1)}) custom-call(s32[1]{0:T(128)} %bitcast.refs_0_, bf16[4,272,768]{2,1,0:T(8,128)(2,1)} %assemble.1.refs_6_.refs_1_.refs_2_.refs_0_, bf16[4,272,768]{2,1,0:T(8,128)(2,1)} %assemble.1.refs_6_.refs_1_.refs_2_.refs_0_, ...), custom_call_target="tpu_custom_call" | custom-call | flops 30000001024 | bytes 30000000 | tf_op jit(solution)/shard_map/experts_both/pallas_call | solution.py:89
  133.3 2.3 all-to-all-done.2.refs_1_
  135.7 2.7 pick.1.refs_2_
  139.3 5.5 %collective-permute-done.12.refs_1_ = bf16[4,528,768]{2,1,0:T(8,128)(2,1)} collective-permute-done((bf16[4,528,768]{2,1,0:T(8,128)(2,1)}, bf16[4,528,768]{2,1,0:T(8,128)(2,1)}, u32[]{:S(2)}, u32[]{:S(2)}) %collective-permute-start.12) | collective-permute-done | bytes 3244064 | tf_op jit(solution)/shard_map/ppermute | solution.py:818
  144.9 3.3 plane_first.1
  148.6 2.2 collective-permute-start.14
  150.8 7.4 %dispatch.1 = (bf16[4,640,768]{2,1,0:T(8,128)(2,1)}, bf16[4,640,768]{2,1,0:T(8,128)(2,1)}) custom-call(s32[1]{0:T(128)} %bitcast.refs_0_, bf16[4,272,768]{2,1,0:T(8,128)(2,1)} %assemble.1.refs_6_.refs_1_.refs_2_.refs_0_, bf16[4,272,768]{2,1,0:T(8,128)(2,1)} %assemble.1.refs_6_.refs_1_.refs_2_.refs_0_, ...), custom_call_target="tpu_custom_call" | custom-call | flops 8000000000 | bytes 16000000 | tf_op jit(solution)/shard_map/dispatch/pallas_call | solution.py:89
  158.2 20.7 %weight_grads.5 = (f32[4,768,768]{2,1,0:T(8,128)}, f32[4,768,768]{2,1,0:T(8,128)}) custom-call(bf16[4,640,768]{2,1,0:T(8,128)(2,1)} %get-tuple-element.76.refs_0_, bf16[4,640,768]{2,1,0:T(8,128)(2,1)} %get-tuple-element.77.refs_1_, bf16[4,768,768]{2,1,0:T(8,128)(2,1)} %refs_2_.9, bf16[4,768,768]{2,1,0:T(8,128)(2,1)} %refs_3_.9), custom_call_target="tpu_custom_call" | custom-call | flops 18119393280 | bytes 7864320 | tf_op jit(solution)/shard_map/weight_grads/pallas_call | solution.py:89
  179.8 4.9 %plane_second.1 = (f32[256,768]{1,0:T(8,128)}, f32[272,768]{1,0:T(8,128)}, bf16[256,768]{1,0:T(8,128)(2,1)}, bf16[272,768]{1,0:T(8,128)(2,1)}) custom-call(bf16[4,528,768]{2,1,0:T(8,128)(2,1)} %get-tuple-element.71.refs_2_.refs_0_, bf16[4,528,768]{2,1,0:T(8,128)(2,1)} %collective-permute-done.12.refs_1_, ...), custom_call_target="tpu_custom_call" | custom-call | bytes 7000000 | tf_op jit(solution)/shard_map/plane_second/pallas_call | solution.py:89
  185.7 16.9 %weight_grads.6 = (f32[1,768,768]{2,1,0:T(8,128)}, f32[1,768,768]{2,1,0:T(8,128)}) custom-call(bf16[4,272,768]{2,1,0:T(8,128)(2,1)} %assemble.1.refs_6_.refs_1_.refs_2_.refs_0_, bf16[4,272,768]{2,1,0:T(8,128)(2,1)} %collective-permute-done.10.refs_4_.refs_5_.refs_1_, bf16[4,256,768]{2,1,0:T(8,128)(2,1)} %get-tuple-element.69.refs_3_.refs_2_, ...), custom_call_target="tpu_custom_call" | custom-call | flops 14495514624 | bytes 6291456 | tf_op jit(solution)/shard_map/weight_grads/pallas_call | solution.py:89
  203.3 1.8 collective-permute-done.16.refs_3_
  205.9 16.4 %attention_backward.1 = (bf16[256,768]{1,0:T(8,128)(2,1)}, f32[256,768]{1,0:T(8,128)}, f32[16,768]{1,0:T(8,128)}, bf16[2,768,768]{2,1,0:T(8,128)(2,1)}, bf16[2,768,768]{2,1,0:T(8,128)(2,1)}) custom-call(f32[256,768]{1,0:T(8,128)} %get-tuple-element.79.refs_6_.refs_0_, bf16[256,768]{1,0:T(8,128)(2,1)} %copy-done.21, f32[272,768]{1,0:T(8,128)} %get-tuple-element.81.refs_2_, ...), custom_call_target="tpu_custom_call" | custom-call | flops 10000000000 | bytes 16000000 | tf_op jit(solution)/shard_map/attention_backward/pallas_call | solution.py:89
  224.6 2.8 all-gather.11.cloned.1.call-done
  227.4 19.0 %shared_grads_other.1 = (f32[768,768]{1,0:T(8,128)}, f32[768,768]{1,0:T(8,128)}, bf16[2,768,768]{2,1,0:T(8,128)(2,1)}) custom-call(bf16[8,3,272,768]{3,2,1,0:T(8,128)(2,1)} %bitcast.43, bf16[8,3,256,768]{3,2,1,0:T(8,128)(2,1)} %bitcast.47, bf16[768,768]{1,0:T(8,128)(2,1)} %refs_2_.6, bf16[768,768]{1,0:T(8,128)(2,1)} %refs_3_.6, ...), custom_call_target="tpu_custom_call" | custom-call | flops 14495514624 | bytes 6291456 | tf_op jit(solution)/shard_map/shared_grads_other/pallas_call | solution.py:89
  246.5 3.4 dense_first.1
  251.5 18.5 %dispatch_hops.1 = (bf16[4,1920,768]{2,1,0:T(8,128)(2,1)}, bf16[4,1920,768]{2,1,0:T(8,128)(2,1)}) custom-call(s32[1]{0:T(128)} %bitcast.refs_0_, bf16[8,3,272,768]{3,2,1,0:T(8,128)(2,1)} %bitcast.44, bf16[8,3,256,768]{3,2,1,0:T(8,128)(2,1)} %bitcast.48, bf16[384,768]{1,0:T(8,128)(2,1)} %get-tuple-element.95.refs_3_), custom_call_target="tpu_custom_call" | custom-call | flops 24000000000 | bytes 48000000 | tf_op jit(solution)/shard_map/dispatch_hops/pallas_call | solution.py:89
  272.0 4.2 %dense_second.1 = (bf16[192,768]{1,0:T(8,128)(2,1)}, bf16[192,768]{1,0:T(8,128)(2,1)}, f32[192,768]{1,0:T(8,128)}, f32[192,768]{1,0:T(8,128)}) custom-call(s32[2]{0:T(128)} %pad_add_fusion.2.refs_0_, bf16[2,768,768]{2,1,0:T(8,128)(2,1)} %get-tuple-element.91.refs_1_, bf16[2,768,768]{2,1,0:T(8,128)(2,1)} %collective-permute-done.17.refs_2_, ...), custom_call_target="tpu_custom_call" | custom-call | bytes 5000000 | tf_op jit(solution)/shard_map/dense_second/pallas_call | solution.py:89
  276.2 1.9 collective-permute-start.20
  278.7 27.2 %weight_grads.7 = (f32[4,768,768]{2,1,0:T(8,128)}, f32[4,768,768]{2,1,0:T(8,128)}) custom-call(bf16[4,1920,768]{2,1,0:T(8,128)(2,1)} %get-tuple-element.96.refs_5_.refs_0_, bf16[4,1920,768]{2,1,0:T(8,128)(2,1)} %get-tuple-element.97.refs_1_, bf16[4,768,768]{2,1,0:T(8,128)(2,1)} %refs_2_.9, ...), custom_call_target="tpu_custom_call", output_to_operand_aliasing={{0}: (4, {}), {1}: (5, {})} | custom-call | flops 27179089920 | bytes 11796480 | tf_op jit(solution)/shard_map/weight_grads/pallas_call | solution.py:89
  306.8 2.4 dense_third.1
  309.2 2.1 collective-permute-start.23
  311.3 2.4 collective-permute-start.25
  313.7 16.5 %weight_grads.8 = (f32[4,768,768]{2,1,0:T(8,128)}, f32[4,768,768]{2,1,0:T(8,128)}) custom-call(bf16[4,1920,768]{2,1,0:T(8,128)(2,1)} %get-tuple-element.96.refs_5_.refs_0_, bf16[4,1920,768]{2,1,0:T(8,128)(2,1)} %get-tuple-element.97.refs_1_, bf16[4,768,768]{2,1,0:T(8,128)(2,1)} %refs_2_.9, ...), custom_call_target="tpu_custom_call", output_to_operand_aliasing={{0}: (4, {}), {1}: (5, {})} | custom-call | flops 13589544960 | bytes 5898240 | tf_op jit(solution)/shard_map/weight_grads/pallas_call | solution.py:89
  331.0 1.9 dense_fourth.1.refs_3_.refs_1_
  332.8 2.0 collective-permute-start.28
  334.9 1.5 collective-permute-start.26
  336.4 5.5 %shared_last.1 = (f32[768,768]{1,0:T(8,128)}, f32[768,768]{1,0:T(8,128)}) custom-call(f32[768,768]{1,0:T(8,128)} %get-tuple-element.109.refs_0_, f32[768,768]{1,0:T(8,128)} %get-tuple-element.110.refs_1_, bf16[2,768,768]{2,1,0:T(8,128)(2,1)} %collective-permute-done.22.refs_2_, bf16[96,768]{1,0:T(8,128)(2,1)} %dense_fourth.1.refs_3_.refs_1_), custom_call_target="tpu_custom_call" | custom-call | bytes 12000000 | tf_op jit(solution)/shard_map/shared_last/pallas_call | solution.py:89
  341.9 16.4 %weight_grads.9 = (f32[4,768,768]{2,1,0:T(8,128)}, f32[4,768,768]{2,1,0:T(8,128)}) custom-call(bf16[4,1920,768]{2,1,0:T(8,128)(2,1)} %get-tuple-element.96.refs_5_.refs_0_, bf16[4,1920,768]{2,1,0:T(8,128)(2,1)} %get-tuple-element.97.refs_1_, bf16[4,768,768]{2,1,0:T(8,128)(2,1)} %refs_2_.9, ...), custom_call_target="tpu_custom_call", output_to_operand_aliasing={{0}: (4, {}), {1}: (5, {})} | custom-call | flops 13589544960 | bytes 5898240 | tf_op jit(solution)/shard_map/weight_grads/pallas_call | solution.py:89
  359.1 2.0 dense_fifth.1.refs_1_.refs_3_
  367.3 3.4 fusion
  370.7 3.4 collective-permute-done.29.refs_2_
  375.0 2.9 dense_last.1
  (133 shorter events, 34.0 us)
Async XLA Ops:
  7.2 7.8 %copy-start.5 = (bf16[768,3,192]{0,2,1:T(8,128)(2,1)S(1)}, bf16[768,3,192]{0,2,1:T(8,128)(2,1)}, u32[]{:S(2)}) copy-start(bf16[768,3,192]{0,2,1:T(8,128)(2,1)} %param.19) | copy-start | bytes 2654212
  7.2 11.9 %copy-start.9 = (bf16[256,768]{1,0:T(8,128)(2,1)S(1)}, bf16[256,768]{1,0:T(8,128)(2,1)}, u32[]{:S(2)}) copy-start(bf16[256,768]{1,0:T(8,128)(2,1)} %refs_6_.1) | copy-start | bytes 1179652
  10.8 8.2 %all-to-all-start = ((f32[4,6,192]{2,1,0:T(8,128)}), f32[4,6,192]{2,1,0:T(8,128)S(1)}, u32[]{:S(2)}, u32[]{:S(2)}) async-start(f32[4,6,192]{2,1,0:T(8,128)} %copy.43), calls=%async_computation | async-start | bytes 65536 | tf_op jit(solution)/shard_map/all_to_all | solution.py:953
  19.9 1.0 copy-start
  19.9 27.9 %collective-permute-start.1 = (bf16[768,768]{1,0:T(8,128)(2,1)}, bf16[768,768]{1,0:T(8,128)(2,1)}, u32[]{:S(2)}, u32[]{:S(2)}) collective-permute-start(bf16[768,768]{1,0:T(8,128)(2,1)} %ordered.5.refs_4_.refs_15_), channel_id=1, source_target_pairs={{0,2},{1,3},{2,0},{3,1},{4,6},{5,7},{6,4},{7,5},{8,10},{9,11},{10,... | collective-permute-start | bytes 3538952 | tf_op jit(solution)/shard_map/ppermute | solution.py:821
  20.9 11.0 %collective-permute-start.2 = (bf16[256,768]{1,0:T(8,128)(2,1)S(1)}, bf16[256,768]{1,0:T(8,128)(2,1)S(1)}, u32[]{:S(2)}, u32[]{:S(2)}) collective-permute-start(bf16[256,768]{1,0:T(8,128)(2,1)S(1)} %copy-done), channel_id=1, source_target_pairs={{0,4},{4,0},{1,5},{5,1},{2,6},{6,2},{3,7},{7,3},{8,12},{12,8},{9,1... | collective-permute-start | bytes 1179656 | tf_op jit(solution)/shard_map/ppermute | solution.py:824
  24.1 23.7 %copy-start.18 = (s32[256,2]{0,1:T(2,128)S(1)}, s32[256,2]{0,1:T(2,128)}, u32[]{:S(2)}) copy-start(s32[256,2]{0,1:T(2,128)} %param.27) | copy-start | bytes 6148
  24.1 23.7 %copy-start.19 = (s32[256,2]{0,1:T(2,128)S(1)}, s32[256,2]{0,1:T(2,128)}, u32[]{:S(2)}) copy-start(s32[256,2]{0,1:T(2,128)} %param.26) | copy-start | bytes 6148
  24.1 62.4 %all-to-all-start.1 = ((bf16[4,256,768]{2,1,0:T(8,128)(2,1)}), bf16[4,256,768]{2,1,0:T(8,128)(2,1)}, u32[]{:S(2)}, u32[]{:S(2)}) async-start(bf16[4,256,768]{2,1,0:T(8,128)(2,1)} %broadcast_in_dim.6), calls=%async_computation.1 | async-start | bytes 3145728 | tf_op jit(solution)/shard_map/all_to_all | solution.py:833
  29.1 156.6 %all-gather.7.cloned.1.call-start = ((), (), s32[]{:S(2)}) async-start(), calls=%async_computation.3 | async-start | bytes 10616832 | tf_op jit(solution)/shard_map/all_gather | solution.py:1005
  29.1 20.6 %collective-permute-start = (bf16[768,768]{1,0:T(8,128)(2,1)}, bf16[768,768]{1,0:T(8,128)(2,1)}, u32[]{:S(2)}, u32[]{:S(2)}) collective-permute-start(bf16[768,768]{1,0:T(8,128)(2,1)} %ordered.5.refs_4_.refs_15_), channel_id=1, source_target_pairs={{0,1},{1,0},{2,3},{3,2},{4,5},{5,4},{6,7},{7,6},{8,9},{9,8},{10,11... | collective-permute-start | bytes 3538952 | tf_op jit(solution)/shard_map/ppermute | solution.py:818
  31.9 15.9 %copy-start.4 = (bf16[256,768]{1,0:T(8,128)(2,1)}, bf16[256,768]{1,0:T(8,128)(2,1)S(1)}, u32[]{:S(2)}) copy-start(bf16[256,768]{1,0:T(8,128)(2,1)S(1)} %collective-permute-done.2.refs_1_) | copy-start | bytes 1179652
  47.8 3.2 collective-permute-start.3
  49.2 12.3 %collective-permute-start.8 = (bf16[256,768]{1,0:T(8,128)(2,1)}, bf16[256,768]{1,0:T(8,128)(2,1)}, u32[]{:S(2)}, u32[]{:S(2)}) collective-permute-start(bf16[256,768]{1,0:T(8,128)(2,1)} %ordered.7), channel_id=1, source_target_pairs={{0,2},{1,3},{2,0},{3,1},{4,6},{5,7},{6,4},{7,5},{8,10},{9,11},{10,... | collective-permute-start | bytes 1179656 | tf_op jit(solution)/shard_map/ppermute | solution.py:821
  58.9 12.7 %collective-permute-start.5 = (bf16[272,768]{1,0:T(8,128)(2,1)}, bf16[272,768]{1,0:T(8,128)(2,1)S(1)}, u32[]{:S(2)}, u32[]{:S(2)}) collective-permute-start(bf16[272,768]{1,0:T(8,128)(2,1)} %get-tuple-element.67.refs_0_.refs_14_), channel_id=1, source_target_pairs={{0,4},{4,0},{1,5},{5,1},{2,6},{6,2},{3,7},{7,3},{8,12},{12,8},{9,1... | collective-permute-start | bytes 1253384 | tf_op jit(solution)/shard_map/ppermute | solution.py:824
  60.9 11.6 %collective-permute-start.4 = (bf16[272,768]{1,0:T(8,128)(2,1)}, bf16[272,768]{1,0:T(8,128)(2,1)S(1)}, u32[]{:S(2)}, u32[]{:S(2)}) collective-permute-start(bf16[272,768]{1,0:T(8,128)(2,1)} %get-tuple-element.67.refs_0_.refs_14_), channel_id=1, source_target_pairs={{0,2},{1,3},{2,0},{3,1},{4,6},{5,7},{6,4},{7,5},{8,10},{9,11},{10,... | collective-permute-start | bytes 1253384 | tf_op jit(solution)/shard_map/ppermute | solution.py:821
  61.5 24.9 %collective-permute-start.9 = (bf16[256,768]{1,0:T(8,128)(2,1)}, bf16[256,768]{1,0:T(8,128)(2,1)}, u32[]{:S(2)}, u32[]{:S(2)}) collective-permute-start(bf16[256,768]{1,0:T(8,128)(2,1)} %collective-permute-done.8.refs_2_), channel_id=1, source_target_pairs={{0,4},{4,0},{1,5},{5,1},{2,6},{6,2},{3,7},{7,3},{8,12},{12,8},{9,1... | collective-permute-start | bytes 1179656 | tf_op jit(solution)/shard_map/ppermute | solution.py:824
  71.6 12.2 %copy-start.2 = (bf16[272,768]{1,0:T(8,128)(2,1)}, bf16[272,768]{1,0:T(8,128)(2,1)S(1)}, u32[]{:S(2)}) copy-start(bf16[272,768]{1,0:T(8,128)(2,1)S(1)} %collective-permute-done.5.refs_2_) | copy-start | bytes 1253380
  71.6 12.2 %collective-permute-start.6 = (bf16[144,768]{1,0:T(8,128)(2,1)S(1)}, bf16[144,768]{1,0:T(8,128)(2,1)}, u32[]{:S(2)}, u32[]{:S(2)}) collective-permute-start(bf16[144,768]{1,0:T(8,128)(2,1)S(1)} %slice.39), channel_id=1, source_target_pairs={{0,2},{1,3},{2,0},{3,1},{4,6},{5,7},{6,4},{7,5},{8,10},{9,11},{10,... | collective-permute-start | bytes 663560 | tf_op jit(solution)/shard_map/ppermute | solution.py:821
  72.6 11.3 %copy-start.3 = (bf16[272,768]{1,0:T(8,128)(2,1)}, bf16[272,768]{1,0:T(8,128)(2,1)S(1)}, u32[]{:S(2)}) copy-start(bf16[272,768]{1,0:T(8,128)(2,1)S(1)} %collective-permute-done.4.refs_1_) | copy-start | bytes 1253380
  72.6 11.3 %collective-permute-start.7 = (bf16[128,768]{1,0:T(8,128)(2,1)S(1)}, bf16[128,768]{1,0:T(8,128)(2,1)}, u32[]{:S(2)}, u32[]{:S(2)}) collective-permute-start(bf16[128,768]{1,0:T(8,128)(2,1)S(1)} %slice.40), channel_id=1, source_target_pairs={{0,4},{4,0},{1,5},{5,1},{2,6},{6,2},{3,7},{7,3},{8,12},{12,8},{9,1... | collective-permute-start | bytes 589832 | tf_op jit(solution)/shard_map/ppermute | solution.py:824
  90.6 6.2 %collective-permute-start.10 = (bf16[4,272,768]{2,1,0:T(8,128)(2,1)}, bf16[4,272,768]{2,1,0:T(8,128)(2,1)}, u32[]{:S(2)}, u32[]{:S(2)}) collective-permute-start(bf16[4,272,768]{2,1,0:T(8,128)(2,1)} %assemble.1.refs_6_.refs_1_.refs_2_.refs_0_), channel_id=1, source_target_pairs={{0,1},{1,0},{2,3},{3,2},{4,5},{5,4},{6,7},{7,6},{8,9},{9,8},{10,11... | collective-permute-start | bytes 5013512 | tf_op jit(solution)/shard_map/ppermute | solution.py:818
  90.7 6.1 %collective-permute-start.11 = (bf16[4,256,768]{2,1,0:T(8,128)(2,1)}, bf16[4,256,768]{2,1,0:T(8,128)(2,1)}, u32[]{:S(2)}, u32[]{:S(2)}) collective-permute-start(bf16[4,256,768]{2,1,0:T(8,128)(2,1)} %get-tuple-element.69.refs_3_.refs_2_), channel_id=1, source_target_pairs={{0,1},{1,0},{2,3},{3,2},{4,5},{5,4},{6,7},{7,6},{8,9},{9,8},{10,11... | collective-permute-start | bytes 4718600 | tf_op jit(solution)/shard_map/ppermute | solution.py:818
  91.2 44.5 %all-to-all-start.2 = ((bf16[4,272,768]{2,1,0:T(8,128)(2,1)}), bf16[4,272,768]{2,1,0:T(8,128)(2,1)}, u32[]{:S(2)}, u32[]{:S(2)}) async-start(bf16[4,272,768]{2,1,0:T(8,128)(2,1)} %ordered.8), calls=%async_computation.2 | async-start | bytes 3342336 | tf_op jit(solution)/shard_map/all_to_all | solution.py:833
  96.2 131.1 %all-gather.11.cloned.1.call-start = ((), (), s32[]{:S(2)}) async-start(), calls=%async_computation.5 | async-start | bytes 11280384 | tf_op jit(solution)/shard_map/all_gather | solution.py:841
  138.4 225.0 %all-gather.9.cloned.1.call-start = ((), (), s32[]{:S(2)}) async-start(), calls=%async_computation.4 | async-start | bytes 1622016 | tf_op jit(solution)/shard_map/all_gather | solution.py:1026
  138.7 6.2 %collective-permute-start.12 = (bf16[4,528,768]{2,1,0:T(8,128)(2,1)}, bf16[4,528,768]{2,1,0:T(8,128)(2,1)}, u32[]{:S(2)}, u32[]{:S(2)}) collective-permute-start(bf16[4,528,768]{2,1,0:T(8,128)(2,1)} %get-tuple-element.72), channel_id=1, source_target_pairs={{0,1},{1,0},{2,3},{3,2},{4,5},{5,4},{6,7},{7,6},{8,9},{9,8},{10,11... | collective-permute-start | bytes 9732104 | tf_op jit(solution)/shard_map/ppermute | solution.py:818
  148.2 30.7 %collective-permute-start.13 = (bf16[2,256,768]{2,1,0:T(8,128)(2,1)}, bf16[2,256,768]{2,1,0:T(8,128)(2,1)}, u32[]{:S(2)}, u32[]{:S(2)}) collective-permute-start(bf16[2,256,768]{2,1,0:T(8,128)(2,1)} %get-tuple-element.74.refs_7_), channel_id=1, source_target_pairs={{0,2},{1,3},{2,0},{3,1},{4,6},{5,7},{6,4},{7,5},{8,10},{9,11},{10,... | collective-permute-start | bytes 2359304 | tf_op jit(solution)/shard_map/ppermute | solution.py:821
  148.6 30.3 %collective-permute-start.14 = (bf16[2,272,768]{2,1,0:T(8,128)(2,1)}, bf16[2,272,768]{2,1,0:T(8,128)(2,1)S(1)}, u32[]{:S(2)}, u32[]{:S(2)}) collective-permute-start(bf16[2,272,768]{2,1,0:T(8,128)(2,1)} %get-tuple-element.75), channel_id=1, source_target_pairs={{0,4},{4,0},{1,5},{5,1},{2,6},{6,2},{3,7},{7,3},{8,12},{12,8},{9,1... | collective-permute-start | bytes 2506760 | tf_op jit(solution)/shard_map/ppermute | solution.py:824
  178.9 0.9 copy-start.6
  184.7 18.6 %collective-permute-start.15 = (bf16[256,768]{1,0:T(8,128)(2,1)}, bf16[256,768]{1,0:T(8,128)(2,1)S(1)}, u32[]{:S(2)}, u32[]{:S(2)}) collective-permute-start(bf16[256,768]{1,0:T(8,128)(2,1)} %get-tuple-element.80), channel_id=1, source_target_pairs={{0,4},{4,0},{1,5},{5,1},{2,6},{6,2},{3,7},{7,3},{8,12},{12,8},{9,1... | collective-permute-start | bytes 1179656 | tf_op jit(solution)/shard_map/ppermute | solution.py:824
  185.6 19.6 %collective-permute-start.16 = (bf16[272,768]{1,0:T(8,128)(2,1)}, bf16[272,768]{1,0:T(8,128)(2,1)S(1)}, u32[]{:S(2)}, u32[]{:S(2)}) collective-permute-start(bf16[272,768]{1,0:T(8,128)(2,1)} %get-tuple-element.82), channel_id=1, source_target_pairs={{0,2},{1,3},{2,0},{3,1},{4,6},{5,7},{6,4},{7,5},{8,10},{9,11},{10,... | collective-permute-start | bytes 1253384 | tf_op jit(solution)/shard_map/ppermute | solution.py:821
  203.3 1.8 copy-start.21
  222.3 24.2 %collective-permute-start.17 = (bf16[2,768,768]{2,1,0:T(8,128)(2,1)}, bf16[2,768,768]{2,1,0:T(8,128)(2,1)}, u32[]{:S(2)}, u32[]{:S(2)}) collective-permute-start(bf16[2,768,768]{2,1,0:T(8,128)(2,1)} %get-tuple-element.92), channel_id=1, source_target_pairs={{0,1},{1,0},{2,3},{3,2},{4,5},{5,4},{6,7},{7,6},{8,9},{9,8},{10,11... | collective-permute-start | bytes 7077896 | tf_op jit(solution)/shard_map/ppermute | solution.py:818
  246.4 90.0 %collective-permute-start.22 = (bf16[2,768,768]{2,1,0:T(8,128)(2,1)}, bf16[2,768,768]{2,1,0:T(8,128)(2,1)}, u32[]{:S(2)}, u32[]{:S(2)}) collective-permute-start(bf16[2,768,768]{2,1,0:T(8,128)(2,1)} %get-tuple-element.94.refs_3_), channel_id=1, source_target_pairs={{0,8},{8,0},{16,24},{24,16},{1,9},{9,1},{17,25},{25,17},{2,10},{10... | collective-permute-start | bytes 7077896 | tf_op jit(solution)/shard_map/ppermute | solution.py:827
  249.9 21.2 %collective-permute-start.19 = (bf16[2,192,768]{2,1,0:T(8,128)(2,1)}, bf16[2,192,768]{2,1,0:T(8,128)(2,1)S(1)}, u32[]{:S(2)}, u32[]{:S(2)}) collective-permute-start(bf16[2,192,768]{2,1,0:T(8,128)(2,1)} %get-tuple-element.99), channel_id=1, source_target_pairs={{0,4},{4,0},{1,5},{5,1},{2,6},{6,2},{3,7},{7,3},{8,12},{12,8},{9,1... | collective-permute-start | bytes 1769480 | tf_op jit(solution)/shard_map/ppermute | solution.py:824
  251.3 19.9 %collective-permute-start.18 = (bf16[384,768]{1,0:T(8,128)(2,1)}, bf16[384,768]{1,0:T(8,128)(2,1)}, u32[]{:S(2)}, u32[]{:S(2)}) collective-permute-start(bf16[384,768]{1,0:T(8,128)(2,1)} %get-tuple-element.95.refs_3_), channel_id=1, source_target_pairs={{0,2},{1,3},{2,0},{3,1},{4,6},{5,7},{6,4},{7,5},{8,10},{9,11},{10,... | collective-permute-start | bytes 1769480 | tf_op jit(solution)/shard_map/ppermute | solution.py:821
  276.2 29.7 %collective-permute-start.20 = (bf16[192,768]{1,0:T(8,128)(2,1)}, bf16[192,768]{1,0:T(8,128)(2,1)S(1)}, u32[]{:S(2)}, u32[]{:S(2)}) collective-permute-start(bf16[192,768]{1,0:T(8,128)(2,1)} %get-tuple-element.104), channel_id=1, source_target_pairs={{0,2},{1,3},{2,0},{3,1},{4,6},{5,7},{6,4},{7,5},{8,10},{9,11},{10,... | collective-permute-start | bytes 884744 | tf_op jit(solution)/shard_map/ppermute | solution.py:821
  278.1 27.9 %collective-permute-start.21 = (bf16[192,768]{1,0:T(8,128)(2,1)}, bf16[192,768]{1,0:T(8,128)(2,1)S(1)}, u32[]{:S(2)}, u32[]{:S(2)}) collective-permute-start(bf16[192,768]{1,0:T(8,128)(2,1)} %get-tuple-element.105), channel_id=1, source_target_pairs={{0,4},{4,0},{1,5},{5,1},{2,6},{6,2},{3,7},{7,3},{8,12},{12,8},{9,1... | collective-permute-start | bytes 884744 | tf_op jit(solution)/shard_map/ppermute | solution.py:824
  309.2 21.0 %collective-permute-start.23 = (bf16[96,768]{1,0:T(8,128)(2,1)}, bf16[96,768]{1,0:T(8,128)(2,1)S(1)}, u32[]{:S(2)}, u32[]{:S(2)}) collective-permute-start(bf16[96,768]{1,0:T(8,128)(2,1)} %get-tuple-element.111), channel_id=1, source_target_pairs={{0,8},{8,16},{16,24},{24,0},{1,9},{9,17},{17,25},{25,1},{2,10},{10... | collective-permute-start | bytes 442376 | tf_op jit(solution)/shard_map/ppermute | solution.py:830
  311.3 18.9 %collective-permute-start.24 = (bf16[96,768]{1,0:T(8,128)(2,1)}, bf16[96,768]{1,0:T(8,128)(2,1)S(1)}, u32[]{:S(2)}, u32[]{:S(2)}) collective-permute-start(bf16[96,768]{1,0:T(8,128)(2,1)} %get-tuple-element.112), channel_id=1, source_target_pairs={{0,16},{8,24},{16,0},{24,8},{1,17},{9,25},{17,1},{25,9},{2,18},{10... | collective-permute-start | bytes 442376 | tf_op jit(solution)/shard_map/ppermute | solution.py:830
  311.3 18.9 %collective-permute-start.25 = (bf16[96,768]{1,0:T(8,128)(2,1)}, bf16[96,768]{1,0:T(8,128)(2,1)S(1)}, u32[]{:S(2)}, u32[]{:S(2)}) collective-permute-start(bf16[96,768]{1,0:T(8,128)(2,1)} %get-tuple-element.113), channel_id=1, source_target_pairs={{0,24},{8,0},{16,8},{24,16},{1,25},{9,1},{17,9},{25,17},{2,26},{10... | collective-permute-start | bytes 442376 | tf_op jit(solution)/shard_map/ppermute | solution.py:830
  332.8 25.5 %collective-permute-start.28 = (bf16[96,768]{1,0:T(8,128)(2,1)}, bf16[96,768]{1,0:T(8,128)(2,1)S(1)}, u32[]{:S(2)}, u32[]{:S(2)}) collective-permute-start(bf16[96,768]{1,0:T(8,128)(2,1)} %dense_fourth.1.refs_3_.refs_1_), channel_id=1, source_target_pairs={{0,24},{8,0},{16,8},{24,16},{1,25},{9,1},{17,9},{25,17},{2,26},{10... | collective-permute-start | bytes 442376 | tf_op jit(solution)/shard_map/ppermute | solution.py:830
  334.9 23.4 %collective-permute-start.27 = (bf16[96,768]{1,0:T(8,128)(2,1)}, bf16[96,768]{1,0:T(8,128)(2,1)S(1)}, u32[]{:S(2)}, u32[]{:S(2)}) collective-permute-start(bf16[96,768]{1,0:T(8,128)(2,1)} %dense_fourth.1.refs_3_.refs_1_), channel_id=1, source_target_pairs={{0,16},{8,24},{16,0},{24,8},{1,17},{9,25},{17,1},{25,9},{2,18},{10... | collective-permute-start | bytes 442376 | tf_op jit(solution)/shard_map/ppermute | solution.py:830
  334.9 23.5 %collective-permute-start.26 = (bf16[96,768]{1,0:T(8,128)(2,1)}, bf16[96,768]{1,0:T(8,128)(2,1)S(1)}, u32[]{:S(2)}, u32[]{:S(2)}) collective-permute-start(bf16[96,768]{1,0:T(8,128)(2,1)} %dense_fourth.1.refs_3_.refs_1_), channel_id=1, source_target_pairs={{0,8},{8,16},{16,24},{24,0},{1,9},{9,17},{17,25},{25,1},{2,10},{10... | collective-permute-start | bytes 442376 | tf_op jit(solution)/shard_map/ppermute | solution.py:830
  361.1 13.0 %collective-permute-start.29 = (bf16[384,768]{1,0:T(8,128)(2,1)}, bf16[384,768]{1,0:T(8,128)(2,1)S(1)}, u32[]{:S(2)}, u32[]{:S(2)}) collective-permute-start(bf16[384,768]{1,0:T(8,128)(2,1)} %dense_fifth.1.refs_1_.refs_3_), channel_id=1, source_target_pairs={{0,4},{4,0},{1,5},{5,1},{2,6},{6,2},{3,7},{7,3},{8,12},{12,8},{9,1... | collective-permute-start | bytes 1769480 | tf_op jit(solution)/shard_map/ppermute | solution.py:824
  363.4 3.3 copy-start.1
  374.1 0.8 copy-start.8
  (10 other events, 7.3 us)
Sparse Core Ops, SparseCore 0:
  90.7 59.3 all-gather.6
  152.6 74.7 all-gather.10
  230.2 53.8 all-gather.8

commit v7 on v6

--- a/solution.py
+++ b/solution.py
@@ -958,7 +958,7 @@
         [qkv_weight.transpose(1, 2, 0).reshape(3 * local_width, width), out_weight], axis=0
     )
     if full:
-        (weight,) = ordered([weight], [shared_cot])
+        (weight,) = ordered([weight], [mod])
     across = links.to_side(weight)
     near_shard = links.to_core(weight)
     if full:
@@ -979,6 +979,15 @@
         tokens, mod, router_t, pairs, shards, local_width, links.dp if full else 1
     )
     feed = (shared_up, shared_down, expert_up, expert_down)
+
+    def small_grads(small_all):
+        condition_all = small_all[:, 6].astype(bf16)
+        mod_grad = lax.dynamic_slice_in_dim(small_all[:, 0:6], me * local_width, local_width, axis=2)
+        ada_grad = jnp.einsum(
+            "id,icf->dcf", condition_all.astype(f32), mod_grad, precision=lax.Precision.HIGHEST
+        )
+        return ada_grad, jnp.sum(mod_grad, axis=0), jnp.sum(small_all[:, 8:16], axis=0).T
+
     backward = functools.partial(
         attention_backward, cond=own_condition, tokens=tokens, cotangent=cotangent, mod=mod, router_t=router_t,
         pairs=pairs, attn_in=attn_in, qkv=qkv, context=context, attn_out=attn_out, ext=ext, shards=shards,
@@ -1036,10 +1045,10 @@
             shared_last_kernel, "shared_last", [(shared_up.shape, f32), (shared_down.shape, f32)],
             [*shared, shared_more], after=[step], moved=12 * 10**6,
         )
-        routed = routed_grads([slots], expert_up, expert_down, routed, after=[shared[0]], span=(3, members))
-        step = dense.send([routed[0]])
-        qkv_grad, out_grad = dense.send([step])
-        (small_all,) = ordered([small_all], [routed[0]])
+        ada_grad, ada_bias_grad, router_grad = small_grads(ordered([small_all], [shared[0]])[0])
+        step = dense.send([shared[0], ada_grad.transpose(1, 2, 0)])
+        routed = routed_grads([slots], expert_up, expert_down, routed, after=[step], span=(3, members))
+        qkv_grad, out_grad = dense.send([routed[0]])
         routes_all = jnp.concatenate(
             [value[..., PATCHES, : TOPK * PATCHES].reshape(-1, TOPK * PATCHES) for value in (ext_mine, ext_near, exts)],
             axis=0,
@@ -1076,14 +1085,8 @@
         dense = lax.psum_scatter(grads, "tensor", scatter_dimension=0, tiled=True)[0]
         dense = lax.psum(dense, ("dp", "expert")).astype(f32)
         qkv_grad, out_grad = dense[: 3 * local_width], dense[3 * local_width :]
-
-    condition_all = small_all[:, 6].astype(bf16)
-    mod_grad = lax.dynamic_slice_in_dim(small_all[:, 0:6], me * local_width, local_width, axis=2)
-    ada_grad = jnp.einsum(
-        "id,icf->dcf", condition_all.astype(f32), mod_grad, precision=lax.Precision.HIGHEST
-    )
-    ada_bias_grad = jnp.sum(mod_grad, axis=0)
-    router_grad = jnp.sum(small_all[:, 8:16], axis=0).T
+        ada_grad, ada_bias_grad, router_grad = small_grads(small_all)
+
     counts = jnp.sum(
         (routes_all[:, :, None] == jnp.arange(EXPERTS).astype(routes_all.dtype)).astype(jnp.int32),
         axis=(0, 1),

time: 390 us -> 387 us (level)
  transfers between devices with their start and end apart: 36 -> 36, of which waited for: 14 -> 13; matrix products, arithmetic and copies ran while one was open for 5% -> 5% of each run, Pallas kernels for 61% -> 61%
where the time goes in v7:
time: 387 us; the launch traced here: 382 us
  Pallas kernels  243 us (63%)
  waiting for transfers between devices  53.8 us (14%)
  starting transfers between devices  42.6 us (11%)
  between operations  14.3 us (4%)
  local copies, waits for them, and re-layouts  14.1 us (4%)
  other arithmetic  8.87 us (2%)
  matrix products  5.43 us (1%)
    pallas_call x28, Pallas kernels, launch(): pl.pallas_call(body, out_shape=tuple((jax.ShapeDtypeStruct(*out) for out...  243 us
    ppermute x9, waiting for transfers between devices, to_other(): return lax.ppermute(value, 'expert', self.other)  21.2 us
    ppermute x8, waiting for transfers between devices, to_side(): return lax.ppermute(value, 'tensor', self.side)  18.4 us
    ppermute x9, starting transfers between devices, to_other(): return lax.ppermute(value, 'expert', self.other)  13.9 us
    all_to_all x2, starting transfers between devices, column(): return lax.all_to_all(copies, 'dp', split_axis=0, concat_axis=0)  10.1 us
    ppermute x6, starting transfers between devices, along(): lax.ppermute(value, 'dp', [(i, (i + hop) % self.dp) for i in range(self.d...  8.4 us
  transfers between devices with their start and end apart: 36, of which 13 were waited for; matrix products, arithmetic and copies ran while one was open for 5% of the time, Pallas kernels for 61%

profile of v7, /device:TPU:0, one launch (start us, length us, event | category | flops | bytes accessed | tf_op | source)
XLA Modules:
  0.0 382.2 jit_solution(17546505391271192566)
XLA Ops:
  8.1 2.0 convolution_add_fusion
  10.8 4.2 %all-to-all-start = ((f32[4,6,192]{2,1,0:T(8,128)}), f32[4,6,192]{2,1,0:T(8,128)S(1)}, u32[]{:S(2)}, u32[]{:S(2)}) async-start(f32[4,6,192]{2,1,0:T(8,128)} %copy.43), calls=%async_computation | async-start | bytes 65536 | tf_op jit(solution)/shard_map/all_to_all | solution.py:953
  15.0 2.1 pad_maximum_fusion.refs_0_
  17.1 1.8 all-to-all-done
  20.0 2.1 collective-permute-start.2
  23.3 5.0 %all-to-all-start.1 = ((bf16[4,256,768]{2,1,0:T(8,128)(2,1)}), bf16[4,256,768]{2,1,0:T(8,128)(2,1)}, u32[]{:S(2)}, u32[]{:S(2)}) async-start(bf16[4,256,768]{2,1,0:T(8,128)(2,1)} %broadcast_in_dim.6), calls=%async_computation.1 | async-start | bytes 3145728 | tf_op jit(solution)/shard_map/all_to_all | solution.py:833
  28.3 2.9 collective-permute-done.2.refs_1_
  31.2 16.3 %collective-permute-done.1.refs_0_ = bf16[768,768]{1,0:T(8,128)(2,1)} collective-permute-done((bf16[768,768]{1,0:T(8,128)(2,1)}, bf16[768,768]{1,0:T(8,128)(2,1)}, u32[]{:S(2)}, u32[]{:S(2)}) %collective-permute-start.1) | collective-permute-done | bytes 1179680 | tf_op jit(solution)/shard_map/ppermute | solution.py:821
  50.7 8.0 %attention_forward.1 = (bf16[256,768]{1,0:T(8,128)(2,1)}, bf16[3,256,768]{2,1,0:T(8,128)(2,1)}, bf16[256,768]{1,0:T(8,128)(2,1)}, f32[256,768]{1,0:T(8,128)}, bf...) custom-call(bf16[256,768]{1,0:T(8,128)(2,1)} %refs_5_.1, f32[6,768]{1,0:T(8,128)} %squeeze.10.refs_1_.refs_2_.refs_7_, ...), custom_call_target="tpu_custom_call" | custom-call | flops 5000000000 | bytes 9000000 | tf_op jit(solution)/shard_map/attention_forward/pallas_call | solution.py:89
  58.7 2.0 collective-permute-start.5
  62.8 8.6 %collective-permute-done.5.refs_2_ = bf16[272,768]{1,0:T(8,128)(2,1)S(1)} collective-permute-done((bf16[272,768]{1,0:T(8,128)(2,1)}, bf16[272,768]{1,0:T(8,128)(2,1)S(1)}, u32[]{:S(2)}, u32[]{:S(2)}) %collective-permute-start.5) | collective-permute-done | bytes 417824 | tf_op jit(solution)/shard_map/ppermute | solution.py:824
  72.3 1.9 collective-permute-start.7
  74.8 8.8 %collective-permute-done.7.refs_4_ = bf16[128,768]{1,0:T(8,128)(2,1)} collective-permute-done((bf16[128,768]{1,0:T(8,128)(2,1)S(1)}, bf16[128,768]{1,0:T(8,128)(2,1)}, u32[]{:S(2)}, u32[]{:S(2)}) %collective-permute-start.7) | collective-permute-done | bytes 196640 | tf_op jit(solution)/shard_map/ppermute | solution.py:824
  83.6 2.6 assemble.1.refs_6_.refs_1_.refs_2_.refs_0_
  86.2 4.1 %pick_both.1 = (bf16[3,256,768]{2,1,0:T(8,128)(2,1)}, bf16[4,256,768]{2,1,0:T(8,128)(2,1)}) custom-call(s32[3]{0:T(128)} %pad_add_fusion.1.refs_0_, bf16[256,768]{1,0:T(8,128)(2,1)} %copy-done, bf16[256,768]{1,0:T(8,128)(2,1)} %collective-permute-done.8.refs_2_, bf16[256,768]{1,0:T(8,128)(2,1)} %get-tuple-element.68.refs_3_, ...), custom_call_target="tpu_custom_call" | custom-call | bytes 5000000 | tf_op jit(solution)/shard_map/pick_both/pallas_call | solution.py:89
  90.9 5.1 %all-to-all-start.2 = ((bf16[4,272,768]{2,1,0:T(8,128)(2,1)}), bf16[4,272,768]{2,1,0:T(8,128)(2,1)}, u32[]{:S(2)}, u32[]{:S(2)}) async-start(bf16[4,272,768]{2,1,0:T(8,128)(2,1)} %ordered.8), calls=%async_computation.2 | async-start | bytes 3342336 | tf_op jit(solution)/shard_map/all_to_all | solution.py:833
  96.5 36.5 %experts_both.1 = (bf16[4,528,768]{2,1,0:T(8,128)(2,1)}, bf16[4,528,768]{2,1,0:T(8,128)(2,1)}) custom-call(s32[1]{0:T(128)} %bitcast.refs_0_, bf16[4,272,768]{2,1,0:T(8,128)(2,1)} %assemble.1.refs_6_.refs_1_.refs_2_.refs_0_, bf16[4,272,768]{2,1,0:T(8,128)(2,1)} %assemble.1.refs_6_.refs_1_.refs_2_.refs_0_, ...), custom_call_target="tpu_custom_call" | custom-call | flops 30000001024 | bytes 30000000 | tf_op jit(solution)/shard_map/experts_both/pallas_call | solution.py:89
  133.1 2.3 all-to-all-done.2.refs_1_
  135.4 2.7 pick.1.refs_2_
  139.1 5.5 %collective-permute-done.12.refs_1_ = bf16[4,528,768]{2,1,0:T(8,128)(2,1)} collective-permute-done((bf16[4,528,768]{2,1,0:T(8,128)(2,1)}, bf16[4,528,768]{2,1,0:T(8,128)(2,1)}, u32[]{:S(2)}, u32[]{:S(2)}) %collective-permute-start.12) | collective-permute-done | bytes 3244064 | tf_op jit(solution)/shard_map/ppermute | solution.py:818
  144.6 3.3 plane_first.1
  148.5 2.2 collective-permute-start.14
  150.7 7.4 %dispatch.1 = (bf16[4,640,768]{2,1,0:T(8,128)(2,1)}, bf16[4,640,768]{2,1,0:T(8,128)(2,1)}) custom-call(s32[1]{0:T(128)} %bitcast.refs_0_, bf16[4,272,768]{2,1,0:T(8,128)(2,1)} %assemble.1.refs_6_.refs_1_.refs_2_.refs_0_, bf16[4,272,768]{2,1,0:T(8,128)(2,1)} %assemble.1.refs_6_.refs_1_.refs_2_.refs_0_, ...), custom_call_target="tpu_custom_call" | custom-call | flops 8000000000 | bytes 16000000 | tf_op jit(solution)/shard_map/dispatch/pallas_call | solution.py:89
  158.1 20.7 %weight_grads.5 = (f32[4,768,768]{2,1,0:T(8,128)}, f32[4,768,768]{2,1,0:T(8,128)}) custom-call(bf16[4,640,768]{2,1,0:T(8,128)(2,1)} %get-tuple-element.76.refs_0_, bf16[4,640,768]{2,1,0:T(8,128)(2,1)} %get-tuple-element.77.refs_1_, bf16[4,768,768]{2,1,0:T(8,128)(2,1)} %refs_2_.9, bf16[4,768,768]{2,1,0:T(8,128)(2,1)} %refs_3_.9), custom_call_target="tpu_custom_call" | custom-call | flops 18119393280 | bytes 7864320 | tf_op jit(solution)/shard_map/weight_grads/pallas_call | solution.py:89
  179.7 4.9 %plane_second.1 = (f32[256,768]{1,0:T(8,128)}, f32[272,768]{1,0:T(8,128)}, bf16[256,768]{1,0:T(8,128)(2,1)}, bf16[272,768]{1,0:T(8,128)(2,1)}) custom-call(bf16[4,528,768]{2,1,0:T(8,128)(2,1)} %get-tuple-element.71.refs_2_.refs_0_, bf16[4,528,768]{2,1,0:T(8,128)(2,1)} %collective-permute-done.12.refs_1_, ...), custom_call_target="tpu_custom_call" | custom-call | bytes 7000000 | tf_op jit(solution)/shard_map/plane_second/pallas_call | solution.py:89
  185.5 16.9 %weight_grads.6 = (f32[1,768,768]{2,1,0:T(8,128)}, f32[1,768,768]{2,1,0:T(8,128)}) custom-call(bf16[4,272,768]{2,1,0:T(8,128)(2,1)} %assemble.1.refs_6_.refs_1_.refs_2_.refs_0_, bf16[4,272,768]{2,1,0:T(8,128)(2,1)} %collective-permute-done.10.refs_4_.refs_5_.refs_1_, bf16[4,256,768]{2,1,0:T(8,128)(2,1)} %get-tuple-element.69.refs_3_.refs_2_, ...), custom_call_target="tpu_custom_call" | custom-call | flops 14495514624 | bytes 6291456 | tf_op jit(solution)/shard_map/weight_grads/pallas_call | solution.py:89
  203.2 1.8 collective-permute-done.16.refs_3_
  205.8 16.4 %attention_backward.1 = (bf16[256,768]{1,0:T(8,128)(2,1)}, f32[256,768]{1,0:T(8,128)}, f32[16,768]{1,0:T(8,128)}, bf16[2,768,768]{2,1,0:T(8,128)(2,1)}, bf16[2,768,768]{2,1,0:T(8,128)(2,1)}) custom-call(f32[256,768]{1,0:T(8,128)} %get-tuple-element.79.refs_6_.refs_0_, bf16[256,768]{1,0:T(8,128)(2,1)} %copy-done.20, f32[272,768]{1,0:T(8,128)} %get-tuple-element.81.refs_2_, ...), custom_call_target="tpu_custom_call" | custom-call | flops 10000000000 | bytes 16000000 | tf_op jit(solution)/shard_map/attention_backward/pallas_call | solution.py:89
  224.4 2.9 all-gather.11.cloned.1.call-done
  227.3 19.0 %shared_grads_other.1 = (f32[768,768]{1,0:T(8,128)}, f32[768,768]{1,0:T(8,128)}, bf16[2,768,768]{2,1,0:T(8,128)(2,1)}) custom-call(bf16[8,3,272,768]{3,2,1,0:T(8,128)(2,1)} %bitcast.45, bf16[8,3,256,768]{3,2,1,0:T(8,128)(2,1)} %bitcast.49, bf16[768,768]{1,0:T(8,128)(2,1)} %refs_2_.6, bf16[768,768]{1,0:T(8,128)(2,1)} %refs_3_.6, ...), custom_call_target="tpu_custom_call" | custom-call | flops 14495514624 | bytes 6291456 | tf_op jit(solution)/shard_map/shared_grads_other/pallas_call | solution.py:89
  246.3 3.4 dense_first.1
  251.4 18.6 %dispatch_hops.1 = (bf16[4,1920,768]{2,1,0:T(8,128)(2,1)}, bf16[4,1920,768]{2,1,0:T(8,128)(2,1)}) custom-call(s32[1]{0:T(128)} %bitcast.refs_0_, bf16[8,3,272,768]{3,2,1,0:T(8,128)(2,1)} %bitcast.46, bf16[8,3,256,768]{3,2,1,0:T(8,128)(2,1)} %bitcast.50, bf16[384,768]{1,0:T(8,128)(2,1)} %get-tuple-element.97.refs_3_), custom_call_target="tpu_custom_call" | custom-call | flops 24000000000 | bytes 48000000 | tf_op jit(solution)/shard_map/dispatch_hops/pallas_call | solution.py:89
  272.7 4.2 %dense_second.1 = (bf16[192,768]{1,0:T(8,128)(2,1)}, bf16[192,768]{1,0:T(8,128)(2,1)}, f32[192,768]{1,0:T(8,128)}, f32[192,768]{1,0:T(8,128)}) custom-call(s32[2]{0:T(128)} %pad_add_fusion.2.refs_0_, bf16[2,768,768]{2,1,0:T(8,128)(2,1)} %get-tuple-element.95.refs_1_, bf16[2,768,768]{2,1,0:T(8,128)(2,1)} %collective-permute-done.18.refs_2_, ...), custom_call_target="tpu_custom_call" | custom-call | bytes 5000000 | tf_op jit(solution)/shard_map/dense_second/pallas_call | solution.py:89
  277.0 1.9 collective-permute-start.21
  279.5 26.8 %weight_grads.7 = (f32[4,768,768]{2,1,0:T(8,128)}, f32[4,768,768]{2,1,0:T(8,128)}) custom-call(bf16[4,1920,768]{2,1,0:T(8,128)(2,1)} %get-tuple-element.99.refs_5_.refs_0_, bf16[4,1920,768]{2,1,0:T(8,128)(2,1)} %get-tuple-element.104.refs_1_, bf16[4,768,768]{2,1,0:T(8,128)(2,1)} %refs_2_.9, ...), custom_call_target="tpu_custom_call", output_to_operand_aliasing={{0}: (4, {}), {1}: (5, {})} | custom-call | flops 27179089920 | bytes 11796480 | tf_op jit(solution)/shard_map/weight_grads/pallas_call | solution.py:89
  307.2 2.4 dense_third.1
  309.6 2.0 collective-permute-start.23
  311.6 2.8 collective-permute-start.25
  314.4 16.6 %weight_grads.8 = (f32[4,768,768]{2,1,0:T(8,128)}, f32[4,768,768]{2,1,0:T(8,128)}) custom-call(bf16[4,1920,768]{2,1,0:T(8,128)(2,1)} %get-tuple-element.99.refs_5_.refs_0_, bf16[4,1920,768]{2,1,0:T(8,128)(2,1)} %get-tuple-element.104.refs_1_, bf16[4,768,768]{2,1,0:T(8,128)(2,1)} %refs_2_.9, ...), custom_call_target="tpu_custom_call", output_to_operand_aliasing={{0}: (4, {}), {1}: (5, {})} | custom-call | flops 13589544960 | bytes 5898240 | tf_op jit(solution)/shard_map/weight_grads/pallas_call | solution.py:89
  331.7 1.9 dense_fourth.1.refs_3_.refs_1_
  333.6 2.0 collective-permute-start.28
  335.6 1.6 collective-permute-start.26
  337.2 5.5 %shared_last.1 = (f32[768,768]{1,0:T(8,128)}, f32[768,768]{1,0:T(8,128)}) custom-call(f32[768,768]{1,0:T(8,128)} %get-tuple-element.92.refs_0_, f32[768,768]{1,0:T(8,128)} %get-tuple-element.93.refs_1_, bf16[2,768,768]{2,1,0:T(8,128)(2,1)} %collective-permute-done.17.refs_2_, bf16[96,768]{1,0:T(8,128)(2,1)} %dense_fourth.1.refs_3_.refs_1_), custom_call_target="tpu_custom_call" | custom-call | bytes 12000000 | tf_op jit(solution)/shard_map/shared_last/pallas_call | solution.py:89
  345.8 3.4 fusion
  350.0 2.0 dense_fifth.1.refs_6_.refs_1_
  353.4 16.4 %weight_grads.9 = (f32[4,768,768]{2,1,0:T(8,128)}, f32[4,768,768]{2,1,0:T(8,128)}) custom-call(bf16[4,1920,768]{2,1,0:T(8,128)(2,1)} %get-tuple-element.99.refs_5_.refs_0_, bf16[4,1920,768]{2,1,0:T(8,128)(2,1)} %get-tuple-element.104.refs_1_, bf16[4,768,768]{2,1,0:T(8,128)(2,1)} %refs_2_.9, ...), custom_call_target="tpu_custom_call", output_to_operand_aliasing={{0}: (4, {}), {1}: (5, {})} | custom-call | flops 13589544960 | bytes 5898240 | tf_op jit(solution)/shard_map/weight_grads/pallas_call | solution.py:89
  369.9 1.8 slice_reduce_fusion
  372.5 2.9 dense_last.1
  (131 shorter events, 31.6 us)
Async XLA Ops:
  7.2 7.8 %copy-start.4 = (bf16[768,3,192]{0,2,1:T(8,128)(2,1)S(1)}, bf16[768,3,192]{0,2,1:T(8,128)(2,1)}, u32[]{:S(2)}) copy-start(bf16[768,3,192]{0,2,1:T(8,128)(2,1)} %param.19) | copy-start | bytes 2654212
  10.8 8.2 %all-to-all-start = ((f32[4,6,192]{2,1,0:T(8,128)}), f32[4,6,192]{2,1,0:T(8,128)S(1)}, u32[]{:S(2)}, u32[]{:S(2)}) async-start(f32[4,6,192]{2,1,0:T(8,128)} %copy.43), calls=%async_computation | async-start | bytes 65536 | tf_op jit(solution)/shard_map/all_to_all | solution.py:953
  15.0 5.0 %copy-start.8 = (bf16[256,768]{1,0:T(8,128)(2,1)S(1)}, bf16[256,768]{1,0:T(8,128)(2,1)}, u32[]{:S(2)}) copy-start(bf16[256,768]{1,0:T(8,128)(2,1)} %refs_6_.1) | copy-start | bytes 1179652
  19.6 27.9 %collective-permute-start.1 = (bf16[768,768]{1,0:T(8,128)(2,1)}, bf16[768,768]{1,0:T(8,128)(2,1)}, u32[]{:S(2)}, u32[]{:S(2)}) collective-permute-start(bf16[768,768]{1,0:T(8,128)(2,1)} %ordered.5.refs_4_.refs_15_), channel_id=1, source_target_pairs={{0,2},{1,3},{2,0},{3,1},{4,6},{5,7},{6,4},{7,5},{8,10},{9,11},{10,... | collective-permute-start | bytes 3538952 | tf_op jit(solution)/shard_map/ppermute | solution.py:821
  20.0 28.2 %copy-start = (bf16[256,768]{1,0:T(8,128)(2,1)}, bf16[256,768]{1,0:T(8,128)(2,1)S(1)}, u32[]{:S(2)}) copy-start(bf16[256,768]{1,0:T(8,128)(2,1)S(1)} %multiply_convert_fusion.refs_1_) | copy-start | bytes 1179652
  20.0 11.2 %collective-permute-start.2 = (bf16[256,768]{1,0:T(8,128)(2,1)S(1)}, bf16[256,768]{1,0:T(8,128)(2,1)S(1)}, u32[]{:S(2)}, u32[]{:S(2)}) collective-permute-start(bf16[256,768]{1,0:T(8,128)(2,1)S(1)} %multiply_convert_fusion.refs_1_), channel_id=1, source_target_pairs={{0,4},{4,0},{1,5},{5,1},{2,6},{6,2},{3,7},{7,3},{8,12},{12,8},{9,1... | collective-permute-start | bytes 1179656 | tf_op jit(solution)/shard_map/ppermute | solution.py:824
  23.3 24.2 %copy-start.17 = (s32[256,2]{0,1:T(2,128)S(1)}, s32[256,2]{0,1:T(2,128)}, u32[]{:S(2)}) copy-start(s32[256,2]{0,1:T(2,128)} %param.27) | copy-start | bytes 6148
  23.3 24.2 %copy-start.18 = (s32[256,2]{0,1:T(2,128)S(1)}, s32[256,2]{0,1:T(2,128)}, u32[]{:S(2)}) copy-start(s32[256,2]{0,1:T(2,128)} %param.26) | copy-start | bytes 6148
  23.3 62.9 %all-to-all-start.1 = ((bf16[4,256,768]{2,1,0:T(8,128)(2,1)}), bf16[4,256,768]{2,1,0:T(8,128)(2,1)}, u32[]{:S(2)}, u32[]{:S(2)}) async-start(bf16[4,256,768]{2,1,0:T(8,128)(2,1)} %broadcast_in_dim.6), calls=%async_computation.1 | async-start | bytes 3145728 | tf_op jit(solution)/shard_map/all_to_all | solution.py:833
  28.3 157.2 %all-gather.7.cloned.1.call-start = ((), (), s32[]{:S(2)}) async-start(), calls=%async_computation.3 | async-start | bytes 10616832 | tf_op jit(solution)/shard_map/all_gather | solution.py:1014
  28.3 21.2 %collective-permute-start = (bf16[768,768]{1,0:T(8,128)(2,1)}, bf16[768,768]{1,0:T(8,128)(2,1)}, u32[]{:S(2)}, u32[]{:S(2)}) collective-permute-start(bf16[768,768]{1,0:T(8,128)(2,1)} %ordered.5.refs_4_.refs_15_), channel_id=1, source_target_pairs={{0,1},{1,0},{2,3},{3,2},{4,5},{5,4},{6,7},{7,6},{8,9},{9,8},{10,11... | collective-permute-start | bytes 3538952 | tf_op jit(solution)/shard_map/ppermute | solution.py:818
  31.2 16.3 %copy-start.3 = (bf16[256,768]{1,0:T(8,128)(2,1)}, bf16[256,768]{1,0:T(8,128)(2,1)S(1)}, u32[]{:S(2)}) copy-start(bf16[256,768]{1,0:T(8,128)(2,1)S(1)} %collective-permute-done.2.refs_1_) | copy-start | bytes 1179652
  47.6 3.2 collective-permute-start.3
  48.9 12.4 %collective-permute-start.8 = (bf16[256,768]{1,0:T(8,128)(2,1)}, bf16[256,768]{1,0:T(8,128)(2,1)}, u32[]{:S(2)}, u32[]{:S(2)}) collective-permute-start(bf16[256,768]{1,0:T(8,128)(2,1)} %ordered.7), channel_id=1, source_target_pairs={{0,2},{1,3},{2,0},{3,1},{4,6},{5,7},{6,4},{7,5},{8,10},{9,11},{10,... | collective-permute-start | bytes 1179656 | tf_op jit(solution)/shard_map/ppermute | solution.py:821
  58.7 12.7 %collective-permute-start.5 = (bf16[272,768]{1,0:T(8,128)(2,1)}, bf16[272,768]{1,0:T(8,128)(2,1)S(1)}, u32[]{:S(2)}, u32[]{:S(2)}) collective-permute-start(bf16[272,768]{1,0:T(8,128)(2,1)} %get-tuple-element.67.refs_0_.refs_14_), channel_id=1, source_target_pairs={{0,4},{4,0},{1,5},{5,1},{2,6},{6,2},{3,7},{7,3},{8,12},{12,8},{9,1... | collective-permute-start | bytes 1253384 | tf_op jit(solution)/shard_map/ppermute | solution.py:824
  60.7 11.6 %collective-permute-start.4 = (bf16[272,768]{1,0:T(8,128)(2,1)}, bf16[272,768]{1,0:T(8,128)(2,1)S(1)}, u32[]{:S(2)}, u32[]{:S(2)}) collective-permute-start(bf16[272,768]{1,0:T(8,128)(2,1)} %get-tuple-element.67.refs_0_.refs_14_), channel_id=1, source_target_pairs={{0,2},{1,3},{2,0},{3,1},{4,6},{5,7},{6,4},{7,5},{8,10},{9,11},{10,... | collective-permute-start | bytes 1253384 | tf_op jit(solution)/shard_map/ppermute | solution.py:821
  61.3 24.9 %collective-permute-start.9 = (bf16[256,768]{1,0:T(8,128)(2,1)}, bf16[256,768]{1,0:T(8,128)(2,1)}, u32[]{:S(2)}, u32[]{:S(2)}) collective-permute-start(bf16[256,768]{1,0:T(8,128)(2,1)} %collective-permute-done.8.refs_2_), channel_id=1, source_target_pairs={{0,4},{4,0},{1,5},{5,1},{2,6},{6,2},{3,7},{7,3},{8,12},{12,8},{9,1... | collective-permute-start | bytes 1179656 | tf_op jit(solution)/shard_map/ppermute | solution.py:824
  71.4 12.2 %copy-start.1 = (bf16[272,768]{1,0:T(8,128)(2,1)}, bf16[272,768]{1,0:T(8,128)(2,1)S(1)}, u32[]{:S(2)}) copy-start(bf16[272,768]{1,0:T(8,128)(2,1)S(1)} %collective-permute-done.5.refs_2_) | copy-start | bytes 1253380
  71.4 12.2 %collective-permute-start.6 = (bf16[144,768]{1,0:T(8,128)(2,1)S(1)}, bf16[144,768]{1,0:T(8,128)(2,1)}, u32[]{:S(2)}, u32[]{:S(2)}) collective-permute-start(bf16[144,768]{1,0:T(8,128)(2,1)S(1)} %slice.39), channel_id=1, source_target_pairs={{0,2},{1,3},{2,0},{3,1},{4,6},{5,7},{6,4},{7,5},{8,10},{9,11},{10,... | collective-permute-start | bytes 663560 | tf_op jit(solution)/shard_map/ppermute | solution.py:821
  72.3 11.3 %copy-start.2 = (bf16[272,768]{1,0:T(8,128)(2,1)}, bf16[272,768]{1,0:T(8,128)(2,1)S(1)}, u32[]{:S(2)}) copy-start(bf16[272,768]{1,0:T(8,128)(2,1)S(1)} %collective-permute-done.4.refs_1_) | copy-start | bytes 1253380
  72.3 11.3 %collective-permute-start.7 = (bf16[128,768]{1,0:T(8,128)(2,1)S(1)}, bf16[128,768]{1,0:T(8,128)(2,1)}, u32[]{:S(2)}, u32[]{:S(2)}) collective-permute-start(bf16[128,768]{1,0:T(8,128)(2,1)S(1)} %slice.40), channel_id=1, source_target_pairs={{0,4},{4,0},{1,5},{5,1},{2,6},{6,2},{3,7},{7,3},{8,12},{12,8},{9,1... | collective-permute-start | bytes 589832 | tf_op jit(solution)/shard_map/ppermute | solution.py:824
  90.3 6.2 %collective-permute-start.10 = (bf16[4,272,768]{2,1,0:T(8,128)(2,1)}, bf16[4,272,768]{2,1,0:T(8,128)(2,1)}, u32[]{:S(2)}, u32[]{:S(2)}) collective-permute-start(bf16[4,272,768]{2,1,0:T(8,128)(2,1)} %assemble.1.refs_6_.refs_1_.refs_2_.refs_0_), channel_id=1, source_target_pairs={{0,1},{1,0},{2,3},{3,2},{4,5},{5,4},{6,7},{7,6},{8,9},{9,8},{10,11... | collective-permute-start | bytes 5013512 | tf_op jit(solution)/shard_map/ppermute | solution.py:818
  90.4 6.1 %collective-permute-start.11 = (bf16[4,256,768]{2,1,0:T(8,128)(2,1)}, bf16[4,256,768]{2,1,0:T(8,128)(2,1)}, u32[]{:S(2)}, u32[]{:S(2)}) collective-permute-start(bf16[4,256,768]{2,1,0:T(8,128)(2,1)} %get-tuple-element.69.refs_3_.refs_2_), channel_id=1, source_target_pairs={{0,1},{1,0},{2,3},{3,2},{4,5},{5,4},{6,7},{7,6},{8,9},{9,8},{10,11... | collective-permute-start | bytes 4718600 | tf_op jit(solution)/shard_map/ppermute | solution.py:818
  90.9 44.5 %all-to-all-start.2 = ((bf16[4,272,768]{2,1,0:T(8,128)(2,1)}), bf16[4,272,768]{2,1,0:T(8,128)(2,1)}, u32[]{:S(2)}, u32[]{:S(2)}) async-start(bf16[4,272,768]{2,1,0:T(8,128)(2,1)} %ordered.8), calls=%async_computation.2 | async-start | bytes 3342336 | tf_op jit(solution)/shard_map/all_to_all | solution.py:833
  96.0 131.3 %all-gather.11.cloned.1.call-start = ((), (), s32[]{:S(2)}) async-start(), calls=%async_computation.5 | async-start | bytes 11280384 | tf_op jit(solution)/shard_map/all_gather | solution.py:841
  138.1 204.5 %all-gather.9.cloned.1.call-start = ((), (), s32[]{:S(2)}) async-start(), calls=%async_computation.4 | async-start | bytes 1622016 | tf_op jit(solution)/shard_map/all_gather | solution.py:1035
  138.4 6.2 %collective-permute-start.12 = (bf16[4,528,768]{2,1,0:T(8,128)(2,1)}, bf16[4,528,768]{2,1,0:T(8,128)(2,1)}, u32[]{:S(2)}, u32[]{:S(2)}) collective-permute-start(bf16[4,528,768]{2,1,0:T(8,128)(2,1)} %get-tuple-element.72), channel_id=1, source_target_pairs={{0,1},{1,0},{2,3},{3,2},{4,5},{5,4},{6,7},{7,6},{8,9},{9,8},{10,11... | collective-permute-start | bytes 9732104 | tf_op jit(solution)/shard_map/ppermute | solution.py:818
  147.9 30.8 %collective-permute-start.13 = (bf16[2,256,768]{2,1,0:T(8,128)(2,1)}, bf16[2,256,768]{2,1,0:T(8,128)(2,1)}, u32[]{:S(2)}, u32[]{:S(2)}) collective-permute-start(bf16[2,256,768]{2,1,0:T(8,128)(2,1)} %get-tuple-element.74.refs_7_), channel_id=1, source_target_pairs={{0,2},{1,3},{2,0},{3,1},{4,6},{5,7},{6,4},{7,5},{8,10},{9,11},{10,... | collective-permute-start | bytes 2359304 | tf_op jit(solution)/shard_map/ppermute | solution.py:821
  148.5 30.3 %collective-permute-start.14 = (bf16[2,272,768]{2,1,0:T(8,128)(2,1)}, bf16[2,272,768]{2,1,0:T(8,128)(2,1)S(1)}, u32[]{:S(2)}, u32[]{:S(2)}) collective-permute-start(bf16[2,272,768]{2,1,0:T(8,128)(2,1)} %get-tuple-element.75), channel_id=1, source_target_pairs={{0,4},{4,0},{1,5},{5,1},{2,6},{6,2},{3,7},{7,3},{8,12},{12,8},{9,1... | collective-permute-start | bytes 2506760 | tf_op jit(solution)/shard_map/ppermute | solution.py:824
  178.8 0.9 copy-start.5
  184.6 18.6 %collective-permute-start.15 = (bf16[256,768]{1,0:T(8,128)(2,1)}, bf16[256,768]{1,0:T(8,128)(2,1)S(1)}, u32[]{:S(2)}, u32[]{:S(2)}) collective-permute-start(bf16[256,768]{1,0:T(8,128)(2,1)} %get-tuple-element.80), channel_id=1, source_target_pairs={{0,4},{4,0},{1,5},{5,1},{2,6},{6,2},{3,7},{7,3},{8,12},{12,8},{9,1... | collective-permute-start | bytes 1179656 | tf_op jit(solution)/shard_map/ppermute | solution.py:824
  185.5 19.5 %collective-permute-start.16 = (bf16[272,768]{1,0:T(8,128)(2,1)}, bf16[272,768]{1,0:T(8,128)(2,1)S(1)}, u32[]{:S(2)}, u32[]{:S(2)}) collective-permute-start(bf16[272,768]{1,0:T(8,128)(2,1)} %get-tuple-element.82), channel_id=1, source_target_pairs={{0,2},{1,3},{2,0},{3,1},{4,6},{5,7},{6,4},{7,5},{8,10},{9,11},{10,... | collective-permute-start | bytes 1253384 | tf_op jit(solution)/shard_map/ppermute | solution.py:821
  203.2 1.8 copy-start.20
  222.2 24.2 %collective-permute-start.18 = (bf16[2,768,768]{2,1,0:T(8,128)(2,1)}, bf16[2,768,768]{2,1,0:T(8,128)(2,1)}, u32[]{:S(2)}, u32[]{:S(2)}) collective-permute-start(bf16[2,768,768]{2,1,0:T(8,128)(2,1)} %get-tuple-element.96), channel_id=1, source_target_pairs={{0,1},{1,0},{2,3},{3,2},{4,5},{5,4},{6,7},{7,6},{8,9},{9,8},{10,11... | collective-permute-start | bytes 7077896 | tf_op jit(solution)/shard_map/ppermute | solution.py:818
  246.2 90.9 %collective-permute-start.17 = (bf16[2,768,768]{2,1,0:T(8,128)(2,1)}, bf16[2,768,768]{2,1,0:T(8,128)(2,1)}, u32[]{:S(2)}, u32[]{:S(2)}) collective-permute-start(bf16[2,768,768]{2,1,0:T(8,128)(2,1)} %get-tuple-element.94.refs_3_), channel_id=1, source_target_pairs={{0,8},{8,0},{16,24},{24,16},{1,9},{9,1},{17,25},{25,17},{2,10},{10... | collective-permute-start | bytes 7077896 | tf_op jit(solution)/shard_map/ppermute | solution.py:827
  249.8 22.1 %collective-permute-start.20 = (bf16[2,192,768]{2,1,0:T(8,128)(2,1)}, bf16[2,192,768]{2,1,0:T(8,128)(2,1)S(1)}, u32[]{:S(2)}, u32[]{:S(2)}) collective-permute-start(bf16[2,192,768]{2,1,0:T(8,128)(2,1)} %get-tuple-element.98), channel_id=1, source_target_pairs={{0,4},{4,0},{1,5},{5,1},{2,6},{6,2},{3,7},{7,3},{8,12},{12,8},{9,1... | collective-permute-start | bytes 1769480 | tf_op jit(solution)/shard_map/ppermute | solution.py:824
  251.3 20.7 %collective-permute-start.19 = (bf16[384,768]{1,0:T(8,128)(2,1)}, bf16[384,768]{1,0:T(8,128)(2,1)}, u32[]{:S(2)}, u32[]{:S(2)}) collective-permute-start(bf16[384,768]{1,0:T(8,128)(2,1)} %get-tuple-element.97.refs_3_), channel_id=1, source_target_pairs={{0,2},{1,3},{2,0},{3,1},{4,6},{5,7},{6,4},{7,5},{8,10},{9,11},{10,... | collective-permute-start | bytes 1769480 | tf_op jit(solution)/shard_map/ppermute | solution.py:821
  271.9 0.8 copy-start.6
  277.0 29.4 %collective-permute-start.21 = (bf16[192,768]{1,0:T(8,128)(2,1)}, bf16[192,768]{1,0:T(8,128)(2,1)S(1)}, u32[]{:S(2)}, u32[]{:S(2)}) collective-permute-start(bf16[192,768]{1,0:T(8,128)(2,1)} %get-tuple-element.102), channel_id=1, source_target_pairs={{0,2},{1,3},{2,0},{3,1},{4,6},{5,7},{6,4},{7,5},{8,10},{9,11},{10,... | collective-permute-start | bytes 884744 | tf_op jit(solution)/shard_map/ppermute | solution.py:821
  278.9 27.5 %collective-permute-start.22 = (bf16[192,768]{1,0:T(8,128)(2,1)}, bf16[192,768]{1,0:T(8,128)(2,1)S(1)}, u32[]{:S(2)}, u32[]{:S(2)}) collective-permute-start(bf16[192,768]{1,0:T(8,128)(2,1)} %get-tuple-element.103), channel_id=1, source_target_pairs={{0,4},{4,0},{1,5},{5,1},{2,6},{6,2},{3,7},{7,3},{8,12},{12,8},{9,1... | collective-permute-start | bytes 884744 | tf_op jit(solution)/shard_map/ppermute | solution.py:824
  309.6 21.4 %collective-permute-start.23 = (bf16[96,768]{1,0:T(8,128)(2,1)}, bf16[96,768]{1,0:T(8,128)(2,1)S(1)}, u32[]{:S(2)}, u32[]{:S(2)}) collective-permute-start(bf16[96,768]{1,0:T(8,128)(2,1)} %get-tuple-element.108), channel_id=1, source_target_pairs={{0,8},{8,16},{16,24},{24,0},{1,9},{9,17},{17,25},{25,1},{2,10},{10... | collective-permute-start | bytes 442376 | tf_op jit(solution)/shard_map/ppermute | solution.py:830
  311.6 19.3 %collective-permute-start.24 = (bf16[96,768]{1,0:T(8,128)(2,1)}, bf16[96,768]{1,0:T(8,128)(2,1)S(1)}, u32[]{:S(2)}, u32[]{:S(2)}) collective-permute-start(bf16[96,768]{1,0:T(8,128)(2,1)} %get-tuple-element.109), channel_id=1, source_target_pairs={{0,16},{8,24},{16,0},{24,8},{1,17},{9,25},{17,1},{25,9},{2,18},{10... | collective-permute-start | bytes 442376 | tf_op jit(solution)/shard_map/ppermute | solution.py:830
  311.6 19.3 %collective-permute-start.25 = (bf16[96,768]{1,0:T(8,128)(2,1)}, bf16[96,768]{1,0:T(8,128)(2,1)S(1)}, u32[]{:S(2)}, u32[]{:S(2)}) collective-permute-start(bf16[96,768]{1,0:T(8,128)(2,1)} %get-tuple-element.110), channel_id=1, source_target_pairs={{0,24},{8,0},{16,8},{24,16},{1,25},{9,1},{17,9},{25,17},{2,26},{10... | collective-permute-start | bytes 442376 | tf_op jit(solution)/shard_map/ppermute | solution.py:830
  333.6 15.6 %collective-permute-start.28 = (bf16[96,768]{1,0:T(8,128)(2,1)}, bf16[96,768]{1,0:T(8,128)(2,1)S(1)}, u32[]{:S(2)}, u32[]{:S(2)}) collective-permute-start(bf16[96,768]{1,0:T(8,128)(2,1)} %dense_fourth.1.refs_3_.refs_1_), channel_id=1, source_target_pairs={{0,24},{8,0},{16,8},{24,16},{1,25},{9,1},{17,9},{25,17},{2,26},{10... | collective-permute-start | bytes 442376 | tf_op jit(solution)/shard_map/ppermute | solution.py:830
  335.6 13.6 %collective-permute-start.27 = (bf16[96,768]{1,0:T(8,128)(2,1)}, bf16[96,768]{1,0:T(8,128)(2,1)S(1)}, u32[]{:S(2)}, u32[]{:S(2)}) collective-permute-start(bf16[96,768]{1,0:T(8,128)(2,1)} %dense_fourth.1.refs_3_.refs_1_), channel_id=1, source_target_pairs={{0,16},{8,24},{16,0},{24,8},{1,17},{9,25},{17,1},{25,9},{2,18},{10... | collective-permute-start | bytes 442376 | tf_op jit(solution)/shard_map/ppermute | solution.py:830
  335.6 13.6 %collective-permute-start.26 = (bf16[96,768]{1,0:T(8,128)(2,1)}, bf16[96,768]{1,0:T(8,128)(2,1)S(1)}, u32[]{:S(2)}, u32[]{:S(2)}) collective-permute-start(bf16[96,768]{1,0:T(8,128)(2,1)} %dense_fourth.1.refs_3_.refs_1_), channel_id=1, source_target_pairs={{0,8},{8,16},{16,24},{24,0},{1,9},{9,17},{17,25},{25,1},{2,10},{10... | collective-permute-start | bytes 442376 | tf_op jit(solution)/shard_map/ppermute | solution.py:830
  352.0 19.6 %collective-permute-start.29 = (bf16[384,768]{1,0:T(8,128)(2,1)}, bf16[384,768]{1,0:T(8,128)(2,1)S(1)}, u32[]{:S(2)}, u32[]{:S(2)}) collective-permute-start(bf16[384,768]{1,0:T(8,128)(2,1)} %dense_fifth.1.refs_6_.refs_1_), channel_id=1, source_target_pairs={{0,4},{4,0},{1,5},{5,1},{2,6},{6,2},{3,7},{7,3},{8,12},{12,8},{9,1... | collective-permute-start | bytes 1769480 | tf_op jit(solution)/shard_map/ppermute | solution.py:824
  371.7 0.9 copy-start.7
  (9 other events, 6.5 us)
Sparse Core Ops, SparseCore 0:
  90.5 59.4 all-gather.6
  152.4 74.7 all-gather.10
  230.1 53.9 all-gather.8
